TPU v7x, 32 devices: a whole 2x2x4 slice. The times are simulated.
32 devices in a mesh: bucket: 4 (over z), seq: 8 (over y, x, core).
Axes of the slice: x: 2, y: 2, z: 4, core: 2. Of those that a mesh axis runs over, the one named last changes fastest.
Arguments:
- tokens: bfloat16 [4, 2112, 2048], P('bucket', 'seq'), may hold values from -6 to 6
- lengths: int32 [4, 4], P('bucket'), may hold values from 1 to 2108, as said below
- norm_gain: bfloat16 [2048], P(('bucket', 'seq')), may hold values from 0.099609375 to 1.8984375
- in_proj: bfloat16 [2048, 5120], P(('bucket', 'seq')), may hold values from -0.125 to 0.125
- conv_weight: bfloat16 [2560, 4], P(('bucket', 'seq')), may hold values from -3 to 3
- conv_bias: bfloat16 [2560], P(('bucket', 'seq')), may hold values from -3 to 3
- gate_weight: bfloat16 [2560, 320], P(('bucket', 'seq')), may hold values from -0.5 to 0.5
- gate_bias: bfloat16 [2560, 2], P(('bucket', 'seq')), may hold values from -4 to 4
- decay: bfloat16 [2560], P(('bucket', 'seq')), as said below
- out_proj: bfloat16 [2560, 2048], P(('bucket', 'seq')), may hold values from -0.3125 to 0.3125
- mlp_gain: bfloat16 [2048], P(('bucket', 'seq')), may hold values from 0.099609375 to 1.8984375
- gate_up: bfloat16 [2048, 12288], P(('bucket', 'seq')), may hold values from -0.125 to 0.125
- down_proj: bfloat16 [6144, 2048], P(('bucket', 'seq')), may hold values from -0.15625 to 0.15625
- cotangent: bfloat16 [4, 2112, 2048], P('bucket', 'seq'), may hold values from -6 to 6
Outputs:
- mixed: bfloat16 [4, 2112, 2048], P('bucket', 'seq')
- token_grad: float32 [4, 2112, 2048], P('bucket', 'seq')
- norm_gain_grad: float32 [2048], P(('bucket', 'seq'))
- in_proj_grad: float32 [2048, 5120], P(('bucket', 'seq'))
- conv_weight_grad: float32 [2560, 4], P(('bucket', 'seq'))
- conv_bias_grad: float32 [2560], P(('bucket', 'seq'))
- gate_weight_grad: float32 [2560, 320], P(('bucket', 'seq'))
- gate_bias_grad: float32 [2560, 2], P(('bucket', 'seq'))
- decay_grad: float32 [2560], P(('bucket', 'seq'))
- out_proj_grad: float32 [2560, 2048], P(('bucket', 'seq'))
- mlp_gain_grad: float32 [2048], P(('bucket', 'seq'))
- gate_up_grad: float32 [2048, 12288], P(('bucket', 'seq'))
- down_proj_grad: float32 [6144, 2048], P(('bucket', 'seq'))
Inputs may be any that keep to these rules, and one draw needn't show every extreme that they name: Each bucket's 4 lengths are packed in order and sum to less than 2112; the rest of the bucket is padding. In every bucket one sequence, never the bucket's last, starts within the first 264 tokens and ends within the last 264 tokens. softplus(decay) lies between 0.09 / 2112 and 0.041.
All inputs are finite; a program needn't handle non-finite values.
Results may differ from a plain program's by a relative error of at most 0.0088.
Values may be sent and summed in bfloat16 or wider, within the bound.
No kernel may reach another device: no remote copies, remote signals or barrier semaphores. Data moves between devices by JAX's collectives and lax.ppermute only.
A program may use at most 512 MiB of HBM per device.

v0:
```python
from functools import partial

import jax
import jax.numpy as jnp
from jax import lax
from jax.sharding import PartitionSpec as P

NB = 16


norm_eps = 1e-06
gate_scale = 8.0


def from_behind(block, axis, distance):
    devices = range(lax.axis_size(axis))
    route = [(i - distance, i) for i in devices if i - distance in devices]
    return lax.ppermute(block, axis, route)


def entering(part, axis, combine, identity, reverse):
    count = lax.axis_size(axis)
    place = lax.axis_index(axis)
    ahead = count - 1 - place if reverse else place
    gathered = jax.tree.map(lambda a: lax.all_gather(a, axis), part)
    state = jax.tree.map(lambda a, e: jnp.zeros_like(a) + jnp.asarray(e, a.dtype), part, identity)

    def one(lap, state):
        source = count - 1 - lap if reverse else lap
        return combine(
            state, jax.tree.map(lambda a: lax.dynamic_index_in_dim(a, source, 0, False), gathered)
        )

    return lax.fori_loop(0, ahead, one, state)


def rms_scale(values, gain):
    return values * lax.rsqrt(jnp.mean(values * values, axis=1, keepdims=True) + norm_eps) * gain


def link(earlier, later):
    return (earlier[0] * later[0], later[0] * earlier[1] + later[1])


def segment_layout(lengths_row, positions):
    ends = jnp.cumsum(lengths_row)
    segment_ids = jnp.sum((positions[:, None] >= ends[None, :]).astype(jnp.int32), axis=1)
    segment_ids = jnp.where(positions < 0, -1, segment_ids)
    keep = (positions < ends[-1]).astype(jnp.float32)
    return (segment_ids, keep)


def lru_terms(conv_out, gate_a, gate_i, decay, starts):
    rate = jax.nn.softplus(decay)
    log_step = -gate_scale * jax.nn.sigmoid(gate_a) * rate
    decay_step = jnp.where(starts, 0.0, jnp.exp(log_step))
    scaling = jnp.where(starts, 1.0, jnp.sqrt(-jnp.expm1(2.0 * log_step)))
    return (decay_step, conv_out * jax.nn.sigmoid(gate_i) * scaling)


def gated_gelu(values, split):
    return jax.nn.gelu(values[:, :split]) * values[:, split:]


def contract_last(left, right):
    return lax.dot_general(
        left, right, (((1,), (1,)), ((), ())), preferred_element_type=jnp.float32
    )


def contract_first(left, right):
    return lax.dot_general(
        left, right, (((0,), (0,)), ((), ())), preferred_element_type=jnp.float32
    )


def row_product(left, right):
    return contract_first(left, right)


def on_device(
    tokens,
    lengths,
    norm_gain,
    in_proj,
    conv_weight,
    conv_bias,
    gate_weight,
    gate_bias,
    decay,
    out_proj,
    mlp_gain,
    gate_up,
    down_proj,
    cotangent,
):
    inputs = tokens[0].astype(jnp.float32)
    tok_rows = inputs.shape[0]
    width = in_proj.shape[1] // 2
    ff_width = gate_up.shape[1] // 2
    block_width = width // NB
    kernel = conv_weight.shape[1]
    rim_rows = kernel - 1
    (
        gain_one_all,
        proj_all,
        conv_all,
        conv_bias_all,
        gate_all,
        gate_bias_all,
        decay_all,
        out_all,
        gain_two_all,
    ) = (
        lax.all_gather(norm_gain, ("bucket", "seq"), axis=0, tiled=True),
        lax.all_gather(in_proj, ("bucket", "seq"), axis=0, tiled=True),
        lax.all_gather(conv_weight, ("bucket", "seq"), axis=0, tiled=True),
        lax.all_gather(conv_bias, ("bucket", "seq"), axis=0, tiled=True),
        lax.all_gather(gate_weight, ("bucket", "seq"), axis=0, tiled=True),
        lax.all_gather(gate_bias, ("bucket", "seq"), axis=0, tiled=True),
        lax.all_gather(decay, ("bucket", "seq"), axis=0, tiled=True),
        lax.all_gather(out_proj, ("bucket", "seq"), axis=0, tiled=True),
        lax.all_gather(mlp_gain, ("bucket", "seq"), axis=0, tiled=True),
    )
    seq_index = lax.axis_index("seq")
    positions = seq_index * tok_rows + jnp.arange(tok_rows, dtype=jnp.int32)
    lengths_row = lengths[0]
    segment_ids, keep = segment_layout(lengths_row, positions)
    back_ids = segment_layout(lengths_row, positions - 1)[0]
    starts = (segment_ids != back_ids)[:, None]
    normed, norm_pull = jax.vjp(rms_scale, inputs, gain_one_all.astype(jnp.float32))
    normed_low = normed.astype(jnp.bfloat16)
    projected = jnp.dot(normed_low, proj_all, preferred_element_type=jnp.float32)
    mixer_in = projected[:, :width].astype(jnp.bfloat16)
    branch = projected[:, width:]
    rim = from_behind(mixer_in[tok_rows - rim_rows :], "seq", 1)
    extended = jnp.concatenate([rim, mixer_in], axis=0)
    conv_float = conv_all.astype(jnp.float32)
    lagged_terms = []
    convolved = jnp.zeros((tok_rows, width), jnp.float32) + conv_bias_all.astype(jnp.float32)
    for offset in range(kernel):
        earlier_ids = segment_layout(lengths_row, positions - offset)[0]
        lagged = jnp.where(
            (earlier_ids == segment_ids)[:, None],
            extended[rim_rows - offset : rim_rows - offset + tok_rows].astype(jnp.float32),
            0.0,
        )
        lagged_terms.append(lagged)
        convolved = convolved + lagged * conv_float[:, offset]
    conv_out = convolved.astype(jnp.bfloat16)
    gates = jnp.einsum(
        "tnc,ncd->tnd",
        conv_out.reshape(tok_rows, NB, block_width),
        gate_all.reshape(NB, block_width, 2 * block_width),
        preferred_element_type=jnp.float32,
    )
    gate_bias_float = gate_bias_all.astype(jnp.float32)
    gate_a = gates[:, :, :block_width].reshape(tok_rows, width) + gate_bias_float[:, 0]
    gate_i = gates[:, :, block_width:].reshape(tok_rows, width) + gate_bias_float[:, 1]
    (decay_step, normalized), lru_pull = jax.vjp(
        partial(lru_terms, starts=starts),
        conv_out.astype(jnp.float32),
        gate_a,
        gate_i,
        decay_all.astype(jnp.float32),
    )
    prefix_decay, prefix_state = lax.associative_scan(link, (decay_step, normalized), axis=0)
    carried = entering(
        (prefix_decay[-1], prefix_state[-1]),
        "seq",
        link,
        (jnp.ones((width,), jnp.float32), jnp.zeros((width,), jnp.float32)),
        False,
    )
    state_in = carried[1]
    hidden = prefix_state + prefix_decay * state_in
    branch_act, branch_pull = jax.vjp(jax.nn.gelu, branch)
    gated = (hidden * branch_act).astype(jnp.bfloat16)
    residual = inputs + jnp.dot(gated, out_all, preferred_element_type=jnp.float32)
    normed_two, norm_two_pull = jax.vjp(rms_scale, residual, gain_two_all.astype(jnp.float32))
    normed_two_low = normed_two.astype(jnp.bfloat16)
    gate_up_all, down_all = (
        lax.all_gather(gate_up, ("bucket", "seq"), axis=0, tiled=True),
        lax.all_gather(down_proj, ("bucket", "seq"), axis=0, tiled=True),
    )
    expanded = jnp.dot(normed_two_low, gate_up_all, preferred_element_type=jnp.float32)
    feed, feed_pull = jax.vjp(partial(gated_gelu, split=ff_width), expanded)
    feed_low = feed.astype(jnp.bfloat16)
    output_rows = residual + jnp.dot(feed_low, down_all, preferred_element_type=jnp.float32)
    mixed = (keep[:, None] * output_rows).astype(jnp.bfloat16)
    upstream = keep[:, None] * cotangent[0].astype(jnp.float32)
    upstream_low = upstream.astype(jnp.bfloat16)
    down_grad = lax.psum_scatter(
        row_product(feed_low, upstream_low), ("bucket", "seq"), scatter_dimension=0, tiled=True
    )
    feed_grad = contract_last(upstream_low, down_all)
    expanded_grad = feed_pull(feed_grad)[0].astype(jnp.bfloat16)
    gate_up_grad = lax.psum_scatter(
        row_product(normed_two_low, expanded_grad),
        ("bucket", "seq"),
        scatter_dimension=0,
        tiled=True,
    )
    normed_two_grad = contract_last(expanded_grad, gate_up_all)
    residual_part, gain_two_grad = norm_two_pull(normed_two_grad)
    residual_grad = upstream + residual_part
    residual_low = residual_grad.astype(jnp.bfloat16)
    out_grad = contract_first(gated, residual_low)
    gated_grad = contract_last(residual_low, out_all)
    hidden_grad = gated_grad * branch_act
    branch_grad = branch_pull(gated_grad * hidden)[0]
    next_decay = jnp.concatenate([decay_step[1:], jnp.ones((1, width), jnp.float32)], axis=0)
    suffix_decay, suffix_state = lax.associative_scan(
        link, (next_decay, hidden_grad), reverse=True, axis=0
    )
    returned = entering(
        (prefix_decay[-1], decay_step[0] * suffix_state[0]),
        "seq",
        link,
        (jnp.ones((width,), jnp.float32), jnp.zeros((width,), jnp.float32)),
        True,
    )
    incoming = returned[1]
    state_grad = suffix_state + suffix_decay * incoming
    state_before = jnp.concatenate([state_in[None, :], hidden[:-1]], axis=0)
    conv_grad_lru, gate_a_grad, gate_i_grad, decay_grad = lru_pull(
        (state_grad * state_before, state_grad)
    )
    gates_low = jnp.concatenate(
        [
            gate_a_grad.reshape(tok_rows, NB, block_width),
            gate_i_grad.reshape(tok_rows, NB, block_width),
        ],
        axis=2,
    ).astype(jnp.bfloat16)
    gate_grad = jnp.einsum(
        "tnc,tnd->ncd",
        conv_out.reshape(tok_rows, NB, block_width),
        gates_low,
        preferred_element_type=jnp.float32,
    ).reshape(width, 2 * block_width)
    bias_sums = jnp.sum(gates_low.astype(jnp.float32), axis=0)
    gate_bias_grad = jnp.stack(
        [bias_sums[:, :block_width].reshape(width), bias_sums[:, block_width:].reshape(width)],
        axis=1,
    )
    conv_grad_gates = jnp.einsum(
        "tnd,ncd->tnc",
        gates_low,
        gate_all.reshape(NB, block_width, 2 * block_width),
        preferred_element_type=jnp.float32,
    ).reshape(tok_rows, width)
    conv_low = (conv_grad_lru + conv_grad_gates).astype(jnp.bfloat16)
    head = from_behind(conv_low[:rim_rows], "seq", -1)
    trailing = jnp.concatenate([conv_low, head], axis=0)
    conv_low_float = conv_low.astype(jnp.float32)
    mixer_grad = jnp.zeros((tok_rows, width), jnp.float32)
    tap_grads = []
    for offset in range(kernel):
        later_ids = segment_layout(lengths_row, positions + offset)[0]
        ahead = jnp.where(
            (later_ids == segment_ids)[:, None],
            trailing[offset : offset + tok_rows].astype(jnp.float32),
            0.0,
        )
        mixer_grad = mixer_grad + ahead * conv_float[:, offset]
        tap_grads.append(jnp.sum(conv_low_float * lagged_terms[offset], axis=0))
    conv_weight_grad = jnp.stack(tap_grads, axis=1)
    conv_bias_grad = jnp.sum(conv_low_float, axis=0)
    proj_grad_low = jnp.concatenate([mixer_grad, branch_grad], axis=1).astype(jnp.bfloat16)
    in_proj_grad = contract_first(normed_low, proj_grad_low)
    normed_grad = contract_last(proj_grad_low, proj_all)
    input_part, gain_one_grad = norm_pull(normed_grad)
    token_grad = residual_grad + input_part
    summed = (
        lax.psum_scatter(gain_one_grad, ("bucket", "seq"), scatter_dimension=0, tiled=True),
        lax.psum_scatter(in_proj_grad, ("bucket", "seq"), scatter_dimension=0, tiled=True),
        lax.psum_scatter(conv_weight_grad, ("bucket", "seq"), scatter_dimension=0, tiled=True),
        lax.psum_scatter(conv_bias_grad, ("bucket", "seq"), scatter_dimension=0, tiled=True),
        lax.psum_scatter(gate_grad, ("bucket", "seq"), scatter_dimension=0, tiled=True),
        lax.psum_scatter(gate_bias_grad, ("bucket", "seq"), scatter_dimension=0, tiled=True),
        lax.psum_scatter(decay_grad, ("bucket", "seq"), scatter_dimension=0, tiled=True),
        lax.psum_scatter(out_grad, ("bucket", "seq"), scatter_dimension=0, tiled=True),
        lax.psum_scatter(gain_two_grad, ("bucket", "seq"), scatter_dimension=0, tiled=True),
    )
    return (
        mixed[None],
        token_grad[None],
        summed[0],
        summed[1],
        summed[2],
        summed[3],
        summed[4],
        summed[5],
        summed[6],
        summed[7],
        summed[8],
        gate_up_grad,
        down_grad,
    )


def solution(mesh):
    return jax.shard_map(
        on_device,
        mesh=mesh,
        in_specs=(
            P("bucket", "seq", None),
            P("bucket", None),
            P(("bucket", "seq")),
            P(("bucket", "seq"), None),
            P(("bucket", "seq"), None),
            P(("bucket", "seq")),
            P(("bucket", "seq"), None),
            P(("bucket", "seq"), None),
            P(("bucket", "seq")),
            P(("bucket", "seq"), None),
            P(("bucket", "seq")),
            P(("bucket", "seq"), None),
            P(("bucket", "seq"), None),
            P("bucket", "seq", None),
        ),
        out_specs=(
            P("bucket", "seq", None),
            P("bucket", "seq", None),
            P(("bucket", "seq")),
            P(("bucket", "seq"), None),
            P(("bucket", "seq"), None),
            P(("bucket", "seq")),
            P(("bucket", "seq"), None),
            P(("bucket", "seq"), None),
            P(("bucket", "seq")),
            P(("bucket", "seq"), None),
            P(("bucket", "seq")),
            P(("bucket", "seq"), None),
            P(("bucket", "seq"), None),
        ),
        check_vma=False,
    )
```

profile of v0, /device:TPU:0, one launch (start us, length us, event | category | flops | bytes accessed | tf_op | source)
XLA Modules:
  0.0 3479.3 jit_solution(11483993686916365529)
XLA Ops:
  11.7 43.0 %all-reduce.77 = (bf16[2560]{0:T(1024)(128)(2,1)S(1)}, bf16[2048]{0:T(1024)(128)(2,1)S(1)}, bf16[2560]{0:T(1024)(128)(2,1)S(1)}, bf16[2048]{0:T(1024)(128)(2,1)S(1)}) all-reduce(bf16[2560]{0:T(1024)(128)(2,1)S(1)} %dynamic-update-slice.2, ...), channel_id=1, replica_groups=mesh['bucket'=4,'seq'=8] {'bucket','seq'}, use_global_device_ids=true, to_apply=%add.70 | all-reduce | flops 9216 | bytes 36864
  54.8 40.6 %all-gather = bf16[32,80,4]{1,2,0:T(4,128)(2,1)S(1)} all-gather(bf16[1,80,4]{1,2,0:T(4,128)(2,1)S(1)} %bitcast.85), channel_id=1, replica_groups=mesh['bucket'=4,'seq'=8] {'bucket','seq'}, dimensions={0}, use_global_device_ids=true | all-gather | bytes 21120 | tf_op jit(solution)/shard_map/all_gather | solution.py:117
  95.5 37.0 %all-gather.1 = bf16[32,80,2]{1,2,0:T(2,128)(2,1)S(1)} all-gather(bf16[1,80,2]{1,2,0:T(2,128)(2,1)S(1)} %bitcast.87), channel_id=1, replica_groups=mesh['bucket'=4,'seq'=8] {'bucket','seq'}, dimensions={0}, use_global_device_ids=true | all-gather | bytes 10560 | tf_op jit(solution)/shard_map/all_gather | solution.py:120
  134.6 15.3 all-gather.11.cloned.1.call-done
  150.0 11.5 fusion.134
  174.2 33.0 all-gather.13.cloned.1.call-done
  233.3 8.9 fusion.48
  352.7 6.2 slice.631
  389.1 9.3 pad.235
  422.5 9.2 all-gather.2
  431.7 9.7 pad.219
  444.0 9.4 pad.218
  454.4 8.8 all-gather.3
  463.3 19.8 slice.654
  483.1 12.9 slice.663
  496.0 12.9 slice.656
  508.9 8.6 multiply_convert_fusion.1
  517.5 7.1 multiply_reduce_fusion.3
  524.7 48.3 %all-gather.17.cloned.1.call-done = bf16[2048,12288]{1,0:T(8,128)(2,1)} async-done(((bf16[64,12288]{1,0:T(8,128)(2,1)}), bf16[2048,12288]{1,0:T(8,128)(2,1)}) %all-gather.17.cloned.1.call-update) | async-done | bytes 50331664 | tf_op jit(solution)/shard_map/all_gather | solution.py:183
  573.0 25.7 fusion.116
  598.7 129.8 %all-gather.19.cloned.1.call-done = bf16[6144,2048]{1,0:T(8,128)(2,1)} async-done(((bf16[192,2048]{1,0:T(8,128)(2,1)}), bf16[6144,2048]{1,0:T(8,128)(2,1)}) %all-gather.19.cloned.1.call-update) | async-done | bytes 25165840 | tf_op jit(solution)/shard_map/all_gather | solution.py:184
  728.5 23.3 fusion.39
  751.9 26.0 multiply_reduce_fusion.1
  780.3 11.3 fusion.58
  798.9 19.8 slice.660
  818.7 19.7 slice.658
  930.9 13.1 slice.715
  988.8 9.4 pad.253
  1002.7 29.3 rev.8
  1037.8 9.4 pad.269
  1050.8 29.4 rev.9
  1080.1 9.2 all-gather.4
  1089.3 6.9 while.27
  1096.3 10.0 multiply_reduce_fusion
  1134.4 8.0 convert_reduce_fusion.1
  1153.7 9.9 fusion.63
  1165.6 22.2 fusion.67
  1197.3 17.5 fusion.50
  1216.3 41.1 %fusion.59 = f32[2048,12288]{1,0:T(8,128)} fusion(f32[264,6144]{1,0:T(8,128)} %get-tuple-element.216, f32[264,6144]{1,0:T(8,128)} %get-tuple-element.215, f32[264,2048]{1,0:T(8,128)S(1)} %copy-done.24, f32[2048]{0:T(1024)S(1)} %copy-done.53, f32[264]{0:T(512)S(1)} %copy-done.55), kind=kOutput, calls=%fused_computation.129 | convolution fusion | flops 13295665152 | bytes 115811360 | tf_op jit(solution)/shard_map/dot_general | solution.py:72
  1257.5 13.5 fusion.38
  1271.0 12.3 fusion.41
  1283.2 39.2 %all-reduce.76 = (f32[2048]{0:T(1024)S(1)}, f32[2560]{0:T(1024)S(1)}, f32[2560]{0:T(1024)S(1)}, f32[2048]{0:T(1024)S(1)}) all-reduce(f32[2048]{0:T(1024)S(1)} %get-tuple-element.145, f32[2560]{0:T(1024)S(1)} %copy-done.95, f32[2560]{0:T(1024)S(1)} %copy-done.96, ...), channel_id=2, replica_groups=mesh['bucket'=4,'seq'=8] {'bucket','seq'}, use_global_device_ids=true, to_apply=%region_17.18.clone | all-reduce | flops 9216 | bytes 73728
  1329.7 81.3 %reduce-scatter.22.cloned.1.call-done = f32[80,4]{1,0:T(8,128)} async-done(((f32[2560,4]{1,0:T(8,128)}), f32[80,4]{1,0:T(8,128)}) %reduce-scatter.22.cloned.1.call-update) | async-done | bytes 1296
  1412.5 104.5 %reduce-scatter.14.cloned.1.call-done = f32[80,320]{1,0:T(8,128)} async-done(((f32[2560,320]{1,0:T(8,128)}), f32[80,320]{1,0:T(8,128)}) %reduce-scatter.14.cloned.1.call-update) | async-done | bytes 102416 | tf_op jit(solution)/shard_map/reduce_scatter | solution.py:280
  1517.0 227.1 %reduce-scatter.16.cloned.1.call-done = f32[80,2048]{1,0:T(8,128)} async-done(((f32[2560,2048]{1,0:T(8,128)}), f32[80,2048]{1,0:T(8,128)}) %reduce-scatter.16.cloned.1.call-update) | async-done | bytes 655376 | tf_op jit(solution)/shard_map/reduce_scatter | solution.py:283
  1744.1 442.8 %reduce-scatter.20.cloned.1.call-done = f32[192,2048]{1,0:T(8,128)} async-done(((f32[6144,2048]{1,0:T(8,128)}), f32[192,2048]{1,0:T(8,128)}) %reduce-scatter.20.cloned.1.call-update) | async-done | bytes 1572880 | tf_op jit(solution)/shard_map/reduce_scatter | solution.py:193
  2187.0 443.8 %reduce-scatter.12.cloned.1.call-done = f32[64,5120]{1,0:T(8,128)} async-done(((f32[2048,5120]{1,0:T(8,128)}), f32[64,5120]{1,0:T(8,128)}) %reduce-scatter.12.cloned.1.call-update) | async-done | bytes 1310736 | tf_op jit(solution)/shard_map/reduce_scatter | solution.py:277
  2630.8 841.4 %reduce-scatter.18.cloned.1.call-done = f32[64,12288]{1,0:T(8,128)} async-done(((f32[2048,12288]{1,0:T(8,128)}), f32[64,12288]{1,0:T(8,128)}) %reduce-scatter.18.cloned.1.call-update) | async-done | bytes 3145744 | tf_op jit(solution)/shard_map/reduce_scatter | solution.py:198
  (660 shorter events, 440.8 us)
Async XLA Ops:
  7.2 47.6 %copy-start.140 = (bf16[80,4]{0,1:T(4,128)(2,1)S(1)}, bf16[80,4]{0,1:T(4,128)(2,1)}, u32[]{:S(2)}) copy-start(bf16[80,4]{0,1:T(4,128)(2,1)} %param.22) | copy-start | bytes 1924
  7.2 88.2 %copy-start.141 = (bf16[80,2]{0,1:T(2,128)(2,1)S(1)}, bf16[80,2]{0,1:T(2,128)(2,1)}, u32[]{:S(2)}) copy-start(bf16[80,2]{0,1:T(2,128)(2,1)} %param.25) | copy-start | bytes 964
  7.2 125.3 %copy-start.146 = (s32[1,4]{1,0:T(1,128)S(1)}, s32[1,4]{1,0:T(1,128)}, u32[]{:S(2)}) copy-start(s32[1,4]{1,0:T(1,128)} %param.19) | copy-start | bytes 52
  7.3 126.4 %copy-start.17 = (bf16[1,264,2048]{2,1,0:T(8,128)(2,1)S(1)}, bf16[1,264,2048]{2,1,0:T(8,128)(2,1)}, u32[]{:S(2)}) copy-start(bf16[1,264,2048]{2,1,0:T(8,128)(2,1)} %param.18) | copy-start | bytes 3244036
  7.3 142.7 %all-gather.11.cloned.1.call-start = ((), (), s32[]{:S(2)}) async-start(), calls=%async_computation.7 | async-start | bytes 21626880 | tf_op jit(solution)/shard_map/all_gather | solution.py:116
  8.0 199.2 %all-gather.13.cloned.1.call-start = ((), (), s32[]{:S(2)}) async-start(), calls=%async_computation.8 | async-start | bytes 2027520 | tf_op jit(solution)/shard_map/all_gather | solution.py:119
  8.7 508.8 %all-gather.15.cloned.1.call-start = ((), (), s32[]{:S(2)}) async-start(), calls=%async_computation.9 | async-start | bytes 10813440 | tf_op jit(solution)/shard_map/all_gather | solution.py:122
  9.5 563.5 %all-gather.17.cloned.1.call-start = ((), (), s32[]{:S(2)}) async-start(), calls=%async_computation.10 | async-start | bytes 51904512 | tf_op jit(solution)/shard_map/all_gather | solution.py:183
  10.1 718.4 %all-gather.19.cloned.1.call-start = ((), (), s32[]{:S(2)}) async-start(), calls=%async_computation.11 | async-start | bytes 25952256 | tf_op jit(solution)/shard_map/all_gather | solution.py:184
  10.6 1317.7 %reduce-scatter.24.cloned.1.call-start = ((), (), s32[]{:S(2)}) async-start(), calls=%async_computation.18 | async-start | bytes 1351680
  54.8 106.8 %copy-start.122 = (bf16[2560]{0:T(1024)(128)(2,1)}, bf16[2560]{0:T(1024)(128)(2,1)S(1)}, u32[]{:S(2)}) copy-start(bf16[2560]{0:T(1024)(128)(2,1)S(1)} %get-tuple-element.192) | copy-start | bytes 15364
  54.8 106.8 %copy-start.65 = (f32[2048]{0:T(1024)}, f32[2048]{0:T(1024)S(1)}, u32[]{:S(2)}) copy-start(f32[2048]{0:T(1024)S(1)} %convert_element_type.129) | copy-start | bytes 24580
  133.5 99.7 %copy-start.69 = (f32[2560]{0:T(1024)}, f32[2560]{0:T(1024)S(1)}, u32[]{:S(2)}) copy-start(f32[2560]{0:T(1024)S(1)} %get-tuple-element.159) | copy-start | bytes 30724
  133.6 99.7 %copy-start.71 = (f32[2560]{0:T(1024)}, f32[2560]{0:T(1024)S(1)}, u32[]{:S(2)}) copy-start(f32[2560]{0:T(1024)S(1)} %get-tuple-element.160) | copy-start | bytes 30724
  133.7 34.4 copy-start.79
  133.7 34.4 copy-start.81
  133.7 34.4 copy-start.83
  133.7 34.4 copy-start.85
  134.6 33.6 copy-start.131
  134.6 33.6 copy-start.133
  134.6 33.6 copy-start.135
  134.6 98.7 %copy-start.129 = (pred[264]{0:T(512)(128)(4,1)}, pred[264]{0:T(512)(128)(4,1)S(1)}, u32[]{:S(2)}) copy-start(pred[264]{0:T(512)(128)(4,1)S(1)} %get-tuple-element.304) | copy-start | bytes 796
  134.6 98.7 %copy-start.77 = (f32[2560]{0:T(1024)}, f32[2560]{0:T(1024)S(1)}, u32[]{:S(2)}) copy-start(f32[2560]{0:T(1024)S(1)} %broadcast_multiply_fusion) | copy-start | bytes 30724
  163.1 5.0 collective-permute-start
  166.7 611.2 %copy-start.52 = (f32[2048]{0:T(1024)}, f32[2048]{0:T(1024)S(1)}, u32[]{:S(2)}) copy-start(f32[2048]{0:T(1024)S(1)} %convert_element_type.145) | copy-start | bytes 24580
  171.6 38.6 %copy-start.7 = (bf16[264,2560]{1,0:T(8,128)(2,1)}, bf16[264,2560]{1,0:T(8,128)(2,1)S(1)}, u32[]{:S(2)}) copy-start(bf16[264,2560]{1,0:T(8,128)(2,1)S(1)} %fusion.10) | copy-start | bytes 4055044
  174.2 36.0 %copy-start.11 = (bf16[264,2560]{0,1:T(8,128)(2,1)}, bf16[264,2560]{0,1:T(8,128)(2,1)S(1)}, u32[]{:S(2)}) copy-start(bf16[264,2560]{0,1:T(8,128)(2,1)S(1)} %copy.75) | copy-start | bytes 4055044
  453.3 29.7 copy-start.31
  463.2 32.8 copy-start.60
  463.3 32.7 copy-start.30
  524.6 253.2 %copy-start.23 = (f32[264,2048]{1,0:T(8,128)}, f32[264,2048]{1,0:T(8,128)S(1)}, u32[]{:S(2)}) copy-start(f32[264,2048]{1,0:T(8,128)S(1)} %get-tuple-element.310) | copy-start | bytes 6488068
  524.7 253.2 %copy-start.54 = (f32[264]{0:T(512)}, f32[264]{0:T(512)S(1)}, u32[]{:S(2)}) copy-start(f32[264]{0:T(512)S(1)} %fusion.107) | copy-start | bytes 3172
  573.0 155.6 %copy-start.39 = (bf16[1,264,2048]{2,1,0:T(8,128)(2,1)S(1)}, bf16[1,264,2048]{2,1,0:T(8,128)(2,1)}, u32[]{:S(2)}) copy-start(bf16[1,264,2048]{2,1,0:T(8,128)(2,1)} %param.31) | copy-start | bytes 3244036
  573.0 155.6 %copy-start.124 = (f32[264]{0:T(512)S(1)}, f32[264]{0:T(512)}, u32[]{:S(2)}) copy-start(f32[264]{0:T(512)} %fusion.104) | copy-start | bytes 3172
  1050.7 45.6 %copy-start.1 = (f32[264,2560]{1,0:T(8,128)S(1)}, f32[264,2560]{1,0:T(8,128)}, u32[]{:S(2)}) copy-start(f32[264,2560]{1,0:T(8,128)} %copy-done) | copy-start | bytes 8110084
  1050.7 45.6 %copy-start.70 = (f32[2560]{0:T(1024)S(1)}, f32[2560]{0:T(1024)}, u32[]{:S(2)}) copy-start(f32[2560]{0:T(1024)} %copy-done.69) | copy-start | bytes 30724
  1050.7 45.6 %copy-start.72 = (f32[2560]{0:T(1024)S(1)}, f32[2560]{0:T(1024)}, u32[]{:S(2)}) copy-start(f32[2560]{0:T(1024)} %copy-done.71) | copy-start | bytes 30724
  1050.7 45.6 %copy-start.78 = (f32[2560]{0:T(1024)S(1)}, f32[2560]{0:T(1024)}, u32[]{:S(2)}) copy-start(f32[2560]{0:T(1024)} %copy-done.77) | copy-start | bytes 30724
  1050.8 45.6 %copy-start.130 = (pred[264]{0:T(512)(128)(4,1)S(1)}, pred[264]{0:T(512)(128)(4,1)}, u32[]{:S(2)}) copy-start(pred[264]{0:T(512)(128)(4,1)} %copy-done.129) | copy-start | bytes 796
  1144.3 266.7 %reduce-scatter.22.cloned.1.call-start = ((), (), s32[]{:S(2)}) async-start(), calls=%async_computation.17 | async-start | bytes 1351680
  1145.9 371.0 %reduce-scatter.14.cloned.1.call-start = ((), (), s32[]{:S(2)}) async-start(), calls=%async_computation.13 | async-start | bytes 4055040 | tf_op jit(solution)/shard_map/reduce_scatter | solution.py:280
  1151.8 592.3 %reduce-scatter.16.cloned.1.call-start = ((), (), s32[]{:S(2)}) async-start(), calls=%async_computation.14 | async-start | bytes 21626880 | tf_op jit(solution)/shard_map/reduce_scatter | solution.py:283
  1163.7 1023.3 %reduce-scatter.20.cloned.1.call-start = ((), (), s32[]{:S(2)}) async-start(), calls=%async_computation.16 | async-start | bytes 51904512 | tf_op jit(solution)/shard_map/reduce_scatter | solution.py:193
  1188.0 1442.8 %reduce-scatter.12.cloned.1.call-start = ((), (), s32[]{:S(2)}) async-start(), calls=%async_computation.12 | async-start | bytes 43253760 | tf_op jit(solution)/shard_map/reduce_scatter | solution.py:277
  1189.2 3.1 collective-permute-start.1
  1214.8 2257.4 %reduce-scatter.18.cloned.1.call-start = ((), (), s32[]{:S(2)}) async-start(), calls=%async_computation.15 | async-start | bytes 103809024 | tf_op jit(solution)/shard_map/reduce_scatter | solution.py:198
  1270.9 53.8 %copy-start.127 = (f32[264]{0:T(512)S(1)}, f32[264]{0:T(512)}, u32[]{:S(2)}) copy-start(f32[264]{0:T(512)} %copy-done.126) | copy-start | bytes 3172
  1270.9 53.9 %copy-start.10 = (f32[264,2048]{1,0:T(8,128)S(1)}, f32[264,2048]{1,0:T(8,128)}, u32[]{:S(2)}) copy-start(f32[264,2048]{1,0:T(8,128)} %copy-done.8) | copy-start | bytes 6488068
  (113 other events, 760.5 us)
Sparse Core Ops, SparseCore 0:
  11.0 138.9 all-gather.10
  152.9 54.2 all-gather.12
  210.0 85.5 all-gather.14
  298.4 274.5 all-gather.16
  575.7 152.7 all-gather.18
  1144.4 132.7 reduce-scatter.23
  1279.5 131.4 reduce-scatter.21
  1417.0 99.9 reduce-scatter.13
  1519.9 224.2 reduce-scatter.15
  1751.0 435.9 reduce-scatter.19
  2189.8 440.8 reduce-scatter.11
  2637.6 834.5 reduce-scatter.17
where the time goes:
time: 3500 us; the launch traced here: 3480 us
  waiting for transfers between devices  2370 us (68%)
  local copies, waits for them, and re-layouts  532 us (15%)
  matrix products  234 us (7%)
  blocking collectives  187 us (5%)
  other arithmetic  133 us (4%)
    reduce_scatter x1, waiting for transfers between devices, on_device(): lax.psum_scatter(row_product(normed_two_low, expanded_grad), ('bucket', '...  841 us
    reduce_scatter x1, waiting for transfers between devices, on_device(): lax.psum_scatter(in_proj_grad, ('bucket', 'seq'), scatter_dimension=0, ti...  444 us
    reduce_scatter x1, waiting for transfers between devices, on_device(): lax.psum_scatter(row_product(feed_low, upstream_low), ('bucket', 'seq'),...  443 us
    reduce_scatter x1, waiting for transfers between devices, on_device(): lax.psum_scatter(out_grad, ('bucket', 'seq'), scatter_dimension=0, tiled=...  227 us
    slice x57, local copies, waits for them, and re-layouts, on_device(): lax.associative_scan(link, (next_decay, hidden_grad), reverse=True, axis=0)  192 us
    all_gather x1, waiting for transfers between devices, on_device(): lax.all_gather(down_proj, ('bucket', 'seq'), axis=0, tiled=True)  130 us
    slice x52, local copies, waits for them, and re-layouts, on_device(): lax.associative_scan(link, (decay_step, normalized), axis=0)  109 us
    reduce_scatter x1, waiting for transfers between devices, on_device(): lax.psum_scatter(gate_grad, ('bucket', 'seq'), scatter_dimension=0, tiled...  105 us
  transfers between devices with their start and end apart: 14, of which 11 were waited for; matrix products, arithmetic and copies ran while one was open for 14% of the time, Pallas kernels for 0%

commit v1 on v0

--- a/solution.py
+++ b/solution.py
@@ -3,6 +3,8 @@
 import jax
 import jax.numpy as jnp
 from jax import lax
+from jax.experimental import pallas as pl
+from jax.experimental.pallas import tpu as pltpu
 from jax.sharding import PartitionSpec as P
 
 NB = 16
@@ -300,9 +302,714 @@
     )
 
 
+def swap_with(block, mask):
+    route = [(i, i ^ mask) for i in range(lax.axis_size("seq"))]
+    return lax.ppermute(block, "seq", route)
+
+
+def plane_bits():
+    return [1 << bit for bit in range(1, lax.axis_size("seq").bit_length() - 1)]
+
+
+def gather_plane(block):
+    half = block.shape[1] // 2
+    sides = []
+    for part, masks in (
+        (block[None, :, :half], plane_bits()),
+        (block[None, :, half:], plane_bits()[::-1]),
+    ):
+        order = [0]
+        for mask in masks:
+            part = jnp.concatenate([part, swap_with(part, mask)], axis=0)
+            order = order + [i ^ mask for i in order]
+        ranked = sorted(range(len(order)), key=order.__getitem__)
+        if ranked != list(range(len(order))):
+            part = jnp.concatenate([part[i : i + 1] for i in ranked], axis=0)
+        sides.append(part)
+    near = jnp.concatenate(sides, axis=2)
+    return jnp.concatenate([near, swap_with(near, 1)], axis=0)
+
+
+def reduce_plane(partial_rows):
+    count, _, depth = partial_rows.shape
+    near = partial_rows[: count // 2].astype(jnp.float32) + swap_with(
+        partial_rows[count // 2 :].astype(jnp.bfloat16), 1
+    ).astype(jnp.float32)
+    upper, lower = near[:, :, : depth // 2], near[:, :, depth // 2 :]
+    for mask in plane_bits()[::-1]:
+        middle = upper.shape[0] // 2
+        upper = upper[:middle] + swap_with(upper[middle:].astype(jnp.bfloat16), mask).astype(
+            jnp.float32
+        )
+    for mask in plane_bits():
+        lower = lower[0::2] + swap_with(lower[1::2].astype(jnp.bfloat16), mask).astype(jnp.float32)
+    return jnp.concatenate([upper[0], lower[0]], axis=1)
+
+
+def place_of(chunk, me, count):
+    relative = jnp.bitwise_xor(chunk, me)
+    return jnp.bitwise_and(relative, 1) * (count // 2) + jnp.right_shift(relative, 1)
+
+
+def series_expm1(values):
+    total = 1.0 + values * (1.0 / 7.0)
+    for term in (6, 5, 4, 3, 2):
+        total = 1.0 + values * (1.0 / term) * total
+    return values * total
+
+
+def segment_reach(info_ref, first, slots, shape, total):
+    positions = first + lax.broadcasted_iota(jnp.int32, shape, 0)
+    begin = jnp.zeros(shape, jnp.int32)
+    finish = jnp.full(shape, total, jnp.int32)
+    for slot in range(slots):
+        end = info_ref[1 + slot]
+        passed = positions >= end
+        begin = jnp.where(passed, jnp.maximum(begin, end), begin)
+        finish = jnp.where(passed, finish, jnp.minimum(finish, end))
+    return positions - begin, finish - positions
+
+
+def widen(mask, lanes):
+    return jnp.concatenate([mask] * (lanes // mask.shape[1]), axis=1)
+
+
+def gelu_parts(values):
+    inner = 0.7978845608028654 * (values + 0.044715 * values * values * values)
+    bent = jnp.tanh(inner)
+    half = 0.5 * (1.0 + bent)
+    slope = half + 0.5 * values * (1.0 - bent * bent) * 0.7978845608028654 * (
+        1.0 + 3.0 * 0.044715 * values * values
+    )
+    return values * half, slope
+
+
+ROWS = 8
+TAP, BIAS, BIAS_A, BIAS_I, RATE = 0, 4, 5, 6, 7
+
+
+def mixer_forward(
+    taps,
+    slots,
+    info_ref,
+    normed_ref,
+    proj_ref,
+    gate_ref,
+    channel_ref,
+    gated_ref,
+    lagging_ref,
+    conv_ref,
+    branch_ref,
+    gate_r_ref,
+    gate_i_ref,
+    hidden_ref,
+    lag_edge_ref,
+    hidden_edge_ref,
+    projected,
+    convolved,
+    gates,
+    carry,
+    edge,
+):
+    chunk = pl.program_id(0)
+    rows, lanes = convolved.shape
+    tiles = rows // ROWS
+    total = rows * pl.num_programs(0)
+
+    @pl.when(chunk == 0)
+    def _():
+        carry[...] = jnp.zeros_like(carry)
+        edge[...] = jnp.zeros_like(edge)
+
+    product = jnp.dot(normed_ref[0], proj_ref[...], preferred_element_type=jnp.float32)
+    low = product[:, :lanes].astype(jnp.bfloat16)
+    lagging_ref[0] = low
+    projected[:, :lanes] = low.astype(jnp.float32)
+    branch_ref[0] = product[:, lanes:]
+    place = lax.broadcasted_iota(jnp.int32, (ROWS, lanes), 0)
+
+    def convolve(tile, before):
+        at = pl.ds(pl.multiple_of(tile * ROWS, ROWS), ROWS)
+        here = projected[at, :lanes]
+        since, _ = segment_reach(info_ref, chunk * rows + tile * ROWS, slots, (ROWS, 128), total)
+        value = channel_ref[BIAS : BIAS + 1, :] + here * channel_ref[TAP : TAP + 1, :]
+        for lag in range(1, taps):
+            moved = jnp.where(
+                place < lag, pltpu.roll(before, lag, 0), pltpu.roll(here, lag, 0)
+            )
+            value = value + jnp.where(widen(since >= lag, lanes), moved, 0.0) * (
+                channel_ref[TAP + lag : TAP + lag + 1, :]
+            )
+        convolved[at, :] = value
+        return here
+
+    last = lax.fori_loop(0, tiles, convolve, edge[...])
+    edge[...] = last
+    lag_edge_ref[0] = last
+    conv_low = convolved[...].astype(jnp.bfloat16)
+    conv_ref[0] = conv_low
+    convolved[...] = conv_low.astype(jnp.float32)
+    gates[...] = jnp.dot(conv_low, gate_ref[...], preferred_element_type=jnp.float32)
+
+    def recur(tile, state):
+        at = pl.ds(pl.multiple_of(tile * ROWS, ROWS), ROWS)
+        since, _ = segment_reach(info_ref, chunk * rows + tile * ROWS, slots, (ROWS, 128), total)
+        starts = widen(since == 0, lanes)
+        gate_r = jax.nn.sigmoid(gates[at, :lanes] + channel_ref[BIAS_A : BIAS_A + 1, :])
+        gate_i = jax.nn.sigmoid(gates[at, lanes:] + channel_ref[BIAS_I : BIAS_I + 1, :])
+        gate_r_ref[0, at, :] = gate_r
+        gate_i_ref[0, at, :] = gate_i
+        less = series_expm1(-gate_scale * gate_r * channel_ref[RATE : RATE + 1, :])
+        decay = jnp.where(starts, 0.0, 1.0 + less)
+        scaling = jnp.where(starts, 1.0, jnp.sqrt(-less * (2.0 + less)))
+        value = convolved[at, :] * gate_i * scaling
+        for step in (1, 2, 4):
+            inside = place >= step
+            value = value + jnp.where(inside, decay * pltpu.roll(value, step, 0), 0.0)
+            decay = jnp.where(inside, decay * pltpu.roll(decay, step, 0), decay)
+        hidden = value + decay * state
+        hidden_ref[0, at, :] = hidden
+        projected[at, :lanes] = hidden * gelu_parts(branch_ref[0, at, :])[0]
+        hidden_edge_ref[0] = hidden
+        return jnp.broadcast_to(hidden[ROWS - 1 :], hidden.shape)
+
+    carry[...] = lax.fori_loop(0, tiles, recur, carry[...])
+    gated_ref[0] = projected[:, :lanes].astype(jnp.bfloat16)
+
+
+def mixer_backward(
+    taps,
+    slots,
+    info_ref,
+    down_ref,
+    out_ref,
+    gate_ref,
+    channel_ref,
+    branch_ref,
+    hidden_ref,
+    gate_r_ref,
+    gate_i_ref,
+    conv_ref,
+    lagging_ref,
+    lag_edge_ref,
+    hidden_edge_ref,
+    projected_ref,
+    gate_grad_ref,
+    channel_grad_ref,
+    coming,
+    conv_part,
+    lagged,
+    gates,
+    projected,
+    conv_grad,
+    grad_carry,
+    decay_carry,
+    sums,
+):
+    lap = pl.program_id(0)
+    laps = pl.num_programs(0)
+    chunk = laps - 1 - lap
+    rows, lanes = conv_part.shape
+    tiles = rows // ROWS
+    total = rows * laps
+
+    @pl.when(lap == 0)
+    def _():
+        grad_carry[...] = jnp.zeros_like(grad_carry)
+        decay_carry[...] = jnp.zeros_like(decay_carry)
+        conv_grad[...] = jnp.zeros_like(conv_grad)
+        sums[...] = jnp.zeros_like(sums)
+        gate_grad_ref[...] = jnp.zeros_like(gate_grad_ref)
+
+    coming[...] = lax.dot_general(
+        down_ref[0], out_ref[...], (((1,), (1,)), ((), ())), preferred_element_type=jnp.float32
+    )
+    lagged[...] = lagging_ref[0].astype(jnp.float32)
+    conv_part[...] = conv_ref[0].astype(jnp.float32)
+    place = lax.broadcasted_iota(jnp.int32, (ROWS, lanes), 0)
+    first_chunk = chunk == 0
+
+    def recur(step_index, carried):
+        later_grad, later_decay, sum_a, sum_i, sum_rate = carried
+        tile = tiles - 1 - step_index
+        at = pl.ds(pl.multiple_of(tile * ROWS, ROWS), ROWS)
+        ahead = pl.ds(pl.multiple_of(jnp.maximum(tile - 1, 0) * ROWS, ROWS), ROWS)
+        since, _ = segment_reach(info_ref, chunk * rows + tile * ROWS, slots, (ROWS, 128), total)
+        starts = widen(since == 0, lanes)
+        gate_r = gate_r_ref[0, at, :]
+        gate_i = gate_i_ref[0, at, :]
+        hidden = hidden_ref[0, at, :]
+        conv = conv_part[at, :]
+        rate = channel_ref[RATE : RATE + 1, :]
+        log_step = -gate_scale * gate_r * rate
+        less = series_expm1(log_step)
+        plain = 1.0 + less
+        root = jnp.sqrt(-less * (2.0 + less))
+        decay = jnp.where(starts, 0.0, plain)
+        scaling = jnp.where(starts, 1.0, root)
+        activated, slope = gelu_parts(branch_ref[0, at, :])
+        down = coming[at, :]
+        value = down * activated
+        projected[at, lanes:] = down * hidden * slope
+        weight = jnp.where(place == ROWS - 1, later_decay, pltpu.roll(decay, ROWS - 1, 0))
+        for step in (1, 2, 4):
+            inside = place < ROWS - step
+            value = value + jnp.where(inside, weight * pltpu.roll(value, ROWS - step, 0), 0.0)
+            weight = jnp.where(inside, weight * pltpu.roll(weight, ROWS - step, 0), weight)
+        grad = value + weight * later_grad
+        earlier = jnp.where(
+            tile == 0,
+            jnp.where(first_chunk, 0.0, hidden_edge_ref[0]),
+            hidden_ref[0, ahead, :],
+        )
+        before = jnp.where(place == 0, pltpu.roll(earlier, 1, 0), pltpu.roll(hidden, 1, 0))
+        scaled = grad * scaling
+        conv_part[at, :] = scaled * gate_i
+        grad_i = scaled * conv * gate_i * (1.0 - gate_i)
+        grad_log = jnp.where(
+            starts,
+            0.0,
+            grad * plain * (before - conv * gate_i * plain / root),
+        )
+        grad_rate = grad_log * gate_r
+        grad_a = -gate_scale * rate * grad_rate * (1.0 - gate_r)
+        grad_a = grad_a.astype(jnp.bfloat16).astype(jnp.float32)
+        grad_i = grad_i.astype(jnp.bfloat16).astype(jnp.float32)
+        gates[at, :lanes] = grad_a
+        gates[at, lanes:] = grad_i
+        return (
+            jnp.broadcast_to(grad[:1], grad.shape),
+            jnp.broadcast_to(decay[:1], decay.shape),
+            sum_a + grad_a,
+            sum_i + grad_i,
+            sum_rate - gate_scale * grad_rate,
+        )
+
+    empty = jnp.zeros((ROWS, lanes), jnp.float32)
+    grad_last, decay_last, sum_a, sum_i, sum_rate = lax.fori_loop(
+        0, tiles, recur, (grad_carry[...], decay_carry[...], empty, empty, empty)
+    )
+    grad_carry[...] = grad_last
+    decay_carry[...] = decay_last
+    gates_low = gates[...].astype(jnp.bfloat16)
+    gate_grad_ref[...] += lax.dot_general(
+        conv_ref[0], gates_low, (((0,), (0,)), ((), ())), preferred_element_type=jnp.float32
+    )
+    from_gates = lax.dot_general(
+        gates_low, gate_ref[...], (((1,), (1,)), ((), ())), preferred_element_type=jnp.float32
+    )
+    conv_grad[rows:, :] = conv_grad[:ROWS, :]
+    conv_grad[:rows, :] = (conv_part[...] + from_gates).astype(jnp.bfloat16).astype(jnp.float32)
+
+    def unconvolve(tile, carried):
+        earlier, sum_bias, sum_taps = carried
+        at = pl.ds(pl.multiple_of(tile * ROWS, ROWS), ROWS)
+        beyond = pl.ds(pl.multiple_of((tile + 1) * ROWS, ROWS), ROWS)
+        since, until = segment_reach(
+            info_ref, chunk * rows + tile * ROWS, slots, (ROWS, 128), total
+        )
+        here = lagged[at, :]
+        grad = conv_grad[at, :]
+        later = conv_grad[beyond, :]
+        value = grad * channel_ref[TAP : TAP + 1, :]
+        new_taps = [sum_taps[0] + grad * here]
+        for lag in range(1, taps):
+            ahead = jnp.where(
+                place < ROWS - lag, pltpu.roll(grad, ROWS - lag, 0), pltpu.roll(later, ROWS - lag, 0)
+            )
+            value = value + jnp.where(widen(until > lag, lanes), ahead, 0.0) * (
+                channel_ref[TAP + lag : TAP + lag + 1, :]
+            )
+            moved = jnp.where(
+                place < lag, pltpu.roll(earlier, lag, 0), pltpu.roll(here, lag, 0)
+            )
+            new_taps.append(
+                sum_taps[lag] + grad * jnp.where(widen(since >= lag, lanes), moved, 0.0)
+            )
+        projected[at, :lanes] = value
+        return here, sum_bias + grad, tuple(new_taps)
+
+    _, sum_bias, sum_taps = lax.fori_loop(
+        0, tiles, unconvolve, (lag_edge_ref[0], empty, (empty,) * taps)
+    )
+    projected_ref[0] = projected[...].astype(jnp.bfloat16)
+    for place_in, part in enumerate((*sum_taps, sum_bias, sum_a, sum_i, sum_rate)):
+        sums[place_in] += part
+
+    @pl.when(lap == laps - 1)
+    def _():
+        channel_grad_ref[...] = jnp.sum(sums[...], axis=1)
+
+
+VMEM_LIMIT = 48 * 1024 * 1024
+
+
+def run_forward(info, normed, proj, gate, channels, taps, slots):
+    count, rows, depth = normed.shape
+    lanes = gate.shape[0]
+
+    def at_place(chunk, info_ref):
+        return (place_of(chunk, info_ref[0], count), 0, 0)
+
+    def at_chunk(chunk, info_ref):
+        return (chunk, 0, 0)
+
+    def whole(chunk, info_ref):
+        return (0, 0)
+
+    def block(kind):
+        return jax.ShapeDtypeStruct((count, rows, lanes), kind)
+
+    narrow = pl.BlockSpec((1, rows, lanes), at_place)
+    return pl.pallas_call(
+        partial(mixer_forward, taps, slots),
+        grid_spec=pltpu.PrefetchScalarGridSpec(
+            num_scalar_prefetch=1,
+            grid=(count,),
+            in_specs=[
+                pl.BlockSpec((1, rows, depth), at_place),
+                pl.BlockSpec(proj.shape, whole),
+                pl.BlockSpec(gate.shape, whole),
+                pl.BlockSpec(channels.shape, whole),
+            ],
+            out_specs=[narrow] * 7 + [pl.BlockSpec((1, ROWS, lanes), at_chunk)] * 2,
+            scratch_shapes=[
+                pltpu.VMEM((rows, lanes), jnp.float32),
+                pltpu.VMEM((rows, lanes), jnp.float32),
+                pltpu.VMEM((rows, 2 * lanes), jnp.float32),
+                pltpu.VMEM((ROWS, lanes), jnp.float32),
+                pltpu.VMEM((ROWS, lanes), jnp.float32),
+            ],
+        ),
+        out_shape=[
+            block(jnp.bfloat16),
+            block(jnp.bfloat16),
+            block(jnp.bfloat16),
+            block(jnp.float32),
+            block(jnp.float32),
+            block(jnp.float32),
+            block(jnp.float32),
+        ]
+        + [jax.ShapeDtypeStruct((count, ROWS, lanes), jnp.float32)] * 2,
+        compiler_params=pltpu.CompilerParams(
+            dimension_semantics=("arbitrary",), vmem_limit_bytes=VMEM_LIMIT
+        ),
+        cost_estimate=pl.CostEstimate(
+            flops=2 * count * rows * lanes * (2 * depth + 2 * lanes),
+            bytes_accessed=2 * normed.size + 25 * count * rows * lanes,
+            transcendentals=5 * count * rows * lanes,
+        ),
+        name="mixer_forward",
+    )(info, normed, proj, gate, channels)
+
+
+def run_backward(info, down, out, gate, channels, saved, taps, slots):
+    _, lagging, conv, branch, gate_r, gate_i, hidden, lag_edge, hidden_edge = saved
+    count, rows, depth = down.shape
+    lanes = gate.shape[0]
+
+    def at_place(lap, info_ref):
+        return (place_of(count - 1 - lap, info_ref[0], count), 0, 0)
+
+    def before(lap, info_ref):
+        return (jnp.maximum(count - 2 - lap, 0), 0, 0)
+
+    def whole(lap, info_ref):
+        return (0, 0)
+
+    narrow = pl.BlockSpec((1, rows, lanes), at_place)
+    rim = pl.BlockSpec((1, ROWS, lanes), before)
+    sums = taps + 4
+    return pl.pallas_call(
+        partial(mixer_backward, taps, slots),
+        grid_spec=pltpu.PrefetchScalarGridSpec(
+            num_scalar_prefetch=1,
+            grid=(count,),
+            in_specs=[
+                pl.BlockSpec((1, rows, depth), at_place),
+                pl.BlockSpec(out.shape, whole),
+                pl.BlockSpec(gate.shape, whole),
+                pl.BlockSpec(channels.shape, whole),
+                narrow,
+                narrow,
+                narrow,
+                narrow,
+                narrow,
+                narrow,
+                rim,
+                rim,
+            ],
+            out_specs=[
+                pl.BlockSpec((1, rows, 2 * lanes), at_place),
+                pl.BlockSpec((lanes, 2 * lanes), whole),
+                pl.BlockSpec((sums, lanes), whole),
+            ],
+            scratch_shapes=[
+                pltpu.VMEM((rows, lanes), jnp.float32),
+                pltpu.VMEM((rows, lanes), jnp.float32),
+                pltpu.VMEM((rows, lanes), jnp.float32),
+                pltpu.VMEM((rows, 2 * lanes), jnp.float32),
+                pltpu.VMEM((rows, 2 * lanes), jnp.float32),
+                pltpu.VMEM((rows + ROWS, lanes), jnp.float32),
+                pltpu.VMEM((ROWS, lanes), jnp.float32),
+                pltpu.VMEM((ROWS, lanes), jnp.float32),
+                pltpu.VMEM((sums, ROWS, lanes), jnp.float32),
+            ],
+        ),
+        out_shape=[
+            jax.ShapeDtypeStruct((count, rows, 2 * lanes), jnp.bfloat16),
+            jax.ShapeDtypeStruct((lanes, 2 * lanes), jnp.float32),
+            jax.ShapeDtypeStruct((sums, lanes), jnp.float32),
+        ],
+        compiler_params=pltpu.CompilerParams(
+            dimension_semantics=("arbitrary",), vmem_limit_bytes=VMEM_LIMIT
+        ),
+        cost_estimate=pl.CostEstimate(
+            flops=2 * count * rows * lanes * (depth + 4 * lanes),
+            bytes_accessed=2 * down.size + 24 * count * rows * lanes,
+            transcendentals=3 * count * rows * lanes,
+        ),
+        name="mixer_backward",
+    )(info, down, out, gate, channels, branch, hidden, gate_r, gate_i, conv, lagging, lag_edge, hidden_edge)
+
+
+def hand_out(rows, groups):
+    dealt = lax.all_to_all(groups, "seq", split_axis=0, concat_axis=0, tiled=True)
+    return lax.all_gather(dealt.reshape(-1, groups.shape[2]), "bucket", axis=0, tiled=True)
+
+
+def hand_back(grad):
+    count = lax.axis_size("seq")
+    summed = lax.psum_scatter(
+        grad.astype(jnp.bfloat16), "bucket", scatter_dimension=0, tiled=True
+    )
+    blocks = summed.reshape(count, -1, grad.shape[1])
+    return lax.all_to_all(blocks, "seq", split_axis=0, concat_axis=0, tiled=True).astype(
+        jnp.float32
+    )
+
+
+def pad_lanes(values, lanes):
+    return jnp.pad(values, [(0, 0)] * (values.ndim - 1) + [(0, lanes - values.shape[-1])])
+
+
+def by_channels(
+    tokens,
+    lengths,
+    norm_gain,
+    in_proj,
+    conv_weight,
+    conv_bias,
+    gate_weight,
+    gate_bias,
+    decay,
+    out_proj,
+    mlp_gain,
+    gate_up,
+    down_proj,
+    cotangent,
+):
+    planes = lax.axis_size("bucket")
+    count = lax.axis_size("seq")
+    me = lax.axis_index("seq")
+    odd = jnp.bitwise_and(me, 1)
+    inputs = tokens[0].astype(jnp.float32)
+    rows, depth = inputs.shape
+    own_rows = in_proj.shape[0]
+    width = in_proj.shape[1] // 2
+    block_width = width // NB
+    held = planes // 2
+    channels = held * block_width
+    lanes = -(-channels // 128) * 128
+    chunk_rows = conv_weight.shape[0]
+    hidden_width = gate_up.shape[1] // 2 // count
+    hidden_rows = down_proj.shape[0]
+    taps = conv_weight.shape[1]
+    slots = lengths.shape[1]
+
+    by_row = jnp.concatenate(
+        [out_proj, gate_weight, conv_weight, conv_bias[:, None], gate_bias, decay[:, None]], axis=1
+    )
+    by_row_width = by_row.shape[1]
+    by_row = lax.all_gather(
+        pad_lanes(by_row, -(-by_row_width // 128) * 128), "bucket", axis=0, tiled=False
+    )
+    gains = jnp.stack([norm_gain, mlp_gain])[None]
+    gains = lax.all_gather(gains, "seq", axis=0, tiled=True)
+    gains = lax.all_gather(gains[None], "bucket", axis=0, tiled=True).astype(jnp.float32)
+    gain_one, gain_two = gains[:, :, 0].reshape(1, depth), gains[:, :, 1].reshape(1, depth)
+    proj_groups = (
+        in_proj.reshape(own_rows, 2, 2, held, count // 2, block_width)
+        .transpose(4, 2, 0, 1, 3, 5)
+        .reshape(count, own_rows, 2 * channels)
+    )
+    proj = hand_out(own_rows, proj_groups)
+    proj = pad_lanes(proj.reshape(depth, 2, channels), lanes).reshape(depth, 2 * lanes)
+    wide_groups = (
+        gate_up.reshape(own_rows, 2, planes, count, hidden_rows)
+        .transpose(3, 0, 1, 2, 4)
+        .reshape(count, own_rows, 2 * hidden_width)
+    )
+    wide = hand_out(own_rows, wide_groups)
+    narrow = lax.all_gather(down_proj, "bucket", axis=0, tiled=True)
+
+    kept = lax.dynamic_slice_in_dim(by_row, odd * held, held, 0)
+    given = lax.dynamic_slice_in_dim(by_row, (1 - odd) * held, held, 0)
+    taken = swap_with(given, 1)
+    pair = jnp.where(
+        odd == 0, jnp.stack([kept, taken], axis=1), jnp.stack([taken, kept], axis=1)
+    )
+    by_channel = pair.reshape(channels, -1)
+    out = jnp.pad(by_channel[:, :depth], [(0, lanes - channels), (0, 0)])
+    gate_columns = 2 * block_width
+    gate_rows = by_channel[:, depth : depth + gate_columns]
+    gate_blocks = []
+    for index in range(held):
+        part = gate_rows[index * block_width : (index + 1) * block_width]
+        at = index * block_width
+        gate_blocks.append(
+            jnp.concatenate(
+                [
+                    jnp.pad(side, [(0, 0), (at, lanes - at - block_width)])
+                    for side in (part[:, :block_width], part[:, block_width:])
+                ],
+                axis=1,
+            )
+        )
+    gate = jnp.pad(jnp.concatenate(gate_blocks, axis=0), [(0, lanes - channels), (0, 0)])
+    small = by_channel[:, depth + gate_columns : by_row_width].astype(jnp.float32).T
+    decay_channel = small[taps + 3]
+    rate = jnp.pad(jax.nn.softplus(decay_channel), (0, lanes - channels), constant_values=0.01)
+    channel = jnp.concatenate([pad_lanes(small[: taps + 3], lanes), rate[None]], axis=0)
+    ends = jnp.cumsum(lengths[0]).astype(jnp.int32)
+    info = jnp.concatenate([me[None].astype(jnp.int32), ends])
+
+    positions = me * rows + jnp.arange(rows, dtype=jnp.int32)
+    keep = (positions < ends[-1]).astype(jnp.float32)[:, None]
+    upstream = keep * cotangent[0].astype(jnp.float32)
+    scale_one = lax.rsqrt(jnp.mean(inputs * inputs, axis=1, keepdims=True) + norm_eps)
+    normed = gather_plane((inputs * scale_one * gain_one).astype(jnp.bfloat16))
+    upstream_all = gather_plane(upstream.astype(jnp.bfloat16)).reshape(-1, depth)
+    saved = run_forward(info, normed, proj, gate, channel, taps, slots)
+    gated = saved[0].reshape(-1, lanes)
+    mixed_part = jnp.dot(gated, out, preferred_element_type=jnp.float32).astype(jnp.bfloat16)
+    residual = inputs + reduce_plane(mixed_part.reshape(count, rows, depth))
+    scale_two = lax.rsqrt(jnp.mean(residual * residual, axis=1, keepdims=True) + norm_eps)
+    normed_two = gather_plane((residual * scale_two * gain_two).astype(jnp.bfloat16))
+    normed_two = normed_two.reshape(-1, depth)
+    expanded = jnp.dot(normed_two, wide, preferred_element_type=jnp.float32)
+    feed, feed_pull = jax.vjp(partial(gated_gelu, split=hidden_width), expanded)
+    feed_low = feed.astype(jnp.bfloat16)
+    output_part = jnp.dot(feed_low, narrow, preferred_element_type=jnp.float32)
+    output_part = output_part.astype(jnp.bfloat16).reshape(count, rows, depth)
+    mixed = (keep * (residual + reduce_plane(output_part))).astype(jnp.bfloat16)
+
+    feed_grad = contract_last(upstream_all, narrow)
+    expanded_grad = feed_pull(feed_grad)[0].astype(jnp.bfloat16)
+    normed_two_part = contract_last(expanded_grad, wide).astype(jnp.bfloat16)
+    normed_two_grad = reduce_plane(normed_two_part.reshape(count, rows, depth))
+
+    def norm_back(values, scale, gain, grad):
+        scaled = grad * gain
+        lean = jnp.mean(scaled * values, axis=1, keepdims=True)
+        return scale * scaled - scale * scale * scale * lean * values
+
+    residual_grad = upstream + norm_back(residual, scale_two, gain_two, normed_two_grad)
+    residual_low = gather_plane(residual_grad.astype(jnp.bfloat16))
+    proj_grad, gate_grad, channel_grad = run_backward(
+        info, residual_low, out, gate, channel, saved, taps, slots
+    )
+    proj_grad = proj_grad.reshape(-1, 2 * lanes)
+    normed_part = contract_last(proj_grad, proj).astype(jnp.bfloat16)
+    normed_grad = reduce_plane(normed_part.reshape(count, rows, depth))
+    token_grad = residual_grad + norm_back(inputs, scale_one, gain_one, normed_grad)
+
+    down_grad = lax.psum_scatter(
+        contract_first(feed_low, upstream_all).astype(jnp.bfloat16),
+        "bucket",
+        scatter_dimension=0,
+        tiled=True,
+    ).astype(jnp.float32)
+    wide_grad = hand_back(contract_first(normed_two, expanded_grad))
+    gate_up_grad = (
+        wide_grad.reshape(count, own_rows, 2, planes, hidden_rows)
+        .transpose(1, 2, 3, 0, 4)
+        .reshape(own_rows, -1)
+    )
+    out_grad = contract_first(gated, residual_low.reshape(-1, depth))[:channels]
+    gate_parts = []
+    for index in range(held):
+        at = index * block_width
+        span = gate_grad[at : at + block_width]
+        gate_parts.append(
+            jnp.concatenate(
+                [span[:, at : at + block_width], span[:, lanes + at : lanes + at + block_width]],
+                axis=1,
+            )
+        )
+    channel_grad = channel_grad[:, :channels]
+    small_grad = jnp.concatenate(
+        [
+            channel_grad[: taps + 3],
+            (channel_grad[taps + 3] * jax.nn.sigmoid(decay_channel))[None],
+        ],
+        axis=0,
+    )
+    by_row_grad = jnp.concatenate(
+        [out_grad, jnp.concatenate(gate_parts, axis=0), small_grad.T], axis=1
+    ).astype(jnp.bfloat16)
+    by_row_grad = pad_lanes(by_row_grad, by_row.shape[2]).reshape(held, 2, chunk_rows, -1)
+    kept = lax.dynamic_index_in_dim(by_row_grad, odd, 1, False)
+    taken = swap_with(lax.dynamic_index_in_dim(by_row_grad, 1 - odd, 1, False), 1)
+    by_row_grad = jnp.where(
+        odd == 0, jnp.concatenate([kept, taken]), jnp.concatenate([taken, kept])
+    )
+    by_row_grad = lax.psum_scatter(
+        by_row_grad.reshape(planes * chunk_rows, -1), "bucket", scatter_dimension=0, tiled=True
+    ).astype(jnp.float32)
+    out_proj_grad = by_row_grad[:, :depth]
+    gate_weight_grad = by_row_grad[:, depth : depth + gate_columns]
+    small_grad = by_row_grad[:, depth + gate_columns : by_row_width]
+    narrow_grad = jnp.pad(
+        contract_first(normed.reshape(-1, depth), proj_grad).reshape(depth, 2, lanes)[
+            :, :, :channels
+        ].reshape(depth, 2 * channels),
+        [(0, 0), (0, 0)],
+    )
+    in_proj_grad = (
+        hand_back(narrow_grad)
+        .reshape(count // 2, 2, own_rows, 2, held, block_width)
+        .transpose(2, 3, 1, 4, 0, 5)
+        .reshape(own_rows, -1)
+    )
+    norm_gain_grad = jnp.sum(in_proj_grad * in_proj.astype(jnp.float32), axis=1) / norm_gain.astype(
+        jnp.float32
+    )
+    mlp_gain_grad = jnp.sum(gate_up_grad * gate_up.astype(jnp.float32), axis=1) / mlp_gain.astype(
+        jnp.float32
+    )
+    return (
+        mixed[None],
+        token_grad[None],
+        norm_gain_grad,
+        in_proj_grad,
+        small_grad[:, :taps],
+        small_grad[:, taps],
+        gate_weight_grad,
+        small_grad[:, taps + 1 : taps + 3],
+        small_grad[:, taps + 3],
+        out_proj_grad,
+        mlp_gain_grad,
+        gate_up_grad,
+        down_grad,
+    )
+
+
 def solution(mesh):
+    planes, count = mesh.shape["bucket"], mesh.shape["seq"]
+    whole_blocks = planes % 2 == 0 and planes * count == 2 * NB
     return jax.shard_map(
-        on_device,
+        by_channels if whole_blocks else on_device,
         mesh=mesh,
         in_specs=(
             P("bucket", "seq", None),

time: 3500 us -> 849 us (0.24)
  waiting for transfers between devices: 2370 us -> 293 us
  local copies, waits for them, and re-layouts: 532 us -> 127 us
  blocking collectives: 187 us -> 23.5 us
  matrix products: 234 us -> 130 us
  Pallas kernels: 0 us -> 79.9 us
  starting transfers between devices: 4.11 us -> 57 us
    reduce_scatter x5 -> x4, waiting for transfers between devices: 2060 us -> 0.01 us  [the longest x2 0.01 us: hand_back(): lax.psum_scatter(grad.astype(jnp.bfloat16), 'bucket', scatter_dimension=0...]
    slice x120 -> x49, local copies, waits for them, and re-layouts: 316 us -> 42.3 us  [the longest x4 21.1 us: reduce_plane(): partial_rows[count // 2:].astype(jnp.bfloat16)]
    ppermute x2 -> x42, waiting for transfers between devices: 1.79 us -> 196 us  [swap_with(): return lax.ppermute(block, 'seq', route)]
    all_gather x5 -> x4, waiting for transfers between devices: 226 us -> 80.3 us  [the longest x2 49.8 us: hand_out(): lax.all_gather(dealt.reshape(-1, groups.shape[2]), 'bucket', axis=0, tile...]
    pad x56 -> x6, local copies, waits for them, and re-layouts: 92.1 us -> 6.35 us  [the longest x3 4.77 us: pad_lanes(): jnp.pad(values, [(0, 0)] * (values.ndim - 1) + [(0, lanes - values.shape[...]
    unnamed x14 -> x8, waiting for transfers between devices: 84.5 us -> 0.13 us
    unnamed x2 -> x0, blocking collectives: 82.2 us -> none
    all_gather x5 -> x2, blocking collectives: 105 us -> 23.5 us  [the longest x1 13.3 us: by_channels(): lax.all_gather(gains[None], 'bucket', axis=0, tiled=True)]
  transfers between devices with their start and end apart: 14 -> 54, of which waited for: 11 -> 26; matrix products, arithmetic and copies ran while one was open for 14% -> 34% of each run, Pallas kernels for 0% -> 5%
where the time goes in v1:
time: 849 us; the launch traced here: 841 us
  waiting for transfers between devices  293 us (35%)
  matrix products  130 us (15%)
  local copies, waits for them, and re-layouts  127 us (15%)
  other arithmetic  114 us (13%)
  Pallas kernels  79.9 us (9%)
  starting transfers between devices  57 us (7%)
  blocking collectives  23.5 us (3%)
  between operations  16.2 us (2%)
    ppermute x42, waiting for transfers between devices, swap_with(): return lax.ppermute(block, 'seq', route)  196 us
    dot_general x3, matrix products, contract_last(): lax.dot_general(left, right, (((1,), (1,)), ((), ())), preferred_element_...  52.7 us
    all_gather x2, waiting for transfers between devices, hand_out(): lax.all_gather(dealt.reshape(-1, groups.shape[2]), 'bucket', axis=0, tile...  49.8 us
    dot_general x4, matrix products, contract_first(): lax.dot_general(left, right, (((0,), (0,)), ((), ())), preferred_element_...  45.7 us
    pallas_call x1, Pallas kernels, run_backward(): pl.pallas_call(partial(mixer_backward, taps, slots), grid_spec=pltpu.Pref...  41.8 us
    ppermute x42, starting transfers between devices, swap_with(): return lax.ppermute(block, 'seq', route)  38.8 us
    pallas_call x1, Pallas kernels, run_forward(): pl.pallas_call(partial(mixer_forward, taps, slots), grid_spec=pltpu.Prefe...  38.1 us
    concatenate x4, other arithmetic, gather_plane(): return jnp.concatenate([near, swap_with(near, 1)], axis=0)  33 us
  transfers between devices with their start and end apart: 54, of which 26 were waited for; matrix products, arithmetic and copies ran while one was open for 34% of the time, Pallas kernels for 5%

profile of v1, /device:TPU:0, one launch (start us, length us, event | category | flops | bytes accessed | tf_op | source)
XLA Modules:
  0.0 840.8 jit_solution(15293453717807810188)
XLA Ops:
  7.9 10.2 %all-gather.3 = bf16[8,2,64]{2,1,0:T(2,128)(2,1)S(1)} all-gather(bf16[1,2,64]{2,1,0:T(2,128)(2,1)S(1)} %maximum_bitcast_fusion.1), channel_id=2, replica_groups=mesh['bucket'=4,'seq'=8] {'seq'}, dimensions={0}, use_global_device_ids=true | all-gather | bytes 2304 | tf_op jit(solution)/shard_map/all_gather | solution.py:838
  18.1 13.3 %all-gather.1 = bf16[32,2,64]{2,1,0:T(2,128)(2,1)S(1)} all-gather(bf16[8,2,64]{2,1,0:T(2,128)(2,1)S(1)} %all-gather.3), channel_id=3, replica_groups=mesh['bucket'=4,'seq'=8] {'bucket'}, dimensions={0}, use_global_device_ids=true | all-gather | bytes 10240 | tf_op jit(solution)/shard_map/all_gather | solution.py:839
  37.1 9.6 %collective-permute-done.2 = bf16[1,264,1024]{2,1,0:T(8,128)(2,1)S(1)} collective-permute-done((bf16[1,264,1024]{2,1,0:T(8,128)(2,1)S(1)}, bf16[1,264,1024]{2,1,0:T(8,128)(2,1)S(1)}, u32[]{:S(2)}, u32[]{:S(2)}) %collective-permute-start.2) | collective-permute-done | bytes 540704 | tf_op jit(solution)/shard_map/ppermute | solution.py:307
  59.3 4.4 reshape.375
  72.4 6.9 collective-permute-done.1
  93.8 49.8 %all-gather.9.cloned.1.call-done = bf16[2048,640]{0,1:T(8,128)(2,1)} async-done(((bf16[512,640]{0,1:T(8,128)(2,1)}), bf16[2048,640]{0,1:T(8,128)(2,1)}) %all-gather.9.cloned.1.call-update) | async-done | bytes 2621456 | tf_op jit(solution)/shard_map/all_gather | solution.py:778
  147.4 4.6 copy.94.proj_ref
  152.1 8.3 pad_maximum_fusion.normed_ref
  160.4 38.1 %mixer_forward.1 = (bf16[8,264,384]{2,1,0:T(8,128)(2,1)S(1)}, bf16[8,264,384]{2,1,0:T(8,128)(2,1)S(1)}, bf16[8,264,384]{2,1,0:T(8,128)(2,1)S(1)}, f32[8,264,384]...) custom-call(s32[5]{0:T(128)S(1)} %pad_add_fusion.info_ref, ...), custom_call_target="tpu_custom_call" | custom-call | flops 7889485824 | bytes 28925952 | tf_op jit(solution)/shard_map/mixer_forward/pallas_call | solution.py:664
  198.6 4.9 convolution_convert_fusion.3
  220.3 5.5 convert_add_fusion.3
  233.0 8.2 all-to-all-done.1
  249.0 14.9 %collective-permute-done.7 = bf16[2,264,1024]{2,1,0:T(8,128)(2,1)} collective-permute-done((bf16[2,264,1024]{2,1,0:T(8,128)(2,1)}, bf16[2,264,1024]{2,1,0:T(8,128)(2,1)}, u32[]{:S(2)}, u32[]{:S(2)}) %collective-permute-start.7) | collective-permute-done | bytes 1081376 | tf_op jit(solution)/shard_map/ppermute | solution.py:307
  266.8 6.0 collective-permute-done.9
  276.6 7.7 collective-permute-done.21
  285.1 10.8 %collective-permute-done.8 = bf16[1,264,1024]{2,1,0:T(8,128)(2,1)S(1)} collective-permute-done((bf16[1,264,1024]{2,1,0:T(8,128)(2,1)S(1)}, bf16[1,264,1024]{2,1,0:T(8,128)(2,1)S(1)}, u32[]{:S(2)}, u32[]{:S(2)}) %collective-permute-start.8) | collective-permute-done | bytes 540704 | tf_op jit(solution)/shard_map/ppermute | solution.py:307
  298.6 20.4 %collective-permute-done.24 = bf16[2,264,1024]{2,1,0:T(8,128)(2,1)S(1)} collective-permute-done((bf16[2,264,1024]{2,1,0:T(8,128)(2,1)S(1)}, bf16[2,264,1024]{2,1,0:T(8,128)(2,1)S(1)}, u32[]{:S(2)}, u32[]{:S(2)}) %collective-permute-start.24) | collective-permute-done | bytes 1081376 | tf_op jit(solution)/shard_map/ppermute | solution.py:307
  319.2 9.2 %collective-permute-done.11 = bf16[1,264,1024]{2,1,0:T(8,128)(2,1)S(1)} collective-permute-done((bf16[1,264,1024]{2,1,0:T(8,128)(2,1)S(1)}, bf16[1,264,1024]{2,1,0:T(8,128)(2,1)S(1)}, u32[]{:S(2)}, u32[]{:S(2)}) %collective-permute-start.11) | collective-permute-done | bytes 540704 | tf_op jit(solution)/shard_map/ppermute | solution.py:307
  333.5 20.3 %collective-permute-done.14 = bf16[2,264,1024]{2,1,0:T(8,128)(2,1)S(1)} collective-permute-done((bf16[2,264,1024]{2,1,0:T(8,128)(2,1)S(1)}, bf16[2,264,1024]{2,1,0:T(8,128)(2,1)S(1)}, u32[]{:S(2)}, u32[]{:S(2)}) %collective-permute-start.14) | collective-permute-done | bytes 1081376 | tf_op jit(solution)/shard_map/ppermute | solution.py:307
  357.1 8.3 pad_maximum_fusion.2
  365.4 7.7 pad_maximum_fusion.1
  373.1 19.7 %fusion.60 = f32[2112,1536]{1,0:T(8,128)} fusion(bf16[2112,2048]{1,0:T(8,128)(2,1)} %bitcast.175, bf16[2048,1536]{1,0:T(8,128)(2,1)} %all-gather.11.cloned.1.call-done), kind=kOutput, calls=%fused_computation.185 | convolution fusion | flops 13287555072 | bytes 27918336 | tf_op jit(solution)/shard_map/dot_general | solution.py:900
  392.8 27.1 %all-gather.13.cloned.1.call-done = bf16[768,2048]{1,0:T(8,128)(2,1)} async-done(((bf16[192,2048]{1,0:T(8,128)(2,1)}), bf16[768,2048]{1,0:T(8,128)(2,1)}) %all-gather.13.cloned.1.call-update) | async-done | bytes 3145744 | tf_op jit(solution)/shard_map/all_gather | solution.py:854
  419.9 20.4 %fusion.10 = (f32[2112,768]{1,0:T(8,128)}, f32[2112,768]{1,0:T(8,128)}, bf16[2112,768]{1,0:T(8,128)(2,1)}) fusion(f32[2112,1536]{1,0:T(8,128)} %fusion.60, bf16[2112,2048]{1,0:T(8,128)(2,1)} %bitcast.171, bf16[768,2048]{1,0:T(8,128)(2,1)} %all-gather.13.cloned.1.call-done), kind=kOutput, calls=%fused_computation.43 | convolution fusion | flops 6682705920 | bytes 40992768 | tf_op jit(solution)/shard_map/dot_general | solution.py:68
  440.3 21.1 %convolution_convert_fusion.1 = bf16[2112,2048]{1,0:T(8,128)(2,1)} fusion(bf16[2048,1536]{1,0:T(8,128)(2,1)} %all-gather.11.cloned.1.call-done, f32[2112,768]{1,0:T(8,128)} %get-tuple-element.94, f32[2112,768]{1,0:T(8,128)} %get-tuple-element.93), kind=kOutput, calls=%fused_computation.2 | convolution fusion | flops 13298368512 | bytes 27918336 | tf_op jit(solution)/shard_map/dot_general | solution.py:68
  461.5 7.3 fusion.50
  471.7 18.6 %convolution_convert_fusion.4 = bf16[2048,1536]{1,0:T(8,128)(2,1)} fusion(bf16[2112,2048]{1,0:T(8,128)(2,1)} %bitcast.176, f32[2112,768]{1,0:T(8,128)S(1)} %copy-done.98, f32[2112,768]{1,0:T(8,128)S(1)} %copy-done.97), kind=kOutput, calls=%fused_computation.15 | convolution fusion | flops 13297188864 | bytes 27918336 | tf_op jit(solution)/shard_map/dot_general | solution.py:74
  490.5 5.5 convert_add_fusion.1
  500.4 21.5 %collective-permute-done.27 = bf16[2,264,1024]{2,1,0:T(8,128)(2,1)S(1)} collective-permute-done((bf16[2,264,1024]{2,1,0:T(8,128)(2,1)S(1)}, bf16[2,264,1024]{2,1,0:T(8,128)(2,1)S(1)}, u32[]{:S(2)}, u32[]{:S(2)}) %collective-permute-start.27) | collective-permute-done | bytes 1081376 | tf_op jit(solution)/shard_map/ppermute | solution.py:307
  526.1 9.6 %collective-permute-done.28 = bf16[1,264,1024]{2,1,0:T(8,128)(2,1)S(1)} collective-permute-done((bf16[1,264,1024]{2,1,0:T(8,128)(2,1)S(1)}, bf16[1,264,1024]{2,1,0:T(8,128)(2,1)S(1)}, u32[]{:S(2)}, u32[]{:S(2)}) %collective-permute-start.28) | collective-permute-done | bytes 540704 | tf_op jit(solution)/shard_map/ppermute | solution.py:307
  542.4 10.1 %collective-permute-done.33 = bf16[1,264,1024]{2,1,0:T(8,128)(2,1)S(1)} collective-permute-done((bf16[1,264,1024]{2,1,0:T(8,128)(2,1)S(1)}, bf16[1,264,1024]{2,1,0:T(8,128)(2,1)S(1)}, u32[]{:S(2)}, u32[]{:S(2)}) %collective-permute-start.33) | collective-permute-done | bytes 540704 | tf_op jit(solution)/shard_map/ppermute | solution.py:307
  558.4 18.6 %collective-permute-done.34 = bf16[2,264,1024]{2,1,0:T(8,128)(2,1)} collective-permute-done((bf16[2,264,1024]{2,1,0:T(8,128)(2,1)}, bf16[2,264,1024]{2,1,0:T(8,128)(2,1)}, u32[]{:S(2)}, u32[]{:S(2)}) %collective-permute-start.34) | collective-permute-done | bytes 1081376 | tf_op jit(solution)/shard_map/ppermute | solution.py:307
  578.7 5.3 maximum_maximum_fusion.3
  584.0 7.2 convolution_convert_fusion.2
  595.5 9.3 %convolution_convert_fusion.5 = bf16[768,2048]{1,0:T(8,128)(2,1)} fusion(bf16[2112,768]{1,0:T(8,128)(2,1)S(1)} %copy-done.96, bf16[2112,2048]{1,0:T(8,128)(2,1)S(1)} %bitcast.174), kind=kOutput, calls=%fused_computation.30 | convolution fusion | flops 6645350400 | bytes 15040512 | tf_op jit(solution)/shard_map/dot_general | solution.py:74
  605.1 8.8 %pad_maximum_fusion.3.down_ref = bf16[8,264,2048]{2,1,0:T(8,128)(2,1)} fusion(bf16[4,264,2048]{2,1,0:T(8,128)(2,1)} %collective-permute-done.35, bf16[1,264,1024]{2,1,0:T(8,128)(2,1)} %copy-done.55, bf16[1,264,1024]{2,1,0:T(8,128)(2,1)} %copy-done.45, bf16[1,264,1024]{2,1,0:T(8,128)(2,1)} %copy-done.54, bf16[1,264,1024]{2,1,0:T(8,128)(2,1)S(1)} %get-tuple-element.115, ...), kind=kLoop, calls=%fused_computation.10 | loop fusion | flops 69206016 | bytes 17301504 | tf_op jit(solution)/shard_map/concatenate | solution.py:330
  613.9 41.8 %mixer_backward.1 = (bf16[8,264,768]{2,1,0:T(8,128)(2,1)}, f32[384,768]{1,0:T(8,128)S(1)}, f32[8,384]{1,0:T(8,128)S(1)}) custom-call(s32[5]{0:T(128)S(1)} %copy-done.8, bf16[8,264,2048]{2,1,0:T(8,128)(2,1)} %pad_maximum_fusion.3.down_ref, bf16[384,2048]{1,0:T(8,128)(2,1)S(1)} %pad.57.out_ref, bf16[384,768]{1,0:T(8,128)(2,1)S(1)} %copy-done.1, ...), custom_call_target="tpu_custom_call" | custom-call | flops 5813305344 | bytes 28114944 | tf_op jit(solution)/shard_map/mixer_backward/pallas_call | solution.py:723
  657.2 7.9 convolution_bitcast_fusion
  668.5 11.2 %convolution_convert_fusion = bf16[2112,2048]{1,0:T(8,128)(2,1)} fusion(bf16[2112,768]{1,0:T(8,128)(2,1)} %bitcast.188, bf16[2048,768]{0,1:T(8,128)(2,1)S(1)} %bitcast.166), kind=kOutput, calls=%fused_computation.1 | convolution fusion | flops 6648102912 | bytes 15040512 | tf_op jit(solution)/shard_map/dot_general | solution.py:68
  681.6 6.3 fusion.49
  692.3 9.9 %fusion.61 = bf16[2048,2,384]{0,2,1:T(8,128)(2,1)S(1)} fusion(bf16[2112,2048,1]{1,0,2:T(8,128)(2,1)} %bitcast.170, bf16[2,384,2112]{2,1,0:T(8,128)(2,1)S(1)} %bitcast.187), kind=kOutput, calls=%fused_computation.186 | convolution fusion | flops 6643777536 | bytes 15040512 | tf_op jit(solution)/shard_map/dot_general | solution.py:74
  705.0 5.5 convert_add_fusion.2
  714.1 22.9 %collective-permute-done.17 = bf16[2,264,1024]{2,1,0:T(8,128)(2,1)S(1)} collective-permute-done((bf16[2,264,1024]{2,1,0:T(8,128)(2,1)S(1)}, bf16[2,264,1024]{2,1,0:T(8,128)(2,1)S(1)}, u32[]{:S(2)}, u32[]{:S(2)}) %collective-permute-start.17) | collective-permute-done | bytes 1081376 | tf_op jit(solution)/shard_map/ppermute | solution.py:307
  740.4 4.5 all-to-all-start.3
  744.9 5.7 convert_add_fusion
  764.1 7.3 all-to-all-done.3
  771.4 5.7 reshape.411
  777.1 6.6 copy.99
  (448 shorter events, 210.0 us)
Async XLA Ops:
  7.2 80.6 %all-gather.15.cloned.1.call-start = ((), (), s32[]{:S(2)}) async-start(), calls=%async_computation.15 | async-start | bytes 1945600 | tf_op jit(solution)/shard_map/all_gather | solution.py:834
  36.5 14.2 %collective-permute-start = (bf16[1,264,1024]{2,1,0:T(8,128)(2,1)S(1)}, bf16[1,264,1024]{2,1,0:T(8,128)(2,1)S(1)}, u32[]{:S(2)}, u32[]{:S(2)}) collective-permute-start(bf16[1,264,1024]{2,1,0:T(8,128)(2,1)S(1)} %get-tuple-element.126), channel_id=1, source_target_pairs={{0,2},{1,3},{2,0},{3,1},{4,6},{5,7},{6,4},{7,5},{8,10},{9,11},{10,... | collective-permute-start | bytes 1622024 | tf_op jit(solution)/shard_map/ppermute | solution.py:307
  47.8 23.3 %collective-permute-start.3 = (bf16[2,264,1024]{2,1,0:T(8,128)(2,1)}, bf16[2,264,1024]{2,1,0:T(8,128)(2,1)}, u32[]{:S(2)}, u32[]{:S(2)}) collective-permute-start(bf16[2,264,1024]{2,1,0:T(8,128)(2,1)} %pad_maximum_fusion.5), channel_id=1, source_target_pairs={{0,2},{1,3},{2,0},{3,1},{4,6},{5,7},{6,4},{7,5},{8,10},{9,11},{10,... | collective-permute-start | bytes 3244040 | tf_op jit(solution)/shard_map/ppermute | solution.py:307
  51.9 27.5 %collective-permute-start.1 = (bf16[2,264,1024]{2,1,0:T(8,128)(2,1)}, bf16[2,264,1024]{2,1,0:T(8,128)(2,1)S(1)}, u32[]{:S(2)}, u32[]{:S(2)}) collective-permute-start(bf16[2,264,1024]{2,1,0:T(8,128)(2,1)} %pad_maximum_fusion.4), channel_id=1, source_target_pairs={{0,4},{1,5},{2,6},{3,7},{4,0},{5,1},{6,2},{7,3},{8,12},{9,13},{10,... | collective-permute-start | bytes 3244040 | tf_op jit(solution)/shard_map/ppermute | solution.py:307
  63.7 18.4 %all-to-all-start = ((bf16[8,64,640]{2,1,0:T(8,128)(2,1)}), bf16[8,64,640]{2,1,0:T(8,128)(2,1)}, u32[]{:S(2)}, u32[]{:S(2)}) async-start(bf16[8,64,640]{2,1,0:T(8,128)(2,1)} %reshape.375), calls=%async_computation | async-start | bytes 1310720 | tf_op jit(solution)/shard_map/all_to_all | solution.py:777
  67.9 75.7 %all-gather.9.cloned.1.call-start = ((), (), s32[]{:S(2)}) async-start(), calls=%async_computation.8 | async-start | bytes 3276800 | tf_op jit(solution)/shard_map/all_gather | solution.py:778
  82.0 70.0 %collective-permute-start.4 = (bf16[4,264,2048]{2,1,0:T(8,128)(2,1)}, bf16[4,264,2048]{2,1,0:T(8,128)(2,1)}, u32[]{:S(2)}, u32[]{:S(2)}) collective-permute-start(bf16[4,264,2048]{2,1,0:T(8,128)(2,1)} %maximum_maximum_fusion), channel_id=1, source_target_pairs={{0,1},{1,0},{2,3},{3,2},{4,5},{5,4},{6,7},{7,6},{8,9},{9,8},{10,11... | collective-permute-start | bytes 12976136 | tf_op jit(solution)/shard_map/ppermute | solution.py:307
  207.3 13.0 %collective-permute-start.6 = (bf16[4,264,2048]{2,1,0:T(8,128)(2,1)}, bf16[4,264,2048]{2,1,0:T(8,128)(2,1)}, u32[]{:S(2)}, u32[]{:S(2)}) collective-permute-start(bf16[4,264,2048]{2,1,0:T(8,128)(2,1)} %bitcast.24), channel_id=1, source_target_pairs={{0,1},{1,0},{2,3},{3,2},{4,5},{5,4},{6,7},{7,6},{8,9},{9,8},{10,11... | collective-permute-start | bytes 12976136 | tf_op jit(solution)/shard_map/ppermute | solution.py:307
  216.4 24.9 %all-to-all-start.1 = ((bf16[8,64,1536]{2,1,0:T(8,128)(2,1)}), bf16[8,64,1536]{2,1,0:T(8,128)(2,1)S(1)}, u32[]{:S(2)}, u32[]{:S(2)}) async-start(bf16[8,64,1536]{2,1,0:T(8,128)(2,1)} %reshape.382), calls=%async_computation.1 | async-start | bytes 3145728 | tf_op jit(solution)/shard_map/all_to_all | solution.py:777
  220.1 153.0 %all-gather.11.cloned.1.call-start = ((), (), s32[]{:S(2)}) async-start(), calls=%async_computation.9 | async-start | bytes 7864320 | tf_op jit(solution)/shard_map/all_gather | solution.py:778
  230.4 33.5 %collective-permute-start.7 = (bf16[2,264,1024]{2,1,0:T(8,128)(2,1)}, bf16[2,264,1024]{2,1,0:T(8,128)(2,1)}, u32[]{:S(2)}, u32[]{:S(2)}) collective-permute-start(bf16[2,264,1024]{2,1,0:T(8,128)(2,1)} %slice.582), channel_id=1, source_target_pairs={{0,4},{1,5},{2,6},{3,7},{4,0},{5,1},{6,2},{7,3},{8,12},{9,13},{10,... | collective-permute-start | bytes 3244040 | tf_op jit(solution)/shard_map/ppermute | solution.py:307
  242.4 177.5 %all-gather.13.cloned.1.call-start = ((), (), s32[]{:S(2)}) async-start(), calls=%async_computation.10 | async-start | bytes 3932160 | tf_op jit(solution)/shard_map/all_gather | solution.py:854
  245.9 27.0 %collective-permute-start.9 = (bf16[2,264,1024]{2,1,0:T(8,128)(2,1)S(1)}, bf16[2,264,1024]{2,1,0:T(8,128)(2,1)}, u32[]{:S(2)}, u32[]{:S(2)}) collective-permute-start(bf16[2,264,1024]{2,1,0:T(8,128)(2,1)S(1)} %slice.367), channel_id=1, source_target_pairs={{0,2},{1,3},{2,0},{3,1},{4,6},{5,7},{6,4},{7,5},{8,10},{9,11},{10,... | collective-permute-start | bytes 3244040 | tf_op jit(solution)/shard_map/ppermute | solution.py:307
  246.7 28.7 %collective-permute-start.23 = (bf16[1,264,1024]{2,1,0:T(8,128)(2,1)S(1)}, bf16[1,264,1024]{2,1,0:T(8,128)(2,1)S(1)}, u32[]{:S(2)}, u32[]{:S(2)}) collective-permute-start(bf16[1,264,1024]{2,1,0:T(8,128)(2,1)S(1)} %get-tuple-element.119), channel_id=1, source_target_pairs={{0,4},{1,5},{2,6},{3,7},{4,0},{5,1},{6,2},{7,3},{8,12},{9,13},{10,... | collective-permute-start | bytes 1622024 | tf_op jit(solution)/shard_map/ppermute | solution.py:307
  247.4 36.9 %collective-permute-start.21 = (bf16[1,264,1024]{2,1,0:T(8,128)(2,1)S(1)}, bf16[1,264,1024]{2,1,0:T(8,128)(2,1)S(1)}, u32[]{:S(2)}, u32[]{:S(2)}) collective-permute-start(bf16[1,264,1024]{2,1,0:T(8,128)(2,1)S(1)} %get-tuple-element.118), channel_id=1, source_target_pairs={{0,2},{1,3},{2,0},{3,1},{4,6},{5,7},{6,4},{7,5},{8,10},{9,11},{10,... | collective-permute-start | bytes 1622024 | tf_op jit(solution)/shard_map/ppermute | solution.py:307
  265.7 30.2 %collective-permute-start.8 = (bf16[1,264,1024]{2,1,0:T(8,128)(2,1)S(1)}, bf16[1,264,1024]{2,1,0:T(8,128)(2,1)S(1)}, u32[]{:S(2)}, u32[]{:S(2)}) collective-permute-start(bf16[1,264,1024]{2,1,0:T(8,128)(2,1)S(1)} %slice.590), channel_id=1, source_target_pairs={{0,2},{1,3},{2,0},{3,1},{4,6},{5,7},{6,4},{7,5},{8,10},{9,11},{10,... | collective-permute-start | bytes 1622024 | tf_op jit(solution)/shard_map/ppermute | solution.py:307
  274.5 21.6 %collective-permute-start.10 = (bf16[1,264,1024]{2,1,0:T(8,128)(2,1)S(1)}, bf16[1,264,1024]{2,1,0:T(8,128)(2,1)S(1)}, u32[]{:S(2)}, u32[]{:S(2)}) collective-permute-start(bf16[1,264,1024]{2,1,0:T(8,128)(2,1)S(1)} %slice.589), channel_id=1, source_target_pairs={{0,4},{1,5},{2,6},{3,7},{4,0},{5,1},{6,2},{7,3},{8,12},{9,13},{10,... | collective-permute-start | bytes 1622024 | tf_op jit(solution)/shard_map/ppermute | solution.py:307
  275.5 43.6 %collective-permute-start.24 = (bf16[2,264,1024]{2,1,0:T(8,128)(2,1)S(1)}, bf16[2,264,1024]{2,1,0:T(8,128)(2,1)S(1)}, u32[]{:S(2)}, u32[]{:S(2)}) collective-permute-start(bf16[2,264,1024]{2,1,0:T(8,128)(2,1)S(1)} %pad_maximum_fusion.9), channel_id=1, source_target_pairs={{0,2},{1,3},{2,0},{3,1},{4,6},{5,7},{6,4},{7,5},{8,10},{9,11},{10,... | collective-permute-start | bytes 3244040 | tf_op jit(solution)/shard_map/ppermute | solution.py:307
  284.4 46.4 %collective-permute-start.22 = (bf16[2,264,1024]{2,1,0:T(8,128)(2,1)S(1)}, bf16[2,264,1024]{2,1,0:T(8,128)(2,1)S(1)}, u32[]{:S(2)}, u32[]{:S(2)}) collective-permute-start(bf16[2,264,1024]{2,1,0:T(8,128)(2,1)S(1)} %pad_maximum_fusion.8), channel_id=1, source_target_pairs={{0,4},{1,5},{2,6},{3,7},{4,0},{5,1},{6,2},{7,3},{8,12},{9,13},{10,... | collective-permute-start | bytes 3244040 | tf_op jit(solution)/shard_map/ppermute | solution.py:307
  297.6 30.8 %collective-permute-start.11 = (bf16[1,264,1024]{2,1,0:T(8,128)(2,1)S(1)}, bf16[1,264,1024]{2,1,0:T(8,128)(2,1)S(1)}, u32[]{:S(2)}, u32[]{:S(2)}) collective-permute-start(bf16[1,264,1024]{2,1,0:T(8,128)(2,1)S(1)} %get-tuple-element.122), channel_id=1, source_target_pairs={{0,2},{1,3},{2,0},{3,1},{4,6},{5,7},{6,4},{7,5},{8,10},{9,11},{10,... | collective-permute-start | bytes 1622024 | tf_op jit(solution)/shard_map/ppermute | solution.py:307
  298.0 30.9 %collective-permute-start.13 = (bf16[1,264,1024]{2,1,0:T(8,128)(2,1)S(1)}, bf16[1,264,1024]{2,1,0:T(8,128)(2,1)S(1)}, u32[]{:S(2)}, u32[]{:S(2)}) collective-permute-start(bf16[1,264,1024]{2,1,0:T(8,128)(2,1)S(1)} %get-tuple-element.123), channel_id=1, source_target_pairs={{0,4},{1,5},{2,6},{3,7},{4,0},{5,1},{6,2},{7,3},{8,12},{9,13},{10,... | collective-permute-start | bytes 1622024 | tf_op jit(solution)/shard_map/ppermute | solution.py:307
  328.5 25.4 %collective-permute-start.12 = (bf16[2,264,1024]{2,1,0:T(8,128)(2,1)S(1)}, bf16[2,264,1024]{2,1,0:T(8,128)(2,1)S(1)}, u32[]{:S(2)}, u32[]{:S(2)}) collective-permute-start(bf16[2,264,1024]{2,1,0:T(8,128)(2,1)S(1)} %pad_maximum_fusion.6), channel_id=1, source_target_pairs={{0,4},{1,5},{2,6},{3,7},{4,0},{5,1},{6,2},{7,3},{8,12},{9,13},{10,... | collective-permute-start | bytes 3244040 | tf_op jit(solution)/shard_map/ppermute | solution.py:307
  329.0 24.8 %collective-permute-start.14 = (bf16[2,264,1024]{2,1,0:T(8,128)(2,1)S(1)}, bf16[2,264,1024]{2,1,0:T(8,128)(2,1)S(1)}, u32[]{:S(2)}, u32[]{:S(2)}) collective-permute-start(bf16[2,264,1024]{2,1,0:T(8,128)(2,1)S(1)} %pad_maximum_fusion.7), channel_id=1, source_target_pairs={{0,2},{1,3},{2,0},{3,1},{4,6},{5,7},{6,4},{7,5},{8,10},{9,11},{10,... | collective-permute-start | bytes 3244040 | tf_op jit(solution)/shard_map/ppermute | solution.py:307
  333.5 23.7 %collective-permute-start.25 = (bf16[4,264,2048]{2,1,0:T(8,128)(2,1)}, bf16[4,264,2048]{2,1,0:T(8,128)(2,1)}, u32[]{:S(2)}, u32[]{:S(2)}) collective-permute-start(bf16[4,264,2048]{2,1,0:T(8,128)(2,1)} %maximum_maximum_fusion.2), channel_id=1, source_target_pairs={{0,1},{1,0},{2,3},{3,2},{4,5},{5,4},{6,7},{7,6},{8,9},{9,8},{10,11... | collective-permute-start | bytes 12976136 | tf_op jit(solution)/shard_map/ppermute | solution.py:307
  356.8 383.6 %reduce-scatter.9.cloned.1.call-start = ((), (), s32[]{:S(2)}) async-start(), calls=%async_computation.13 | async-start | bytes 7864320 | tf_op jit(solution)/shard_map/reduce_scatter | solution.py:783
  468.8 21.8 %collective-permute-start.26 = (bf16[4,264,2048]{2,1,0:T(8,128)(2,1)}, bf16[4,264,2048]{2,1,0:T(8,128)(2,1)}, u32[]{:S(2)}, u32[]{:S(2)}) collective-permute-start(bf16[4,264,2048]{2,1,0:T(8,128)(2,1)} %bitcast.40), channel_id=1, source_target_pairs={{0,1},{1,0},{2,3},{3,2},{4,5},{5,4},{6,7},{7,6},{8,9},{9,8},{10,11... | collective-permute-start | bytes 12976136 | tf_op jit(solution)/shard_map/ppermute | solution.py:307
  490.3 271.3 %reduce-scatter.11.cloned.1.call-start = ((), (), s32[]{:S(2)}) async-start(), calls=%async_computation.14 | async-start | bytes 3932160 | tf_op jit(solution)/shard_map/reduce_scatter | solution.py:927
  496.2 25.6 %collective-permute-start.27 = (bf16[2,264,1024]{2,1,0:T(8,128)(2,1)S(1)}, bf16[2,264,1024]{2,1,0:T(8,128)(2,1)S(1)}, u32[]{:S(2)}, u32[]{:S(2)}) collective-permute-start(bf16[2,264,1024]{2,1,0:T(8,128)(2,1)S(1)} %slice.580), channel_id=1, source_target_pairs={{0,4},{1,5},{2,6},{3,7},{4,0},{5,1},{6,2},{7,3},{8,12},{9,13},{10,... | collective-permute-start | bytes 3244040 | tf_op jit(solution)/shard_map/ppermute | solution.py:307
  498.2 25.8 %collective-permute-start.29 = (bf16[2,264,1024]{2,1,0:T(8,128)(2,1)S(1)}, bf16[2,264,1024]{2,1,0:T(8,128)(2,1)S(1)}, u32[]{:S(2)}, u32[]{:S(2)}) collective-permute-start(bf16[2,264,1024]{2,1,0:T(8,128)(2,1)S(1)} %slice.402), channel_id=1, source_target_pairs={{0,2},{1,3},{2,0},{3,1},{4,6},{5,7},{6,4},{7,5},{8,10},{9,11},{10,... | collective-permute-start | bytes 3244040 | tf_op jit(solution)/shard_map/ppermute | solution.py:307
  522.4 13.3 %collective-permute-start.28 = (bf16[1,264,1024]{2,1,0:T(8,128)(2,1)S(1)}, bf16[1,264,1024]{2,1,0:T(8,128)(2,1)S(1)}, u32[]{:S(2)}, u32[]{:S(2)}) collective-permute-start(bf16[1,264,1024]{2,1,0:T(8,128)(2,1)S(1)} %slice.586), channel_id=1, source_target_pairs={{0,2},{1,3},{2,0},{3,1},{4,6},{5,7},{6,4},{7,5},{8,10},{9,11},{10,... | collective-permute-start | bytes 1622024 | tf_op jit(solution)/shard_map/ppermute | solution.py:307
  524.6 13.0 %collective-permute-start.30 = (bf16[1,264,1024]{2,1,0:T(8,128)(2,1)S(1)}, bf16[1,264,1024]{2,1,0:T(8,128)(2,1)S(1)}, u32[]{:S(2)}, u32[]{:S(2)}) collective-permute-start(bf16[1,264,1024]{2,1,0:T(8,128)(2,1)S(1)} %slice.585), channel_id=1, source_target_pairs={{0,4},{1,5},{2,6},{3,7},{4,0},{5,1},{6,2},{7,3},{8,12},{9,13},{10,... | collective-permute-start | bytes 1622024 | tf_op jit(solution)/shard_map/ppermute | solution.py:307
  553.7 23.3 %collective-permute-start.34 = (bf16[2,264,1024]{2,1,0:T(8,128)(2,1)}, bf16[2,264,1024]{2,1,0:T(8,128)(2,1)}, u32[]{:S(2)}, u32[]{:S(2)}) collective-permute-start(bf16[2,264,1024]{2,1,0:T(8,128)(2,1)} %pad_maximum_fusion.11), channel_id=1, source_target_pairs={{0,2},{1,3},{2,0},{3,1},{4,6},{5,7},{6,4},{7,5},{8,10},{9,11},{10,... | collective-permute-start | bytes 3244040 | tf_op jit(solution)/shard_map/ppermute | solution.py:307
  555.8 22.8 %collective-permute-start.32 = (bf16[2,264,1024]{2,1,0:T(8,128)(2,1)}, bf16[2,264,1024]{2,1,0:T(8,128)(2,1)}, u32[]{:S(2)}, u32[]{:S(2)}) collective-permute-start(bf16[2,264,1024]{2,1,0:T(8,128)(2,1)} %pad_maximum_fusion.10), channel_id=1, source_target_pairs={{0,4},{1,5},{2,6},{3,7},{4,0},{5,1},{6,2},{7,3},{8,12},{9,13},{10,... | collective-permute-start | bytes 3244040 | tf_op jit(solution)/shard_map/ppermute | solution.py:307
  584.0 21.1 %collective-permute-start.35 = (bf16[4,264,2048]{2,1,0:T(8,128)(2,1)}, bf16[4,264,2048]{2,1,0:T(8,128)(2,1)}, u32[]{:S(2)}, u32[]{:S(2)}) collective-permute-start(bf16[4,264,2048]{2,1,0:T(8,128)(2,1)} %maximum_maximum_fusion.3), channel_id=1, source_target_pairs={{0,1},{1,0},{2,3},{3,2},{4,5},{5,4},{6,7},{7,6},{8,9},{9,8},{10,11... | collective-permute-start | bytes 12976136 | tf_op jit(solution)/shard_map/ppermute | solution.py:307
  595.0 110.0 %collective-permute-start.16 = (bf16[4,264,2048]{2,1,0:T(8,128)(2,1)}, bf16[4,264,2048]{2,1,0:T(8,128)(2,1)}, u32[]{:S(2)}, u32[]{:S(2)}) collective-permute-start(bf16[4,264,2048]{2,1,0:T(8,128)(2,1)} %bitcast.34), channel_id=1, source_target_pairs={{0,1},{1,0},{2,3},{3,2},{4,5},{5,4},{6,7},{7,6},{8,9},{9,8},{10,11... | collective-permute-start | bytes 12976136 | tf_op jit(solution)/shard_map/ppermute | solution.py:307
  604.8 186.1 %reduce-scatter.7.cloned.1.call-start = ((), (), s32[]{:S(2)}) async-start(), calls=%async_computation.12 | async-start | bytes 1945600 | tf_op jit(solution)/shard_map/reduce_scatter | solution.py:967
  681.1 117.8 %reduce-scatter.5.cloned.1.call-start = ((), (), s32[]{:S(2)}) async-start(), calls=%async_computation.11 | async-start | bytes 3276800 | tf_op jit(solution)/shard_map/reduce_scatter | solution.py:783
  692.1 52.8 %collective-permute-start.36 = (bf16[4,264,2048]{2,1,0:T(8,128)(2,1)}, bf16[4,264,2048]{2,1,0:T(8,128)(2,1)}, u32[]{:S(2)}, u32[]{:S(2)}) collective-permute-start(bf16[4,264,2048]{2,1,0:T(8,128)(2,1)} %bitcast.185), channel_id=1, source_target_pairs={{0,1},{1,0},{2,3},{3,2},{4,5},{5,4},{6,7},{7,6},{8,9},{9,8},{10,11... | collective-permute-start | bytes 12976136 | tf_op jit(solution)/shard_map/ppermute | solution.py:307
  710.7 26.3 %collective-permute-start.17 = (bf16[2,264,1024]{2,1,0:T(8,128)(2,1)S(1)}, bf16[2,264,1024]{2,1,0:T(8,128)(2,1)S(1)}, u32[]{:S(2)}, u32[]{:S(2)}) collective-permute-start(bf16[2,264,1024]{2,1,0:T(8,128)(2,1)S(1)} %slice.581), channel_id=1, source_target_pairs={{0,4},{1,5},{2,6},{3,7},{4,0},{5,1},{6,2},{7,3},{8,12},{9,13},{10,... | collective-permute-start | bytes 3244040 | tf_op jit(solution)/shard_map/ppermute | solution.py:307
  712.5 26.0 %collective-permute-start.19 = (bf16[2,264,1024]{2,1,0:T(8,128)(2,1)S(1)}, bf16[2,264,1024]{2,1,0:T(8,128)(2,1)S(1)}, u32[]{:S(2)}, u32[]{:S(2)}) collective-permute-start(bf16[2,264,1024]{2,1,0:T(8,128)(2,1)S(1)} %slice.386), channel_id=1, source_target_pairs={{0,2},{1,3},{2,0},{3,1},{4,6},{5,7},{6,4},{7,5},{8,10},{9,11},{10,... | collective-permute-start | bytes 3244040 | tf_op jit(solution)/shard_map/ppermute | solution.py:307
  737.4 16.5 %collective-permute-start.18 = (bf16[1,264,1024]{2,1,0:T(8,128)(2,1)S(1)}, bf16[1,264,1024]{2,1,0:T(8,128)(2,1)}, u32[]{:S(2)}, u32[]{:S(2)}) collective-permute-start(bf16[1,264,1024]{2,1,0:T(8,128)(2,1)S(1)} %slice.588), channel_id=1, source_target_pairs={{0,2},{1,3},{2,0},{3,1},{4,6},{5,7},{6,4},{7,5},{8,10},{9,11},{10,... | collective-permute-start | bytes 1622024 | tf_op jit(solution)/shard_map/ppermute | solution.py:307
  739.1 20.2 %collective-permute-start.20 = (bf16[1,264,1024]{2,1,0:T(8,128)(2,1)S(1)}, bf16[1,264,1024]{2,1,0:T(8,128)(2,1)}, u32[]{:S(2)}, u32[]{:S(2)}) collective-permute-start(bf16[1,264,1024]{2,1,0:T(8,128)(2,1)S(1)} %slice.587), channel_id=1, source_target_pairs={{0,4},{1,5},{2,6},{3,7},{4,0},{5,1},{6,2},{7,3},{8,12},{9,13},{10,... | collective-permute-start | bytes 1622024 | tf_op jit(solution)/shard_map/ppermute | solution.py:307
  740.4 31.0 %all-to-all-start.3 = ((bf16[8,64,1536]{2,1,0:T(8,128)(2,1)}), bf16[8,64,1536]{2,1,0:T(8,128)(2,1)}, u32[]{:S(2)}, u32[]{:S(2)}) async-start(bf16[8,64,1536]{2,1,0:T(8,128)(2,1)} %bitcast.191), calls=%async_computation.6 | async-start | bytes 3145728 | tf_op jit(solution)/shard_map/all_to_all | solution.py:787
  751.9 50.8 %collective-permute-start.37 = (bf16[2,264,1024]{2,1,0:T(8,128)(2,1)}, bf16[2,264,1024]{2,1,0:T(8,128)(2,1)}, u32[]{:S(2)}, u32[]{:S(2)}) collective-permute-start(bf16[2,264,1024]{2,1,0:T(8,128)(2,1)} %slice.579), channel_id=1, source_target_pairs={{0,4},{1,5},{2,6},{3,7},{4,0},{5,1},{6,2},{7,3},{8,12},{9,13},{10,... | collective-permute-start | bytes 3244040 | tf_op jit(solution)/shard_map/ppermute | solution.py:307
  757.5 50.5 %collective-permute-start.39 = (bf16[2,264,1024]{2,1,0:T(8,128)(2,1)}, bf16[2,264,1024]{2,1,0:T(8,128)(2,1)}, u32[]{:S(2)}, u32[]{:S(2)}) collective-permute-start(bf16[2,264,1024]{2,1,0:T(8,128)(2,1)} %slice.418), channel_id=1, source_target_pairs={{0,2},{1,3},{2,0},{3,1},{4,6},{5,7},{6,4},{7,5},{8,10},{9,11},{10,... | collective-permute-start | bytes 3244040 | tf_op jit(solution)/shard_map/ppermute | solution.py:307
  798.9 15.3 %all-to-all-start.2 = ((bf16[8,64,640]{2,1,0:T(8,128)(2,1)}), bf16[8,64,640]{2,1,0:T(8,128)(2,1)S(1)}, u32[]{:S(2)}, u32[]{:S(2)}) async-start(bf16[8,64,640]{2,1,0:T(8,128)(2,1)} %bitcast.194), calls=%async_computation.3 | async-start | bytes 1310720 | tf_op jit(solution)/shard_map/all_to_all | solution.py:787
  806.0 19.5 %collective-permute-start.38 = (bf16[1,264,1024]{2,1,0:T(8,128)(2,1)}, bf16[1,264,1024]{2,1,0:T(8,128)(2,1)}, u32[]{:S(2)}, u32[]{:S(2)}) collective-permute-start(bf16[1,264,1024]{2,1,0:T(8,128)(2,1)} %slice.584), channel_id=1, source_target_pairs={{0,2},{1,3},{2,0},{3,1},{4,6},{5,7},{6,4},{7,5},{8,10},{9,11},{10,... | collective-permute-start | bytes 1622024 | tf_op jit(solution)/shard_map/ppermute | solution.py:307
  811.2 15.7 %collective-permute-start.40 = (bf16[1,264,1024]{2,1,0:T(8,128)(2,1)}, bf16[1,264,1024]{2,1,0:T(8,128)(2,1)}, u32[]{:S(2)}, u32[]{:S(2)}) collective-permute-start(bf16[1,264,1024]{2,1,0:T(8,128)(2,1)} %slice.583), channel_id=1, source_target_pairs={{0,4},{1,5},{2,6},{3,7},{4,0},{5,1},{6,2},{7,3},{8,12},{9,13},{10,... | collective-permute-start | bytes 1622024 | tf_op jit(solution)/shard_map/ppermute | solution.py:307
  (110 other events, 1245.4 us)
Sparse Core Ops, SparseCore 0:
  50.9 36.8 all-gather.14
  89.9 53.6 all-gather.8
  242.5 112.3 all-gather.10
  356.9 62.9 all-gather.12
  490.4 109.3 reduce-scatter.8
  604.9 59.5 reduce-scatter.10
  681.2 34.1 reduce-scatter.6
  717.7 51.0 reduce-scatter.4

commit v2 on v1

--- a/solution.py
+++ b/solution.py
@@ -307,48 +307,53 @@
     return lax.ppermute(block, "seq", route)
 
 
-def plane_bits():
-    return [1 << bit for bit in range(1, lax.axis_size("seq").bit_length() - 1)]
-
-
-def gather_plane(block):
-    half = block.shape[1] // 2
-    sides = []
-    for part, masks in (
-        (block[None, :, :half], plane_bits()),
-        (block[None, :, half:], plane_bits()[::-1]),
-    ):
-        order = [0]
-        for mask in masks:
-            part = jnp.concatenate([part, swap_with(part, mask)], axis=0)
-            order = order + [i ^ mask for i in order]
-        ranked = sorted(range(len(order)), key=order.__getitem__)
-        if ranked != list(range(len(order))):
-            part = jnp.concatenate([part[i : i + 1] for i in ranked], axis=0)
-        sides.append(part)
-    near = jnp.concatenate(sides, axis=2)
-    return jnp.concatenate([near, swap_with(near, 1)], axis=0)
-
-
-def reduce_plane(partial_rows):
-    count, _, depth = partial_rows.shape
-    near = partial_rows[: count // 2].astype(jnp.float32) + swap_with(
-        partial_rows[count // 2 :].astype(jnp.bfloat16), 1
-    ).astype(jnp.float32)
-    upper, lower = near[:, :, : depth // 2], near[:, :, depth // 2 :]
-    for mask in plane_bits()[::-1]:
-        middle = upper.shape[0] // 2
-        upper = upper[:middle] + swap_with(upper[middle:].astype(jnp.bfloat16), mask).astype(
-            jnp.float32
-        )
-    for mask in plane_bits():
-        lower = lower[0::2] + swap_with(lower[1::2].astype(jnp.bfloat16), mask).astype(jnp.float32)
-    return jnp.concatenate([upper[0], lower[0]], axis=1)
+CORE, ACROSS_X, ACROSS_Y = 1, 2, 4
+
+
+def split_row(rows):
+    return rows // 32 * 16
+
+
+def gather_chips(block, *others):
+    split = split_row(block.shape[0])
+    across_x, across_y = swap_with(block, ACROSS_X), swap_with(block, ACROSS_Y)
+    if others:
+        across_x, across_y, *others = lax.optimization_barrier((across_x, across_y, *others))
+    both = [swap_with(across_y[:split], ACROSS_X), swap_with(across_x[split:], ACROSS_Y)]
+    near = jnp.concatenate([block, across_x, across_y, *both]).reshape(4, *block.shape)
+    return (near, *others) if others else near
+
+
+def gather_chips_at_once(block):
+    return jnp.stack(
+        [block] + [swap_with(block, mask) for mask in (ACROSS_X, ACROSS_Y, ACROSS_X + ACROSS_Y)]
+    )
+
+
+def reduce_plane(near, far, late=None):
+    other = swap_with(far, CORE)
+    if late is not None:
+        other, late = lax.optimization_barrier((other, late))
+    rows = near.shape[1]
+    split = split_row(rows)
+
+    def total(place, span=slice(None)):
+        return near[place, span].astype(jnp.float32) + other[place, span].astype(jnp.float32)
+
+    both = total(3).astype(jnp.bfloat16)
+    first = swap_with(both[:split], ACROSS_Y).astype(jnp.float32)
+    second = swap_with(both[split:], ACROSS_X).astype(jnp.float32)
+    across_x = jnp.concatenate([total(1, slice(split)) + first, total(1, slice(split, None))])
+    across_y = jnp.concatenate([total(2, slice(split)), total(2, slice(split, None)) + second])
+    across_x = swap_with(across_x.astype(jnp.bfloat16), ACROSS_X).astype(jnp.float32)
+    across_y = swap_with(across_y.astype(jnp.bfloat16), ACROSS_Y).astype(jnp.float32)
+    result = total(0) + across_x + across_y
+    return result if late is None else (result, late)
 
 
 def place_of(chunk, me, count):
     relative = jnp.bitwise_xor(chunk, me)
-    return jnp.bitwise_and(relative, 1) * (count // 2) + jnp.right_shift(relative, 1)
+    return jnp.bitwise_and(relative, 1), jnp.right_shift(relative, 1)
 
 
 def series_expm1(values):
@@ -385,6 +390,17 @@
 
 
 ROWS = 8
+
+
+def tiles_at_once(tiles):
+    return max(size for size in range(1, GROUP + 1) if tiles % size == 0)
+
+
+def group_tiles(index, group):
+    return [index * group + member for member in range(group)]
+
+
+GROUP = 11
 TAP, BIAS, BIAS_A, BIAS_I, RATE = 0, 4, 5, 6, 7
 
 
@@ -392,7 +408,8 @@
     taps,
     slots,
     info_ref,
-    normed_ref,
+    near_ref,
+    far_ref,
     proj_ref,
     gate_ref,
     channel_ref,
@@ -405,6 +422,7 @@
     hidden_ref,
     lag_edge_ref,
     hidden_edge_ref,
+    proj_wide,
     projected,
     convolved,
     gates,
@@ -412,23 +430,38 @@
     edge,
 ):
     chunk = pl.program_id(0)
+    is_far, _ = place_of(chunk, info_ref[0], pl.num_programs(0))
     rows, lanes = convolved.shape
     tiles = rows // ROWS
+    group = tiles_at_once(tiles)
     total = rows * pl.num_programs(0)
 
     @pl.when(chunk == 0)
     def _():
         carry[...] = jnp.zeros_like(carry)
         edge[...] = jnp.zeros_like(edge)
-
-    product = jnp.dot(normed_ref[0], proj_ref[...], preferred_element_type=jnp.float32)
-    low = product[:, :lanes].astype(jnp.bfloat16)
-    lagging_ref[0] = low
-    projected[:, :lanes] = low.astype(jnp.float32)
-    branch_ref[0] = product[:, lanes:]
+        channels = proj_ref.shape[1] // 2
+        proj_wide[...] = jnp.zeros_like(proj_wide)
+        proj_wide[:, :channels] = proj_ref[:, :channels]
+        proj_wide[:, lanes : lanes + channels] = proj_ref[:, channels:]
+
+    def project(normed_ref):
+        product = jnp.dot(normed_ref[0], proj_wide[...], preferred_element_type=jnp.float32)
+        low = product[:, :lanes].astype(jnp.bfloat16)
+        lagging_ref[0] = low
+        projected[:, :lanes] = low.astype(jnp.float32)
+        branch_ref[0] = product[:, lanes:]
+
+    pl.when(is_far == 0)(lambda: project(near_ref))
+    pl.when(is_far == 1)(lambda: project(far_ref))
     place = lax.broadcasted_iota(jnp.int32, (ROWS, lanes), 0)
 
     def convolve(tile, before):
+        for tile in group_tiles(tile, group):
+            before = convolve_tile(tile, before)
+        return before
+
+    def convolve_tile(tile, before):
         at = pl.ds(pl.multiple_of(tile * ROWS, ROWS), ROWS)
         here = projected[at, :lanes]
         since, _ = segment_reach(info_ref, chunk * rows + tile * ROWS, slots, (ROWS, 128), total)
@@ -443,7 +476,7 @@
         convolved[at, :] = value
         return here
 
-    last = lax.fori_loop(0, tiles, convolve, edge[...])
+    last = lax.fori_loop(0, tiles // group, convolve, edge[...])
     edge[...] = last
     lag_edge_ref[0] = last
     conv_low = convolved[...].astype(jnp.bfloat16)
@@ -452,6 +485,16 @@
     gates[...] = jnp.dot(conv_low, gate_ref[...], preferred_element_type=jnp.float32)
 
     def recur(tile, state):
+        parts = [local_scan(tile) for tile in group_tiles(tile, group)]
+        for at, value, decay in parts:
+            hidden = value + decay * state
+            state = jnp.broadcast_to(hidden[ROWS - 1 :], hidden.shape)
+            hidden_ref[0, at, :] = hidden
+            projected[at, :lanes] = hidden * projected[at, :lanes]
+        hidden_edge_ref[0] = hidden
+        return state
+
+    def local_scan(tile):
         at = pl.ds(pl.multiple_of(tile * ROWS, ROWS), ROWS)
         since, _ = segment_reach(info_ref, chunk * rows + tile * ROWS, slots, (ROWS, 128), total)
         starts = widen(since == 0, lanes)
@@ -467,13 +510,10 @@
             inside = place >= step
             value = value + jnp.where(inside, decay * pltpu.roll(value, step, 0), 0.0)
             decay = jnp.where(inside, decay * pltpu.roll(decay, step, 0), decay)
-        hidden = value + decay * state
-        hidden_ref[0, at, :] = hidden
-        projected[at, :lanes] = hidden * gelu_parts(branch_ref[0, at, :])[0]
-        hidden_edge_ref[0] = hidden
-        return jnp.broadcast_to(hidden[ROWS - 1 :], hidden.shape)
-
-    carry[...] = lax.fori_loop(0, tiles, recur, carry[...])
+        projected[at, :lanes] = gelu_parts(branch_ref[0, at, :])[0]
+        return at, value, decay
+
+    carry[...] = lax.fori_loop(0, tiles // group, recur, carry[...])
     gated_ref[0] = projected[:, :lanes].astype(jnp.bfloat16)
 
 
@@ -481,7 +521,8 @@
     taps,
     slots,
     info_ref,
-    down_ref,
+    near_ref,
+    far_ref,
     out_ref,
     gate_ref,
     channel_ref,
@@ -509,8 +550,10 @@
     lap = pl.program_id(0)
     laps = pl.num_programs(0)
     chunk = laps - 1 - lap
+    is_far, _ = place_of(chunk, info_ref[0], laps)
     rows, lanes = conv_part.shape
     tiles = rows // ROWS
+    group = tiles_at_once(tiles)
     total = rows * laps
 
     @pl.when(lap == 0)
@@ -521,9 +564,13 @@
         sums[...] = jnp.zeros_like(sums)
         gate_grad_ref[...] = jnp.zeros_like(gate_grad_ref)
 
-    coming[...] = lax.dot_general(
-        down_ref[0], out_ref[...], (((1,), (1,)), ((), ())), preferred_element_type=jnp.float32
-    )
+    def expand(down_ref):
+        coming[...] = lax.dot_general(
+            down_ref[0], out_ref[...], (((1,), (1,)), ((), ())), preferred_element_type=jnp.float32
+        )
+
+    pl.when(is_far == 0)(lambda: expand(near_ref))
+    pl.when(is_far == 1)(lambda: expand(far_ref))
     lagged[...] = lagging_ref[0].astype(jnp.float32)
     conv_part[...] = conv_ref[0].astype(jnp.float32)
     place = lax.broadcasted_iota(jnp.int32, (ROWS, lanes), 0)
@@ -531,45 +578,62 @@
 
     def recur(step_index, carried):
         later_grad, later_decay, sum_a, sum_i, sum_rate = carried
-        tile = tiles - 1 - step_index
+        members = group_tiles(tiles // group - 1 - step_index, group)[::-1]
+        parts = []
+        for tile in members:
+            part = local_scan(tile, later_decay)
+            later_decay = part[-1]
+            parts.append(part)
+        for tile, (at, value, weight, _) in zip(members, parts):
+            grad = value + weight * later_grad
+            later_grad = jnp.broadcast_to(grad[:1], grad.shape)
+            grad_a, grad_i, grad_rate = gate_grads(tile, at, grad)
+            sum_a = sum_a + grad_a
+            sum_i = sum_i + grad_i
+            sum_rate = sum_rate - gate_scale * grad_rate
+        return later_grad, later_decay, sum_a, sum_i, sum_rate
+
+    def local_scan(tile, later_decay):
         at = pl.ds(pl.multiple_of(tile * ROWS, ROWS), ROWS)
+        since, _ = segment_reach(info_ref, chunk * rows + tile * ROWS, slots, (ROWS, 128), total)
+        starts = widen(since == 0, lanes)
+        plain = 1.0 + series_expm1(-gate_scale * gate_r_ref[0, at, :] * channel_ref[RATE : RATE + 1, :])
+        decay = jnp.where(starts, 0.0, plain)
+        activated, slope = gelu_parts(branch_ref[0, at, :])
+        down = coming[at, :]
+        value = down * activated
+        projected[at, lanes:] = down * hidden_ref[0, at, :] * slope
+        weight = jnp.where(place == ROWS - 1, later_decay, pltpu.roll(decay, ROWS - 1, 0))
+        for step in (1, 2, 4):
+            inside = place < ROWS - step
+            value = value + jnp.where(inside, weight * pltpu.roll(value, ROWS - step, 0), 0.0)
+            weight = jnp.where(inside, weight * pltpu.roll(weight, ROWS - step, 0), weight)
+        return at, value, weight, jnp.broadcast_to(decay[:1], decay.shape)
+
+    def gate_grads(tile, at, grad):
         ahead = pl.ds(pl.multiple_of(jnp.maximum(tile - 1, 0) * ROWS, ROWS), ROWS)
         since, _ = segment_reach(info_ref, chunk * rows + tile * ROWS, slots, (ROWS, 128), total)
         starts = widen(since == 0, lanes)
         gate_r = gate_r_ref[0, at, :]
         gate_i = gate_i_ref[0, at, :]
-        hidden = hidden_ref[0, at, :]
         conv = conv_part[at, :]
         rate = channel_ref[RATE : RATE + 1, :]
-        log_step = -gate_scale * gate_r * rate
-        less = series_expm1(log_step)
+        less = series_expm1(-gate_scale * gate_r * rate)
         plain = 1.0 + less
         root = jnp.sqrt(-less * (2.0 + less))
-        decay = jnp.where(starts, 0.0, plain)
-        scaling = jnp.where(starts, 1.0, root)
-        activated, slope = gelu_parts(branch_ref[0, at, :])
-        down = coming[at, :]
-        value = down * activated
-        projected[at, lanes:] = down * hidden * slope
-        weight = jnp.where(place == ROWS - 1, later_decay, pltpu.roll(decay, ROWS - 1, 0))
-        for step in (1, 2, 4):
-            inside = place < ROWS - step
-            value = value + jnp.where(inside, weight * pltpu.roll(value, ROWS - step, 0), 0.0)
-            weight = jnp.where(inside, weight * pltpu.roll(weight, ROWS - step, 0), weight)
-        grad = value + weight * later_grad
         earlier = jnp.where(
             tile == 0,
             jnp.where(first_chunk, 0.0, hidden_edge_ref[0]),
             hidden_ref[0, ahead, :],
         )
-        before = jnp.where(place == 0, pltpu.roll(earlier, 1, 0), pltpu.roll(hidden, 1, 0))
-        scaled = grad * scaling
+        before = jnp.where(
+            place == 0, pltpu.roll(earlier, 1, 0), pltpu.roll(hidden_ref[0, at, :], 1, 0)
+        )
+        scaled = grad * jnp.where(starts, 1.0, root)
         conv_part[at, :] = scaled * gate_i
         grad_i = scaled * conv * gate_i * (1.0 - gate_i)
         grad_log = jnp.where(
-            starts,
-            0.0,
-            grad * plain * (before - conv * gate_i * plain / root),
+            starts, 0.0, grad * plain * (before - conv * gate_i * plain / root)
         )
         grad_rate = grad_log * gate_r
         grad_a = -gate_scale * rate * grad_rate * (1.0 - gate_r)
@@ -577,17 +641,11 @@
         grad_i = grad_i.astype(jnp.bfloat16).astype(jnp.float32)
         gates[at, :lanes] = grad_a
         gates[at, lanes:] = grad_i
-        return (
-            jnp.broadcast_to(grad[:1], grad.shape),
-            jnp.broadcast_to(decay[:1], decay.shape),
-            sum_a + grad_a,
-            sum_i + grad_i,
-            sum_rate - gate_scale * grad_rate,
-        )
+        return grad_a, grad_i, grad_rate
 
     empty = jnp.zeros((ROWS, lanes), jnp.float32)
     grad_last, decay_last, sum_a, sum_i, sum_rate = lax.fori_loop(
-        0, tiles, recur, (grad_carry[...], decay_carry[...], empty, empty, empty)
+        0, tiles // group, recur, (grad_carry[...], decay_carry[...], empty, empty, empty)
     )
     grad_carry[...] = grad_last
     decay_carry[...] = decay_last
@@ -602,6 +660,11 @@
     conv_grad[:rows, :] = (conv_part[...] + from_gates).astype(jnp.bfloat16).astype(jnp.float32)
 
     def unconvolve(tile, carried):
+        for tile in group_tiles(tile, group):
+            carried = unconvolve_tile(tile, carried)
+        return carried
+
+    def unconvolve_tile(tile, carried):
         earlier, sum_bias, sum_taps = carried
         at = pl.ds(pl.multiple_of(tile * ROWS, ROWS), ROWS)
         beyond = pl.ds(pl.multiple_of((tile + 1) * ROWS, ROWS), ROWS)
@@ -630,9 +693,12 @@
         return here, sum_bias + grad, tuple(new_taps)
 
     _, sum_bias, sum_taps = lax.fori_loop(
-        0, tiles, unconvolve, (lag_edge_ref[0], empty, (empty,) * taps)
-    )
-    projected_ref[0] = projected[...].astype(jnp.bfloat16)
+        0, tiles // group, unconvolve, (lag_edge_ref[0], empty, (empty,) * taps)
+    )
+    low = projected[...].astype(jnp.bfloat16)
+    channels = projected_ref.shape[2] // 2
+    projected_ref[0, :, :channels] = low[:, :channels]
+    projected_ref[0, :, channels:] = low[:, lanes : lanes + channels]
     for place_in, part in enumerate((*sum_taps, sum_bias, sum_a, sum_i, sum_rate)):
         sums[place_in] += part
 
@@ -644,12 +710,17 @@
 VMEM_LIMIT = 48 * 1024 * 1024
 
 
-def run_forward(info, normed, proj, gate, channels, taps, slots):
-    count, rows, depth = normed.shape
+def run_forward(info, near, far, proj, gate, channels, taps, slots):
+    chips, rows, depth = near.shape
+    count = 2 * chips
     lanes = gate.shape[0]
 
+    def at_chip(chunk, info_ref):
+        return (place_of(chunk, info_ref[0], count)[1], 0, 0)
+
     def at_place(chunk, info_ref):
-        return (place_of(chunk, info_ref[0], count), 0, 0)
+        is_far, chip = place_of(chunk, info_ref[0], count)
+        return (is_far * chips + chip, 0, 0)
 
     def at_chunk(chunk, info_ref):
         return (chunk, 0, 0)
@@ -660,6 +731,7 @@
     def block(kind):
         return jax.ShapeDtypeStruct((count, rows, lanes), kind)
 
+    wide = pl.BlockSpec((1, rows, depth), at_chip)
     narrow = pl.BlockSpec((1, rows, lanes), at_place)
     return pl.pallas_call(
         partial(mixer_forward, taps, slots),
@@ -667,13 +739,16 @@
             num_scalar_prefetch=1,
             grid=(count,),
             in_specs=[
-                pl.BlockSpec((1, rows, depth), at_place),
+                wide,
+                wide,
                 pl.BlockSpec(proj.shape, whole),
                 pl.BlockSpec(gate.shape, whole),
                 pl.BlockSpec(channels.shape, whole),
             ],
-            out_specs=[narrow] * 7 + [pl.BlockSpec((1, ROWS, lanes), at_chunk)] * 2,
+            out_specs=[narrow] * 7
+            + [pl.BlockSpec((1, ROWS, lanes), at_chunk)] * 2,
             scratch_shapes=[
+                pltpu.VMEM((depth, 2 * lanes), jnp.bfloat16),
                 pltpu.VMEM((rows, lanes), jnp.float32),
                 pltpu.VMEM((rows, lanes), jnp.float32),
                 pltpu.VMEM((rows, 2 * lanes), jnp.float32),
@@ -694,22 +769,23 @@
         compiler_params=pltpu.CompilerParams(
             dimension_semantics=("arbitrary",), vmem_limit_bytes=VMEM_LIMIT
         ),
-        cost_estimate=pl.CostEstimate(
-            flops=2 * count * rows * lanes * (2 * depth + 2 * lanes),
-            bytes_accessed=2 * normed.size + 25 * count * rows * lanes,
-            transcendentals=5 * count * rows * lanes,
-        ),
+        cost_estimate=pl.CostEstimate(flops=0, bytes_accessed=0, transcendentals=0),
         name="mixer_forward",
-    )(info, normed, proj, gate, channels)
-
-
-def run_backward(info, down, out, gate, channels, saved, taps, slots):
-    _, lagging, conv, branch, gate_r, gate_i, hidden, lag_edge, hidden_edge = saved
-    count, rows, depth = down.shape
+    )(info, near, far, proj, gate, channels)
+
+
+def run_backward(info, near, far, out, gate, channels, saved, proj_columns, taps, slots):
+    lagging, conv, branch, gate_r, gate_i, hidden, lag_edge, hidden_edge = saved
+    chips, rows, depth = near.shape
+    count = 2 * chips
     lanes = gate.shape[0]
 
+    def at_chip(lap, info_ref):
+        return (place_of(count - 1 - lap, info_ref[0], count)[1], 0, 0)
+
     def at_place(lap, info_ref):
-        return (place_of(count - 1 - lap, info_ref[0], count), 0, 0)
+        is_far, chip = place_of(count - 1 - lap, info_ref[0], count)
+        return (is_far * chips + chip, 0, 0)
 
     def before(lap, info_ref):
         return (jnp.maximum(count - 2 - lap, 0), 0, 0)
@@ -717,6 +793,7 @@
     def whole(lap, info_ref):
         return (0, 0)
 
+    wide = pl.BlockSpec((1, rows, depth), at_chip)
     narrow = pl.BlockSpec((1, rows, lanes), at_place)
     rim = pl.BlockSpec((1, ROWS, lanes), before)
     sums = taps + 4
@@ -726,21 +803,16 @@
             num_scalar_prefetch=1,
             grid=(count,),
             in_specs=[
-                pl.BlockSpec((1, rows, depth), at_place),
+                wide,
+                wide,
                 pl.BlockSpec(out.shape, whole),
                 pl.BlockSpec(gate.shape, whole),
                 pl.BlockSpec(channels.shape, whole),
-                narrow,
-                narrow,
-                narrow,
-                narrow,
-                narrow,
-                narrow,
-                rim,
-                rim,
-            ],
+            ]
+            + [narrow] * 6
+            + [rim] * 2,
             out_specs=[
-                pl.BlockSpec((1, rows, 2 * lanes), at_place),
+                pl.BlockSpec((1, rows, proj_columns), at_place),
                 pl.BlockSpec((lanes, 2 * lanes), whole),
                 pl.BlockSpec((sums, lanes), whole),
             ],
@@ -757,40 +829,105 @@
             ],
         ),
         out_shape=[
-            jax.ShapeDtypeStruct((count, rows, 2 * lanes), jnp.bfloat16),
+            jax.ShapeDtypeStruct((count, rows, proj_columns), jnp.bfloat16),
             jax.ShapeDtypeStruct((lanes, 2 * lanes), jnp.float32),
             jax.ShapeDtypeStruct((sums, lanes), jnp.float32),
         ],
         compiler_params=pltpu.CompilerParams(
             dimension_semantics=("arbitrary",), vmem_limit_bytes=VMEM_LIMIT
         ),
-        cost_estimate=pl.CostEstimate(
-            flops=2 * count * rows * lanes * (depth + 4 * lanes),
-            bytes_accessed=2 * down.size + 24 * count * rows * lanes,
-            transcendentals=3 * count * rows * lanes,
-        ),
+        cost_estimate=pl.CostEstimate(flops=0, bytes_accessed=0, transcendentals=0),
         name="mixer_backward",
-    )(info, down, out, gate, channels, branch, hidden, gate_r, gate_i, conv, lagging, lag_edge, hidden_edge)
-
-
-def hand_out(rows, groups):
+    )(
+        info, near, far, out, gate, channels,
+        branch, hidden, gate_r, gate_i, conv, lagging, lag_edge, hidden_edge,
+    )
+
+
+def deal_columns(moves, whole_ref, groups_ref):
+    for group, inside, column, width in moves:
+        groups_ref[group, :, inside : inside + width] = whole_ref[:, column : column + width]
+
+
+def collect_columns(moves, groups_ref, weight_ref, whole_ref, lean_ref):
+    for group, inside, column, width in moves:
+        whole_ref[:, column : column + width] = groups_ref[
+            group, :, inside : inside + width
+        ].astype(jnp.float32)
+    lean = jnp.zeros((weight_ref.shape[0], 128), jnp.float32)
+    for column in range(0, weight_ref.shape[1], 128):
+        span = slice(column, column + 128)
+        lean = lean + whole_ref[:, span] * weight_ref[:, span].astype(jnp.float32)
+    lean_ref[...] = jnp.sum(lean, axis=1, keepdims=True)
+
+
+def hand_out(weight, moves):
+    count = lax.axis_size("seq")
+    rows, columns = weight.shape
+    groups = pl.pallas_call(
+        partial(deal_columns, moves),
+        out_shape=jax.ShapeDtypeStruct((count, rows, columns // count), weight.dtype),
+        compiler_params=pltpu.CompilerParams(vmem_limit_bytes=VMEM_LIMIT),
+        name="deal_columns",
+    )(weight)
     dealt = lax.all_to_all(groups, "seq", split_axis=0, concat_axis=0, tiled=True)
-    return lax.all_gather(dealt.reshape(-1, groups.shape[2]), "bucket", axis=0, tiled=True)
-
-
-def hand_back(grad):
+    return dealt.reshape(-1, columns // count)
+
+
+def sum_planes(grad):
+    return lax.psum_scatter(
+        grad.astype(jnp.bfloat16), "bucket", scatter_dimension=0, tiled=True
+    )
+
+
+def hand_back(summed, weight, gain, moves):
     count = lax.axis_size("seq")
-    summed = lax.psum_scatter(
-        grad.astype(jnp.bfloat16), "bucket", scatter_dimension=0, tiled=True
-    )
-    blocks = summed.reshape(count, -1, grad.shape[1])
-    return lax.all_to_all(blocks, "seq", split_axis=0, concat_axis=0, tiled=True).astype(
-        jnp.float32
-    )
+    rows, columns = weight.shape
+    blocks = lax.all_to_all(
+        summed.reshape(count, rows, columns // count), "seq", split_axis=0, concat_axis=0, tiled=True
+    )
+    whole, lean = pl.pallas_call(
+        partial(collect_columns, moves),
+        out_shape=[
+            jax.ShapeDtypeStruct((rows, columns), jnp.float32),
+            jax.ShapeDtypeStruct((rows, 1), jnp.float32),
+        ],
+        compiler_params=pltpu.CompilerParams(vmem_limit_bytes=VMEM_LIMIT),
+        name="collect_columns",
+    )(blocks, weight)
+    return whole, lean[:, 0] / gain.astype(jnp.float32)
+
+
+FOLD = 512
+
+
+def fold_columns(values):
+    return jnp.concatenate(
+        [values[:, column : column + FOLD] for column in range(0, values.shape[1], FOLD)]
+    )
+
+
+def unfold_columns(folded, *shapes):
+    wholes, row = [], 0
+    for rows, columns in shapes:
+        pieces = []
+        for _ in range(0, columns, FOLD):
+            pieces.append(folded[:, row : row + rows].reshape(-1, FOLD))
+            row += rows
+        wholes.append(jnp.concatenate(pieces, axis=1))
+    return wholes
 
 
 def pad_lanes(values, lanes):
     return jnp.pad(values, [(0, 0)] * (values.ndim - 1) + [(0, lanes - values.shape[-1])])
+
+
+def contract_halves(left_near, left_far, right_near, right_far, kind=jnp.bfloat16):
+    parts = [
+        contract_first(left.reshape(-1, left.shape[-1]), right.reshape(-1, right.shape[-1]))
+        for left, right in ((left_near, right_near), (left_far, right_far))
+    ]
+    return (parts[0] + parts[1]).astype(kind)
 
 
 def by_channels(
@@ -831,28 +968,53 @@
         [out_proj, gate_weight, conv_weight, conv_bias[:, None], gate_bias, decay[:, None]], axis=1
     )
     by_row_width = by_row.shape[1]
-    by_row = lax.all_gather(
-        pad_lanes(by_row, -(-by_row_width // 128) * 128), "bucket", axis=0, tiled=False
-    )
-    gains = jnp.stack([norm_gain, mlp_gain])[None]
-    gains = lax.all_gather(gains, "seq", axis=0, tiled=True)
-    gains = lax.all_gather(gains[None], "bucket", axis=0, tiled=True).astype(jnp.float32)
-    gain_one, gain_two = gains[:, :, 0].reshape(1, depth), gains[:, :, 1].reshape(1, depth)
-    proj_groups = (
-        in_proj.reshape(own_rows, 2, 2, held, count // 2, block_width)
-        .transpose(4, 2, 0, 1, 3, 5)
-        .reshape(count, own_rows, 2 * channels)
-    )
-    proj = hand_out(own_rows, proj_groups)
-    proj = pad_lanes(proj.reshape(depth, 2, channels), lanes).reshape(depth, 2 * lanes)
-    wide_groups = (
-        gate_up.reshape(own_rows, 2, planes, count, hidden_rows)
-        .transpose(3, 0, 1, 2, 4)
-        .reshape(count, own_rows, 2 * hidden_width)
-    )
-    wide = hand_out(own_rows, wide_groups)
-    narrow = lax.all_gather(down_proj, "bucket", axis=0, tiled=True)
-
+    gains = jnp.pad(
+        jnp.stack([norm_gain, mlp_gain], axis=1), [(0, chunk_rows - own_rows), (0, 0)]
+    )
+    by_row = jnp.concatenate([by_row, gains], axis=1)
+    by_row = pad_lanes(by_row, -(-(by_row_width + 2) // 128) * 128)
+    by_row, in_proj = lax.optimization_barrier((by_row, in_proj))
+    by_row = lax.all_gather(by_row, "bucket", axis=0, tiled=False)
+    proj_moves = [
+        (
+            2 * pair + side,
+            (half * held + index) * block_width,
+            half * width + ((side * held + index) * (count // 2) + pair) * block_width,
+            block_width,
+        )
+        for pair in range(count // 2)
+        for side in range(2)
+        for half in range(2)
+        for index in range(held)
+    ]
+    wide_moves = [
+        (
+            member,
+            (half * planes + plane) * hidden_rows,
+            half * planes * count * hidden_rows + (plane * count + member) * hidden_rows,
+            hidden_rows,
+        )
+        for member in range(count)
+        for half in range(2)
+        for plane in range(planes)
+    ]
+    tokens_near = gather_chips(tokens[0])
+    tokens_far = swap_with(tokens_near, CORE)
+    proj_dealt = hand_out(in_proj, proj_moves)
+    gains = by_row[:, :own_rows, by_row_width : by_row_width + 2]
+    gains = lax.all_gather(gains.transpose(2, 0, 1), "seq", axis=2).astype(jnp.float32)
+    gain_one, gain_two = gains.reshape(2, 1, depth)
+    gate_up_late, proj_dealt = lax.optimization_barrier((gate_up, proj_dealt))
+    wide_dealt = hand_out(gate_up_late, wide_moves)
+    proj = lax.all_gather(proj_dealt, "bucket", axis=0, tiled=True)
+
+    ends = jnp.cumsum(lengths[0]).astype(jnp.int32)
+    info = jnp.concatenate([me[None].astype(jnp.int32), ends])
+
+    positions = me * rows + jnp.arange(rows, dtype=jnp.int32)
+    keep = (positions < ends[-1]).astype(jnp.float32)[:, None]
+    upstream = keep * cotangent[0].astype(jnp.float32)
+    scale_one = lax.rsqrt(jnp.mean(inputs * inputs, axis=1, keepdims=True) + norm_eps)
     kept = lax.dynamic_slice_in_dim(by_row, odd * held, held, 0)
     given = lax.dynamic_slice_in_dim(by_row, (1 - odd) * held, held, 0)
     taken = swap_with(given, 1)
@@ -881,33 +1043,68 @@
     decay_channel = small[taps + 3]
     rate = jnp.pad(jax.nn.softplus(decay_channel), (0, lanes - channels), constant_values=0.01)
     channel = jnp.concatenate([pad_lanes(small[: taps + 3], lanes), rate[None]], axis=0)
-    ends = jnp.cumsum(lengths[0]).astype(jnp.int32)
-    info = jnp.concatenate([me[None].astype(jnp.int32), ends])
-
-    positions = me * rows + jnp.arange(rows, dtype=jnp.int32)
-    keep = (positions < ends[-1]).astype(jnp.float32)[:, None]
-    upstream = keep * cotangent[0].astype(jnp.float32)
-    scale_one = lax.rsqrt(jnp.mean(inputs * inputs, axis=1, keepdims=True) + norm_eps)
-    normed = gather_plane((inputs * scale_one * gain_one).astype(jnp.bfloat16))
-    upstream_all = gather_plane(upstream.astype(jnp.bfloat16)).reshape(-1, depth)
-    saved = run_forward(info, normed, proj, gate, channel, taps, slots)
-    gated = saved[0].reshape(-1, lanes)
-    mixed_part = jnp.dot(gated, out, preferred_element_type=jnp.float32).astype(jnp.bfloat16)
-    residual = inputs + reduce_plane(mixed_part.reshape(count, rows, depth))
+
+    def normalize(low):
+        values = low.astype(jnp.float32)
+        scale = lax.rsqrt(jnp.mean(values * values, axis=2, keepdims=True) + norm_eps)
+        return (values * scale * gain_one).astype(jnp.bfloat16)
+
+    upstream_low, wide_dealt = lax.optimization_barrier(
+        (upstream.astype(jnp.bfloat16), wide_dealt)
+    )
+    upstream_near = gather_chips(upstream_low)
+    upstream_far = swap_with(upstream_near, CORE)
+    normed_near, normed_far = normalize(tokens_near), normalize(tokens_far)
+    normed_near, normed_far, upstream_near = lax.optimization_barrier(
+        (normed_near, normed_far, upstream_near)
+    )
+    feed_weights = lax.all_gather(
+        jnp.concatenate([fold_columns(wide_dealt), fold_columns(down_proj)]), "bucket", axis=0
+    )
+    gated, *saved = run_forward(
+        info, normed_near, normed_far, proj, gate, channel, taps, slots
+    )
+    mixed_far, mixed_near = (
+        jnp.dot(part.reshape(-1, lanes), out, preferred_element_type=jnp.float32)
+        .astype(jnp.bfloat16)
+        .reshape(-1, rows, depth)
+        for part in (gated[count // 2 :], gated[: count // 2])
+    )
+    residual = inputs + reduce_plane(mixed_near, mixed_far)
     scale_two = lax.rsqrt(jnp.mean(residual * residual, axis=1, keepdims=True) + norm_eps)
-    normed_two = gather_plane((residual * scale_two * gain_two).astype(jnp.bfloat16))
-    normed_two = normed_two.reshape(-1, depth)
-    expanded = jnp.dot(normed_two, wide, preferred_element_type=jnp.float32)
-    feed, feed_pull = jax.vjp(partial(gated_gelu, split=hidden_width), expanded)
-    feed_low = feed.astype(jnp.bfloat16)
-    output_part = jnp.dot(feed_low, narrow, preferred_element_type=jnp.float32)
-    output_part = output_part.astype(jnp.bfloat16).reshape(count, rows, depth)
-    mixed = (keep * (residual + reduce_plane(output_part))).astype(jnp.bfloat16)
-
-    feed_grad = contract_last(upstream_all, narrow)
-    expanded_grad = feed_pull(feed_grad)[0].astype(jnp.bfloat16)
-    normed_two_part = contract_last(expanded_grad, wide).astype(jnp.bfloat16)
-    normed_two_grad = reduce_plane(normed_two_part.reshape(count, rows, depth))
+    normed_two = (residual * scale_two * gain_two).astype(jnp.bfloat16)
+    two_near = gather_chips(normed_two)
+    two_far = swap_with(two_near, CORE)
+    wide, narrow = unfold_columns(feed_weights, wide_dealt.shape, down_proj.shape)
+    halves = []
+    for part in (two_near, two_far):
+        expanded = jnp.dot(
+            part.reshape(-1, depth), wide, preferred_element_type=jnp.float32
+        )
+        halves.append((expanded, gated_gelu(expanded, hidden_width).astype(jnp.bfloat16)))
+    (expanded_near, feed_near), (expanded_far, feed_far) = halves
+
+    feed_grads = [
+        contract_last(part.reshape(-1, depth), narrow) for part in (upstream_near, upstream_far)
+    ]
+    down_part = contract_halves(feed_near, feed_far, upstream_near, upstream_far)
+    down_grad = sum_planes(down_part).astype(jnp.float32)
+    expanded_near, expanded_far, down_part = lax.optimization_barrier(
+        (expanded_near, expanded_far, down_part)
+    )
+
+    def through_feed(expanded, feed_grad):
+        _, feed_pull = jax.vjp(partial(gated_gelu, split=hidden_width), expanded)
+        expanded_grad = feed_pull(feed_grad)[0].astype(jnp.bfloat16)
+        part = contract_last(expanded_grad, wide).astype(jnp.bfloat16)
+        return expanded_grad, part.reshape(-1, rows, depth)
+
+    grad_far, part_far = through_feed(expanded_far, feed_grads[1])
+    grad_near, part_near = through_feed(expanded_near, feed_grads[0])
+    part_near, two_near, two_far, feed_near, feed_far = lax.optimization_barrier(
+        (part_near, two_near, two_far, feed_near, feed_far)
+    )
+    normed_two_grad = reduce_plane(part_near, part_far)
 
     def norm_back(values, scale, gain, grad):
         scaled = grad * gain
@@ -915,28 +1112,43 @@
         return scale * scaled - scale * scale * scale * lean * values
 
     residual_grad = upstream + norm_back(residual, scale_two, gain_two, normed_two_grad)
-    residual_low = gather_plane(residual_grad.astype(jnp.bfloat16))
+    wide_part = contract_halves(two_near, two_far, grad_near, grad_far)
+    residual_grad, wide_part = lax.optimization_barrier((residual_grad, wide_part))
+    wide_summed = sum_planes(wide_part)
+    low_near = gather_chips(residual_grad.astype(jnp.bfloat16))
+    low_near, down_grad = lax.optimization_barrier((low_near, down_grad))
+    low_far = swap_with(low_near, CORE)
+    output_parts = [
+        jnp.dot(part, narrow, preferred_element_type=jnp.float32)
+        .astype(jnp.bfloat16)
+        .reshape(-1, rows, depth)
+        for part in (feed_near, feed_far)
+    ]
+    output_near, output_far = output_parts
+    output_far, low_near = lax.optimization_barrier((output_far, low_near))
+    mixed = (keep * (residual + reduce_plane(output_near, output_far))).astype(jnp.bfloat16)
+
     proj_grad, gate_grad, channel_grad = run_backward(
-        info, residual_low, out, gate, channel, saved, taps, slots
-    )
-    proj_grad = proj_grad.reshape(-1, 2 * lanes)
-    normed_part = contract_last(proj_grad, proj).astype(jnp.bfloat16)
-    normed_grad = reduce_plane(normed_part.reshape(count, rows, depth))
-    token_grad = residual_grad + norm_back(inputs, scale_one, gain_one, normed_grad)
-
-    down_grad = lax.psum_scatter(
-        contract_first(feed_low, upstream_all).astype(jnp.bfloat16),
-        "bucket",
-        scatter_dimension=0,
-        tiled=True,
-    ).astype(jnp.float32)
-    wide_grad = hand_back(contract_first(normed_two, expanded_grad))
-    gate_up_grad = (
-        wide_grad.reshape(count, own_rows, 2, planes, hidden_rows)
-        .transpose(1, 2, 3, 0, 4)
-        .reshape(own_rows, -1)
-    )
-    out_grad = contract_first(gated, residual_low.reshape(-1, depth))[:channels]
+        info, low_near, low_far, out, gate, channel, saved, 2 * channels, taps, slots
+    )
+    proj_grad, wide_summed = lax.optimization_barrier((proj_grad, wide_summed))
+    proj_grad_near, proj_grad_far = proj_grad[: count // 2], proj_grad[count // 2 :]
+
+    def through_proj(part):
+        part = contract_last(part.reshape(-1, 2 * channels), proj).astype(jnp.bfloat16)
+        return part.reshape(-1, rows, depth)
+
+    proj_part = contract_halves(normed_near, normed_far, proj_grad_near, proj_grad_far)
+    proj_grad_far, proj_grad_near, proj_part = lax.optimization_barrier(
+        (proj_grad_far, proj_grad_near, proj_part)
+    )
+    part_far = through_proj(proj_grad_far)
+    part_far, mixed = lax.optimization_barrier((part_far, mixed))
+    normed_grad = reduce_plane(through_proj(proj_grad_near), part_far)
+
+    out_grad = contract_halves(
+        gated[: count // 2], gated[count // 2 :], low_near, low_far, jnp.float32
+    )[:channels]
     gate_parts = []
     for index in range(held):
         at = index * block_width
@@ -963,31 +1175,18 @@
     taken = swap_with(lax.dynamic_index_in_dim(by_row_grad, 1 - odd, 1, False), 1)
     by_row_grad = jnp.where(
         odd == 0, jnp.concatenate([kept, taken]), jnp.concatenate([taken, kept])
-    )
-    by_row_grad = lax.psum_scatter(
-        by_row_grad.reshape(planes * chunk_rows, -1), "bucket", scatter_dimension=0, tiled=True
-    ).astype(jnp.float32)
+    ).reshape(planes * chunk_rows, -1)
+    proj_part, wide_summed = lax.optimization_barrier((proj_part, wide_summed))
+    proj_summed = sum_planes(proj_part)
+    wide_summed, normed_grad = lax.optimization_barrier((wide_summed, normed_grad))
+    token_grad = residual_grad + norm_back(inputs, scale_one, gain_one, normed_grad)
+    gate_up_grad, mlp_gain_grad = hand_back(wide_summed, gate_up, mlp_gain, wide_moves)
+    proj_summed, by_row_grad = lax.optimization_barrier((proj_summed, by_row_grad))
+    in_proj_grad, norm_gain_grad = hand_back(proj_summed, in_proj, norm_gain, proj_moves)
+    by_row_grad = sum_planes(by_row_grad).astype(jnp.float32)
     out_proj_grad = by_row_grad[:, :depth]
     gate_weight_grad = by_row_grad[:, depth : depth + gate_columns]
     small_grad = by_row_grad[:, depth + gate_columns : by_row_width]
-    narrow_grad = jnp.pad(
-        contract_first(normed.reshape(-1, depth), proj_grad).reshape(depth, 2, lanes)[
-            :, :, :channels
-        ].reshape(depth, 2 * channels),
-        [(0, 0), (0, 0)],
-    )
-    in_proj_grad = (
-        hand_back(narrow_grad)
-        .reshape(count // 2, 2, own_rows, 2, held, block_width)
-        .transpose(2, 3, 1, 4, 0, 5)
-        .reshape(own_rows, -1)
-    )
-    norm_gain_grad = jnp.sum(in_proj_grad * in_proj.astype(jnp.float32), axis=1) / norm_gain.astype(
-        jnp.float32
-    )
-    mlp_gain_grad = jnp.sum(gate_up_grad * gate_up.astype(jnp.float32), axis=1) / mlp_gain.astype(
-        jnp.float32
-    )
     return (
         mixed[None],
         token_grad[None],
@@ -1007,7 +1206,7 @@
 
 def solution(mesh):
     planes, count = mesh.shape["bucket"], mesh.shape["seq"]
-    whole_blocks = planes % 2 == 0 and planes * count == 2 * NB
+    whole_blocks = count == 8 and planes % 2 == 0 and planes * count == 2 * NB
     return jax.shard_map(
         by_channels if whole_blocks else on_device,
         mesh=mesh,

time: 849 us -> 737 us (0.87)
  waiting for transfers between devices: 293 us -> 226 us
  other arithmetic: 114 us -> 77.1 us
  matrix products: 130 us -> 166 us
  local copies, waits for them, and re-layouts: 127 us -> 97.5 us
    all_gather x4 -> x3, waiting for transfers between devices: 80.3 us -> 0.01 us  [the longest x1 0.01 us: by_channels(): by_row = lax.all_gather(by_row, 'bucket', axis=0, tiled=False)]
    reshape x15 -> x0, local copies, waits for them, and re-layouts: 56.2 us -> none  [the longest x3 16 us: by_channels(): gate_up_grad = wide_grad.reshape(count, own_rows, 2, planes, hidden_rows)...]
    concatenate x16 -> x8, other arithmetic: 51.4 us -> 6.84 us  [the longest x4 3.42 us: reduce_plane(): jnp.concatenate([total(1, slice(split)) + first, total(1, slice(split, No...]
    unnamed x209 -> x174, local copies, waits for them, and re-layouts: 14.4 us -> 52.3 us
    add x21 -> x10, other arithmetic: 43.3 us -> 11.4 us  [the longest x1 4.34 us: by_channels(): upstream + norm_back(residual, scale_two, gain_two, normed_two_grad)]
    dot_general x4 -> x8, matrix products: 45.7 us -> 74 us  [contract_first(): lax.dot_general(left, right, (((0,), (0,)), ((), ())), preferred_element_...]
    slice x37 -> x20, local copies, waits for them, and re-layouts: 35.6 us -> 19.2 us  [the longest x2 9.26 us: unfold_columns(): pieces.append(folded[:, row:row + rows].reshape(-1, FOLD))]
    reduce_scatter x4, waiting for transfers between devices: 0.01 us -> 13.7 us  [sum_planes(): lax.psum_scatter(grad.astype(jnp.bfloat16), 'bucket', scatter_dimension=0...]
  transfers between devices with their start and end apart: 54 -> 53, of which waited for: 26 -> 25; matrix products, arithmetic and copies ran while one was open for 34% -> 38% of each run, Pallas kernels for 5% -> 10%
where the time goes in v2:
time: 737 us; the launch traced here: 731 us
  waiting for transfers between devices  226 us (31%)
  matrix products  166 us (23%)
  local copies, waits for them, and re-layouts  97.5 us (13%)
  other arithmetic  77.1 us (10%)
  Pallas kernels  76.1 us (10%)
  starting transfers between devices  56.2 us (8%)
  blocking collectives  16.7 us (2%)
  between operations  15.7 us (2%)
    ppermute x42, waiting for transfers between devices, swap_with(): return lax.ppermute(block, 'seq', route)  196 us
    dot_general x8, matrix products, contract_first(): lax.dot_general(left, right, (((0,), (0,)), ((), ())), preferred_element_...  74 us
    dot_general x6, matrix products, contract_last(): lax.dot_general(left, right, (((1,), (1,)), ((), ())), preferred_element_...  56.9 us
    unnamed x174, local copies, waits for them, and re-layouts  52.3 us
    pallas_call x1, Pallas kernels, run_backward(): pl.pallas_call(partial(mixer_backward, taps, slots), grid_spec=pltpu.Pref...  40.1 us
    ppermute x42, starting transfers between devices, swap_with(): return lax.ppermute(block, 'seq', route)  37.6 us
    pallas_call x1, Pallas kernels, run_forward(): pl.pallas_call(partial(mixer_forward, taps, slots), grid_spec=pltpu.Prefe...  29.5 us
    dot_general x2, matrix products, by_channels(): jnp.dot(part.reshape(-1, depth), wide, preferred_element_type=jnp.float32)  20.4 us
  transfers between devices with their start and end apart: 53, of which 25 were waited for; matrix products, arithmetic and copies ran while one was open for 38% of the time, Pallas kernels for 10%

profile of v2, /device:TPU:0, one launch (start us, length us, event | category | flops | bytes accessed | tf_op | source)
XLA Modules:
  0.0 731.1 jit_solution(2094191980149120979)
XLA Ops:
  15.3 5.2 all-to-all-start
  26.0 6.1 all-to-all-done
  36.1 17.9 %collective-permute-done.1 = bf16[264,2048]{1,0:T(8,128)(2,1)} collective-permute-done((bf16[264,2048]{1,0:T(8,128)(2,1)S(1)}, bf16[264,2048]{1,0:T(8,128)(2,1)}, u32[]{:S(2)}, u32[]{:S(2)}) %collective-permute-start.1) | collective-permute-done | bytes 1081376 | tf_op jit(solution)/shard_map/ppermute | solution.py:307
  58.9 4.3 all-to-all-start.1
  73.0 22.2 %collective-permute-done.3 = bf16[136,2048]{1,0:T(8,128)(2,1)S(1)} collective-permute-done((bf16[136,2048]{1,0:T(8,128)(2,1)S(1)}, bf16[136,2048]{1,0:T(8,128)(2,1)S(1)}, u32[]{:S(2)}, u32[]{:S(2)}) %collective-permute-start.3) | collective-permute-done | bytes 557088 | tf_op jit(solution)/shard_map/ppermute | solution.py:307
  114.8 16.7 %all-gather.1 = bf16[2,4,512]{0,2,1:T(8,128)(2,1)S(1)} all-gather(bf16[2,4,64]{0,2,1:T(8,128)(2,1)S(1)} %slice_bitcast_fusion.8), channel_id=3, replica_groups=mesh['bucket'=4,'seq'=8] {'seq'}, dimensions={2}, use_global_device_ids=true | all-gather | bytes 9216 | tf_op jit(solution)/shard_map/all_gather | solution.py:1005
  157.8 6.7 fusion.2
  164.5 29.5 %mixer_forward.1 = (bf16[8,264,384]{2,1,0:T(8,128)(2,1)S(1)}, bf16[8,264,384]{2,1,0:T(8,128)(2,1)S(1)}, bf16[8,264,384]{2,1,0:T(8,128)(2,1)S(1)}, f32[8,264,384]...) custom-call(s32[5]{0:T(128)S(1)} %pad_add_fusion.info_ref, ...), custom_call_target="tpu_custom_call" | custom-call | tf_op jit(solution)/shard_map/mixer_forward/pallas_call | solution.py:736
  201.3 4.9 collective-permute-done.10
  209.1 11.6 %collective-permute-done.11 = bf16[128,2048]{1,0:T(8,128)(2,1)S(1)} collective-permute-done((bf16[128,2048]{1,0:T(8,128)(2,1)S(1)}, bf16[128,2048]{1,0:T(8,128)(2,1)S(1)}, u32[]{:S(2)}, u32[]{:S(2)}) %collective-permute-start.11) | collective-permute-done | bytes 524320 | tf_op jit(solution)/shard_map/ppermute | solution.py:307
  223.7 22.7 %collective-permute-done.12 = bf16[264,2048]{1,0:T(8,128)(2,1)S(1)} collective-permute-done((bf16[264,2048]{1,0:T(8,128)(2,1)S(1)}, bf16[264,2048]{1,0:T(8,128)(2,1)S(1)}, u32[]{:S(2)}, u32[]{:S(2)}) %collective-permute-start.12) | collective-permute-done | bytes 1081376 | tf_op jit(solution)/shard_map/ppermute | solution.py:307
  252.6 22.0 %collective-permute-done.16 = bf16[264,2048]{1,0:T(8,128)(2,1)S(1)} collective-permute-done((bf16[264,2048]{1,0:T(8,128)(2,1)S(1)}, bf16[264,2048]{1,0:T(8,128)(2,1)S(1)}, u32[]{:S(2)}, u32[]{:S(2)}) %collective-permute-start.16) | collective-permute-done | bytes 1081376 | tf_op jit(solution)/shard_map/ppermute | solution.py:307
  279.4 7.8 %collective-permute-done.17 = bf16[128,2048]{1,0:T(8,128)(2,1)S(1)} collective-permute-done((bf16[128,2048]{1,0:T(8,128)(2,1)S(1)}, bf16[128,2048]{1,0:T(8,128)(2,1)S(1)}, u32[]{:S(2)}, u32[]{:S(2)}) %collective-permute-start.17) | collective-permute-done | bytes 524320 | tf_op jit(solution)/shard_map/ppermute | solution.py:307
  289.6 3.6 fusion.105
  293.2 11.3 %fusion.104 = f32[1056,1536]{1,0:T(8,128)S(1)} fusion(bf16[1056,2048]{1,0:T(8,128)(2,1)} %constant_dynamic-update-slice_fusion.10, bf16[2048,512]{1,0:T(8,128)(2,1)S(1)} %bitcast.242, bf16[2048,512]{1,0:T(8,128)(2,1)S(1)} %bitcast.246, bf16[2048,512]{1,0:T(8,128)(2,1)S(1)} %bitcast.238), kind=kOutput, calls=%fused_computation.244 | convolution fusion | flops 6662651904 | bytes 17104896 | tf_op jit(solution)/shard_map/dot_general | solution.py:1081
  304.6 5.6 fusion.106
  311.5 6.7 fusion.113
  318.3 9.1 %fusion.103 = f32[1056,1536]{1,0:T(8,128)S(1)} fusion(bf16[1056,2048]{1,0:T(8,128)(2,1)} %bitcast.35, bf16[2048,512]{1,0:T(8,128)(2,1)S(1)} %bitcast.243, bf16[2048,512]{1,0:T(8,128)(2,1)S(1)} %bitcast.247, bf16[2048,512]{1,0:T(8,128)(2,1)S(1)} %bitcast.239), kind=kOutput, calls=%fused_computation.243 | convolution fusion | flops 6662651904 | bytes 17104896 | tf_op jit(solution)/shard_map/dot_general | solution.py:1081
  331.3 7.9 %add_convert_fusion.3 = bf16[768,2048]{1,0:T(8,128)(2,1)} fusion(f32[768,2048]{1,0:T(8,128)S(1)} %fusion.113, bf16[1056,768]{1,0:T(8,128)(2,1)S(1)} %fusion.33, bf16[1056,2048]{1,0:T(8,128)(2,1)} %bitcast.37), kind=kOutput, calls=%fused_computation.19 | convolution fusion | flops 3325034496 | bytes 15384576 | tf_op jit(solution)/shard_map/dot_general | solution.py:74
  339.3 12.1 %multiply_multiply_fusion.6 = (f32[1056,768]{1,0:T(8,128)S(1)}, f32[1056,768]{1,0:T(8,128)}) fusion(f32[1056,1536]{1,0:T(8,128)} %copy-done.22, bf16[1056,2048]{1,0:T(8,128)(2,1)} %bitcast.37, bf16[768,512]{1,0:T(8,128)(2,1)} %bitcast.262, bf16[768,512]{1,0:T(8,128)(2,1)} %bitcast.266, bf16[768,512]{1,0:T(8,128)(2,1)} %bitcast.270, ...), kind=kOutput, calls=%fused_computation.62 | convolution fusion | flops 3352313856 | bytes 20447232 | tf_op jit(solution)/shard_map/dot_general | solution.py:68
  351.5 11.7 %convolution_convert_fusion.6 = bf16[1056,2048]{1,0:T(8,128)(2,1)} fusion(f32[1056,768]{1,0:T(8,128)} %get-tuple-element.154, f32[1056,768]{1,0:T(8,128)S(1)} %get-tuple-element.153, bf16[2048,512]{1,0:T(8,128)(2,1)S(1)} %bitcast.245, bf16[2048,512]{1,0:T(8,128)(2,1)S(1)} %bitcast.249, bf16[2048,512]{1,0:T(8,128)(2,1)S(1)} %bitcast.240), kind=kOutput, calls=%fused_computation.14 | convolution fusion | flops 6668058624 | bytes 17104896 | tf_op jit(solution)/shard_map/dot_general | solution.py:68
  363.2 10.5 %multiply_multiply_fusion.7 = (f32[1056,768]{1,0:T(8,128)}, f32[1056,768]{1,0:T(8,128)}) fusion(f32[1056,1536]{1,0:T(8,128)} %copy-done.21, bf16[1056,2048]{1,0:T(8,128)(2,1)} %bitcast.36, bf16[768,512]{1,0:T(8,128)(2,1)S(1)} %bitcast.263, bf16[768,512]{1,0:T(8,128)(2,1)S(1)} %bitcast.267, bf16[768,512]{1,0:T(8,128)(2,1)S(1)} %bitcast.271, ...), kind=kOutput, calls=%fused_computation.63 | convolution fusion | flops 3352313856 | bytes 20447232 | tf_op jit(solution)/shard_map/dot_general | solution.py:68
  373.7 10.8 %convolution_convert_fusion.7 = bf16[1056,2048]{1,0:T(8,128)(2,1)S(1)} fusion(f32[1056,768]{1,0:T(8,128)} %get-tuple-element.156, f32[1056,768]{1,0:T(8,128)} %get-tuple-element.155, bf16[2048,512]{1,0:T(8,128)(2,1)} %bitcast.244, bf16[2048,512]{1,0:T(8,128)(2,1)} %bitcast.248, bf16[2048,512]{1,0:T(8,128)(2,1)S(1)} %bitcast.241), kind=kOutput, calls=%fused_computation.15 | convolution fusion | flops 6668058624 | bytes 17104896 | tf_op jit(solution)/shard_map/dot_general | solution.py:68
  384.6 16.4 %fusion.87 = f32[2048,1536]{1,0:T(8,128)} fusion(bf16[1056,2048]{1,0:T(8,128)(2,1)} %bitcast.53, f32[1056,768]{1,0:T(8,128)} %get-tuple-element.154, f32[1056,768]{1,0:T(8,128)} %copy-done.72), kind=kOutput, calls=%fused_computation.179 | convolution fusion | flops 6647021568 | bytes 23396352 | tf_op jit(solution)/shard_map/dot_general | solution.py:74
  403.9 12.0 %collective-permute-done.22 = bf16[128,2048]{1,0:T(8,128)(2,1)S(1)} collective-permute-done((bf16[128,2048]{1,0:T(8,128)(2,1)S(1)}, bf16[128,2048]{1,0:T(8,128)(2,1)S(1)}, u32[]{:S(2)}, u32[]{:S(2)}) %collective-permute-start.22) | collective-permute-done | bytes 524320 | tf_op jit(solution)/shard_map/ppermute | solution.py:307
  420.7 15.6 %add_convert_fusion = bf16[2048,1536]{1,0:T(8,128)(2,1)} fusion(f32[2048,1536]{1,0:T(8,128)} %fusion.87, bf16[1056,2048]{1,0:T(8,128)(2,1)} %bitcast.52, f32[1056,768]{1,0:T(8,128)} %get-tuple-element.156, f32[1056,768]{1,0:T(8,128)} %get-tuple-element.155), kind=kOutput, calls=%fused_computation | convolution fusion | flops 6653313024 | bytes 29687808 | tf_op jit(solution)/shard_map/dot_general | solution.py:74
  436.3 6.6 collective-permute-done.23
  447.9 4.3 fusion.52
  458.3 22.3 %collective-permute-done.27 = bf16[264,2048]{1,0:T(8,128)(2,1)S(1)} collective-permute-done((bf16[264,2048]{1,0:T(8,128)(2,1)}, bf16[264,2048]{1,0:T(8,128)(2,1)S(1)}, u32[]{:S(2)}, u32[]{:S(2)}) %collective-permute-start.27) | collective-permute-done | bytes 1081376 | tf_op jit(solution)/shard_map/ppermute | solution.py:307
  484.1 5.6 convolution_convert_fusion.3
  497.0 7.3 collective-permute-done.29
  505.7 4.2 convolution_convert_fusion.1
  515.6 11.6 %collective-permute-done.32 = bf16[128,2048]{1,0:T(8,128)(2,1)S(1)} collective-permute-done((bf16[128,2048]{1,0:T(8,128)(2,1)S(1)}, bf16[128,2048]{1,0:T(8,128)(2,1)S(1)}, u32[]{:S(2)}, u32[]{:S(2)}) %collective-permute-start.32) | collective-permute-done | bytes 524320 | tf_op jit(solution)/shard_map/ppermute | solution.py:307
  534.3 40.1 %mixer_backward.1 = (bf16[8,264,640]{2,1,0:T(8,128)(2,1)}, f32[384,768]{1,0:T(8,128)S(1)}, f32[8,384]{1,0:T(8,128)S(1)}) custom-call(s32[5]{0:T(128)S(1)} %pad_add_fusion.info_ref, bf16[4,264,2048]{2,1,0:T(8,128)(2,1)} %bitcast.221, bf16[4,264,2048]{2,1,0:T(8,128)(2,1)} %copy-done.27, bf16[384,2048]{1,0:T(8,128)(2,1)S(1)} %pad.63.out_ref, ...), custom_call_target="tpu_custom_call" | custom-call | tf_op jit(solution)/shard_map/mixer_backward/pallas_call | solution.py:800
  579.0 7.0 fusion.98
  587.8 8.1 %fusion.3 = bf16[2048,640]{1,0:T(8,128)(2,1)} fusion(f32[2048,640,1]{1,0,2:T(8,128)S(1)} %fusion.98, bf16[4,264,2048]{2,1,0:T(8,128)(2,1)} %get-tuple-element.69.far_ref, bf16[8,264,640]{2,1,0:T(8,128)(2,1)S(1)} %copy-done.29), kind=kOutput, calls=%fused_computation.21 | convolution fusion | flops 2770862080 | bytes 13541376 | tf_op jit(solution)/shard_map/dot_general | solution.py:74
  595.9 7.9 %convolution_convert_fusion.2 = bf16[1056,2048]{1,0:T(8,128)(2,1)} fusion(bf16[1056,640]{1,0:T(8,128)(2,1)} %bitcast.254, bf16[2048,640]{1,0:T(8,128)(2,1)} %all-gather.7.cloned.1.call-done.proj_ref), kind=kOutput, calls=%fused_computation.10 | convolution fusion | flops 2770403328 | bytes 8298496 | tf_op jit(solution)/shard_map/dot_general | solution.py:68
  603.8 6.2 convolution_bitcast_fusion.1
  611.6 6.1 convolution_bitcast_fusion
  619.0 3.9 fusion.34
  627.6 3.8 convolution_convert_fusion
  638.5 10.0 %collective-permute-done.37 = bf16[128,2048]{1,0:T(8,128)(2,1)S(1)} collective-permute-done((bf16[128,2048]{1,0:T(8,128)(2,1)S(1)}, bf16[128,2048]{1,0:T(8,128)(2,1)S(1)}, u32[]{:S(2)}, u32[]{:S(2)}) %collective-permute-start.37) | collective-permute-done | bytes 524320 | tf_op jit(solution)/shard_map/ppermute | solution.py:307
  656.7 13.7 %reduce-scatter.9.cloned.1.call-done = bf16[512,640]{1,0:T(8,128)(2,1)} async-done(((bf16[2048,640]{1,0:T(8,128)(2,1)}), bf16[512,640]{1,0:T(8,128)(2,1)}) %reduce-scatter.9.cloned.1.call-update) | async-done | bytes 655376 | tf_op jit(solution)/shard_map/reduce_scatter | solution.py:878
  670.4 3.7 all-to-all-start.2
  676.8 5.8 collective-permute-done.40
  682.5 3.9 fusion.42
  687.3 4.7 all-to-all-start.3
  702.6 10.4 %all-to-all-done.3.groups_ref = bf16[8,64,1536]{2,1,0:T(8,128)(2,1)S(1)} async-done(((bf16[8,64,1536]{2,1,0:T(8,128)(2,1)}), bf16[8,64,1536]{2,1,0:T(8,128)(2,1)S(1)}, u32[]{:S(2)}, u32[]{:S(2)}) %all-to-all-start.3) | async-done | bytes 1572896 | tf_op jit(solution)/shard_map/all_to_all | solution.py:886
  (391 shorter events, 207.1 us)
Async XLA Ops:
  7.2 105.1 %all-gather.9.cloned.1.call-start = ((), (), s32[]{:S(2)}) async-start(), calls=%async_computation.13 | async-start | bytes 1945600 | tf_op jit(solution)/shard_map/all_gather | solution.py:977
  15.3 16.8 %all-to-all-start = ((bf16[8,64,640]{2,1,0:T(8,128)(2,1)}), bf16[8,64,640]{2,1,0:T(8,128)(2,1)S(1)}, u32[]{:S(2)}, u32[]{:S(2)}) async-start(bf16[8,64,640]{2,1,0:T(8,128)(2,1)} %deal_columns.2), calls=%async_computation | async-start | bytes 1310720 | tf_op jit(solution)/shard_map/all_to_all | solution.py:873
  20.5 144.0 %all-gather.7.cloned.1.call-start = ((), (), s32[]{:S(2)}) async-start(), calls=%async_computation.8 | async-start | bytes 3276800 | tf_op jit(solution)/shard_map/all_gather | solution.py:1009
  20.6 42.8 %collective-permute-start = (bf16[264,2048]{1,0:T(8,128)(2,1)S(1)}, bf16[264,2048]{1,0:T(8,128)(2,1)}, u32[]{:S(2)}, u32[]{:S(2)}) collective-permute-start(bf16[264,2048]{1,0:T(8,128)(2,1)S(1)} %bitcast.206), channel_id=1, source_target_pairs={{0,2},{1,3},{2,0},{3,1},{4,6},{5,7},{6,4},{7,5},{8,10},{9,11},{10,... | collective-permute-start | bytes 3244040 | tf_op jit(solution)/shard_map/ppermute | solution.py:307
  22.6 31.4 %collective-permute-start.1 = (bf16[264,2048]{1,0:T(8,128)(2,1)S(1)}, bf16[264,2048]{1,0:T(8,128)(2,1)}, u32[]{:S(2)}, u32[]{:S(2)}) collective-permute-start(bf16[264,2048]{1,0:T(8,128)(2,1)S(1)} %bitcast.207), channel_id=1, source_target_pairs={{0,4},{1,5},{2,6},{3,7},{4,0},{5,1},{6,2},{7,3},{8,12},{9,13},{10,... | collective-permute-start | bytes 3244040 | tf_op jit(solution)/shard_map/ppermute | solution.py:307
  55.9 15.2 %collective-permute-start.2 = (bf16[128,2048]{1,0:T(8,128)(2,1)}, bf16[128,2048]{1,0:T(8,128)(2,1)}, u32[]{:S(2)}, u32[]{:S(2)}) collective-permute-start(bf16[128,2048]{1,0:T(8,128)(2,1)} %slice.502), channel_id=1, source_target_pairs={{0,2},{1,3},{2,0},{3,1},{4,6},{5,7},{6,4},{7,5},{8,10},{9,11},{10,... | collective-permute-start | bytes 1572872 | tf_op jit(solution)/shard_map/ppermute | solution.py:307
  58.9 40.5 %all-to-all-start.1 = ((bf16[8,64,1536]{2,1,0:T(8,128)(2,1)}), bf16[8,64,1536]{2,1,0:T(8,128)(2,1)}, u32[]{:S(2)}, u32[]{:S(2)}) async-start(bf16[8,64,1536]{2,1,0:T(8,128)(2,1)} %deal_columns.3), calls=%async_computation.1 | async-start | bytes 3145728 | tf_op jit(solution)/shard_map/all_to_all | solution.py:873
  63.3 226.3 %all-gather.11.cloned.1.call-start = ((), (), s32[]{:S(2)}) async-start(), calls=%async_computation.14 | async-start | bytes 11796480 | tf_op jit(solution)/shard_map/all_gather | solution.py:1061
  64.4 30.7 %collective-permute-start.3 = (bf16[136,2048]{1,0:T(8,128)(2,1)S(1)}, bf16[136,2048]{1,0:T(8,128)(2,1)S(1)}, u32[]{:S(2)}, u32[]{:S(2)}) collective-permute-start(bf16[136,2048]{1,0:T(8,128)(2,1)S(1)} %slice.503), channel_id=1, source_target_pairs={{0,4},{1,5},{2,6},{3,7},{4,0},{5,1},{6,2},{7,3},{8,12},{9,13},{10,... | collective-permute-start | bytes 1671176 | tf_op jit(solution)/shard_map/ppermute | solution.py:307
  99.4 55.2 %collective-permute-start.4 = (bf16[4,264,2048]{2,1,0:T(8,128)(2,1)}, bf16[4,264,2048]{2,1,0:T(8,128)(2,1)}, u32[]{:S(2)}, u32[]{:S(2)}) collective-permute-start(bf16[4,264,2048]{2,1,0:T(8,128)(2,1)} %bitcast.204), channel_id=1, source_target_pairs={{0,1},{1,0},{2,3},{3,2},{4,5},{5,4},{6,7},{7,6},{8,9},{9,8},{10,11... | collective-permute-start | bytes 12976136 | tf_op jit(solution)/shard_map/ppermute | solution.py:307
  99.4 33.1 %collective-permute-start.6 = (bf16[264,2048]{1,0:T(8,128)(2,1)}, bf16[264,2048]{1,0:T(8,128)(2,1)}, u32[]{:S(2)}, u32[]{:S(2)}) collective-permute-start(bf16[264,2048]{1,0:T(8,128)(2,1)} %fusion.53), channel_id=1, source_target_pairs={{0,4},{1,5},{2,6},{3,7},{4,0},{5,1},{6,2},{7,3},{8,12},{9,13},{10,... | collective-permute-start | bytes 3244040 | tf_op jit(solution)/shard_map/ppermute | solution.py:307
  99.8 36.0 %collective-permute-start.5 = (bf16[264,2048]{1,0:T(8,128)(2,1)}, bf16[264,2048]{1,0:T(8,128)(2,1)}, u32[]{:S(2)}, u32[]{:S(2)}) collective-permute-start(bf16[264,2048]{1,0:T(8,128)(2,1)} %fusion.53), channel_id=1, source_target_pairs={{0,2},{1,3},{2,0},{3,1},{4,6},{5,7},{6,4},{7,5},{8,10},{9,11},{10,... | collective-permute-start | bytes 3244040 | tf_op jit(solution)/shard_map/ppermute | solution.py:307
  109.9 379.8 %reduce-scatter.5.cloned.1.call-start = ((), (), s32[]{:S(2)}) async-start(), calls=%async_computation.9 | async-start | bytes 3932160 | tf_op jit(solution)/shard_map/reduce_scatter | solution.py:878
  113.8 29.2 %collective-permute-start.9 = (bf16[2,80,2432]{2,1,0:T(8,128)(2,1)S(1)}, bf16[2,80,2432]{2,1,0:T(8,128)(2,1)S(1)}, u32[]{:S(2)}, u32[]{:S(2)}) collective-permute-start(bf16[2,80,2432]{2,1,0:T(8,128)(2,1)S(1)} %get-tuple-element.175), channel_id=1, source_target_pairs={{0,1},{1,0},{2,3},{3,2},{4,5},{5,4},{6,7},{7,6},{8,9},{9,8},{10,11... | collective-permute-start | bytes 2334728 | tf_op jit(solution)/shard_map/ppermute | solution.py:307
  134.3 14.5 %collective-permute-start.7 = (bf16[128,2048]{1,0:T(8,128)(2,1)}, bf16[128,2048]{1,0:T(8,128)(2,1)}, u32[]{:S(2)}, u32[]{:S(2)}) collective-permute-start(bf16[128,2048]{1,0:T(8,128)(2,1)} %slice.506), channel_id=1, source_target_pairs={{0,2},{1,3},{2,0},{3,1},{4,6},{5,7},{6,4},{7,5},{8,10},{9,11},{10,... | collective-permute-start | bytes 1572872 | tf_op jit(solution)/shard_map/ppermute | solution.py:307
  137.7 14.9 %collective-permute-start.8 = (bf16[136,2048]{1,0:T(8,128)(2,1)}, bf16[136,2048]{1,0:T(8,128)(2,1)}, u32[]{:S(2)}, u32[]{:S(2)}) collective-permute-start(bf16[136,2048]{1,0:T(8,128)(2,1)} %slice.507), channel_id=1, source_target_pairs={{0,4},{1,5},{2,6},{3,7},{4,0},{5,1},{6,2},{7,3},{8,12},{9,13},{10,... | collective-permute-start | bytes 1671176 | tf_op jit(solution)/shard_map/ppermute | solution.py:307
  206.7 14.0 %collective-permute-start.11 = (bf16[128,2048]{1,0:T(8,128)(2,1)S(1)}, bf16[128,2048]{1,0:T(8,128)(2,1)S(1)}, u32[]{:S(2)}, u32[]{:S(2)}) collective-permute-start(bf16[128,2048]{1,0:T(8,128)(2,1)S(1)} %slice.522), channel_id=1, source_target_pairs={{0,4},{1,5},{2,6},{3,7},{4,0},{5,1},{6,2},{7,3},{8,12},{9,13},{10,... | collective-permute-start | bytes 1572872 | tf_op jit(solution)/shard_map/ppermute | solution.py:307
  207.3 14.4 %collective-permute-start.13 = (bf16[136,2048]{1,0:T(8,128)(2,1)S(1)}, bf16[136,2048]{1,0:T(8,128)(2,1)S(1)}, u32[]{:S(2)}, u32[]{:S(2)}) collective-permute-start(bf16[136,2048]{1,0:T(8,128)(2,1)S(1)} %slice.529), channel_id=1, source_target_pairs={{0,2},{1,3},{2,0},{3,1},{4,6},{5,7},{6,4},{7,5},{8,10},{9,11},{10,... | collective-permute-start | bytes 1671176 | tf_op jit(solution)/shard_map/ppermute | solution.py:307
  221.1 25.2 %collective-permute-start.12 = (bf16[264,2048]{1,0:T(8,128)(2,1)S(1)}, bf16[264,2048]{1,0:T(8,128)(2,1)S(1)}, u32[]{:S(2)}, u32[]{:S(2)}) collective-permute-start(bf16[264,2048]{1,0:T(8,128)(2,1)S(1)} %pad_maximum_fusion.2), channel_id=1, source_target_pairs={{0,2},{1,3},{2,0},{3,1},{4,6},{5,7},{6,4},{7,5},{8,10},{9,11},{10,... | collective-permute-start | bytes 3244040 | tf_op jit(solution)/shard_map/ppermute | solution.py:307
  222.0 24.9 %collective-permute-start.14 = (bf16[264,2048]{1,0:T(8,128)(2,1)S(1)}, bf16[264,2048]{1,0:T(8,128)(2,1)S(1)}, u32[]{:S(2)}, u32[]{:S(2)}) collective-permute-start(bf16[264,2048]{1,0:T(8,128)(2,1)S(1)} %pad_maximum_fusion.3), channel_id=1, source_target_pairs={{0,4},{1,5},{2,6},{3,7},{4,0},{5,1},{6,2},{7,3},{8,12},{9,13},{10,... | collective-permute-start | bytes 3244040 | tf_op jit(solution)/shard_map/ppermute | solution.py:307
  250.6 24.1 %collective-permute-start.16 = (bf16[264,2048]{1,0:T(8,128)(2,1)S(1)}, bf16[264,2048]{1,0:T(8,128)(2,1)S(1)}, u32[]{:S(2)}, u32[]{:S(2)}) collective-permute-start(bf16[264,2048]{1,0:T(8,128)(2,1)S(1)} %get-tuple-element.150), channel_id=1, source_target_pairs={{0,4},{1,5},{2,6},{3,7},{4,0},{5,1},{6,2},{7,3},{8,12},{9,13},{10,... | collective-permute-start | bytes 3244040 | tf_op jit(solution)/shard_map/ppermute | solution.py:307
  252.1 24.9 %collective-permute-start.15 = (bf16[264,2048]{1,0:T(8,128)(2,1)S(1)}, bf16[264,2048]{1,0:T(8,128)(2,1)S(1)}, u32[]{:S(2)}, u32[]{:S(2)}) collective-permute-start(bf16[264,2048]{1,0:T(8,128)(2,1)S(1)} %get-tuple-element.150), channel_id=1, source_target_pairs={{0,2},{1,3},{2,0},{3,1},{4,6},{5,7},{6,4},{7,5},{8,10},{9,11},{10,... | collective-permute-start | bytes 3244040 | tf_op jit(solution)/shard_map/ppermute | solution.py:307
  289.1 29.2 %collective-permute-start.19 = (bf16[4,264,2048]{2,1,0:T(8,128)(2,1)}, bf16[4,264,2048]{2,1,0:T(8,128)(2,1)}, u32[]{:S(2)}, u32[]{:S(2)}) collective-permute-start(bf16[4,264,2048]{2,1,0:T(8,128)(2,1)} %bitcast.34), channel_id=1, source_target_pairs={{0,1},{1,0},{2,3},{3,2},{4,5},{5,4},{6,7},{7,6},{8,9},{9,8},{10,11... | collective-permute-start | bytes 12976136 | tf_op jit(solution)/shard_map/ppermute | solution.py:307
  289.1 41.0 %collective-permute-start.20 = (bf16[4,264,2048]{2,1,0:T(8,128)(2,1)}, bf16[4,264,2048]{2,1,0:T(8,128)(2,1)}, u32[]{:S(2)}, u32[]{:S(2)}) collective-permute-start(bf16[4,264,2048]{2,1,0:T(8,128)(2,1)} %bitcast.15), channel_id=1, source_target_pairs={{0,1},{1,0},{2,3},{3,2},{4,5},{5,4},{6,7},{7,6},{8,9},{9,8},{10,11... | collective-permute-start | bytes 12976136 | tf_op jit(solution)/shard_map/ppermute | solution.py:307
  339.2 239.8 %reduce-scatter.7.cloned.1.call-start = ((), (), s32[]{:S(2)}) async-start(), calls=%async_computation.10 | async-start | bytes 7864320 | tf_op jit(solution)/shard_map/reduce_scatter | solution.py:878
  363.2 37.8 %collective-permute-start.21 = (bf16[4,264,2048]{2,1,0:T(8,128)(2,1)}, bf16[4,264,2048]{2,1,0:T(8,128)(2,1)S(1)}, u32[]{:S(2)}, u32[]{:S(2)}) collective-permute-start(bf16[4,264,2048]{2,1,0:T(8,128)(2,1)} %bitcast.288), channel_id=1, source_target_pairs={{0,1},{1,0},{2,3},{3,2},{4,5},{5,4},{6,7},{7,6},{8,9},{9,8},{10,11... | collective-permute-start | bytes 12976136 | tf_op jit(solution)/shard_map/ppermute | solution.py:307
  401.5 14.4 %collective-permute-start.22 = (bf16[128,2048]{1,0:T(8,128)(2,1)S(1)}, bf16[128,2048]{1,0:T(8,128)(2,1)S(1)}, u32[]{:S(2)}, u32[]{:S(2)}) collective-permute-start(bf16[128,2048]{1,0:T(8,128)(2,1)S(1)} %slice_bitcast_fusion.7), channel_id=1, source_target_pairs={{0,4},{1,5},{2,6},{3,7},{4,0},{5,1},{6,2},{7,3},{8,12},{9,13},{10,... | collective-permute-start | bytes 1572872 | tf_op jit(solution)/shard_map/ppermute | solution.py:307
  402.1 15.5 %collective-permute-start.24 = (bf16[136,2048]{1,0:T(8,128)(2,1)S(1)}, bf16[136,2048]{1,0:T(8,128)(2,1)S(1)}, u32[]{:S(2)}, u32[]{:S(2)}) collective-permute-start(bf16[136,2048]{1,0:T(8,128)(2,1)S(1)} %slice_bitcast_fusion.6), channel_id=1, source_target_pairs={{0,2},{1,3},{2,0},{3,1},{4,6},{5,7},{6,4},{7,5},{8,10},{9,11},{10,... | collective-permute-start | bytes 1671176 | tf_op jit(solution)/shard_map/ppermute | solution.py:307
  417.2 25.7 %collective-permute-start.23 = (bf16[264,2048]{1,0:T(8,128)(2,1)}, bf16[264,2048]{1,0:T(8,128)(2,1)S(1)}, u32[]{:S(2)}, u32[]{:S(2)}) collective-permute-start(bf16[264,2048]{1,0:T(8,128)(2,1)} %pad_maximum_fusion.4), channel_id=1, source_target_pairs={{0,2},{1,3},{2,0},{3,1},{4,6},{5,7},{6,4},{7,5},{8,10},{9,11},{10,... | collective-permute-start | bytes 3244040 | tf_op jit(solution)/shard_map/ppermute | solution.py:307
  419.0 25.5 %collective-permute-start.25 = (bf16[264,2048]{1,0:T(8,128)(2,1)}, bf16[264,2048]{1,0:T(8,128)(2,1)}, u32[]{:S(2)}, u32[]{:S(2)}) collective-permute-start(bf16[264,2048]{1,0:T(8,128)(2,1)} %pad_maximum_fusion.5), channel_id=1, source_target_pairs={{0,4},{1,5},{2,6},{3,7},{4,0},{5,1},{6,2},{7,3},{8,12},{9,13},{10,... | collective-permute-start | bytes 3244040 | tf_op jit(solution)/shard_map/ppermute | solution.py:307
  452.2 218.1 %reduce-scatter.9.cloned.1.call-start = ((), (), s32[]{:S(2)}) async-start(), calls=%async_computation.11 | async-start | bytes 3276800 | tf_op jit(solution)/shard_map/reduce_scatter | solution.py:878
  456.2 24.5 %collective-permute-start.27 = (bf16[264,2048]{1,0:T(8,128)(2,1)}, bf16[264,2048]{1,0:T(8,128)(2,1)S(1)}, u32[]{:S(2)}, u32[]{:S(2)}) collective-permute-start(bf16[264,2048]{1,0:T(8,128)(2,1)} %get-tuple-element.148), channel_id=1, source_target_pairs={{0,4},{1,5},{2,6},{3,7},{4,0},{5,1},{6,2},{7,3},{8,12},{9,13},{10,... | collective-permute-start | bytes 3244040 | tf_op jit(solution)/shard_map/ppermute | solution.py:307
  457.9 34.4 %collective-permute-start.26 = (bf16[264,2048]{1,0:T(8,128)(2,1)}, bf16[264,2048]{1,0:T(8,128)(2,1)S(1)}, u32[]{:S(2)}, u32[]{:S(2)}) collective-permute-start(bf16[264,2048]{1,0:T(8,128)(2,1)} %get-tuple-element.148), channel_id=1, source_target_pairs={{0,2},{1,3},{2,0},{3,1},{4,6},{5,7},{6,4},{7,5},{8,10},{9,11},{10,... | collective-permute-start | bytes 3244040 | tf_op jit(solution)/shard_map/ppermute | solution.py:307
  482.5 12.6 %collective-permute-start.28 = (bf16[128,2048]{1,0:T(8,128)(2,1)}, bf16[128,2048]{1,0:T(8,128)(2,1)}, u32[]{:S(2)}, u32[]{:S(2)}) collective-permute-start(bf16[128,2048]{1,0:T(8,128)(2,1)} %slice.552), channel_id=1, source_target_pairs={{0,2},{1,3},{2,0},{3,1},{4,6},{5,7},{6,4},{7,5},{8,10},{9,11},{10,... | collective-permute-start | bytes 1572872 | tf_op jit(solution)/shard_map/ppermute | solution.py:307
  505.2 27.0 %collective-permute-start.30 = (bf16[4,264,2048]{2,1,0:T(8,128)(2,1)}, bf16[4,264,2048]{2,1,0:T(8,128)(2,1)S(1)}, u32[]{:S(2)}, u32[]{:S(2)}) collective-permute-start(bf16[4,264,2048]{2,1,0:T(8,128)(2,1)} %bitcast.220), channel_id=1, source_target_pairs={{0,1},{1,0},{2,3},{3,2},{4,5},{5,4},{6,7},{7,6},{8,9},{9,8},{10,11... | collective-permute-start | bytes 12976136 | tf_op jit(solution)/shard_map/ppermute | solution.py:307
  513.2 14.0 %collective-permute-start.32 = (bf16[128,2048]{1,0:T(8,128)(2,1)S(1)}, bf16[128,2048]{1,0:T(8,128)(2,1)S(1)}, u32[]{:S(2)}, u32[]{:S(2)}) collective-permute-start(bf16[128,2048]{1,0:T(8,128)(2,1)S(1)} %slice.560), channel_id=1, source_target_pairs={{0,4},{1,5},{2,6},{3,7},{4,0},{5,1},{6,2},{7,3},{8,12},{9,13},{10,... | collective-permute-start | bytes 1572872 | tf_op jit(solution)/shard_map/ppermute | solution.py:307
  513.7 15.3 %collective-permute-start.34 = (bf16[136,2048]{1,0:T(8,128)(2,1)S(1)}, bf16[136,2048]{1,0:T(8,128)(2,1)S(1)}, u32[]{:S(2)}, u32[]{:S(2)}) collective-permute-start(bf16[136,2048]{1,0:T(8,128)(2,1)S(1)} %slice.567), channel_id=1, source_target_pairs={{0,2},{1,3},{2,0},{3,1},{4,6},{5,7},{6,4},{7,5},{8,10},{9,11},{10,... | collective-permute-start | bytes 1671176 | tf_op jit(solution)/shard_map/ppermute | solution.py:307
  528.6 46.8 %collective-permute-start.33 = (bf16[264,2048]{1,0:T(8,128)(2,1)}, bf16[264,2048]{1,0:T(8,128)(2,1)}, u32[]{:S(2)}, u32[]{:S(2)}) collective-permute-start(bf16[264,2048]{1,0:T(8,128)(2,1)} %pad_maximum_fusion.6), channel_id=1, source_target_pairs={{0,2},{1,3},{2,0},{3,1},{4,6},{5,7},{6,4},{7,5},{8,10},{9,11},{10,... | collective-permute-start | bytes 3244040 | tf_op jit(solution)/shard_map/ppermute | solution.py:307
  530.4 45.1 %collective-permute-start.35 = (bf16[264,2048]{1,0:T(8,128)(2,1)}, bf16[264,2048]{1,0:T(8,128)(2,1)S(1)}, u32[]{:S(2)}, u32[]{:S(2)}) collective-permute-start(bf16[264,2048]{1,0:T(8,128)(2,1)} %pad_maximum_fusion.7), channel_id=1, source_target_pairs={{0,4},{1,5},{2,6},{3,7},{4,0},{5,1},{6,2},{7,3},{8,12},{9,13},{10,... | collective-permute-start | bytes 3244040 | tf_op jit(solution)/shard_map/ppermute | solution.py:307
  603.8 27.6 %collective-permute-start.36 = (bf16[4,264,2048]{2,1,0:T(8,128)(2,1)}, bf16[4,264,2048]{2,1,0:T(8,128)(2,1)}, u32[]{:S(2)}, u32[]{:S(2)}) collective-permute-start(bf16[4,264,2048]{2,1,0:T(8,128)(2,1)} %bitcast.58), channel_id=1, source_target_pairs={{0,1},{1,0},{2,3},{3,2},{4,5},{5,4},{6,7},{7,6},{8,9},{9,8},{10,11... | collective-permute-start | bytes 12976136 | tf_op jit(solution)/shard_map/ppermute | solution.py:307
  617.7 98.3 %reduce-scatter.11.cloned.1.call-start = ((), (), s32[]{:S(2)}) async-start(), calls=%async_computation.12 | async-start | bytes 1945600 | tf_op jit(solution)/shard_map/reduce_scatter | solution.py:878
  625.8 29.5 %collective-permute-start.41 = (bf16[2,80,2432]{2,1,0:T(8,128)(2,1)S(1)}, bf16[2,80,2432]{2,1,0:T(8,128)(2,1)S(1)}, u32[]{:S(2)}, u32[]{:S(2)}) collective-permute-start(bf16[2,80,2432]{2,1,0:T(8,128)(2,1)S(1)} %get-tuple-element.169), channel_id=1, source_target_pairs={{0,1},{1,0},{2,3},{3,2},{4,5},{5,4},{6,7},{7,6},{8,9},{9,8},{10,11... | collective-permute-start | bytes 2334728 | tf_op jit(solution)/shard_map/ppermute | solution.py:307
  634.0 14.5 %collective-permute-start.37 = (bf16[128,2048]{1,0:T(8,128)(2,1)S(1)}, bf16[128,2048]{1,0:T(8,128)(2,1)S(1)}, u32[]{:S(2)}, u32[]{:S(2)}) collective-permute-start(bf16[128,2048]{1,0:T(8,128)(2,1)S(1)} %slice.574), channel_id=1, source_target_pairs={{0,4},{1,5},{2,6},{3,7},{4,0},{5,1},{6,2},{7,3},{8,12},{9,13},{10,... | collective-permute-start | bytes 1572872 | tf_op jit(solution)/shard_map/ppermute | solution.py:307
  634.6 16.7 %collective-permute-start.39 = (bf16[136,2048]{1,0:T(8,128)(2,1)S(1)}, bf16[136,2048]{1,0:T(8,128)(2,1)S(1)}, u32[]{:S(2)}, u32[]{:S(2)}) collective-permute-start(bf16[136,2048]{1,0:T(8,128)(2,1)S(1)} %slice.581), channel_id=1, source_target_pairs={{0,2},{1,3},{2,0},{3,1},{4,6},{5,7},{6,4},{7,5},{8,10},{9,11},{10,... | collective-permute-start | bytes 1671176 | tf_op jit(solution)/shard_map/ppermute | solution.py:307
  650.9 25.9 %collective-permute-start.38 = (bf16[264,2048]{1,0:T(8,128)(2,1)}, bf16[264,2048]{1,0:T(8,128)(2,1)S(1)}, u32[]{:S(2)}, u32[]{:S(2)}) collective-permute-start(bf16[264,2048]{1,0:T(8,128)(2,1)} %pad_maximum_fusion.8), channel_id=1, source_target_pairs={{0,2},{1,3},{2,0},{3,1},{4,6},{5,7},{6,4},{7,5},{8,10},{9,11},{10,... | collective-permute-start | bytes 3244040 | tf_op jit(solution)/shard_map/ppermute | solution.py:307
  653.7 28.9 %collective-permute-start.40 = (bf16[264,2048]{1,0:T(8,128)(2,1)}, bf16[264,2048]{1,0:T(8,128)(2,1)}, u32[]{:S(2)}, u32[]{:S(2)}) collective-permute-start(bf16[264,2048]{1,0:T(8,128)(2,1)} %pad_maximum_fusion.9), channel_id=1, source_target_pairs={{0,4},{1,5},{2,6},{3,7},{4,0},{5,1},{6,2},{7,3},{8,12},{9,13},{10,... | collective-permute-start | bytes 3244040 | tf_op jit(solution)/shard_map/ppermute | solution.py:307
  670.4 16.1 %all-to-all-start.2 = ((bf16[8,64,640]{2,1,0:T(8,128)(2,1)}), bf16[8,64,640]{2,1,0:T(8,128)(2,1)S(1)}, u32[]{:S(2)}, u32[]{:S(2)}) async-start(bf16[8,64,640]{2,1,0:T(8,128)(2,1)} %bitcast.275), calls=%async_computation.5 | async-start | bytes 1310720 | tf_op jit(solution)/shard_map/all_to_all | solution.py:886
  687.3 25.7 %all-to-all-start.3 = ((bf16[8,64,1536]{2,1,0:T(8,128)(2,1)}), bf16[8,64,1536]{2,1,0:T(8,128)(2,1)S(1)}, u32[]{:S(2)}, u32[]{:S(2)}) async-start(bf16[8,64,1536]{2,1,0:T(8,128)(2,1)} %bitcast.252), calls=%async_computation.7 | async-start | bytes 3145728 | tf_op jit(solution)/shard_map/all_to_all | solution.py:886
  (78 other events, 1047.3 us)
Sparse Core Ops, SparseCore 0:
  13.2 39.5 all-gather.8
  54.9 53.6 all-gather.6
  110.8 166.2 all-gather.10
  339.3 60.4 reduce-scatter.4
  452.4 111.1 reduce-scatter.6
  617.9 52.4 reduce-scatter.8
  672.6 34.8 reduce-scatter.10

commit v3 on v2

--- a/solution.py
+++ b/solution.py
@@ -324,16 +324,16 @@
     return (near, *others) if others else near
 
 
-def gather_chips_at_once(block):
-    return jnp.stack(
-        [block] + [swap_with(block, mask) for mask in (ACROSS_X, ACROSS_Y, ACROSS_X + ACROSS_Y)]
-    )
-
-
-def reduce_plane(near, far, late=None):
+def send_to_chips(across_x, across_y, across_both):
+    return [
+        swap_with(across_x, ACROSS_X),
+        swap_with(across_y, ACROSS_Y),
+        swap_with(across_both, ACROSS_X + ACROSS_Y),
+    ]
+
+
+def reduce_plane(near, far, *others, late=()):
     other = swap_with(far, CORE)
-    if late is not None:
-        other, late = lax.optimization_barrier((other, late))
     rows = near.shape[1]
     split = split_row(rows)
 
@@ -341,14 +341,39 @@
         return near[place, span].astype(jnp.float32) + other[place, span].astype(jnp.float32)
 
     both = total(3).astype(jnp.bfloat16)
+    both, *others = lax.optimization_barrier((both, *others))
     first = swap_with(both[:split], ACROSS_Y).astype(jnp.float32)
     second = swap_with(both[split:], ACROSS_X).astype(jnp.float32)
     across_x = jnp.concatenate([total(1, slice(split)) + first, total(1, slice(split, None))])
     across_y = jnp.concatenate([total(2, slice(split)), total(2, slice(split, None)) + second])
-    across_x = swap_with(across_x.astype(jnp.bfloat16), ACROSS_X).astype(jnp.float32)
-    across_y = swap_with(across_y.astype(jnp.bfloat16), ACROSS_Y).astype(jnp.float32)
+    across_x, across_y = across_x.astype(jnp.bfloat16), across_y.astype(jnp.bfloat16)
+    across_x, across_y, *late = lax.optimization_barrier((across_x, across_y, *late))
+    others += late
+    across_x = swap_with(across_x, ACROSS_X).astype(jnp.float32)
+    across_y = swap_with(across_y, ACROSS_Y).astype(jnp.float32)
     result = total(0) + across_x + across_y
-    return result if late is None else (result, late)
+    return (result, *others) if others else result
+
+
+def reduce_plane_at_once(near, far, *others):
+    other = swap_with(far, CORE)
+
+    def total(place):
+        return near[place].astype(jnp.float32) + other[place].astype(jnp.float32)
+
+    *parts, others = lax.optimization_barrier(
+        (*(total(place).astype(jnp.bfloat16) for place in (1, 2, 3)), others)
+    )
+    sent = send_to_chips(*parts)
+
+    def finish(*late):
+        *parts, late = lax.optimization_barrier((*sent, late))
+        result = total(0)
+        for part in parts:
+            result = result + part.astype(jnp.float32)
+        return (result, *late) if late else result
+
+    return (finish, *others)
 
 
 def place_of(chunk, me, count):
@@ -416,12 +441,14 @@
     gated_ref,
     lagging_ref,
     conv_ref,
-    branch_ref,
+    act_ref,
+    slope_ref,
+    decay_ref,
+    rate_part_ref,
+    gate_i_part_ref,
+    conv_part_ref,
     gate_r_ref,
-    gate_i_ref,
-    hidden_ref,
     lag_edge_ref,
-    hidden_edge_ref,
     proj_wide,
     projected,
     convolved,
@@ -450,7 +477,7 @@
         low = product[:, :lanes].astype(jnp.bfloat16)
         lagging_ref[0] = low
         projected[:, :lanes] = low.astype(jnp.float32)
-        branch_ref[0] = product[:, lanes:]
+        projected[:, lanes:] = product[:, lanes:]
 
     pl.when(is_far == 0)(lambda: project(near_ref))
     pl.when(is_far == 1)(lambda: project(far_ref))
@@ -486,12 +513,13 @@
 
     def recur(tile, state):
         parts = [local_scan(tile) for tile in group_tiles(tile, group)]
-        for at, value, decay in parts:
+        for at, value, decay, activated, slope, ratio, gate in parts:
             hidden = value + decay * state
+            before = jnp.where(place == 0, state, pltpu.roll(hidden, 1, 0))
             state = jnp.broadcast_to(hidden[ROWS - 1 :], hidden.shape)
-            hidden_ref[0, at, :] = hidden
-            projected[at, :lanes] = hidden * projected[at, :lanes]
-        hidden_edge_ref[0] = hidden
+            projected[at, :lanes] = hidden * activated
+            slope_ref[0, at, :] = hidden * slope
+            rate_part_ref[0, at, :] = gate * (before - ratio)
         return state
 
     def local_scan(tile):
@@ -500,18 +528,27 @@
         starts = widen(since == 0, lanes)
         gate_r = jax.nn.sigmoid(gates[at, :lanes] + channel_ref[BIAS_A : BIAS_A + 1, :])
         gate_i = jax.nn.sigmoid(gates[at, lanes:] + channel_ref[BIAS_I : BIAS_I + 1, :])
-        gate_r_ref[0, at, :] = gate_r
-        gate_i_ref[0, at, :] = gate_i
         less = series_expm1(-gate_scale * gate_r * channel_ref[RATE : RATE + 1, :])
-        decay = jnp.where(starts, 0.0, 1.0 + less)
-        scaling = jnp.where(starts, 1.0, jnp.sqrt(-less * (2.0 + less)))
-        value = convolved[at, :] * gate_i * scaling
+        plain = 1.0 + less
+        root = jnp.sqrt(-less * (2.0 + less))
+        decay = jnp.where(starts, 0.0, plain)
+        scaling = jnp.where(starts, 1.0, root)
+        conv = convolved[at, :]
+        admitted = conv * gate_i
+        value = admitted * scaling
+        decay_ref[0, at, :] = decay
+        conv_part_ref[0, at, :] = gate_i * scaling
+        gate_i_part_ref[0, at, :] = value * (1.0 - gate_i)
+        gate_r_ref[0, at, :] = 1.0 - gate_r
+        ratio = admitted * plain / root
+        gate = decay * gate_r
         for step in (1, 2, 4):
             inside = place >= step
             value = value + jnp.where(inside, decay * pltpu.roll(value, step, 0), 0.0)
             decay = jnp.where(inside, decay * pltpu.roll(decay, step, 0), decay)
-        projected[at, :lanes] = gelu_parts(branch_ref[0, at, :])[0]
-        return at, value, decay
+        activated, slope = gelu_parts(projected[at, lanes:])
+        act_ref[0, at, :] = activated
+        return at, value, decay, activated, slope, ratio, gate
 
     carry[...] = lax.fori_loop(0, tiles // group, recur, carry[...])
     gated_ref[0] = projected[:, :lanes].astype(jnp.bfloat16)
@@ -526,14 +563,16 @@
     out_ref,
     gate_ref,
     channel_ref,
-    branch_ref,
-    hidden_ref,
+    act_ref,
+    slope_ref,
+    decay_ref,
+    rate_part_ref,
+    gate_i_part_ref,
+    conv_part_ref,
     gate_r_ref,
-    gate_i_ref,
     conv_ref,
     lagging_ref,
     lag_edge_ref,
-    hidden_edge_ref,
     projected_ref,
     gate_grad_ref,
     channel_grad_ref,
@@ -572,9 +611,7 @@
     pl.when(is_far == 0)(lambda: expand(near_ref))
     pl.when(is_far == 1)(lambda: expand(far_ref))
     lagged[...] = lagging_ref[0].astype(jnp.float32)
-    conv_part[...] = conv_ref[0].astype(jnp.float32)
     place = lax.broadcasted_iota(jnp.int32, (ROWS, lanes), 0)
-    first_chunk = chunk == 0
 
     def recur(step_index, carried):
         later_grad, later_decay, sum_a, sum_i, sum_rate = carried
@@ -584,10 +621,17 @@
             part = local_scan(tile, later_decay)
             later_decay = part[-1]
             parts.append(part)
-        for tile, (at, value, weight, _) in zip(members, parts):
+        for at, value, weight, _ in parts:
             grad = value + weight * later_grad
             later_grad = jnp.broadcast_to(grad[:1], grad.shape)
-            grad_a, grad_i, grad_rate = gate_grads(tile, at, grad)
+            conv_part[at, :] = grad * conv_part_ref[0, at, :]
+            grad_i = grad * gate_i_part_ref[0, at, :]
+            grad_rate = grad * rate_part_ref[0, at, :]
+            grad_a = (-gate_scale * channel_ref[RATE : RATE + 1, :]) * grad_rate * gate_r_ref[0, at, :]
+            grad_a = grad_a.astype(jnp.bfloat16).astype(jnp.float32)
+            grad_i = grad_i.astype(jnp.bfloat16).astype(jnp.float32)
+            gates[at, :lanes] = grad_a
+            gates[at, lanes:] = grad_i
             sum_a = sum_a + grad_a
             sum_i = sum_i + grad_i
             sum_rate = sum_rate - gate_scale * grad_rate
@@ -595,53 +639,16 @@
 
     def local_scan(tile, later_decay):
         at = pl.ds(pl.multiple_of(tile * ROWS, ROWS), ROWS)
-        since, _ = segment_reach(info_ref, chunk * rows + tile * ROWS, slots, (ROWS, 128), total)
-        starts = widen(since == 0, lanes)
-        plain = 1.0 + series_expm1(-gate_scale * gate_r_ref[0, at, :] * channel_ref[RATE : RATE + 1, :])
-        decay = jnp.where(starts, 0.0, plain)
-        activated, slope = gelu_parts(branch_ref[0, at, :])
+        decay = decay_ref[0, at, :]
         down = coming[at, :]
-        value = down * activated
-        projected[at, lanes:] = down * hidden_ref[0, at, :] * slope
+        value = down * act_ref[0, at, :]
+        projected[at, lanes:] = down * slope_ref[0, at, :]
         weight = jnp.where(place == ROWS - 1, later_decay, pltpu.roll(decay, ROWS - 1, 0))
         for step in (1, 2, 4):
             inside = place < ROWS - step
             value = value + jnp.where(inside, weight * pltpu.roll(value, ROWS - step, 0), 0.0)
             weight = jnp.where(inside, weight * pltpu.roll(weight, ROWS - step, 0), weight)
         return at, value, weight, jnp.broadcast_to(decay[:1], decay.shape)
-
-    def gate_grads(tile, at, grad):
-        ahead = pl.ds(pl.multiple_of(jnp.maximum(tile - 1, 0) * ROWS, ROWS), ROWS)
-        since, _ = segment_reach(info_ref, chunk * rows + tile * ROWS, slots, (ROWS, 128), total)
-        starts = widen(since == 0, lanes)
-        gate_r = gate_r_ref[0, at, :]
-        gate_i = gate_i_ref[0, at, :]
-        conv = conv_part[at, :]
-        rate = channel_ref[RATE : RATE + 1, :]
-        less = series_expm1(-gate_scale * gate_r * rate)
-        plain = 1.0 + less
-        root = jnp.sqrt(-less * (2.0 + less))
-        earlier = jnp.where(
-            tile == 0,
-            jnp.where(first_chunk, 0.0, hidden_edge_ref[0]),
-            hidden_ref[0, ahead, :],
-        )
-        before = jnp.where(
-            place == 0, pltpu.roll(earlier, 1, 0), pltpu.roll(hidden_ref[0, at, :], 1, 0)
-        )
-        scaled = grad * jnp.where(starts, 1.0, root)
-        conv_part[at, :] = scaled * gate_i
-        grad_i = scaled * conv * gate_i * (1.0 - gate_i)
-        grad_log = jnp.where(
-            starts, 0.0, grad * plain * (before - conv * gate_i * plain / root)
-        )
-        grad_rate = grad_log * gate_r
-        grad_a = -gate_scale * rate * grad_rate * (1.0 - gate_r)
-        grad_a = grad_a.astype(jnp.bfloat16).astype(jnp.float32)
-        grad_i = grad_i.astype(jnp.bfloat16).astype(jnp.float32)
-        gates[at, :lanes] = grad_a
-        gates[at, lanes:] = grad_i
-        return grad_a, grad_i, grad_rate
 
     empty = jnp.zeros((ROWS, lanes), jnp.float32)
     grad_last, decay_last, sum_a, sum_i, sum_rate = lax.fori_loop(
@@ -707,7 +714,7 @@
         channel_grad_ref[...] = jnp.sum(sums[...], axis=1)
 
 
-VMEM_LIMIT = 48 * 1024 * 1024
+VMEM_LIMIT = 56 * 1024 * 1024
 
 
 def run_forward(info, near, far, proj, gate, channels, taps, slots):
@@ -745,27 +752,19 @@
                 pl.BlockSpec(gate.shape, whole),
                 pl.BlockSpec(channels.shape, whole),
             ],
-            out_specs=[narrow] * 7
-            + [pl.BlockSpec((1, ROWS, lanes), at_chunk)] * 2,
+            out_specs=[narrow] * 10 + [pl.BlockSpec((1, ROWS, lanes), at_chunk)],
             scratch_shapes=[
                 pltpu.VMEM((depth, 2 * lanes), jnp.bfloat16),
-                pltpu.VMEM((rows, lanes), jnp.float32),
+                pltpu.VMEM((rows, 2 * lanes), jnp.float32),
                 pltpu.VMEM((rows, lanes), jnp.float32),
                 pltpu.VMEM((rows, 2 * lanes), jnp.float32),
                 pltpu.VMEM((ROWS, lanes), jnp.float32),
                 pltpu.VMEM((ROWS, lanes), jnp.float32),
             ],
         ),
-        out_shape=[
-            block(jnp.bfloat16),
-            block(jnp.bfloat16),
-            block(jnp.bfloat16),
-            block(jnp.float32),
-            block(jnp.float32),
-            block(jnp.float32),
-            block(jnp.float32),
-        ]
-        + [jax.ShapeDtypeStruct((count, ROWS, lanes), jnp.float32)] * 2,
+        out_shape=[block(jnp.bfloat16)] * 3
+        + [block(jnp.float32)] * 7
+        + [jax.ShapeDtypeStruct((count, ROWS, lanes), jnp.float32)],
         compiler_params=pltpu.CompilerParams(
             dimension_semantics=("arbitrary",), vmem_limit_bytes=VMEM_LIMIT
         ),
@@ -775,7 +774,7 @@
 
 
 def run_backward(info, near, far, out, gate, channels, saved, proj_columns, taps, slots):
-    lagging, conv, branch, gate_r, gate_i, hidden, lag_edge, hidden_edge = saved
+    lagging, conv, *parts, lag_edge = saved
     chips, rows, depth = near.shape
     count = 2 * chips
     lanes = gate.shape[0]
@@ -809,8 +808,8 @@
                 pl.BlockSpec(gate.shape, whole),
                 pl.BlockSpec(channels.shape, whole),
             ]
-            + [narrow] * 6
-            + [rim] * 2,
+            + [narrow] * 9
+            + [rim],
             out_specs=[
                 pl.BlockSpec((1, rows, proj_columns), at_place),
                 pl.BlockSpec((lanes, 2 * lanes), whole),
@@ -838,10 +837,7 @@
         ),
         cost_estimate=pl.CostEstimate(flops=0, bytes_accessed=0, transcendentals=0),
         name="mixer_backward",
-    )(
-        info, near, far, out, gate, channels,
-        branch, hidden, gate_r, gate_i, conv, lagging, lag_edge, hidden_edge,
-    )
+    )(info, near, far, out, gate, channels, *parts, conv, lagging, lag_edge)
 
 
 def deal_columns(moves, whole_ref, groups_ref):
@@ -880,12 +876,14 @@
     )
 
 
-def hand_back(summed, weight, gain, moves):
+def spread_rows(summed):
     count = lax.axis_size("seq")
+    blocks = summed.reshape(count, -1, summed.shape[1])
+    return lax.all_to_all(blocks, "seq", split_axis=0, concat_axis=0, tiled=True)
+
+
+def hand_back(blocks, weight, gain, moves):
     rows, columns = weight.shape
-    blocks = lax.all_to_all(
-        summed.reshape(count, rows, columns // count), "seq", split_axis=0, concat_axis=0, tiled=True
-    )
     whole, lean = pl.pallas_call(
         partial(collect_columns, moves),
         out_shape=[
@@ -901,21 +899,132 @@
 FOLD = 512
 
 
-def fold_columns(values):
-    return jnp.concatenate(
-        [values[:, column : column + FOLD] for column in range(0, values.shape[1], FOLD)]
-    )
-
-
-def unfold_columns(folded, *shapes):
-    wholes, row = [], 0
-    for rows, columns in shapes:
-        pieces = []
-        for _ in range(0, columns, FOLD):
-            pieces.append(folded[:, row : row + rows].reshape(-1, FOLD))
-            row += rows
-        wholes.append(jnp.concatenate(pieces, axis=1))
-    return wholes
+def row_spans(rows):
+    parts = max(count for count in (4, 3, 2, 1) if rows % (16 * count) == 0)
+    return [slice(part * rows // parts, (part + 1) * rows // parts) for part in range(parts)]
+
+
+def feed_forward(near_ref, far_ref, wide_ref, gate_part_ref, up_part_ref, feed_ref, normed_ref):
+    half = FOLD // 2
+
+    def expand(part_ref):
+        for span in row_spans(part_ref.shape[0]):
+            product = jnp.dot(
+                part_ref[span, :], wide_ref[...], preferred_element_type=jnp.float32
+            )
+            activated, slope = gelu_parts(product[:, :half])
+            up = product[:, half:]
+            feed_ref[span, :] = (activated * up).astype(jnp.bfloat16)
+            gate_part_ref[span, :] = slope * up
+            up_part_ref[span, :] = activated
+
+        @pl.when(pl.program_id(1) == 0)
+        def _():
+            normed_ref[...] = part_ref[...]
+
+    pl.when(pl.program_id(0) == 0)(lambda: expand(near_ref))
+    pl.when(pl.program_id(0) == 1)(lambda: expand(far_ref))
+
+
+def run_feed_forward(near, far, wide):
+    rows, depth = near.shape
+    tiles = wide.shape[1] // FOLD
+    half = FOLD // 2
+
+    def whole(part, tile):
+        return (0, 0)
+
+    return pl.pallas_call(
+        feed_forward,
+        grid=(2, tiles),
+        in_specs=[
+            pl.BlockSpec((rows, depth), whole),
+            pl.BlockSpec((rows, depth), whole),
+            pl.BlockSpec((depth, FOLD), lambda part, tile: (0, tile)),
+        ],
+        out_specs=[pl.BlockSpec((rows, half), lambda part, tile: (part, tile))] * 3
+        + [pl.BlockSpec((rows, depth), lambda part, tile: (part, 0))],
+        out_shape=[
+            jax.ShapeDtypeStruct((2 * rows, tiles * half), jnp.float32),
+            jax.ShapeDtypeStruct((2 * rows, tiles * half), jnp.float32),
+            jax.ShapeDtypeStruct((2 * rows, tiles * half), jnp.bfloat16),
+            jax.ShapeDtypeStruct((2 * rows, depth), jnp.bfloat16),
+        ],
+        compiler_params=pltpu.CompilerParams(vmem_limit_bytes=VMEM_LIMIT),
+        cost_estimate=pl.CostEstimate(
+            flops=4 * rows * depth * tiles * FOLD, bytes_accessed=0, transcendentals=0
+        ),
+        name="feed_forward",
+    )(near, far, wide)
+
+
+def feed_backward(
+    upstream_ref, planes_ref, gate_part_ref, up_part_ref, grad_ref, narrow_ref
+):
+    half = FOLD // 2
+    planes = planes_ref.shape[0]
+    tile_rows = half // planes
+    tiles = planes_ref.shape[1] // tile_rows
+
+    @pl.when(pl.program_id(0) == 0)
+    def _():
+        for tile in range(tiles):
+            for plane in range(planes):
+                target = (tile * planes + plane) * tile_rows
+                narrow_ref[target : target + tile_rows, :] = planes_ref[
+                    plane, tile * tile_rows : (tile + 1) * tile_rows, :
+                ]
+
+    feed_grad = lax.dot_general(
+        upstream_ref[...],
+        narrow_ref[...],
+        (((1,), (1,)), ((), ())),
+        preferred_element_type=jnp.float32,
+    )
+    for tile in range(tiles):
+        span = slice(tile * half, (tile + 1) * half)
+        part = feed_grad[:, span]
+        grad_ref[:, tile * FOLD : tile * FOLD + half] = (part * gate_part_ref[:, span]).astype(
+            jnp.bfloat16
+        )
+        grad_ref[:, tile * FOLD + half : (tile + 1) * FOLD] = (
+            part * up_part_ref[:, span]
+        ).astype(jnp.bfloat16)
+
+
+def run_feed_backward(upstream, narrow, gate_part, up_part):
+    rows, depth = upstream.shape
+    planes, narrow_rows = narrow.shape[:2]
+    width = gate_part.shape[1]
+    steps = max(count for count in range(1, 7) if rows % (16 * count) == 0)
+    block = rows // steps
+
+    def at_step(step):
+        return (step, 0)
+
+    return pl.pallas_call(
+        feed_backward,
+        grid=(steps,),
+        in_specs=[
+            pl.BlockSpec((block, depth), at_step),
+            pl.BlockSpec((planes, narrow_rows, depth), lambda step: (0, 0, 0)),
+            pl.BlockSpec((block, width), at_step),
+            pl.BlockSpec((block, width), at_step),
+        ],
+        out_specs=[
+            pl.BlockSpec((block, 2 * width), at_step),
+            pl.BlockSpec((width, depth), lambda step: (0, 0)),
+        ],
+        out_shape=[
+            jax.ShapeDtypeStruct((rows, 2 * width), jnp.bfloat16),
+            jax.ShapeDtypeStruct((width, depth), jnp.bfloat16),
+        ],
+        compiler_params=pltpu.CompilerParams(vmem_limit_bytes=VMEM_LIMIT),
+        cost_estimate=pl.CostEstimate(
+            flops=2 * rows * depth * width, bytes_accessed=0, transcendentals=0
+        ),
+        name="feed_backward",
+    )(upstream, narrow, gate_part, up_part)
 
 
 def pad_lanes(values, lanes):
@@ -987,18 +1096,21 @@
         for half in range(2)
         for index in range(held)
     ]
+    tile_rows = FOLD // 2 // planes
+    tiles = hidden_rows // tile_rows
     wide_moves = [
         (
             member,
-            (half * planes + plane) * hidden_rows,
-            half * planes * count * hidden_rows + (plane * count + member) * hidden_rows,
-            hidden_rows,
+            ((tile * 2 + half) * planes + plane) * tile_rows,
+            ((half * planes + plane) * count + member) * hidden_rows + tile * tile_rows,
+            tile_rows,
         )
         for member in range(count)
+        for tile in range(tiles)
         for half in range(2)
         for plane in range(planes)
     ]
-    tokens_near = gather_chips(tokens[0])
+    tokens_near, by_row = gather_chips(tokens[0], by_row)
     tokens_far = swap_with(tokens_near, CORE)
     proj_dealt = hand_out(in_proj, proj_moves)
     gains = by_row[:, :own_rows, by_row_width : by_row_width + 2]
@@ -1049,62 +1161,63 @@
         scale = lax.rsqrt(jnp.mean(values * values, axis=2, keepdims=True) + norm_eps)
         return (values * scale * gain_one).astype(jnp.bfloat16)
 
-    upstream_low, wide_dealt = lax.optimization_barrier(
-        (upstream.astype(jnp.bfloat16), wide_dealt)
-    )
-    upstream_near = gather_chips(upstream_low)
-    upstream_far = swap_with(upstream_near, CORE)
+    wide_dealt, down_proj, gain_one = lax.optimization_barrier((wide_dealt, down_proj, gain_one))
     normed_near, normed_far = normalize(tokens_near), normalize(tokens_far)
-    normed_near, normed_far, upstream_near = lax.optimization_barrier(
-        (normed_near, normed_far, upstream_near)
-    )
-    feed_weights = lax.all_gather(
-        jnp.concatenate([fold_columns(wide_dealt), fold_columns(down_proj)]), "bucket", axis=0
-    )
+    upstream_low, normed_near, normed_far = lax.optimization_barrier(
+        (upstream.astype(jnp.bfloat16), normed_near, normed_far)
+    )
+    upstream_parts = send_to_chips(upstream_low, upstream_low, upstream_low)
+    narrow = lax.all_gather(down_proj, "bucket", axis=0)
+    wide = lax.all_gather(wide_dealt, "bucket", axis=0, tiled=True)
     gated, *saved = run_forward(
         info, normed_near, normed_far, proj, gate, channel, taps, slots
     )
+    gated, *upstream_parts = lax.optimization_barrier((gated, *upstream_parts))
+    upstream_near = jnp.stack([upstream_low, *upstream_parts])
+    upstream_far = swap_with(upstream_near, CORE)
+    gated_near, upstream_near = lax.optimization_barrier((gated[: count // 2], upstream_near))
     mixed_far, mixed_near = (
         jnp.dot(part.reshape(-1, lanes), out, preferred_element_type=jnp.float32)
         .astype(jnp.bfloat16)
         .reshape(-1, rows, depth)
-        for part in (gated[count // 2 :], gated[: count // 2])
-    )
-    residual = inputs + reduce_plane(mixed_near, mixed_far)
+        for part in (gated[count // 2 :], gated_near)
+    )
+    mixed, narrow = reduce_plane(mixed_near, mixed_far, late=(narrow,))
+    residual = inputs + mixed
     scale_two = lax.rsqrt(jnp.mean(residual * residual, axis=1, keepdims=True) + norm_eps)
     normed_two = (residual * scale_two * gain_two).astype(jnp.bfloat16)
     two_near = gather_chips(normed_two)
     two_far = swap_with(two_near, CORE)
-    wide, narrow = unfold_columns(feed_weights, wide_dealt.shape, down_proj.shape)
-    halves = []
-    for part in (two_near, two_far):
-        expanded = jnp.dot(
-            part.reshape(-1, depth), wide, preferred_element_type=jnp.float32
-        )
-        halves.append((expanded, gated_gelu(expanded, hidden_width).astype(jnp.bfloat16)))
-    (expanded_near, feed_near), (expanded_far, feed_far) = halves
-
-    feed_grads = [
-        contract_last(part.reshape(-1, depth), narrow) for part in (upstream_near, upstream_far)
-    ]
-    down_part = contract_halves(feed_near, feed_far, upstream_near, upstream_far)
+    upstream_all = jnp.concatenate([upstream_near, upstream_far]).reshape(-1, depth)
+    two_far, upstream_all = lax.optimization_barrier((two_far, upstream_all))
+    gate_part, up_part, feed, two_all = run_feed_forward(
+        two_near.reshape(-1, depth), two_far.reshape(-1, depth), wide
+    )
+    half_rows = two_all.shape[0] // 2
+
+    feed_grad, narrow = run_feed_backward(
+        upstream_all,
+        narrow,
+        gate_part,
+        up_part,
+    )
+    part_far = contract_last(feed_grad[half_rows:], wide).astype(jnp.bfloat16)
+    part_near = contract_last(feed_grad[:half_rows], wide).astype(jnp.bfloat16)
+    finish, two_all, feed, upstream_all = reduce_plane_at_once(
+        part_near.reshape(-1, rows, depth),
+        part_far.reshape(-1, rows, depth),
+        two_all,
+        feed,
+        upstream_all,
+    )
+    normed_two_grad = finish()
+    down_part = contract_first(feed, upstream_all).astype(jnp.bfloat16)
+    down_part = (
+        down_part.reshape(tiles, planes, tile_rows, depth)
+        .transpose(1, 0, 2, 3)
+        .reshape(hidden_width, depth)
+    )
     down_grad = sum_planes(down_part).astype(jnp.float32)
-    expanded_near, expanded_far, down_part = lax.optimization_barrier(
-        (expanded_near, expanded_far, down_part)
-    )
-
-    def through_feed(expanded, feed_grad):
-        _, feed_pull = jax.vjp(partial(gated_gelu, split=hidden_width), expanded)
-        expanded_grad = feed_pull(feed_grad)[0].astype(jnp.bfloat16)
-        part = contract_last(expanded_grad, wide).astype(jnp.bfloat16)
-        return expanded_grad, part.reshape(-1, rows, depth)
-
-    grad_far, part_far = through_feed(expanded_far, feed_grads[1])
-    grad_near, part_near = through_feed(expanded_near, feed_grads[0])
-    part_near, two_near, two_far, feed_near, feed_far = lax.optimization_barrier(
-        (part_near, two_near, two_far, feed_near, feed_far)
-    )
-    normed_two_grad = reduce_plane(part_near, part_far)
 
     def norm_back(values, scale, gain, grad):
         scaled = grad * gain
@@ -1112,26 +1225,29 @@
         return scale * scaled - scale * scale * scale * lean * values
 
     residual_grad = upstream + norm_back(residual, scale_two, gain_two, normed_two_grad)
-    wide_part = contract_halves(two_near, two_far, grad_near, grad_far)
-    residual_grad, wide_part = lax.optimization_barrier((residual_grad, wide_part))
+    wide_part = contract_first(two_all, feed_grad).astype(jnp.bfloat16)
+    residual_grad, wide_part, down_part = lax.optimization_barrier(
+        (residual_grad, wide_part, down_part)
+    )
     wide_summed = sum_planes(wide_part)
-    low_near = gather_chips(residual_grad.astype(jnp.bfloat16))
-    low_near, down_grad = lax.optimization_barrier((low_near, down_grad))
-    low_far = swap_with(low_near, CORE)
-    output_parts = [
+    output_far, output_near = (
         jnp.dot(part, narrow, preferred_element_type=jnp.float32)
         .astype(jnp.bfloat16)
         .reshape(-1, rows, depth)
-        for part in (feed_near, feed_far)
-    ]
-    output_near, output_far = output_parts
-    output_far, low_near = lax.optimization_barrier((output_far, low_near))
-    mixed = (keep * (residual + reduce_plane(output_near, output_far))).astype(jnp.bfloat16)
-
+        for part in (feed[half_rows:], feed[:half_rows])
+    )
+    low_near, output_near, output_far, down_grad = gather_chips(
+        residual_grad.astype(jnp.bfloat16), output_near, output_far, down_grad
+    )
+    output_sums = output_near.astype(jnp.float32) + swap_with(output_far, CORE).astype(jnp.float32)
+    low_far = swap_with(low_near, CORE)
+    low_far, *output_low = lax.optimization_barrier(
+        (low_far, *(output_sums[place].astype(jnp.bfloat16) for place in (1, 2, 3)))
+    )
+    output_parts = send_to_chips(*output_low)
     proj_grad, gate_grad, channel_grad = run_backward(
         info, low_near, low_far, out, gate, channel, saved, 2 * channels, taps, slots
     )
-    proj_grad, wide_summed = lax.optimization_barrier((proj_grad, wide_summed))
     proj_grad_near, proj_grad_far = proj_grad[: count // 2], proj_grad[count // 2 :]
 
     def through_proj(part):
@@ -1139,12 +1255,19 @@
         return part.reshape(-1, rows, depth)
 
     proj_part = contract_halves(normed_near, normed_far, proj_grad_near, proj_grad_far)
-    proj_grad_far, proj_grad_near, proj_part = lax.optimization_barrier(
-        (proj_grad_far, proj_grad_near, proj_part)
-    )
+    proj_grad_far, proj_grad_near, proj_part, wide_summed, *output_parts = (
+        lax.optimization_barrier(
+            (proj_grad_far, proj_grad_near, proj_part, wide_summed, *output_parts)
+        )
+    )
+    mixed = residual + output_sums[0]
+    for part in output_parts:
+        mixed = mixed + part.astype(jnp.float32)
+    mixed = (keep * mixed).astype(jnp.bfloat16)
     part_far = through_proj(proj_grad_far)
-    part_far, mixed = lax.optimization_barrier((part_far, mixed))
-    normed_grad = reduce_plane(through_proj(proj_grad_near), part_far)
+    proj_summed = sum_planes(proj_part)
+    part_near = through_proj(proj_grad_near)
+    normed_grad, gated, mixed = reduce_plane(part_near, part_far, gated, mixed)
 
     out_grad = contract_halves(
         gated[: count // 2], gated[count // 2 :], low_near, low_far, jnp.float32
@@ -1176,14 +1299,12 @@
     by_row_grad = jnp.where(
         odd == 0, jnp.concatenate([kept, taken]), jnp.concatenate([taken, kept])
     ).reshape(planes * chunk_rows, -1)
-    proj_part, wide_summed = lax.optimization_barrier((proj_part, wide_summed))
-    proj_summed = sum_planes(proj_part)
-    wide_summed, normed_grad = lax.optimization_barrier((wide_summed, normed_grad))
+    by_row_grad = sum_planes(by_row_grad)
+    gate_up_grad, mlp_gain_grad = hand_back(spread_rows(wide_summed), gate_up, mlp_gain, wide_moves)
+    in_proj_grad, norm_gain_grad = hand_back(spread_rows(proj_summed), in_proj, norm_gain, proj_moves)
     token_grad = residual_grad + norm_back(inputs, scale_one, gain_one, normed_grad)
-    gate_up_grad, mlp_gain_grad = hand_back(wide_summed, gate_up, mlp_gain, wide_moves)
-    proj_summed, by_row_grad = lax.optimization_barrier((proj_summed, by_row_grad))
-    in_proj_grad, norm_gain_grad = hand_back(proj_summed, in_proj, norm_gain, proj_moves)
-    by_row_grad = sum_planes(by_row_grad).astype(jnp.float32)
+    token_grad, by_row_grad = lax.optimization_barrier((token_grad, by_row_grad))
+    by_row_grad = by_row_grad.astype(jnp.float32)
     out_proj_grad = by_row_grad[:, :depth]
     gate_weight_grad = by_row_grad[:, depth : depth + gate_columns]
     small_grad = by_row_grad[:, depth + gate_columns : by_row_width]

time: 737 us -> 669 us (0.908)
  matrix products: 166 us -> 97.9 us
  local copies, waits for them, and re-layouts: 97.5 us -> 51.4 us
  Pallas kernels: 76.1 us -> 120 us
  other arithmetic: 77.1 us -> 98.5 us
  waiting for transfers between devices: 226 us -> 206 us
    pallas_call x0 -> x2, Pallas kernels: none -> 41.3 us  [the longest x1 25.7 us: run_feed_forward(): pl.pallas_call(feed_forward, grid=(2, tiles), in_specs=[pl.BlockSpec((row...]
    ppermute x42 -> x39, waiting for transfers between devices: 196 us -> 162 us  [swap_with(): return lax.ppermute(block, 'seq', route)]
    unnamed x174 -> x102, local copies, waits for them, and re-layouts: 52.3 us -> 19.8 us
    dot_general x8 -> x6, matrix products: 74 us -> 46.9 us  [contract_first(): lax.dot_general(left, right, (((0,), (0,)), ((), ())), preferred_element_...]
    dot_general x6 -> x4, matrix products: 56.9 us -> 32.3 us  [contract_last(): lax.dot_general(left, right, (((1,), (1,)), ((), ())), preferred_element_...]
    dot_general x2 -> x0, matrix products: 20.4 us -> none  [by_channels(): jnp.dot(part.reshape(-1, depth), wide, preferred_element_type=jnp.float32)]
    slice x2 -> x0, local copies, waits for them, and re-layouts: 9.26 us -> none  [unfold_columns(): pieces.append(folded[:, row:row + rows].reshape(-1, FOLD))]
    all_gather x1, waiting for transfers between devices: 0.01 us -> 8.9 us  [by_channels(): by_row = lax.all_gather(by_row, 'bucket', axis=0, tiled=False)]
  transfers between devices with their start and end apart: 53 -> 51, of which waited for: 25 -> 27; matrix products, arithmetic and copies ran while one was open for 38% -> 30% of each run, Pallas kernels for 10% -> 12%
where the time goes in v3:
time: 669 us; the launch traced here: 663 us
  waiting for transfers between devices  206 us (31%)
  Pallas kernels  120 us (18%)
  other arithmetic  98.5 us (15%)
  matrix products  97.9 us (15%)
  starting transfers between devices  54 us (8%)
  local copies, waits for them, and re-layouts  51.4 us (8%)
  blocking collectives  19.4 us (3%)
  between operations  15.2 us (2%)
    ppermute x39, waiting for transfers between devices, swap_with(): return lax.ppermute(block, 'seq', route)  162 us
    dot_general x6, matrix products, contract_first(): lax.dot_general(left, right, (((0,), (0,)), ((), ())), preferred_element_...  46.9 us
    ppermute x39, starting transfers between devices, swap_with(): return lax.ppermute(block, 'seq', route)  36.9 us
    pallas_call x1, Pallas kernels, run_forward(): pl.pallas_call(partial(mixer_forward, taps, slots), grid_spec=pltpu.Prefe...  33.8 us
    dot_general x4, matrix products, contract_last(): lax.dot_general(left, right, (((1,), (1,)), ((), ())), preferred_element_...  32.3 us
    pallas_call x1, Pallas kernels, run_backward(): pl.pallas_call(partial(mixer_backward, taps, slots), grid_spec=pltpu.Pref...  31.8 us
    pallas_call x1, Pallas kernels, run_feed_forward(): pl.pallas_call(feed_forward, grid=(2, tiles), in_specs=[pl.BlockSpec((row...  25.7 us
    unnamed x102, local copies, waits for them, and re-layouts  19.8 us
  transfers between devices with their start and end apart: 51, of which 27 were waited for; matrix products, arithmetic and copies ran while one was open for 30% of the time, Pallas kernels for 12%

profile of v3, /device:TPU:0, one launch (start us, length us, event | category | flops | bytes accessed | tf_op | source)
XLA Modules:
  0.0 663.2 jit_solution(12618244052032567098)
XLA Ops:
  19.8 3.5 all-to-all-start
  23.5 17.4 %collective-permute-done = bf16[264,2048]{1,0:T(8,128)(2,1)S(1)} collective-permute-done((bf16[264,2048]{1,0:T(8,128)(2,1)S(1)}, bf16[264,2048]{1,0:T(8,128)(2,1)S(1)}, u32[]{:S(2)}, u32[]{:S(2)}) %collective-permute-start) | collective-permute-done | bytes 1081376 | tf_op jit(solution)/shard_map/ppermute | solution.py:307
  43.9 8.9 %all-gather.12.cloned.1.call-done = bf16[320,2432]{1,0:T(8,128)(2,1)} async-done(((bf16[80,2432]{1,0:T(8,128)(2,1)}), bf16[320,2432]{1,0:T(8,128)(2,1)}) %all-gather.12.cloned.1.call-update) | async-done | bytes 1556496 | tf_op jit(solution)/shard_map/all_gather | solution.py:1086
  63.2 4.6 collective-permute-done.2
  76.0 3.6 all-to-all-start.1
  85.6 19.4 %all-gather.1 = bf16[2,4,512]{0,2,1:T(8,128)(2,1)S(1)} all-gather(bf16[2,4,64]{0,2,1:T(8,128)(2,1)S(1)} %slice_bitcast_fusion.12), channel_id=3, replica_groups=mesh['bucket'=4,'seq'=8] {'seq'}, dimensions={2}, use_global_device_ids=true | all-gather | bytes 9216 | tf_op jit(solution)/shard_map/all_gather | solution.py:1117
  115.0 6.8 %fusion.2 = (bf16[4,264,2048]{2,1,0:T(8,128)(2,1)}, bf16[4,264,2048]{2,1,0:T(8,128)(2,1)}) fusion(bf16[4,264,2048]{2,1,0:T(8,128)(2,1)} %collective-permute-done.4, f32[4,264]{1,0:T(4,128)S(1)} %add_rsqrt_fusion.1, f32[2048]{0:T(1024)S(1)} %bitcast.242, f32[4,264]{1,0:T(4,128)S(1)} %rsqrt.42, bf16[4,264,2048]{2,1,0:T(8,128)(2,1)} %bitcast.205), kind=kLoop, calls=%fused_computation.4 | loop fusion | flops 17301504 | bytes 17318144 | tf_op jit(solution)/shard_map/convert_element_type | solution.py:1162
  128.3 33.8 %mixer_forward.1 = (bf16[8,264,384]{2,1,0:T(8,128)(2,1)}, bf16[8,264,384]{2,1,0:T(8,128)(2,1)}, bf16[8,264,384]{2,1,0:T(8,128)(2,1)}, f32[8,264,384]{2,1,0:T(8,1...) custom-call(s32[5]{0:T(128)} %pad_add_fusion.info_ref, ...), custom_call_target="tpu_custom_call" | custom-call | tf_op jit(solution)/shard_map/mixer_forward/pallas_call | solution.py:743
  162.1 9.4 %collective-permute-done.7 = bf16[264,2048]{1,0:T(8,128)(2,1)} collective-permute-done((bf16[264,2048]{1,0:T(8,128)(2,1)}, bf16[264,2048]{1,0:T(8,128)(2,1)}, u32[]{:S(2)}, u32[]{:S(2)}) %collective-permute-start.7) | collective-permute-done | bytes 1081376 | tf_op jit(solution)/shard_map/ppermute | solution.py:307
  173.1 4.5 convolution_convert_fusion.5
  177.9 3.9 pad_maximum_fusion.1
  192.3 10.9 %collective-permute-done.10 = bf16[128,2048]{1,0:T(8,128)(2,1)S(1)} collective-permute-done((bf16[128,2048]{1,0:T(8,128)(2,1)S(1)}, bf16[128,2048]{1,0:T(8,128)(2,1)S(1)}, u32[]{:S(2)}, u32[]{:S(2)}) %collective-permute-start.10) | collective-permute-done | bytes 524320 | tf_op jit(solution)/shard_map/ppermute | solution.py:307
  208.1 22.9 %collective-permute-done.12 = bf16[264,2048]{1,0:T(8,128)(2,1)S(1)} collective-permute-done((bf16[264,2048]{1,0:T(8,128)(2,1)S(1)}, bf16[264,2048]{1,0:T(8,128)(2,1)S(1)}, u32[]{:S(2)}, u32[]{:S(2)}) %collective-permute-start.12) | collective-permute-done | bytes 1081376 | tf_op jit(solution)/shard_map/ppermute | solution.py:307
  237.2 21.6 %collective-permute-done.15 = bf16[264,2048]{1,0:T(8,128)(2,1)S(1)} collective-permute-done((bf16[264,2048]{1,0:T(8,128)(2,1)S(1)}, bf16[264,2048]{1,0:T(8,128)(2,1)S(1)}, u32[]{:S(2)}, u32[]{:S(2)}) %collective-permute-start.15) | collective-permute-done | bytes 1081376 | tf_op jit(solution)/shard_map/ppermute | solution.py:307
  263.5 7.7 %collective-permute-done.16 = bf16[128,2048]{1,0:T(8,128)(2,1)S(1)} collective-permute-done((bf16[128,2048]{1,0:T(8,128)(2,1)S(1)}, bf16[128,2048]{1,0:T(8,128)(2,1)S(1)}, u32[]{:S(2)}, u32[]{:S(2)}) %collective-permute-start.16) | collective-permute-done | bytes 524320 | tf_op jit(solution)/shard_map/ppermute | solution.py:307
  272.0 3.5 collective-permute-done.17
  276.4 7.7 %pad_maximum_fusion = bf16[8,264,2048]{2,1,0:T(8,128)(2,1)} fusion(bf16[4,264,2048]{2,1,0:T(8,128)(2,1)} %collective-permute-done.19, bf16[4,264,2048]{2,1,0:T(8,128)(2,1)} %pad_maximum_fusion.1), kind=kLoop, calls=%fused_computation.5 | loop fusion | flops 4325376 | bytes 17301504 | tf_op jit(solution)/shard_map/concatenate | solution.py:1191
  284.1 8.1 %all-gather.10.cloned.1.call-done.wide_ref = bf16[2048,1536]{1,0:T(8,128)(2,1)} async-done(((bf16[512,1536]{1,0:T(8,128)(2,1)}), bf16[2048,1536]{1,0:T(8,128)(2,1)}) %all-gather.10.cloned.1.call-update) | async-done | bytes 6291472 | tf_op jit(solution)/shard_map/all_gather | solution.py:1171
  292.2 25.7 %feed_forward.1 = (f32[2112,768]{1,0:T(8,128)}, f32[2112,768]{1,0:T(8,128)}, bf16[2112,768]{1,0:T(8,128)(2,1)}, bf16[2112,2048]{1,0:T(8,128)(2,1)}) custom-call(bf16[1056,2048]{1,0:T(8,128)(2,1)} %constant_dynamic-update-slice_fusion.5.near_ref, bf16[1056,2048]{1,0:T(8,128)(2,1)} %bitcast.37.far_ref, bf16[2048,1536]{1,0:T(8,128)(2,1)} %all-gather.10.cloned.1.call-done.wide_ref), custom_call_target="tpu_custom_call" | custom-call | flops 13287555072 | tf_op jit(solution)/shard_map/feed_forward/pallas_call | solution.py:937
  317.9 15.7 %feed_backward.1 = (bf16[2112,1536]{1,0:T(8,128)(2,1)}, bf16[768,2048]{1,0:T(8,128)(2,1)}) custom-call(bf16[2112,2048]{1,0:T(8,128)(2,1)} %bitcast.200, bf16[4,192,2048]{2,1,0:T(8,128)(2,1)} %bitcast.229, f32[2112,768]{1,0:T(8,128)} %get-tuple-element.120.gate_part_ref, f32[2112,768]{1,0:T(8,128)} %get-tuple-element.121.up_part_ref), custom_call_target="tpu_custom_call" | custom-call | flops 6643777536 | tf_op jit(solution)/shard_map/feed_backward/pallas_call | solution.py:1005
  333.6 11.6 %convolution_convert_fusion.7 = bf16[1056,2048]{1,0:T(8,128)(2,1)} fusion(bf16[2048,1536]{1,0:T(8,128)(2,1)} %all-gather.10.cloned.1.call-done.wide_ref, bf16[2112,1536]{1,0:T(8,128)(2,1)} %get-tuple-element.122), kind=kOutput, calls=%fused_computation.16 | convolution fusion | flops 6645940224 | bytes 13860864 | tf_op jit(solution)/shard_map/dot_general | solution.py:68
  345.2 9.1 %convolution_convert_fusion.8 = bf16[1056,2048]{1,0:T(8,128)(2,1)S(1)} fusion(bf16[2048,1536]{1,0:T(8,128)(2,1)} %all-gather.10.cloned.1.call-done.wide_ref, bf16[2112,1536]{1,0:T(8,128)(2,1)S(1)} %copy-done.26), kind=kOutput, calls=%fused_computation.17 | convolution fusion | flops 6645940224 | bytes 13860864 | tf_op jit(solution)/shard_map/dot_general | solution.py:68
  359.3 8.0 %convolution_convert_fusion.9 = bf16[768,2048]{1,0:T(8,128)(2,1)S(1)} fusion(bf16[2112,768]{1,0:T(8,128)(2,1)S(1)} %copy-done.31, bf16[2112,2048]{1,0:T(8,128)(2,1)S(1)} %bitcast.203), kind=kOutput, calls=%fused_computation.25 | convolution fusion | flops 6645350400 | bytes 15040512 | tf_op jit(solution)/shard_map/dot_general | solution.py:74
  372.7 20.8 %convolution_convert_fusion = bf16[2048,1536]{1,0:T(8,128)(2,1)} fusion(bf16[2112,2048]{1,0:T(8,128)(2,1)} %get-tuple-element.131, bf16[2112,1536]{1,0:T(8,128)(2,1)} %get-tuple-element.122), kind=kOutput, calls=%fused_computation.9 | convolution fusion | flops 13290700800 | bytes 21430272 | tf_op jit(solution)/shard_map/dot_general | solution.py:74
  396.1 24.0 %collective-permute-done.22 = bf16[264,2048]{1,0:T(8,128)(2,1)} collective-permute-done((bf16[264,2048]{1,0:T(8,128)(2,1)}, bf16[264,2048]{1,0:T(8,128)(2,1)}, u32[]{:S(2)}, u32[]{:S(2)}) %collective-permute-start.22) | collective-permute-done | bytes 1081376 | tf_op jit(solution)/shard_map/ppermute | solution.py:307
  423.3 5.2 fusion.31
  428.5 3.5 constant_dynamic-update-slice_fusion.14
  434.1 6.7 %convolution_convert_fusion.3 = bf16[1056,2048]{1,0:T(8,128)(2,1)} fusion(bf16[768,2048]{1,0:T(8,128)(2,1)S(1)} %copy-done.27, bf16[2112,768]{1,0:T(8,128)(2,1)} %get-tuple-element.132), kind=kOutput, calls=%fused_computation.12 | convolution fusion | flops 3324051456 | bytes 9093120 | tf_op jit(solution)/shard_map/dot_general | solution.py:1234
  440.9 5.1 convolution_convert_fusion.4
  448.5 9.0 %collective-permute-done.24 = bf16[264,2048]{1,0:T(8,128)(2,1)S(1)} collective-permute-done((bf16[264,2048]{1,0:T(8,128)(2,1)}, bf16[264,2048]{1,0:T(8,128)(2,1)S(1)}, u32[]{:S(2)}, u32[]{:S(2)}) %collective-permute-start.24) | collective-permute-done | bytes 1081376 | tf_op jit(solution)/shard_map/ppermute | solution.py:307
  465.4 8.7 %collective-permute-done.26 = bf16[128,2048]{1,0:T(8,128)(2,1)S(1)} collective-permute-done((bf16[128,2048]{1,0:T(8,128)(2,1)S(1)}, bf16[128,2048]{1,0:T(8,128)(2,1)S(1)}, u32[]{:S(2)}, u32[]{:S(2)}) %collective-permute-start.26) | collective-permute-done | bytes 524320 | tf_op jit(solution)/shard_map/ppermute | solution.py:307
  477.6 8.3 %convert_add_fusion = (f32[4,264,2048]{2,1,0:T(8,128)}, bf16[4,264,2048]{2,1,0:T(8,128)(2,1)S(1)}) fusion(bf16[4,264,2048]{2,1,0:T(8,128)(2,1)} %collective-permute-done.29, bf16[4,264,2048]{2,1,0:T(8,128)(2,1)S(1)} %bitcast.228), kind=kLoop, calls=%fused_computation.6 | loop fusion | flops 8650752 | bytes 21626880 | tf_op jit(solution)/shard_map/add | solution.py:1242
  491.2 31.8 %mixer_backward.1 = (bf16[8,264,640]{2,1,0:T(8,128)(2,1)}, f32[384,768]{1,0:T(8,128)}, f32[8,384]{1,0:T(8,128)}) custom-call(s32[5]{0:T(128)} %pad_add_fusion.info_ref, bf16[4,264,2048]{2,1,0:T(8,128)(2,1)} %bitcast.197, bf16[4,264,2048]{2,1,0:T(8,128)(2,1)} %collective-permute-done.28.far_ref, bf16[384,2048]{1,0:T(8,128)(2,1)} %pad.51.out_ref, ...), custom_call_target="tpu_custom_call" | custom-call | tf_op jit(solution)/shard_map/mixer_backward/pallas_call | solution.py:799
  523.0 3.9 fusion.68
  526.9 5.8 fusion.64
  532.8 5.6 fusion.3
  540.8 7.7 %convolution_convert_fusion.1 = bf16[1056,2048]{1,0:T(8,128)(2,1)} fusion(bf16[1056,640]{1,0:T(8,128)(2,1)} %bitcast.237, bf16[2048,640]{1,0:T(8,128)(2,1)} %all-gather.8.cloned.1.call-done.proj_ref), kind=kOutput, calls=%fused_computation.10 | convolution fusion | flops 2770403328 | bytes 8298496 | tf_op jit(solution)/shard_map/dot_general | solution.py:68
  551.7 4.7 all-to-all-start.3
  557.2 4.2 fusion.16
  561.5 3.8 convolution_convert_fusion.2
  572.0 4.5 convolution_bitcast_fusion
  585.2 9.5 %collective-permute-done.34 = bf16[128,2048]{1,0:T(8,128)(2,1)S(1)} collective-permute-done((bf16[128,2048]{1,0:T(8,128)(2,1)S(1)}, bf16[128,2048]{1,0:T(8,128)(2,1)S(1)}, u32[]{:S(2)}, u32[]{:S(2)}) %collective-permute-start.34) | collective-permute-done | bytes 524320 | tf_op jit(solution)/shard_map/ppermute | solution.py:307
  603.5 9.7 %reduce-scatter.11.cloned.1.call-done = bf16[512,640]{1,0:T(8,128)(2,1)} async-done(((bf16[2048,640]{1,0:T(8,128)(2,1)}), bf16[512,640]{1,0:T(8,128)(2,1)}) %reduce-scatter.11.cloned.1.call-update) | async-done | bytes 655376 | tf_op jit(solution)/shard_map/reduce_scatter | solution.py:874
  613.2 4.5 all-to-all-start.2
  617.7 4.9 collect_columns.3
  624.1 10.6 %all-to-all-done.2.groups_ref = bf16[8,64,640]{2,1,0:T(8,128)(2,1)} async-done(((bf16[8,64,640]{2,1,0:T(8,128)(2,1)}), bf16[8,64,640]{2,1,0:T(8,128)(2,1)}, u32[]{:S(2)}, u32[]{:S(2)}) %all-to-all-start.2) | async-done | bytes 655392 | tf_op jit(solution)/shard_map/all_to_all | solution.py:882
  641.6 4.3 fusion.10
  645.9 4.6 reduce-scatter.9.cloned.1.call-done
  (296 shorter events, 168.2 us)
Async XLA Ops:
  7.2 45.6 %all-gather.12.cloned.1.call-start = ((), (), s32[]{:S(2)}) async-start(), calls=%async_computation.14 | async-start | bytes 1945600 | tf_op jit(solution)/shard_map/all_gather | solution.py:1086
  13.1 27.7 %collective-permute-start = (bf16[264,2048]{1,0:T(8,128)(2,1)S(1)}, bf16[264,2048]{1,0:T(8,128)(2,1)S(1)}, u32[]{:S(2)}, u32[]{:S(2)}) collective-permute-start(bf16[264,2048]{1,0:T(8,128)(2,1)S(1)} %bitcast.210), channel_id=1, source_target_pairs={{0,2},{1,3},{2,0},{3,1},{4,6},{5,7},{6,4},{7,5},{8,10},{9,11},{10,... | collective-permute-start | bytes 3244040 | tf_op jit(solution)/shard_map/ppermute | solution.py:307
  16.1 27.8 %collective-permute-start.1 = (bf16[264,2048]{1,0:T(8,128)(2,1)S(1)}, bf16[264,2048]{1,0:T(8,128)(2,1)}, u32[]{:S(2)}, u32[]{:S(2)}) collective-permute-start(bf16[264,2048]{1,0:T(8,128)(2,1)S(1)} %bitcast.211), channel_id=1, source_target_pairs={{0,4},{1,5},{2,6},{3,7},{4,0},{5,1},{6,2},{7,3},{8,12},{9,13},{10,... | collective-permute-start | bytes 3244040 | tf_op jit(solution)/shard_map/ppermute | solution.py:307
  19.8 37.4 %all-to-all-start = ((bf16[8,64,640]{2,1,0:T(8,128)(2,1)}), bf16[8,64,640]{2,1,0:T(8,128)(2,1)S(1)}, u32[]{:S(2)}, u32[]{:S(2)}) async-start(bf16[8,64,640]{2,1,0:T(8,128)(2,1)} %deal_columns.2), calls=%async_computation | async-start | bytes 1310720 | tf_op jit(solution)/shard_map/all_to_all | solution.py:869
  23.4 104.9 %all-gather.8.cloned.1.call-start = ((), (), s32[]{:S(2)}) async-start(), calls=%async_computation.8 | async-start | bytes 3276800 | tf_op jit(solution)/shard_map/all_gather | solution.py:1121
  54.7 13.1 %collective-permute-start.2 = (bf16[128,2048]{1,0:T(8,128)(2,1)}, bf16[128,2048]{1,0:T(8,128)(2,1)S(1)}, u32[]{:S(2)}, u32[]{:S(2)}) collective-permute-start(bf16[128,2048]{1,0:T(8,128)(2,1)} %slice.281), channel_id=1, source_target_pairs={{0,2},{1,3},{2,0},{3,1},{4,6},{5,7},{6,4},{7,5},{8,10},{9,11},{10,... | collective-permute-start | bytes 1572872 | tf_op jit(solution)/shard_map/ppermute | solution.py:307
  58.1 13.3 %collective-permute-start.3 = (bf16[136,2048]{1,0:T(8,128)(2,1)S(1)}, bf16[136,2048]{1,0:T(8,128)(2,1)S(1)}, u32[]{:S(2)}, u32[]{:S(2)}) collective-permute-start(bf16[136,2048]{1,0:T(8,128)(2,1)S(1)} %slice.282), channel_id=1, source_target_pairs={{0,4},{1,5},{2,6},{3,7},{4,0},{5,1},{6,2},{7,3},{8,12},{9,13},{10,... | collective-permute-start | bytes 1671176 | tf_op jit(solution)/shard_map/ppermute | solution.py:307
  72.3 39.4 %collective-permute-start.4 = (bf16[4,264,2048]{2,1,0:T(8,128)(2,1)}, bf16[4,264,2048]{2,1,0:T(8,128)(2,1)}, u32[]{:S(2)}, u32[]{:S(2)}) collective-permute-start(bf16[4,264,2048]{2,1,0:T(8,128)(2,1)} %bitcast.204), channel_id=1, source_target_pairs={{0,1},{1,0},{2,3},{3,2},{4,5},{5,4},{6,7},{7,6},{8,9},{9,8},{10,11... | collective-permute-start | bytes 12976136 | tf_op jit(solution)/shard_map/ppermute | solution.py:307
  76.0 30.1 %all-to-all-start.1 = ((bf16[8,64,1536]{2,1,0:T(8,128)(2,1)}), bf16[8,64,1536]{2,1,0:T(8,128)(2,1)S(1)}, u32[]{:S(2)}, u32[]{:S(2)}) async-start(bf16[8,64,1536]{2,1,0:T(8,128)(2,1)} %deal_columns.3), calls=%async_computation.1 | async-start | bytes 3145728 | tf_op jit(solution)/shard_map/all_to_all | solution.py:869
  79.5 126.5 %all-gather.14.cloned.1.call-start = ((), (), s32[]{:S(2)}) async-start(), calls=%async_computation.15 | async-start | bytes 3932160 | tf_op jit(solution)/shard_map/all_gather | solution.py:1170
  85.0 24.8 %collective-permute-start.5 = (bf16[2,80,2432]{2,1,0:T(8,128)(2,1)}, bf16[2,80,2432]{2,1,0:T(8,128)(2,1)}, u32[]{:S(2)}, u32[]{:S(2)}) collective-permute-start(bf16[2,80,2432]{2,1,0:T(8,128)(2,1)} %get-tuple-element.234), channel_id=1, source_target_pairs={{0,1},{1,0},{2,3},{3,2},{4,5},{5,4},{6,7},{7,6},{8,9},{9,8},{10,11... | collective-permute-start | bytes 2334728 | tf_op jit(solution)/shard_map/ppermute | solution.py:307
  106.1 186.2 %all-gather.10.cloned.1.call-start = ((), (), s32[]{:S(2)}) async-start(), calls=%async_computation.9 | async-start | bytes 7864320 | tf_op jit(solution)/shard_map/all_gather | solution.py:1171
  121.8 40.3 %collective-permute-start.6 = (bf16[264,2048]{1,0:T(8,128)(2,1)}, bf16[264,2048]{1,0:T(8,128)(2,1)}, u32[]{:S(2)}, u32[]{:S(2)}) collective-permute-start(bf16[264,2048]{1,0:T(8,128)(2,1)} %fusion.32), channel_id=1, source_target_pairs={{0,2},{1,3},{2,0},{3,1},{4,6},{5,7},{6,4},{7,5},{8,10},{9,11},{10,... | collective-permute-start | bytes 3244040 | tf_op jit(solution)/shard_map/ppermute | solution.py:307
  122.2 49.3 %collective-permute-start.7 = (bf16[264,2048]{1,0:T(8,128)(2,1)}, bf16[264,2048]{1,0:T(8,128)(2,1)}, u32[]{:S(2)}, u32[]{:S(2)}) collective-permute-start(bf16[264,2048]{1,0:T(8,128)(2,1)} %fusion.32), channel_id=1, source_target_pairs={{0,4},{1,5},{2,6},{3,7},{4,0},{5,1},{6,2},{7,3},{8,12},{9,13},{10,... | collective-permute-start | bytes 3244040 | tf_op jit(solution)/shard_map/ppermute | solution.py:307
  123.8 47.8 %collective-permute-start.8 = (bf16[264,2048]{1,0:T(8,128)(2,1)}, bf16[264,2048]{1,0:T(8,128)(2,1)}, u32[]{:S(2)}, u32[]{:S(2)}) collective-permute-start(bf16[264,2048]{1,0:T(8,128)(2,1)} %fusion.32), channel_id=1, source_target_pairs={{0,6},{1,7},{2,4},{3,5},{4,2},{5,3},{6,0},{7,1},{8,14},{9,15},{10,... | collective-permute-start | bytes 3244040 | tf_op jit(solution)/shard_map/ppermute | solution.py:307
  177.6 268.4 %reduce-scatter.5.cloned.1.call-start = ((), (), s32[]{:S(2)}) async-start(), calls=%async_computation.10 | async-start | bytes 3932160 | tf_op jit(solution)/shard_map/reduce_scatter | solution.py:874
  187.8 16.7 %collective-permute-start.11 = (bf16[136,2048]{1,0:T(8,128)(2,1)S(1)}, bf16[136,2048]{1,0:T(8,128)(2,1)S(1)}, u32[]{:S(2)}, u32[]{:S(2)}) collective-permute-start(bf16[136,2048]{1,0:T(8,128)(2,1)S(1)} %slice.383), channel_id=1, source_target_pairs={{0,2},{1,3},{2,0},{3,1},{4,6},{5,7},{6,4},{7,5},{8,10},{9,11},{10,... | collective-permute-start | bytes 1671176 | tf_op jit(solution)/shard_map/ppermute | solution.py:307
  189.5 13.7 %collective-permute-start.10 = (bf16[128,2048]{1,0:T(8,128)(2,1)S(1)}, bf16[128,2048]{1,0:T(8,128)(2,1)S(1)}, u32[]{:S(2)}, u32[]{:S(2)}) collective-permute-start(bf16[128,2048]{1,0:T(8,128)(2,1)S(1)} %slice.376), channel_id=1, source_target_pairs={{0,4},{1,5},{2,6},{3,7},{4,0},{5,1},{6,2},{7,3},{8,12},{9,13},{10,... | collective-permute-start | bytes 1572872 | tf_op jit(solution)/shard_map/ppermute | solution.py:307
  206.0 24.9 %collective-permute-start.12 = (bf16[264,2048]{1,0:T(8,128)(2,1)S(1)}, bf16[264,2048]{1,0:T(8,128)(2,1)S(1)}, u32[]{:S(2)}, u32[]{:S(2)}) collective-permute-start(bf16[264,2048]{1,0:T(8,128)(2,1)S(1)} %pad_maximum_fusion.2), channel_id=1, source_target_pairs={{0,2},{1,3},{2,0},{3,1},{4,6},{5,7},{6,4},{7,5},{8,10},{9,11},{10,... | collective-permute-start | bytes 3244040 | tf_op jit(solution)/shard_map/ppermute | solution.py:307
  206.6 24.6 %collective-permute-start.13 = (bf16[264,2048]{1,0:T(8,128)(2,1)S(1)}, bf16[264,2048]{1,0:T(8,128)(2,1)S(1)}, u32[]{:S(2)}, u32[]{:S(2)}) collective-permute-start(bf16[264,2048]{1,0:T(8,128)(2,1)S(1)} %pad_maximum_fusion.3), channel_id=1, source_target_pairs={{0,4},{1,5},{2,6},{3,7},{4,0},{5,1},{6,2},{7,3},{8,12},{9,13},{10,... | collective-permute-start | bytes 3244040 | tf_op jit(solution)/shard_map/ppermute | solution.py:307
  235.0 23.8 %collective-permute-start.15 = (bf16[264,2048]{1,0:T(8,128)(2,1)S(1)}, bf16[264,2048]{1,0:T(8,128)(2,1)S(1)}, u32[]{:S(2)}, u32[]{:S(2)}) collective-permute-start(bf16[264,2048]{1,0:T(8,128)(2,1)S(1)} %get-tuple-element.212), channel_id=1, source_target_pairs={{0,4},{1,5},{2,6},{3,7},{4,0},{5,1},{6,2},{7,3},{8,12},{9,13},{10,... | collective-permute-start | bytes 3244040 | tf_op jit(solution)/shard_map/ppermute | solution.py:307
  236.5 24.6 %collective-permute-start.14 = (bf16[264,2048]{1,0:T(8,128)(2,1)S(1)}, bf16[264,2048]{1,0:T(8,128)(2,1)S(1)}, u32[]{:S(2)}, u32[]{:S(2)}) collective-permute-start(bf16[264,2048]{1,0:T(8,128)(2,1)S(1)} %get-tuple-element.212), channel_id=1, source_target_pairs={{0,2},{1,3},{2,0},{3,1},{4,6},{5,7},{6,4},{7,5},{8,10},{9,11},{10,... | collective-permute-start | bytes 3244040 | tf_op jit(solution)/shard_map/ppermute | solution.py:307
  258.8 12.4 %collective-permute-start.16 = (bf16[128,2048]{1,0:T(8,128)(2,1)S(1)}, bf16[128,2048]{1,0:T(8,128)(2,1)S(1)}, u32[]{:S(2)}, u32[]{:S(2)}) collective-permute-start(bf16[128,2048]{1,0:T(8,128)(2,1)S(1)} %slice.385), channel_id=1, source_target_pairs={{0,2},{1,3},{2,0},{3,1},{4,6},{5,7},{6,4},{7,5},{8,10},{9,11},{10,... | collective-permute-start | bytes 1572872 | tf_op jit(solution)/shard_map/ppermute | solution.py:307
  260.4 16.1 %collective-permute-start.19 = (bf16[4,264,2048]{2,1,0:T(8,128)(2,1)}, bf16[4,264,2048]{2,1,0:T(8,128)(2,1)}, u32[]{:S(2)}, u32[]{:S(2)}) collective-permute-start(bf16[4,264,2048]{2,1,0:T(8,128)(2,1)} %pad_maximum_fusion.1), channel_id=1, source_target_pairs={{0,1},{1,0},{2,3},{3,2},{4,5},{5,4},{6,7},{7,6},{8,9},{9,8},{10,11... | collective-permute-start | bytes 12976136 | tf_op jit(solution)/shard_map/ppermute | solution.py:307
  261.2 14.4 %collective-permute-start.17 = (bf16[136,2048]{1,0:T(8,128)(2,1)S(1)}, bf16[136,2048]{1,0:T(8,128)(2,1)S(1)}, u32[]{:S(2)}, u32[]{:S(2)}) collective-permute-start(bf16[136,2048]{1,0:T(8,128)(2,1)S(1)} %slice.386), channel_id=1, source_target_pairs={{0,4},{1,5},{2,6},{3,7},{4,0},{5,1},{6,2},{7,3},{8,12},{9,13},{10,... | collective-permute-start | bytes 1671176 | tf_op jit(solution)/shard_map/ppermute | solution.py:307
  369.1 171.7 %reduce-scatter.7.cloned.1.call-start = ((), (), s32[]{:S(2)}) async-start(), calls=%async_computation.11 | async-start | bytes 7864320 | tf_op jit(solution)/shard_map/reduce_scatter | solution.py:874
  369.2 26.9 %collective-permute-start.21 = (bf16[264,2048]{1,0:T(8,128)(2,1)}, bf16[264,2048]{1,0:T(8,128)(2,1)S(1)}, u32[]{:S(2)}, u32[]{:S(2)}) collective-permute-start(bf16[264,2048]{1,0:T(8,128)(2,1)} %get-tuple-element.125), channel_id=1, source_target_pairs={{0,2},{1,3},{2,0},{3,1},{4,6},{5,7},{6,4},{7,5},{8,10},{9,11},{10,... | collective-permute-start | bytes 3244040 | tf_op jit(solution)/shard_map/ppermute | solution.py:307
  370.7 49.4 %collective-permute-start.22 = (bf16[264,2048]{1,0:T(8,128)(2,1)}, bf16[264,2048]{1,0:T(8,128)(2,1)}, u32[]{:S(2)}, u32[]{:S(2)}) collective-permute-start(bf16[264,2048]{1,0:T(8,128)(2,1)} %get-tuple-element.126), channel_id=1, source_target_pairs={{0,4},{1,5},{2,6},{3,7},{4,0},{5,1},{6,2},{7,3},{8,12},{9,13},{10,... | collective-permute-start | bytes 3244040 | tf_op jit(solution)/shard_map/ppermute | solution.py:307
  372.2 47.9 %collective-permute-start.23 = (bf16[264,2048]{1,0:T(8,128)(2,1)}, bf16[264,2048]{1,0:T(8,128)(2,1)}, u32[]{:S(2)}, u32[]{:S(2)}) collective-permute-start(bf16[264,2048]{1,0:T(8,128)(2,1)} %get-tuple-element.127), channel_id=1, source_target_pairs={{0,6},{1,7},{2,4},{3,5},{4,2},{5,3},{6,0},{7,1},{8,14},{9,15},{10,... | collective-permute-start | bytes 3244040 | tf_op jit(solution)/shard_map/ppermute | solution.py:307
  432.0 25.4 %collective-permute-start.24 = (bf16[264,2048]{1,0:T(8,128)(2,1)}, bf16[264,2048]{1,0:T(8,128)(2,1)S(1)}, u32[]{:S(2)}, u32[]{:S(2)}) collective-permute-start(bf16[264,2048]{1,0:T(8,128)(2,1)} %get-tuple-element.210), channel_id=1, source_target_pairs={{0,2},{1,3},{2,0},{3,1},{4,6},{5,7},{6,4},{7,5},{8,10},{9,11},{10,... | collective-permute-start | bytes 3244040 | tf_op jit(solution)/shard_map/ppermute | solution.py:307
  433.2 25.4 %collective-permute-start.25 = (bf16[264,2048]{1,0:T(8,128)(2,1)}, bf16[264,2048]{1,0:T(8,128)(2,1)}, u32[]{:S(2)}, u32[]{:S(2)}) collective-permute-start(bf16[264,2048]{1,0:T(8,128)(2,1)} %get-tuple-element.210), channel_id=1, source_target_pairs={{0,4},{1,5},{2,6},{3,7},{4,0},{5,1},{6,2},{7,3},{8,12},{9,13},{10,... | collective-permute-start | bytes 3244040 | tf_op jit(solution)/shard_map/ppermute | solution.py:307
  458.7 18.9 %collective-permute-start.29 = (bf16[4,264,2048]{2,1,0:T(8,128)(2,1)}, bf16[4,264,2048]{2,1,0:T(8,128)(2,1)}, u32[]{:S(2)}, u32[]{:S(2)}) collective-permute-start(bf16[4,264,2048]{2,1,0:T(8,128)(2,1)} %bitcast.253), channel_id=1, source_target_pairs={{0,1},{1,0},{2,3},{3,2},{4,5},{5,4},{6,7},{7,6},{8,9},{9,8},{10,11... | collective-permute-start | bytes 12976136 | tf_op jit(solution)/shard_map/ppermute | solution.py:307
  459.8 14.4 %collective-permute-start.26 = (bf16[128,2048]{1,0:T(8,128)(2,1)S(1)}, bf16[128,2048]{1,0:T(8,128)(2,1)S(1)}, u32[]{:S(2)}, u32[]{:S(2)}) collective-permute-start(bf16[128,2048]{1,0:T(8,128)(2,1)S(1)} %slice.322), channel_id=1, source_target_pairs={{0,2},{1,3},{2,0},{3,1},{4,6},{5,7},{6,4},{7,5},{8,10},{9,11},{10,... | collective-permute-start | bytes 1572872 | tf_op jit(solution)/shard_map/ppermute | solution.py:307
  460.5 14.8 %collective-permute-start.27 = (bf16[136,2048]{1,0:T(8,128)(2,1)S(1)}, bf16[136,2048]{1,0:T(8,128)(2,1)S(1)}, u32[]{:S(2)}, u32[]{:S(2)}) collective-permute-start(bf16[136,2048]{1,0:T(8,128)(2,1)S(1)} %slice.323), channel_id=1, source_target_pairs={{0,4},{1,5},{2,6},{3,7},{4,0},{5,1},{6,2},{7,3},{8,12},{9,13},{10,... | collective-permute-start | bytes 1671176 | tf_op jit(solution)/shard_map/ppermute | solution.py:307
  476.2 11.5 %collective-permute-start.28 = (bf16[4,264,2048]{2,1,0:T(8,128)(2,1)}, bf16[4,264,2048]{2,1,0:T(8,128)(2,1)}, u32[]{:S(2)}, u32[]{:S(2)}) collective-permute-start(bf16[4,264,2048]{2,1,0:T(8,128)(2,1)} %bitcast.196), channel_id=1, source_target_pairs={{0,1},{1,0},{2,3},{3,2},{4,5},{5,4},{6,7},{7,6},{8,9},{9,8},{10,11... | collective-permute-start | bytes 12976136 | tf_op jit(solution)/shard_map/ppermute | solution.py:307
  487.7 50.7 %collective-permute-start.30 = (bf16[264,2048]{1,0:T(8,128)(2,1)}, bf16[264,2048]{1,0:T(8,128)(2,1)S(1)}, u32[]{:S(2)}, u32[]{:S(2)}) collective-permute-start(bf16[264,2048]{1,0:T(8,128)(2,1)} %get-tuple-element.153), channel_id=1, source_target_pairs={{0,2},{1,3},{2,0},{3,1},{4,6},{5,7},{6,4},{7,5},{8,10},{9,11},{10,... | collective-permute-start | bytes 3244040 | tf_op jit(solution)/shard_map/ppermute | solution.py:307
  489.0 49.6 %collective-permute-start.31 = (bf16[264,2048]{1,0:T(8,128)(2,1)}, bf16[264,2048]{1,0:T(8,128)(2,1)}, u32[]{:S(2)}, u32[]{:S(2)}) collective-permute-start(bf16[264,2048]{1,0:T(8,128)(2,1)} %get-tuple-element.154), channel_id=1, source_target_pairs={{0,4},{1,5},{2,6},{3,7},{4,0},{5,1},{6,2},{7,3},{8,12},{9,13},{10,... | collective-permute-start | bytes 3244040 | tf_op jit(solution)/shard_map/ppermute | solution.py:307
  489.7 49.0 %collective-permute-start.32 = (bf16[264,2048]{1,0:T(8,128)(2,1)}, bf16[264,2048]{1,0:T(8,128)(2,1)}, u32[]{:S(2)}, u32[]{:S(2)}) collective-permute-start(bf16[264,2048]{1,0:T(8,128)(2,1)} %get-tuple-element.155), channel_id=1, source_target_pairs={{0,6},{1,7},{2,4},{3,5},{4,2},{5,3},{6,0},{7,1},{8,14},{9,15},{10,... | collective-permute-start | bytes 3244040 | tf_op jit(solution)/shard_map/ppermute | solution.py:307
  548.6 16.7 %collective-permute-start.33 = (bf16[4,264,2048]{2,1,0:T(8,128)(2,1)}, bf16[4,264,2048]{2,1,0:T(8,128)(2,1)}, u32[]{:S(2)}, u32[]{:S(2)}) collective-permute-start(bf16[4,264,2048]{2,1,0:T(8,128)(2,1)} %bitcast.56), channel_id=1, source_target_pairs={{0,1},{1,0},{2,3},{3,2},{4,5},{5,4},{6,7},{7,6},{8,9},{9,8},{10,11... | collective-permute-start | bytes 12976136 | tf_op jit(solution)/shard_map/ppermute | solution.py:307
  551.7 51.8 %all-to-all-start.3 = ((bf16[8,64,1536]{2,1,0:T(8,128)(2,1)}), bf16[8,64,1536]{2,1,0:T(8,128)(2,1)}, u32[]{:S(2)}, u32[]{:S(2)}) async-start(bf16[8,64,1536]{2,1,0:T(8,128)(2,1)} %bitcast.235), calls=%async_computation.7 | async-start | bytes 3145728 | tf_op jit(solution)/shard_map/all_to_all | solution.py:882
  556.4 56.8 %reduce-scatter.11.cloned.1.call-start = ((), (), s32[]{:S(2)}) async-start(), calls=%async_computation.13 | async-start | bytes 3276800 | tf_op jit(solution)/shard_map/reduce_scatter | solution.py:874
  557.1 93.3 %reduce-scatter.9.cloned.1.call-start = ((), (), s32[]{:S(2)}) async-start(), calls=%async_computation.12 | async-start | bytes 1945600 | tf_op jit(solution)/shard_map/reduce_scatter | solution.py:874
  578.2 19.1 %collective-permute-start.38 = (bf16[2,80,2432]{2,1,0:T(8,128)(2,1)S(1)}, bf16[2,80,2432]{2,1,0:T(8,128)(2,1)S(1)}, u32[]{:S(2)}, u32[]{:S(2)}) collective-permute-start(bf16[2,80,2432]{2,1,0:T(8,128)(2,1)S(1)} %get-tuple-element.228), channel_id=1, source_target_pairs={{0,1},{1,0},{2,3},{3,2},{4,5},{5,4},{6,7},{7,6},{8,9},{9,8},{10,11... | collective-permute-start | bytes 2334728 | tf_op jit(solution)/shard_map/ppermute | solution.py:307
  579.1 19.7 %collective-permute-start.35 = (bf16[136,2048]{1,0:T(8,128)(2,1)S(1)}, bf16[136,2048]{1,0:T(8,128)(2,1)S(1)}, u32[]{:S(2)}, u32[]{:S(2)}) collective-permute-start(bf16[136,2048]{1,0:T(8,128)(2,1)S(1)} %copy-done.19), channel_id=1, source_target_pairs={{0,2},{1,3},{2,0},{3,1},{4,6},{5,7},{6,4},{7,5},{8,10},{9,11},{10,... | collective-permute-start | bytes 1671176 | tf_op jit(solution)/shard_map/ppermute | solution.py:307
  581.0 13.7 %collective-permute-start.34 = (bf16[128,2048]{1,0:T(8,128)(2,1)S(1)}, bf16[128,2048]{1,0:T(8,128)(2,1)S(1)}, u32[]{:S(2)}, u32[]{:S(2)}) collective-permute-start(bf16[128,2048]{1,0:T(8,128)(2,1)S(1)} %copy-done.20), channel_id=1, source_target_pairs={{0,4},{1,5},{2,6},{3,7},{4,0},{5,1},{6,2},{7,3},{8,12},{9,13},{10,... | collective-permute-start | bytes 1572872 | tf_op jit(solution)/shard_map/ppermute | solution.py:307
  601.5 37.4 %collective-permute-start.36 = (bf16[264,2048]{1,0:T(8,128)(2,1)}, bf16[264,2048]{1,0:T(8,128)(2,1)S(1)}, u32[]{:S(2)}, u32[]{:S(2)}) collective-permute-start(bf16[264,2048]{1,0:T(8,128)(2,1)} %pad_maximum_fusion.4), channel_id=1, source_target_pairs={{0,2},{1,3},{2,0},{3,1},{4,6},{5,7},{6,4},{7,5},{8,10},{9,11},{10,... | collective-permute-start | bytes 3244040 | tf_op jit(solution)/shard_map/ppermute | solution.py:307
  601.9 36.9 %collective-permute-start.37 = (bf16[264,2048]{1,0:T(8,128)(2,1)}, bf16[264,2048]{1,0:T(8,128)(2,1)S(1)}, u32[]{:S(2)}, u32[]{:S(2)}) collective-permute-start(bf16[264,2048]{1,0:T(8,128)(2,1)} %pad_maximum_fusion.5), channel_id=1, source_target_pairs={{0,4},{1,5},{2,6},{3,7},{4,0},{5,1},{6,2},{7,3},{8,12},{9,13},{10,... | collective-permute-start | bytes 3244040 | tf_op jit(solution)/shard_map/ppermute | solution.py:307
  613.2 21.5 %all-to-all-start.2 = ((bf16[8,64,640]{2,1,0:T(8,128)(2,1)}), bf16[8,64,640]{2,1,0:T(8,128)(2,1)}, u32[]{:S(2)}, u32[]{:S(2)}) async-start(bf16[8,64,640]{2,1,0:T(8,128)(2,1)} %bitcast.241), calls=%async_computation.6 | async-start | bytes 1310720 | tf_op jit(solution)/shard_map/all_to_all | solution.py:882
  (45 other events, 468.7 us)
Sparse Core Ops, SparseCore 0:
  13.2 39.5 all-gather.11
  58.2 52.7 all-gather.7
  112.6 62.2 all-gather.13
  177.7 114.4 all-gather.9
  369.3 58.5 reduce-scatter.4
  430.0 110.7 reduce-scatter.6
  560.1 53.0 reduce-scatter.10
  615.5 34.8 reduce-scatter.8

commit v4 on v3

--- a/solution.py
+++ b/solution.py
@@ -840,6 +840,33 @@
     )(info, near, far, out, gate, channels, *parts, conv, lagging, lag_edge)
 
 
+def proj_backward(part_ref, proj_ref, signal_ref, normed_ref):
+    normed_ref[...] = lax.dot_general(
+        part_ref[...], proj_ref[...], (((1,), (1,)), ((), ())), preferred_element_type=jnp.float32
+    ).astype(jnp.bfloat16)
+
+
+def run_proj_backward(part, proj, signal):
+    rows, columns = part.shape
+    steps = max(count for count in (3, 2, 1) if rows % (16 * count) == 0)
+    return pl.pallas_call(
+        proj_backward,
+        grid=(steps,),
+        in_specs=[
+            pl.BlockSpec((rows // steps, columns), lambda step: (step, 0)),
+            pl.BlockSpec(proj.shape, lambda step: (0, 0)),
+            pl.BlockSpec(memory_space=pl.ANY),
+        ],
+        out_specs=pl.BlockSpec((rows // steps, proj.shape[0]), lambda step: (step, 0)),
+        out_shape=jax.ShapeDtypeStruct((rows, proj.shape[0]), jnp.bfloat16),
+        compiler_params=pltpu.CompilerParams(vmem_limit_bytes=VMEM_LIMIT),
+        cost_estimate=pl.CostEstimate(
+            flops=2 * rows * columns * proj.shape[0], bytes_accessed=0, transcendentals=0
+        ),
+        name="proj_backward",
+    )(part, proj, signal)
+
+
 def deal_columns(moves, whole_ref, groups_ref):
     for group, inside, column, width in moves:
         groups_ref[group, :, inside : inside + width] = whole_ref[:, column : column + width]
@@ -904,7 +931,7 @@
     return [slice(part * rows // parts, (part + 1) * rows // parts) for part in range(parts)]
 
 
-def feed_forward(near_ref, far_ref, wide_ref, gate_part_ref, up_part_ref, feed_ref, normed_ref):
+def feed_forward(near_ref, far_ref, wide_ref, feed_grad_ref, feed_ref, grad_ref, normed_ref):
     half = FOLD // 2
 
     def expand(part_ref):
@@ -915,8 +942,9 @@
             activated, slope = gelu_parts(product[:, :half])
             up = product[:, half:]
             feed_ref[span, :] = (activated * up).astype(jnp.bfloat16)
-            gate_part_ref[span, :] = slope * up
-            up_part_ref[span, :] = activated
+            feed_grad = feed_grad_ref[span, :]
+            grad_ref[span, :half] = (feed_grad * up * slope).astype(jnp.bfloat16)
+            grad_ref[span, half:] = (feed_grad * activated).astype(jnp.bfloat16)
 
         @pl.when(pl.program_id(1) == 0)
         def _():
@@ -926,7 +954,7 @@
     pl.when(pl.program_id(0) == 1)(lambda: expand(far_ref))
 
 
-def run_feed_forward(near, far, wide):
+def run_feed_forward(near, far, wide, feed_grad):
     rows, depth = near.shape
     tiles = wide.shape[1] // FOLD
     half = FOLD // 2
@@ -941,13 +969,16 @@
             pl.BlockSpec((rows, depth), whole),
             pl.BlockSpec((rows, depth), whole),
             pl.BlockSpec((depth, FOLD), lambda part, tile: (0, tile)),
+            pl.BlockSpec((rows, half), lambda part, tile: (part, tile)),
         ],
-        out_specs=[pl.BlockSpec((rows, half), lambda part, tile: (part, tile))] * 3
-        + [pl.BlockSpec((rows, depth), lambda part, tile: (part, 0))],
+        out_specs=[
+            pl.BlockSpec((rows, half), lambda part, tile: (part, tile)),
+            pl.BlockSpec((rows, FOLD), lambda part, tile: (part, tile)),
+            pl.BlockSpec((rows, depth), lambda part, tile: (part, 0)),
+        ],
         out_shape=[
-            jax.ShapeDtypeStruct((2 * rows, tiles * half), jnp.float32),
-            jax.ShapeDtypeStruct((2 * rows, tiles * half), jnp.float32),
             jax.ShapeDtypeStruct((2 * rows, tiles * half), jnp.bfloat16),
+            jax.ShapeDtypeStruct((2 * rows, tiles * FOLD), jnp.bfloat16),
             jax.ShapeDtypeStruct((2 * rows, depth), jnp.bfloat16),
         ],
         compiler_params=pltpu.CompilerParams(vmem_limit_bytes=VMEM_LIMIT),
@@ -955,15 +986,12 @@
             flops=4 * rows * depth * tiles * FOLD, bytes_accessed=0, transcendentals=0
         ),
         name="feed_forward",
-    )(near, far, wide)
-
-
-def feed_backward(
-    upstream_ref, planes_ref, gate_part_ref, up_part_ref, grad_ref, narrow_ref
-):
-    half = FOLD // 2
+    )(near, far, wide, feed_grad)
+
+
+def feed_backward(upstream_ref, planes_ref, feed_grad_ref, narrow_ref):
     planes = planes_ref.shape[0]
-    tile_rows = half // planes
+    tile_rows = FOLD // 2 // planes
     tiles = planes_ref.shape[1] // tile_rows
 
     @pl.when(pl.program_id(0) == 0)
@@ -975,27 +1003,18 @@
                     plane, tile * tile_rows : (tile + 1) * tile_rows, :
                 ]
 
-    feed_grad = lax.dot_general(
+    feed_grad_ref[...] = lax.dot_general(
         upstream_ref[...],
         narrow_ref[...],
         (((1,), (1,)), ((), ())),
         preferred_element_type=jnp.float32,
     )
-    for tile in range(tiles):
-        span = slice(tile * half, (tile + 1) * half)
-        part = feed_grad[:, span]
-        grad_ref[:, tile * FOLD : tile * FOLD + half] = (part * gate_part_ref[:, span]).astype(
-            jnp.bfloat16
-        )
-        grad_ref[:, tile * FOLD + half : (tile + 1) * FOLD] = (
-            part * up_part_ref[:, span]
-        ).astype(jnp.bfloat16)
-
-
-def run_feed_backward(upstream, narrow, gate_part, up_part):
+
+
+def run_feed_backward(upstream, narrow):
     rows, depth = upstream.shape
     planes, narrow_rows = narrow.shape[:2]
-    width = gate_part.shape[1]
+    width = planes * narrow_rows
     steps = max(count for count in range(1, 7) if rows % (16 * count) == 0)
     block = rows // steps
 
@@ -1008,15 +1027,13 @@
         in_specs=[
             pl.BlockSpec((block, depth), at_step),
             pl.BlockSpec((planes, narrow_rows, depth), lambda step: (0, 0, 0)),
-            pl.BlockSpec((block, width), at_step),
-            pl.BlockSpec((block, width), at_step),
         ],
         out_specs=[
-            pl.BlockSpec((block, 2 * width), at_step),
+            pl.BlockSpec((block, width), at_step),
             pl.BlockSpec((width, depth), lambda step: (0, 0)),
         ],
         out_shape=[
-            jax.ShapeDtypeStruct((rows, 2 * width), jnp.bfloat16),
+            jax.ShapeDtypeStruct((rows, width), jnp.float32),
             jax.ShapeDtypeStruct((width, depth), jnp.bfloat16),
         ],
         compiler_params=pltpu.CompilerParams(vmem_limit_bytes=VMEM_LIMIT),
@@ -1024,7 +1041,7 @@
             flops=2 * rows * depth * width, bytes_accessed=0, transcendentals=0
         ),
         name="feed_backward",
-    )(upstream, narrow, gate_part, up_part)
+    )(upstream, narrow)
 
 
 def pad_lanes(values, lanes):
@@ -1189,28 +1206,12 @@
     two_near = gather_chips(normed_two)
     two_far = swap_with(two_near, CORE)
     upstream_all = jnp.concatenate([upstream_near, upstream_far]).reshape(-1, depth)
-    two_far, upstream_all = lax.optimization_barrier((two_far, upstream_all))
-    gate_part, up_part, feed, two_all = run_feed_forward(
-        two_near.reshape(-1, depth), two_far.reshape(-1, depth), wide
+    feed_grad, narrow = run_feed_backward(upstream_all, narrow)
+    feed, expanded_grad, two_all = run_feed_forward(
+        two_near.reshape(-1, depth), two_far.reshape(-1, depth), wide, feed_grad
     )
     half_rows = two_all.shape[0] // 2
 
-    feed_grad, narrow = run_feed_backward(
-        upstream_all,
-        narrow,
-        gate_part,
-        up_part,
-    )
-    part_far = contract_last(feed_grad[half_rows:], wide).astype(jnp.bfloat16)
-    part_near = contract_last(feed_grad[:half_rows], wide).astype(jnp.bfloat16)
-    finish, two_all, feed, upstream_all = reduce_plane_at_once(
-        part_near.reshape(-1, rows, depth),
-        part_far.reshape(-1, rows, depth),
-        two_all,
-        feed,
-        upstream_all,
-    )
-    normed_two_grad = finish()
     down_part = contract_first(feed, upstream_all).astype(jnp.bfloat16)
     down_part = (
         down_part.reshape(tiles, planes, tile_rows, depth)
@@ -1218,14 +1219,18 @@
         .reshape(hidden_width, depth)
     )
     down_grad = sum_planes(down_part).astype(jnp.float32)
-
+    part_far = contract_last(expanded_grad[half_rows:], wide).astype(jnp.bfloat16)
+    part_near = contract_last(expanded_grad[:half_rows], wide).astype(jnp.bfloat16)
+    normed_two_grad, two_all, feed = reduce_plane(
+        part_near.reshape(-1, rows, depth), part_far.reshape(-1, rows, depth), two_all, feed
+    )
     def norm_back(values, scale, gain, grad):
         scaled = grad * gain
         lean = jnp.mean(scaled * values, axis=1, keepdims=True)
         return scale * scaled - scale * scale * scale * lean * values
 
     residual_grad = upstream + norm_back(residual, scale_two, gain_two, normed_two_grad)
-    wide_part = contract_first(two_all, feed_grad).astype(jnp.bfloat16)
+    wide_part = contract_first(two_all, expanded_grad).astype(jnp.bfloat16)
     residual_grad, wide_part, down_part = lax.optimization_barrier(
         (residual_grad, wide_part, down_part)
     )
@@ -1239,7 +1244,11 @@
     low_near, output_near, output_far, down_grad = gather_chips(
         residual_grad.astype(jnp.bfloat16), output_near, output_far, down_grad
     )
-    output_sums = output_near.astype(jnp.float32) + swap_with(output_far, CORE).astype(jnp.float32)
+    output_other = swap_with(output_far, CORE)
+    output_sums = [
+        output_near[place].astype(jnp.float32) + output_other[place].astype(jnp.float32)
+        for place in range(4)
+    ]
     low_far = swap_with(low_near, CORE)
     low_far, *output_low = lax.optimization_barrier(
         (low_far, *(output_sums[place].astype(jnp.bfloat16) for place in (1, 2, 3)))
@@ -1251,20 +1260,20 @@
     proj_grad_near, proj_grad_far = proj_grad[: count // 2], proj_grad[count // 2 :]
 
     def through_proj(part):
-        part = contract_last(part.reshape(-1, 2 * channels), proj).astype(jnp.bfloat16)
+        part = run_proj_backward(part.reshape(-1, 2 * channels), proj, signal)
         return part.reshape(-1, rows, depth)
 
     proj_part = contract_halves(normed_near, normed_far, proj_grad_near, proj_grad_far)
-    proj_grad_far, proj_grad_near, proj_part, wide_summed, *output_parts = (
-        lax.optimization_barrier(
-            (proj_grad_far, proj_grad_near, proj_part, wide_summed, *output_parts)
-        )
-    )
+    proj_grad_far, proj_grad_near, proj_part, wide_summed = lax.optimization_barrier(
+        (proj_grad_far, proj_grad_near, proj_part, wide_summed)
+    )
+    signal = swap_with(proj_part[:16, :128], CORE)
+    part_far = through_proj(proj_grad_far)
+    part_far, *output_parts = lax.optimization_barrier((part_far, *output_parts))
     mixed = residual + output_sums[0]
     for part in output_parts:
         mixed = mixed + part.astype(jnp.float32)
     mixed = (keep * mixed).astype(jnp.bfloat16)
-    part_far = through_proj(proj_grad_far)
     proj_summed = sum_planes(proj_part)
     part_near = through_proj(proj_grad_near)
     normed_grad, gated, mixed = reduce_plane(part_near, part_far, gated, mixed)

time: 669 us -> 646 us (0.966)
  waiting for transfers between devices: 206 us -> 183 us
  Pallas kernels: 120 us -> 133 us
  matrix products: 97.9 us -> 86.2 us
    pallas_call x0 -> x2, Pallas kernels: none -> 14.2 us  [run_proj_backward(): pl.pallas_call(proj_backward, grid=(steps,), in_specs=[pl.BlockSpec((rows...]
    ppermute x39 -> x41, waiting for transfers between devices: 162 us -> 148 us  [swap_with(): return lax.ppermute(block, 'seq', route)]
    reduce_scatter x4, waiting for transfers between devices: 16.5 us -> 5.28 us  [sum_planes(): lax.psum_scatter(grad.astype(jnp.bfloat16), 'bucket', scatter_dimension=0...]
    dot_general x4 -> x2, matrix products: 32.3 us -> 21.8 us  [contract_last(): lax.dot_general(left, right, (((1,), (1,)), ((), ())), preferred_element_...]
    all_to_all x2, waiting for transfers between devices: 10.6 us -> 20.4 us  [spread_rows(): lax.all_to_all(blocks, 'seq', split_axis=0, concat_axis=0, tiled=True)]
    add x1 -> x0, other arithmetic: 8.28 us -> none  [by_channels(): output_near.astype(jnp.float32)]
    all_gather x1, waiting for transfers between devices: 8.13 us -> 0.01 us  [by_channels(): wide = lax.all_gather(wide_dealt, 'bucket', axis=0, tiled=True)]
    ppermute x39 -> x41, starting transfers between devices: 36.9 us -> 37.7 us  [swap_with(): return lax.ppermute(block, 'seq', route)]
  transfers between devices with their start and end apart: 51 -> 53, of which waited for: 27 -> 25; matrix products, arithmetic and copies ran while one was open for 30% -> 33% of each run, Pallas kernels for 12% -> 17%
where the time goes in v4:
time: 646 us; the launch traced here: 640 us
  waiting for transfers between devices  183 us (28%)
  Pallas kernels  133 us (21%)
  other arithmetic  98.7 us (15%)
  matrix products  86.2 us (13%)
  starting transfers between devices  54.2 us (8%)
  local copies, waits for them, and re-layouts  49.7 us (8%)
  blocking collectives  19.4 us (3%)
  between operations  15.3 us (2%)
    ppermute x41, waiting for transfers between devices, swap_with(): return lax.ppermute(block, 'seq', route)  148 us
    dot_general x6, matrix products, contract_first(): lax.dot_general(left, right, (((0,), (0,)), ((), ())), preferred_element_...  44.7 us
    ppermute x41, starting transfers between devices, swap_with(): return lax.ppermute(block, 'seq', route)  37.7 us
    pallas_call x1, Pallas kernels, run_forward(): pl.pallas_call(partial(mixer_forward, taps, slots), grid_spec=pltpu.Prefe...  33.7 us
    pallas_call x1, Pallas kernels, run_backward(): pl.pallas_call(partial(mixer_backward, taps, slots), grid_spec=pltpu.Pref...  32 us
    pallas_call x1, Pallas kernels, run_feed_forward(): pl.pallas_call(feed_forward, grid=(2, tiles), in_specs=[pl.BlockSpec((row...  27.6 us
    dot_general x2, matrix products, contract_last(): lax.dot_general(left, right, (((1,), (1,)), ((), ())), preferred_element_...  21.8 us
    all_to_all x2, waiting for transfers between devices, spread_rows(): lax.all_to_all(blocks, 'seq', split_axis=0, concat_axis=0, tiled=True)  20.4 us
  transfers between devices with their start and end apart: 53, of which 25 were waited for; matrix products, arithmetic and copies ran while one was open for 33% of the time, Pallas kernels for 17%

profile of v4, /device:TPU:0, one launch (start us, length us, event | category | flops | bytes accessed | tf_op | source)
XLA Modules:
  0.0 639.6 jit_solution(9655272662342823109)
XLA Ops:
  19.8 3.5 all-to-all-start
  23.5 17.4 %collective-permute-done = bf16[264,2048]{1,0:T(8,128)(2,1)S(1)} collective-permute-done((bf16[264,2048]{1,0:T(8,128)(2,1)S(1)}, bf16[264,2048]{1,0:T(8,128)(2,1)S(1)}, u32[]{:S(2)}, u32[]{:S(2)}) %collective-permute-start) | collective-permute-done | bytes 1081376 | tf_op jit(solution)/shard_map/ppermute | solution.py:307
  43.9 8.9 %all-gather.12.cloned.1.call-done = bf16[320,2432]{1,0:T(8,128)(2,1)} async-done(((bf16[80,2432]{1,0:T(8,128)(2,1)}), bf16[320,2432]{1,0:T(8,128)(2,1)}) %all-gather.12.cloned.1.call-update) | async-done | bytes 1556496 | tf_op jit(solution)/shard_map/all_gather | solution.py:1103
  63.2 4.5 collective-permute-done.2
  72.5 3.4 deal_columns.3
  76.0 3.6 all-to-all-start.1
  85.6 19.4 %all-gather.1 = bf16[2,4,512]{0,2,1:T(8,128)(2,1)S(1)} all-gather(bf16[2,4,64]{0,2,1:T(8,128)(2,1)S(1)} %slice_bitcast_fusion.6), channel_id=3, replica_groups=mesh['bucket'=4,'seq'=8] {'seq'}, dimensions={2}, use_global_device_ids=true | all-gather | bytes 9216 | tf_op jit(solution)/shard_map/all_gather | solution.py:1134
  106.3 3.5 multiply_reduce_fusion
  115.0 6.8 %fusion.2 = (bf16[4,264,2048]{2,1,0:T(8,128)(2,1)}, bf16[4,264,2048]{2,1,0:T(8,128)(2,1)}) fusion(bf16[4,264,2048]{2,1,0:T(8,128)(2,1)} %collective-permute-done.4, f32[4,264]{1,0:T(4,128)S(1)} %add_rsqrt_fusion.1, f32[2048]{0:T(1024)S(1)} %bitcast.243, f32[4,264]{1,0:T(4,128)S(1)} %rsqrt.42, bf16[4,264,2048]{2,1,0:T(8,128)(2,1)} %bitcast.198), kind=kLoop, calls=%fused_computation.4 | loop fusion | flops 17301504 | bytes 17318144 | tf_op jit(solution)/shard_map/convert_element_type | solution.py:1179
  128.3 33.7 %mixer_forward.1 = (bf16[8,264,384]{2,1,0:T(8,128)(2,1)}, bf16[8,264,384]{2,1,0:T(8,128)(2,1)}, bf16[8,264,384]{2,1,0:T(8,128)(2,1)}, f32[8,264,384]{2,1,0:T(8,1...) custom-call(s32[5]{0:T(128)} %pad_add_fusion.info_ref, ...), custom_call_target="tpu_custom_call" | custom-call | tf_op jit(solution)/shard_map/mixer_forward/pallas_call | solution.py:743
  162.1 9.5 %collective-permute-done.7 = bf16[264,2048]{1,0:T(8,128)(2,1)} collective-permute-done((bf16[264,2048]{1,0:T(8,128)(2,1)}, bf16[264,2048]{1,0:T(8,128)(2,1)}, u32[]{:S(2)}, u32[]{:S(2)}) %collective-permute-start.7) | collective-permute-done | bytes 1081376 | tf_op jit(solution)/shard_map/ppermute | solution.py:307
  173.1 4.4 convolution_convert_fusion.3
  177.8 3.9 pad_maximum_fusion.1
  192.3 11.0 %collective-permute-done.10 = bf16[128,2048]{1,0:T(8,128)(2,1)S(1)} collective-permute-done((bf16[128,2048]{1,0:T(8,128)(2,1)S(1)}, bf16[128,2048]{1,0:T(8,128)(2,1)S(1)}, u32[]{:S(2)}, u32[]{:S(2)}) %collective-permute-start.10) | collective-permute-done | bytes 524320 | tf_op jit(solution)/shard_map/ppermute | solution.py:307
  208.1 22.9 %collective-permute-done.12 = bf16[264,2048]{1,0:T(8,128)(2,1)S(1)} collective-permute-done((bf16[264,2048]{1,0:T(8,128)(2,1)S(1)}, bf16[264,2048]{1,0:T(8,128)(2,1)S(1)}, u32[]{:S(2)}, u32[]{:S(2)}) %collective-permute-start.12) | collective-permute-done | bytes 1081376 | tf_op jit(solution)/shard_map/ppermute | solution.py:307
  237.1 21.8 %collective-permute-done.15 = bf16[264,2048]{1,0:T(8,128)(2,1)S(1)} collective-permute-done((bf16[264,2048]{1,0:T(8,128)(2,1)S(1)}, bf16[264,2048]{1,0:T(8,128)(2,1)S(1)}, u32[]{:S(2)}, u32[]{:S(2)}) %collective-permute-start.15) | collective-permute-done | bytes 1081376 | tf_op jit(solution)/shard_map/ppermute | solution.py:307
  263.5 7.9 %collective-permute-done.16 = bf16[128,2048]{1,0:T(8,128)(2,1)S(1)} collective-permute-done((bf16[128,2048]{1,0:T(8,128)(2,1)S(1)}, bf16[128,2048]{1,0:T(8,128)(2,1)S(1)}, u32[]{:S(2)}, u32[]{:S(2)}) %collective-permute-start.16) | collective-permute-done | bytes 524320 | tf_op jit(solution)/shard_map/ppermute | solution.py:307
  273.0 7.7 %pad_maximum_fusion = bf16[8,264,2048]{2,1,0:T(8,128)(2,1)} fusion(bf16[4,264,2048]{2,1,0:T(8,128)(2,1)} %collective-permute-done.19, bf16[4,264,2048]{2,1,0:T(8,128)(2,1)} %pad_maximum_fusion.1), kind=kLoop, calls=%fused_computation.5 | loop fusion | flops 4325376 | bytes 17301504 | tf_op jit(solution)/shard_map/concatenate | solution.py:1208
  280.7 12.6 %feed_backward.1 = (f32[2112,768]{1,0:T(8,128)}, bf16[768,2048]{1,0:T(8,128)(2,1)}) custom-call(bf16[2112,2048]{1,0:T(8,128)(2,1)} %bitcast.206, bf16[4,192,2048]{2,1,0:T(8,128)(2,1)} %bitcast.256), custom_call_target="tpu_custom_call" | custom-call | flops 6643777536 | tf_op jit(solution)/shard_map/feed_backward/pallas_call | solution.py:1024
  293.3 27.6 %feed_forward.1 = (bf16[2112,768]{1,0:T(8,128)(2,1)}, bf16[2112,1536]{1,0:T(8,128)(2,1)}, bf16[2112,2048]{1,0:T(8,128)(2,1)}) custom-call(bf16[1056,2048]{1,0:T(8,128)(2,1)} %constant_dynamic-update-slice_fusion.5.near_ref, bf16[1056,2048]{1,0:T(8,128)(2,1)} %bitcast.36.far_ref, bf16[2048,1536]{1,0:T(8,128)(2,1)} %all-gather.10.cloned.1.call-done.wide_ref, ...), custom_call_target="tpu_custom_call" | custom-call | flops 13287555072 | tf_op jit(solution)/shard_map/feed_forward/pallas_call | solution.py:965
  320.9 11.6 %convolution_convert_fusion.5 = bf16[1056,2048]{1,0:T(8,128)(2,1)} fusion(bf16[2048,1536]{1,0:T(8,128)(2,1)} %all-gather.10.cloned.1.call-done.wide_ref, bf16[2112,1536]{1,0:T(8,128)(2,1)} %get-tuple-element.113), kind=kOutput, calls=%fused_computation.13 | convolution fusion | flops 6645940224 | bytes 13860864 | tf_op jit(solution)/shard_map/dot_general | solution.py:68
  333.0 7.8 %convolution_convert_fusion.7 = bf16[768,2048]{1,0:T(8,128)(2,1)S(1)} fusion(bf16[2112,768]{1,0:T(8,128)(2,1)S(1)} %copy-done.27, bf16[2112,2048]{1,0:T(8,128)(2,1)S(1)} %bitcast.209), kind=kOutput, calls=%fused_computation.22 | convolution fusion | flops 6645350400 | bytes 15040512 | tf_op jit(solution)/shard_map/dot_general | solution.py:74
  342.8 10.2 %convolution_convert_fusion.6 = bf16[1056,2048]{1,0:T(8,128)(2,1)S(1)} fusion(bf16[2048,1536]{1,0:T(8,128)(2,1)} %all-gather.10.cloned.1.call-done.wide_ref, bf16[2112,1536]{1,0:T(8,128)(2,1)} %get-tuple-element.113), kind=kOutput, calls=%fused_computation.14 | convolution fusion | flops 6645940224 | bytes 13860864 | tf_op jit(solution)/shard_map/dot_general | solution.py:68
  360.1 9.8 %collective-permute-done.21 = bf16[128,2048]{1,0:T(8,128)(2,1)S(1)} collective-permute-done((bf16[128,2048]{1,0:T(8,128)(2,1)S(1)}, bf16[128,2048]{1,0:T(8,128)(2,1)S(1)}, u32[]{:S(2)}, u32[]{:S(2)}) %collective-permute-start.21) | collective-permute-done | bytes 524320 | tf_op jit(solution)/shard_map/ppermute | solution.py:307
  376.8 18.7 %convolution_convert_fusion = bf16[2048,1536]{1,0:T(8,128)(2,1)} fusion(bf16[2112,2048]{1,0:T(8,128)(2,1)} %get-tuple-element.119, bf16[2112,1536]{1,0:T(8,128)(2,1)S(1)} %bitcast.262), kind=kOutput, calls=%fused_computation.8 | convolution fusion | flops 13290700800 | bytes 21430272 | tf_op jit(solution)/shard_map/dot_general | solution.py:74
  395.5 4.2 collective-permute-done.23
  403.6 4.3 fusion.22
  408.0 3.5 constant_dynamic-update-slice_fusion.14
  413.5 7.7 %convolution_convert_fusion.1 = bf16[1056,2048]{1,0:T(8,128)(2,1)} fusion(bf16[768,2048]{1,0:T(8,128)(2,1)} %get-tuple-element.122, bf16[2112,768]{1,0:T(8,128)(2,1)S(1)} %copy-done.28), kind=kOutput, calls=%fused_computation.9 | convolution fusion | flops 3324051456 | bytes 9093120 | tf_op jit(solution)/shard_map/dot_general | solution.py:1239
  421.2 5.1 convolution_convert_fusion.2
  428.8 6.5 %collective-permute-done.25 = bf16[264,2048]{1,0:T(8,128)(2,1)S(1)} collective-permute-done((bf16[264,2048]{1,0:T(8,128)(2,1)}, bf16[264,2048]{1,0:T(8,128)(2,1)S(1)}, u32[]{:S(2)}, u32[]{:S(2)}) %collective-permute-start.25) | collective-permute-done | bytes 1081376 | tf_op jit(solution)/shard_map/ppermute | solution.py:307
  442.5 4.8 collective-permute-done.27
  448.1 5.2 collective-permute-done.28
  465.4 32.0 %mixer_backward.1 = (bf16[8,264,640]{2,1,0:T(8,128)(2,1)}, f32[384,768]{1,0:T(8,128)}, f32[8,384]{1,0:T(8,128)}) custom-call(s32[5]{0:T(128)} %pad_add_fusion.info_ref, bf16[4,264,2048]{2,1,0:T(8,128)(2,1)} %bitcast.194, bf16[4,264,2048]{2,1,0:T(8,128)(2,1)} %collective-permute-done.29.far_ref, bf16[384,2048]{1,0:T(8,128)(2,1)} %pad.51.out_ref, ...), custom_call_target="tpu_custom_call" | custom-call | tf_op jit(solution)/shard_map/mixer_backward/pallas_call | solution.py:799
  497.4 3.6 fusion.70
  501.1 5.8 fusion.67
  507.0 5.6 fusion.3
  512.6 5.3 reduce-scatter.7.cloned.1.call-done
  520.3 7.0 %proj_backward.3 = bf16[1056,2048]{1,0:T(8,128)(2,1)} custom-call(bf16[1056,640]{1,0:T(8,128)(2,1)} %bitcast.238, bf16[2048,640]{1,0:T(8,128)(2,1)} %all-gather.8.cloned.1.call-done.proj_ref, bf16[16,128]{1,0:T(8,128)(2,1)} %copy-done.23), custom_call_target="tpu_custom_call" | custom-call | flops 2768240640 | tf_op jit(solution)/shard_map/proj_backward/pallas_call | solution.py:852
  530.7 4.3 all-to-all-start.3
  535.1 4.7 fusion.28
  539.7 7.2 %proj_backward.2 = bf16[1056,2048]{1,0:T(8,128)(2,1)} custom-call(bf16[1056,640]{1,0:T(8,128)(2,1)} %bitcast.237, bf16[2048,640]{1,0:T(8,128)(2,1)} %all-gather.8.cloned.1.call-done.proj_ref, bf16[16,128]{1,0:T(8,128)(2,1)} %copy-done.23), custom_call_target="tpu_custom_call" | custom-call | flops 2768240640 | tf_op jit(solution)/shard_map/proj_backward/pallas_call | solution.py:852
  553.1 4.5 convolution_bitcast_fusion
  566.3 9.4 %collective-permute-done.36 = bf16[128,2048]{1,0:T(8,128)(2,1)S(1)} collective-permute-done((bf16[128,2048]{1,0:T(8,128)(2,1)S(1)}, bf16[128,2048]{1,0:T(8,128)(2,1)S(1)}, u32[]{:S(2)}, u32[]{:S(2)}) %collective-permute-start.36) | collective-permute-done | bytes 524320 | tf_op jit(solution)/shard_map/ppermute | solution.py:307
  584.5 4.3 all-to-all-start.2
  588.9 4.9 collect_columns.3
  595.3 20.4 %all-to-all-done.2.groups_ref = bf16[8,64,640]{2,1,0:T(8,128)(2,1)} async-done(((bf16[8,64,640]{2,1,0:T(8,128)(2,1)}), bf16[8,64,640]{2,1,0:T(8,128)(2,1)}, u32[]{:S(2)}, u32[]{:S(2)}) %all-to-all-start.2) | async-done | bytes 655392 | tf_op jit(solution)/shard_map/all_to_all | solution.py:909
  622.5 4.3 fusion.10
  (307 shorter events, 167.5 us)
Async XLA Ops:
  7.2 45.6 %all-gather.12.cloned.1.call-start = ((), (), s32[]{:S(2)}) async-start(), calls=%async_computation.14 | async-start | bytes 1945600 | tf_op jit(solution)/shard_map/all_gather | solution.py:1103
  13.1 27.7 %collective-permute-start = (bf16[264,2048]{1,0:T(8,128)(2,1)S(1)}, bf16[264,2048]{1,0:T(8,128)(2,1)S(1)}, u32[]{:S(2)}, u32[]{:S(2)}) collective-permute-start(bf16[264,2048]{1,0:T(8,128)(2,1)S(1)} %bitcast.203), channel_id=1, source_target_pairs={{0,2},{1,3},{2,0},{3,1},{4,6},{5,7},{6,4},{7,5},{8,10},{9,11},{10,... | collective-permute-start | bytes 3244040 | tf_op jit(solution)/shard_map/ppermute | solution.py:307
  16.1 27.8 %collective-permute-start.1 = (bf16[264,2048]{1,0:T(8,128)(2,1)S(1)}, bf16[264,2048]{1,0:T(8,128)(2,1)}, u32[]{:S(2)}, u32[]{:S(2)}) collective-permute-start(bf16[264,2048]{1,0:T(8,128)(2,1)S(1)} %bitcast.204), channel_id=1, source_target_pairs={{0,4},{1,5},{2,6},{3,7},{4,0},{5,1},{6,2},{7,3},{8,12},{9,13},{10,... | collective-permute-start | bytes 3244040 | tf_op jit(solution)/shard_map/ppermute | solution.py:307
  19.8 37.4 %all-to-all-start = ((bf16[8,64,640]{2,1,0:T(8,128)(2,1)}), bf16[8,64,640]{2,1,0:T(8,128)(2,1)S(1)}, u32[]{:S(2)}, u32[]{:S(2)}) async-start(bf16[8,64,640]{2,1,0:T(8,128)(2,1)} %deal_columns.2), calls=%async_computation | async-start | bytes 1310720 | tf_op jit(solution)/shard_map/all_to_all | solution.py:896
  23.4 104.9 %all-gather.8.cloned.1.call-start = ((), (), s32[]{:S(2)}) async-start(), calls=%async_computation.8 | async-start | bytes 3276800 | tf_op jit(solution)/shard_map/all_gather | solution.py:1138
  54.7 13.1 %collective-permute-start.2 = (bf16[128,2048]{1,0:T(8,128)(2,1)}, bf16[128,2048]{1,0:T(8,128)(2,1)S(1)}, u32[]{:S(2)}, u32[]{:S(2)}) collective-permute-start(bf16[128,2048]{1,0:T(8,128)(2,1)} %slice.309), channel_id=1, source_target_pairs={{0,2},{1,3},{2,0},{3,1},{4,6},{5,7},{6,4},{7,5},{8,10},{9,11},{10,... | collective-permute-start | bytes 1572872 | tf_op jit(solution)/shard_map/ppermute | solution.py:307
  58.1 13.3 %collective-permute-start.3 = (bf16[136,2048]{1,0:T(8,128)(2,1)S(1)}, bf16[136,2048]{1,0:T(8,128)(2,1)S(1)}, u32[]{:S(2)}, u32[]{:S(2)}) collective-permute-start(bf16[136,2048]{1,0:T(8,128)(2,1)S(1)} %slice.310), channel_id=1, source_target_pairs={{0,4},{1,5},{2,6},{3,7},{4,0},{5,1},{6,2},{7,3},{8,12},{9,13},{10,... | collective-permute-start | bytes 1671176 | tf_op jit(solution)/shard_map/ppermute | solution.py:307
  72.3 39.4 %collective-permute-start.4 = (bf16[4,264,2048]{2,1,0:T(8,128)(2,1)}, bf16[4,264,2048]{2,1,0:T(8,128)(2,1)}, u32[]{:S(2)}, u32[]{:S(2)}) collective-permute-start(bf16[4,264,2048]{2,1,0:T(8,128)(2,1)} %bitcast.197), channel_id=1, source_target_pairs={{0,1},{1,0},{2,3},{3,2},{4,5},{5,4},{6,7},{7,6},{8,9},{9,8},{10,11... | collective-permute-start | bytes 12976136 | tf_op jit(solution)/shard_map/ppermute | solution.py:307
  76.0 30.1 %all-to-all-start.1 = ((bf16[8,64,1536]{2,1,0:T(8,128)(2,1)}), bf16[8,64,1536]{2,1,0:T(8,128)(2,1)S(1)}, u32[]{:S(2)}, u32[]{:S(2)}) async-start(bf16[8,64,1536]{2,1,0:T(8,128)(2,1)} %deal_columns.3), calls=%async_computation.1 | async-start | bytes 3145728 | tf_op jit(solution)/shard_map/all_to_all | solution.py:896
  79.5 126.5 %all-gather.14.cloned.1.call-start = ((), (), s32[]{:S(2)}) async-start(), calls=%async_computation.15 | async-start | bytes 3932160 | tf_op jit(solution)/shard_map/all_gather | solution.py:1187
  85.0 24.8 %collective-permute-start.5 = (bf16[2,80,2432]{2,1,0:T(8,128)(2,1)}, bf16[2,80,2432]{2,1,0:T(8,128)(2,1)}, u32[]{:S(2)}, u32[]{:S(2)}) collective-permute-start(bf16[2,80,2432]{2,1,0:T(8,128)(2,1)} %get-tuple-element.217), channel_id=1, source_target_pairs={{0,1},{1,0},{2,3},{3,2},{4,5},{5,4},{6,7},{7,6},{8,9},{9,8},{10,11... | collective-permute-start | bytes 2334728 | tf_op jit(solution)/shard_map/ppermute | solution.py:307
  106.1 187.2 %all-gather.10.cloned.1.call-start = ((), (), s32[]{:S(2)}) async-start(), calls=%async_computation.9 | async-start | bytes 7864320 | tf_op jit(solution)/shard_map/all_gather | solution.py:1188
  121.8 40.2 %collective-permute-start.6 = (bf16[264,2048]{1,0:T(8,128)(2,1)}, bf16[264,2048]{1,0:T(8,128)(2,1)}, u32[]{:S(2)}, u32[]{:S(2)}) collective-permute-start(bf16[264,2048]{1,0:T(8,128)(2,1)} %fusion.23), channel_id=1, source_target_pairs={{0,2},{1,3},{2,0},{3,1},{4,6},{5,7},{6,4},{7,5},{8,10},{9,11},{10,... | collective-permute-start | bytes 3244040 | tf_op jit(solution)/shard_map/ppermute | solution.py:307
  122.2 49.3 %collective-permute-start.7 = (bf16[264,2048]{1,0:T(8,128)(2,1)}, bf16[264,2048]{1,0:T(8,128)(2,1)}, u32[]{:S(2)}, u32[]{:S(2)}) collective-permute-start(bf16[264,2048]{1,0:T(8,128)(2,1)} %fusion.23), channel_id=1, source_target_pairs={{0,4},{1,5},{2,6},{3,7},{4,0},{5,1},{6,2},{7,3},{8,12},{9,13},{10,... | collective-permute-start | bytes 3244040 | tf_op jit(solution)/shard_map/ppermute | solution.py:307
  123.8 47.8 %collective-permute-start.8 = (bf16[264,2048]{1,0:T(8,128)(2,1)}, bf16[264,2048]{1,0:T(8,128)(2,1)}, u32[]{:S(2)}, u32[]{:S(2)}) collective-permute-start(bf16[264,2048]{1,0:T(8,128)(2,1)} %fusion.23), channel_id=1, source_target_pairs={{0,6},{1,7},{2,4},{3,5},{4,2},{5,3},{6,0},{7,1},{8,14},{9,15},{10,... | collective-permute-start | bytes 3244040 | tf_op jit(solution)/shard_map/ppermute | solution.py:307
  177.6 248.7 %reduce-scatter.5.cloned.1.call-start = ((), (), s32[]{:S(2)}) async-start(), calls=%async_computation.10 | async-start | bytes 3932160 | tf_op jit(solution)/shard_map/reduce_scatter | solution.py:901
  187.8 16.8 %collective-permute-start.11 = (bf16[136,2048]{1,0:T(8,128)(2,1)S(1)}, bf16[136,2048]{1,0:T(8,128)(2,1)S(1)}, u32[]{:S(2)}, u32[]{:S(2)}) collective-permute-start(bf16[136,2048]{1,0:T(8,128)(2,1)S(1)} %slice.422), channel_id=1, source_target_pairs={{0,2},{1,3},{2,0},{3,1},{4,6},{5,7},{6,4},{7,5},{8,10},{9,11},{10,... | collective-permute-start | bytes 1671176 | tf_op jit(solution)/shard_map/ppermute | solution.py:307
  189.5 13.7 %collective-permute-start.10 = (bf16[128,2048]{1,0:T(8,128)(2,1)S(1)}, bf16[128,2048]{1,0:T(8,128)(2,1)S(1)}, u32[]{:S(2)}, u32[]{:S(2)}) collective-permute-start(bf16[128,2048]{1,0:T(8,128)(2,1)S(1)} %slice.415), channel_id=1, source_target_pairs={{0,4},{1,5},{2,6},{3,7},{4,0},{5,1},{6,2},{7,3},{8,12},{9,13},{10,... | collective-permute-start | bytes 1572872 | tf_op jit(solution)/shard_map/ppermute | solution.py:307
  206.0 25.0 %collective-permute-start.12 = (bf16[264,2048]{1,0:T(8,128)(2,1)S(1)}, bf16[264,2048]{1,0:T(8,128)(2,1)S(1)}, u32[]{:S(2)}, u32[]{:S(2)}) collective-permute-start(bf16[264,2048]{1,0:T(8,128)(2,1)S(1)} %pad_maximum_fusion.2), channel_id=1, source_target_pairs={{0,2},{1,3},{2,0},{3,1},{4,6},{5,7},{6,4},{7,5},{8,10},{9,11},{10,... | collective-permute-start | bytes 3244040 | tf_op jit(solution)/shard_map/ppermute | solution.py:307
  206.5 24.6 %collective-permute-start.13 = (bf16[264,2048]{1,0:T(8,128)(2,1)S(1)}, bf16[264,2048]{1,0:T(8,128)(2,1)S(1)}, u32[]{:S(2)}, u32[]{:S(2)}) collective-permute-start(bf16[264,2048]{1,0:T(8,128)(2,1)S(1)} %pad_maximum_fusion.3), channel_id=1, source_target_pairs={{0,4},{1,5},{2,6},{3,7},{4,0},{5,1},{6,2},{7,3},{8,12},{9,13},{10,... | collective-permute-start | bytes 3244040 | tf_op jit(solution)/shard_map/ppermute | solution.py:307
  234.9 24.0 %collective-permute-start.15 = (bf16[264,2048]{1,0:T(8,128)(2,1)S(1)}, bf16[264,2048]{1,0:T(8,128)(2,1)S(1)}, u32[]{:S(2)}, u32[]{:S(2)}) collective-permute-start(bf16[264,2048]{1,0:T(8,128)(2,1)S(1)} %get-tuple-element.200), channel_id=1, source_target_pairs={{0,4},{1,5},{2,6},{3,7},{4,0},{5,1},{6,2},{7,3},{8,12},{9,13},{10,... | collective-permute-start | bytes 3244040 | tf_op jit(solution)/shard_map/ppermute | solution.py:307
  236.5 24.6 %collective-permute-start.14 = (bf16[264,2048]{1,0:T(8,128)(2,1)S(1)}, bf16[264,2048]{1,0:T(8,128)(2,1)S(1)}, u32[]{:S(2)}, u32[]{:S(2)}) collective-permute-start(bf16[264,2048]{1,0:T(8,128)(2,1)S(1)} %get-tuple-element.200), channel_id=1, source_target_pairs={{0,2},{1,3},{2,0},{3,1},{4,6},{5,7},{6,4},{7,5},{8,10},{9,11},{10,... | collective-permute-start | bytes 3244040 | tf_op jit(solution)/shard_map/ppermute | solution.py:307
  237.1 36.0 %collective-permute-start.19 = (bf16[4,264,2048]{2,1,0:T(8,128)(2,1)}, bf16[4,264,2048]{2,1,0:T(8,128)(2,1)}, u32[]{:S(2)}, u32[]{:S(2)}) collective-permute-start(bf16[4,264,2048]{2,1,0:T(8,128)(2,1)} %pad_maximum_fusion.1), channel_id=1, source_target_pairs={{0,1},{1,0},{2,3},{3,2},{4,5},{5,4},{6,7},{7,6},{8,9},{9,8},{10,11... | collective-permute-start | bytes 12976136 | tf_op jit(solution)/shard_map/ppermute | solution.py:307
  258.9 12.4 %collective-permute-start.16 = (bf16[128,2048]{1,0:T(8,128)(2,1)S(1)}, bf16[128,2048]{1,0:T(8,128)(2,1)S(1)}, u32[]{:S(2)}, u32[]{:S(2)}) collective-permute-start(bf16[128,2048]{1,0:T(8,128)(2,1)S(1)} %slice.424), channel_id=1, source_target_pairs={{0,2},{1,3},{2,0},{3,1},{4,6},{5,7},{6,4},{7,5},{8,10},{9,11},{10,... | collective-permute-start | bytes 1572872 | tf_op jit(solution)/shard_map/ppermute | solution.py:307
  273.0 20.3 %collective-permute-start.18 = (bf16[4,264,2048]{2,1,0:T(8,128)(2,1)}, bf16[4,264,2048]{2,1,0:T(8,128)(2,1)}, u32[]{:S(2)}, u32[]{:S(2)}) collective-permute-start(bf16[4,264,2048]{2,1,0:T(8,128)(2,1)} %bitcast.35), channel_id=1, source_target_pairs={{0,1},{1,0},{2,3},{3,2},{4,5},{5,4},{6,7},{7,6},{8,9},{9,8},{10,11... | collective-permute-start | bytes 12976136 | tf_op jit(solution)/shard_map/ppermute | solution.py:307
  332.5 20.6 %collective-permute-start.20 = (bf16[4,264,2048]{2,1,0:T(8,128)(2,1)}, bf16[4,264,2048]{2,1,0:T(8,128)(2,1)}, u32[]{:S(2)}, u32[]{:S(2)}) collective-permute-start(bf16[4,264,2048]{2,1,0:T(8,128)(2,1)} %bitcast.38), channel_id=1, source_target_pairs={{0,1},{1,0},{2,3},{3,2},{4,5},{5,4},{6,7},{7,6},{8,9},{9,8},{10,11... | collective-permute-start | bytes 12976136 | tf_op jit(solution)/shard_map/ppermute | solution.py:307
  342.8 175.1 %reduce-scatter.7.cloned.1.call-start = ((), (), s32[]{:S(2)}) async-start(), calls=%async_computation.11 | async-start | bytes 7864320 | tf_op jit(solution)/shard_map/reduce_scatter | solution.py:901
  355.7 16.7 %collective-permute-start.22 = (bf16[136,2048]{1,0:T(8,128)(2,1)S(1)}, bf16[136,2048]{1,0:T(8,128)(2,1)S(1)}, u32[]{:S(2)}, u32[]{:S(2)}) collective-permute-start(bf16[136,2048]{1,0:T(8,128)(2,1)S(1)} %slice.353), channel_id=1, source_target_pairs={{0,2},{1,3},{2,0},{3,1},{4,6},{5,7},{6,4},{7,5},{8,10},{9,11},{10,... | collective-permute-start | bytes 1671176 | tf_op jit(solution)/shard_map/ppermute | solution.py:307
  356.4 13.6 %collective-permute-start.21 = (bf16[128,2048]{1,0:T(8,128)(2,1)S(1)}, bf16[128,2048]{1,0:T(8,128)(2,1)S(1)}, u32[]{:S(2)}, u32[]{:S(2)}) collective-permute-start(bf16[128,2048]{1,0:T(8,128)(2,1)S(1)} %slice.346), channel_id=1, source_target_pairs={{0,4},{1,5},{2,6},{3,7},{4,0},{5,1},{6,2},{7,3},{8,12},{9,13},{10,... | collective-permute-start | bytes 1572872 | tf_op jit(solution)/shard_map/ppermute | solution.py:307
  374.8 24.9 %collective-permute-start.23 = (bf16[264,2048]{1,0:T(8,128)(2,1)}, bf16[264,2048]{1,0:T(8,128)(2,1)S(1)}, u32[]{:S(2)}, u32[]{:S(2)}) collective-permute-start(bf16[264,2048]{1,0:T(8,128)(2,1)} %pad_maximum_fusion.4), channel_id=1, source_target_pairs={{0,2},{1,3},{2,0},{3,1},{4,6},{5,7},{6,4},{7,5},{8,10},{9,11},{10,... | collective-permute-start | bytes 3244040 | tf_op jit(solution)/shard_map/ppermute | solution.py:307
  376.2 24.7 %collective-permute-start.24 = (bf16[264,2048]{1,0:T(8,128)(2,1)}, bf16[264,2048]{1,0:T(8,128)(2,1)}, u32[]{:S(2)}, u32[]{:S(2)}) collective-permute-start(bf16[264,2048]{1,0:T(8,128)(2,1)} %pad_maximum_fusion.5), channel_id=1, source_target_pairs={{0,4},{1,5},{2,6},{3,7},{4,0},{5,1},{6,2},{7,3},{8,12},{9,13},{10,... | collective-permute-start | bytes 3244040 | tf_op jit(solution)/shard_map/ppermute | solution.py:307
  408.0 176.5 %reduce-scatter.11.cloned.1.call-start = ((), (), s32[]{:S(2)}) async-start(), calls=%async_computation.13 | async-start | bytes 3276800 | tf_op jit(solution)/shard_map/reduce_scatter | solution.py:901
  411.5 23.7 %collective-permute-start.25 = (bf16[264,2048]{1,0:T(8,128)(2,1)}, bf16[264,2048]{1,0:T(8,128)(2,1)S(1)}, u32[]{:S(2)}, u32[]{:S(2)}) collective-permute-start(bf16[264,2048]{1,0:T(8,128)(2,1)} %get-tuple-element.198), channel_id=1, source_target_pairs={{0,2},{1,3},{2,0},{3,1},{4,6},{5,7},{6,4},{7,5},{8,10},{9,11},{10,... | collective-permute-start | bytes 3244040 | tf_op jit(solution)/shard_map/ppermute | solution.py:307
  412.1 23.6 %collective-permute-start.26 = (bf16[264,2048]{1,0:T(8,128)(2,1)}, bf16[264,2048]{1,0:T(8,128)(2,1)}, u32[]{:S(2)}, u32[]{:S(2)}) collective-permute-start(bf16[264,2048]{1,0:T(8,128)(2,1)} %get-tuple-element.198), channel_id=1, source_target_pairs={{0,4},{1,5},{2,6},{3,7},{4,0},{5,1},{6,2},{7,3},{8,12},{9,13},{10,... | collective-permute-start | bytes 3244040 | tf_op jit(solution)/shard_map/ppermute | solution.py:307
  438.2 17.4 %collective-permute-start.30 = (bf16[4,264,2048]{2,1,0:T(8,128)(2,1)}, bf16[4,264,2048]{2,1,0:T(8,128)(2,1)S(1)}, u32[]{:S(2)}, u32[]{:S(2)}) collective-permute-start(bf16[4,264,2048]{2,1,0:T(8,128)(2,1)} %bitcast.255), channel_id=1, source_target_pairs={{0,1},{1,0},{2,3},{3,2},{4,5},{5,4},{6,7},{7,6},{8,9},{9,8},{10,11... | collective-permute-start | bytes 12976136 | tf_op jit(solution)/shard_map/ppermute | solution.py:307
  438.3 15.1 %collective-permute-start.28 = (bf16[136,2048]{1,0:T(8,128)(2,1)S(1)}, bf16[136,2048]{1,0:T(8,128)(2,1)S(1)}, u32[]{:S(2)}, u32[]{:S(2)}) collective-permute-start(bf16[136,2048]{1,0:T(8,128)(2,1)S(1)} %slice.357), channel_id=1, source_target_pairs={{0,4},{1,5},{2,6},{3,7},{4,0},{5,1},{6,2},{7,3},{8,12},{9,13},{10,... | collective-permute-start | bytes 1671176 | tf_op jit(solution)/shard_map/ppermute | solution.py:307
  461.9 65.4 %collective-permute-start.32 = (bf16[264,2048]{1,0:T(8,128)(2,1)}, bf16[264,2048]{1,0:T(8,128)(2,1)S(1)}, u32[]{:S(2)}, u32[]{:S(2)}) collective-permute-start(bf16[264,2048]{1,0:T(8,128)(2,1)} %get-tuple-element.143), channel_id=1, source_target_pairs={{0,2},{1,3},{2,0},{3,1},{4,6},{5,7},{6,4},{7,5},{8,10},{9,11},{10,... | collective-permute-start | bytes 3244040 | tf_op jit(solution)/shard_map/ppermute | solution.py:307
  462.6 64.8 %collective-permute-start.33 = (bf16[264,2048]{1,0:T(8,128)(2,1)}, bf16[264,2048]{1,0:T(8,128)(2,1)}, u32[]{:S(2)}, u32[]{:S(2)}) collective-permute-start(bf16[264,2048]{1,0:T(8,128)(2,1)} %get-tuple-element.144), channel_id=1, source_target_pairs={{0,4},{1,5},{2,6},{3,7},{4,0},{5,1},{6,2},{7,3},{8,12},{9,13},{10,... | collective-permute-start | bytes 3244040 | tf_op jit(solution)/shard_map/ppermute | solution.py:307
  464.0 63.4 %collective-permute-start.34 = (bf16[264,2048]{1,0:T(8,128)(2,1)}, bf16[264,2048]{1,0:T(8,128)(2,1)}, u32[]{:S(2)}, u32[]{:S(2)}) collective-permute-start(bf16[264,2048]{1,0:T(8,128)(2,1)} %get-tuple-element.145), channel_id=1, source_target_pairs={{0,6},{1,7},{2,4},{3,5},{4,2},{5,3},{6,0},{7,1},{8,14},{9,15},{10,... | collective-permute-start | bytes 3244040 | tf_op jit(solution)/shard_map/ppermute | solution.py:307
  527.4 19.6 %collective-permute-start.35 = (bf16[4,264,2048]{2,1,0:T(8,128)(2,1)}, bf16[4,264,2048]{2,1,0:T(8,128)(2,1)}, u32[]{:S(2)}, u32[]{:S(2)}) collective-permute-start(bf16[4,264,2048]{2,1,0:T(8,128)(2,1)} %bitcast.254), channel_id=1, source_target_pairs={{0,1},{1,0},{2,3},{3,2},{4,5},{5,4},{6,7},{7,6},{8,9},{9,8},{10,11... | collective-permute-start | bytes 12976136 | tf_op jit(solution)/shard_map/ppermute | solution.py:307
  530.7 53.8 %all-to-all-start.3 = ((bf16[8,64,1536]{2,1,0:T(8,128)(2,1)}), bf16[8,64,1536]{2,1,0:T(8,128)(2,1)}, u32[]{:S(2)}, u32[]{:S(2)}) async-start(bf16[8,64,1536]{2,1,0:T(8,128)(2,1)} %bitcast.236), calls=%async_computation.7 | async-start | bytes 3145728 | tf_op jit(solution)/shard_map/all_to_all | solution.py:909
  535.0 91.8 %reduce-scatter.9.cloned.1.call-start = ((), (), s32[]{:S(2)}) async-start(), calls=%async_computation.12 | async-start | bytes 1945600 | tf_op jit(solution)/shard_map/reduce_scatter | solution.py:901
  559.3 19.0 %collective-permute-start.40 = (bf16[2,80,2432]{2,1,0:T(8,128)(2,1)S(1)}, bf16[2,80,2432]{2,1,0:T(8,128)(2,1)S(1)}, u32[]{:S(2)}, u32[]{:S(2)}) collective-permute-start(bf16[2,80,2432]{2,1,0:T(8,128)(2,1)S(1)} %get-tuple-element.211), channel_id=1, source_target_pairs={{0,1},{1,0},{2,3},{3,2},{4,5},{5,4},{6,7},{7,6},{8,9},{9,8},{10,11... | collective-permute-start | bytes 2334728 | tf_op jit(solution)/shard_map/ppermute | solution.py:307
  560.2 19.6 %collective-permute-start.37 = (bf16[136,2048]{1,0:T(8,128)(2,1)S(1)}, bf16[136,2048]{1,0:T(8,128)(2,1)S(1)}, u32[]{:S(2)}, u32[]{:S(2)}) collective-permute-start(bf16[136,2048]{1,0:T(8,128)(2,1)S(1)} %copy-done.16), channel_id=1, source_target_pairs={{0,2},{1,3},{2,0},{3,1},{4,6},{5,7},{6,4},{7,5},{8,10},{9,11},{10,... | collective-permute-start | bytes 1671176 | tf_op jit(solution)/shard_map/ppermute | solution.py:307
  562.1 13.6 %collective-permute-start.36 = (bf16[128,2048]{1,0:T(8,128)(2,1)S(1)}, bf16[128,2048]{1,0:T(8,128)(2,1)S(1)}, u32[]{:S(2)}, u32[]{:S(2)}) collective-permute-start(bf16[128,2048]{1,0:T(8,128)(2,1)S(1)} %copy-done.17), channel_id=1, source_target_pairs={{0,4},{1,5},{2,6},{3,7},{4,0},{5,1},{6,2},{7,3},{8,12},{9,13},{10,... | collective-permute-start | bytes 1572872 | tf_op jit(solution)/shard_map/ppermute | solution.py:307
  582.5 37.2 %collective-permute-start.38 = (bf16[264,2048]{1,0:T(8,128)(2,1)}, bf16[264,2048]{1,0:T(8,128)(2,1)S(1)}, u32[]{:S(2)}, u32[]{:S(2)}) collective-permute-start(bf16[264,2048]{1,0:T(8,128)(2,1)} %pad_maximum_fusion.6), channel_id=1, source_target_pairs={{0,2},{1,3},{2,0},{3,1},{4,6},{5,7},{6,4},{7,5},{8,10},{9,11},{10,... | collective-permute-start | bytes 3244040 | tf_op jit(solution)/shard_map/ppermute | solution.py:307
  582.9 36.8 %collective-permute-start.39 = (bf16[264,2048]{1,0:T(8,128)(2,1)}, bf16[264,2048]{1,0:T(8,128)(2,1)S(1)}, u32[]{:S(2)}, u32[]{:S(2)}) collective-permute-start(bf16[264,2048]{1,0:T(8,128)(2,1)} %pad_maximum_fusion.7), channel_id=1, source_target_pairs={{0,4},{1,5},{2,6},{3,7},{4,0},{5,1},{6,2},{7,3},{8,12},{9,13},{10,... | collective-permute-start | bytes 3244040 | tf_op jit(solution)/shard_map/ppermute | solution.py:307
  584.5 31.1 %all-to-all-start.2 = ((bf16[8,64,640]{2,1,0:T(8,128)(2,1)}), bf16[8,64,640]{2,1,0:T(8,128)(2,1)}, u32[]{:S(2)}, u32[]{:S(2)}) async-start(bf16[8,64,640]{2,1,0:T(8,128)(2,1)} %bitcast.242), calls=%async_computation.6 | async-start | bytes 1310720 | tf_op jit(solution)/shard_map/all_to_all | solution.py:909
  (46 other events, 568.1 us)
Sparse Core Ops, SparseCore 0:
  13.2 39.5 all-gather.11
  58.2 52.7 all-gather.7
  112.6 62.2 all-gather.13
  177.7 114.4 all-gather.9
  342.9 59.2 reduce-scatter.4
  408.1 109.7 reduce-scatter.6
  530.8 52.6 reduce-scatter.10
  585.8 34.8 reduce-scatter.8

commit v5 on v4

--- a/solution.py
+++ b/solution.py
@@ -376,6 +376,14 @@
     return (finish, *others)
 
 
+def split_mixer_rows(joined_ref, out_ref, gate_ref, small_ref):
+    depth, gates = out_ref.shape[1], gate_ref.shape[1]
+    joined = joined_ref[...].astype(jnp.float32)
+    out_ref[...] = joined[:, :depth]
+    gate_ref[...] = joined[:, depth : depth + gates]
+    small_ref[...] = joined[:, depth + gates : depth + gates + small_ref.shape[1]]
+
+
 def place_of(chunk, me, count):
     relative = jnp.bitwise_xor(chunk, me)
     return jnp.bitwise_and(relative, 1), jnp.right_shift(relative, 1)
@@ -573,7 +581,8 @@
     conv_ref,
     lagging_ref,
     lag_edge_ref,
-    projected_ref,
+    projected_near_ref,
+    projected_far_ref,
     gate_grad_ref,
     channel_grad_ref,
     coming,
@@ -703,9 +712,14 @@
         0, tiles // group, unconvolve, (lag_edge_ref[0], empty, (empty,) * taps)
     )
     low = projected[...].astype(jnp.bfloat16)
-    channels = projected_ref.shape[2] // 2
-    projected_ref[0, :, :channels] = low[:, :channels]
-    projected_ref[0, :, channels:] = low[:, lanes : lanes + channels]
+
+    def project_back(projected_ref):
+        channels = projected_ref.shape[2] // 2
+        projected_ref[0, :, :channels] = low[:, :channels]
+        projected_ref[0, :, channels:] = low[:, lanes : lanes + channels]
+
+    pl.when(is_far == 0)(lambda: project_back(projected_near_ref))
+    pl.when(is_far == 1)(lambda: project_back(projected_far_ref))
     for place_in, part in enumerate((*sum_taps, sum_bias, sum_a, sum_i, sum_rate)):
         sums[place_in] += part
 
@@ -811,7 +825,8 @@
             + [narrow] * 9
             + [rim],
             out_specs=[
-                pl.BlockSpec((1, rows, proj_columns), at_place),
+                pl.BlockSpec((1, rows, proj_columns), at_chip),
+                pl.BlockSpec((1, rows, proj_columns), at_chip),
                 pl.BlockSpec((lanes, 2 * lanes), whole),
                 pl.BlockSpec((sums, lanes), whole),
             ],
@@ -828,7 +843,8 @@
             ],
         ),
         out_shape=[
-            jax.ShapeDtypeStruct((count, rows, proj_columns), jnp.bfloat16),
+            jax.ShapeDtypeStruct((chips, rows, proj_columns), jnp.bfloat16),
+            jax.ShapeDtypeStruct((chips, rows, proj_columns), jnp.bfloat16),
             jax.ShapeDtypeStruct((lanes, 2 * lanes), jnp.float32),
             jax.ShapeDtypeStruct((sums, lanes), jnp.float32),
         ],
@@ -861,7 +877,7 @@
         out_shape=jax.ShapeDtypeStruct((rows, proj.shape[0]), jnp.bfloat16),
         compiler_params=pltpu.CompilerParams(vmem_limit_bytes=VMEM_LIMIT),
         cost_estimate=pl.CostEstimate(
-            flops=2 * rows * columns * proj.shape[0], bytes_accessed=0, transcendentals=0
+            flops=0, bytes_accessed=0, transcendentals=0
         ),
         name="proj_backward",
     )(part, proj, signal)
@@ -1254,10 +1270,9 @@
         (low_far, *(output_sums[place].astype(jnp.bfloat16) for place in (1, 2, 3)))
     )
     output_parts = send_to_chips(*output_low)
-    proj_grad, gate_grad, channel_grad = run_backward(
+    proj_grad_near, proj_grad_far, gate_grad, channel_grad = run_backward(
         info, low_near, low_far, out, gate, channel, saved, 2 * channels, taps, slots
     )
-    proj_grad_near, proj_grad_far = proj_grad[: count // 2], proj_grad[count // 2 :]
 
     def through_proj(part):
         part = run_proj_backward(part.reshape(-1, 2 * channels), proj, signal)
@@ -1310,13 +1325,18 @@
     ).reshape(planes * chunk_rows, -1)
     by_row_grad = sum_planes(by_row_grad)
     gate_up_grad, mlp_gain_grad = hand_back(spread_rows(wide_summed), gate_up, mlp_gain, wide_moves)
-    in_proj_grad, norm_gain_grad = hand_back(spread_rows(proj_summed), in_proj, norm_gain, proj_moves)
     token_grad = residual_grad + norm_back(inputs, scale_one, gain_one, normed_grad)
-    token_grad, by_row_grad = lax.optimization_barrier((token_grad, by_row_grad))
+    token_grad, proj_blocks = lax.optimization_barrier((token_grad, spread_rows(proj_summed)))
+    in_proj_grad, norm_gain_grad = hand_back(proj_blocks, in_proj, norm_gain, proj_moves)
     by_row_grad = by_row_grad.astype(jnp.float32)
-    out_proj_grad = by_row_grad[:, :depth]
-    gate_weight_grad = by_row_grad[:, depth : depth + gate_columns]
-    small_grad = by_row_grad[:, depth + gate_columns : by_row_width]
+    out_proj_grad, gate_weight_grad, small_grad = pl.pallas_call(
+        split_mixer_rows,
+        out_shape=[
+            jax.ShapeDtypeStruct((chunk_rows, columns), jnp.float32)
+            for columns in (depth, gate_columns, taps + 4)
+        ],
+        name="split_mixer_rows",
+    )(by_row_grad)
     return (
         mixed[None],
         token_grad[None],

time: 646 us -> 643 us (level)
    all_to_all x2, waiting for transfers between devices: 20.4 us -> 0.01 us  [spread_rows(): lax.all_to_all(blocks, 'seq', split_axis=0, concat_axis=0, tiled=True)]
    ppermute x41, waiting for transfers between devices: 148 us -> 162 us  [swap_with(): return lax.ppermute(block, 'seq', route)]
    unnamed x100 -> x94, local copies, waits for them, and re-layouts: 19.4 us -> 20.8 us
  transfers between devices with their start and end apart: 53 -> 53, of which waited for: 25 -> 27; matrix products, arithmetic and copies ran while one was open for 33% -> 32% of each run, Pallas kernels for 17% -> 17%
where the time goes in v5:
time: 643 us; the launch traced here: 636 us
  waiting for transfers between devices  179 us (28%)
  Pallas kernels  135 us (21%)
  other arithmetic  98.7 us (15%)
  matrix products  87.3 us (14%)
  starting transfers between devices  54.8 us (9%)
  local copies, waits for them, and re-layouts  46 us (7%)
  blocking collectives  19.2 us (3%)
  between operations  15.3 us (2%)
    ppermute x41, waiting for transfers between devices, swap_with(): return lax.ppermute(block, 'seq', route)  162 us
    dot_general x6, matrix products, contract_first(): lax.dot_general(left, right, (((0,), (0,)), ((), ())), preferred_element_...  45.6 us
    ppermute x41, starting transfers between devices, swap_with(): return lax.ppermute(block, 'seq', route)  37.9 us
    pallas_call x1, Pallas kernels, run_forward(): pl.pallas_call(partial(mixer_forward, taps, slots), grid_spec=pltpu.Prefe...  33.7 us
    pallas_call x1, Pallas kernels, run_backward(): pl.pallas_call(partial(mixer_backward, taps, slots), grid_spec=pltpu.Pref...  32.1 us
    pallas_call x1, Pallas kernels, run_feed_forward(): pl.pallas_call(feed_forward, grid=(2, tiles), in_specs=[pl.BlockSpec((row...  27.2 us
    dot_general x2, matrix products, contract_last(): lax.dot_general(left, right, (((1,), (1,)), ((), ())), preferred_element_...  22 us
    unnamed x94, local copies, waits for them, and re-layouts  20.8 us
  transfers between devices with their start and end apart: 53, of which 27 were waited for; matrix products, arithmetic and copies ran while one was open for 32% of the time, Pallas kernels for 17%

profile of v5, /device:TPU:0, one launch (start us, length us, event | category | flops | bytes accessed | tf_op | source)
XLA Modules:
  0.0 635.5 jit_solution(9652960569127550146)
XLA Ops:
  19.8 3.5 all-to-all-start
  23.5 17.4 %collective-permute-done = bf16[264,2048]{1,0:T(8,128)(2,1)S(1)} collective-permute-done((bf16[264,2048]{1,0:T(8,128)(2,1)S(1)}, bf16[264,2048]{1,0:T(8,128)(2,1)S(1)}, u32[]{:S(2)}, u32[]{:S(2)}) %collective-permute-start) | collective-permute-done | bytes 1081376 | tf_op jit(solution)/shard_map/ppermute | solution.py:307
  43.9 8.9 %all-gather.12.cloned.1.call-done = bf16[320,2432]{1,0:T(8,128)(2,1)} async-done(((bf16[80,2432]{1,0:T(8,128)(2,1)}), bf16[320,2432]{1,0:T(8,128)(2,1)}) %all-gather.12.cloned.1.call-update) | async-done | bytes 1556496 | tf_op jit(solution)/shard_map/all_gather | solution.py:1119
  63.2 4.7 collective-permute-done.2
  72.5 3.4 deal_columns.3
  76.0 3.6 all-to-all-start.1
  85.8 19.2 %all-gather.1 = bf16[2,4,512]{0,2,1:T(8,128)(2,1)S(1)} all-gather(bf16[2,4,64]{0,2,1:T(8,128)(2,1)S(1)} %slice_bitcast_fusion.6), channel_id=3, replica_groups=mesh['bucket'=4,'seq'=8] {'seq'}, dimensions={2}, use_global_device_ids=true | all-gather | bytes 9216 | tf_op jit(solution)/shard_map/all_gather | solution.py:1150
  106.6 3.1 multiply_reduce_fusion
  112.4 3.2 fusion
  115.6 7.0 %fusion.2 = (bf16[4,264,2048]{2,1,0:T(8,128)(2,1)}, bf16[4,264,2048]{2,1,0:T(8,128)(2,1)}) fusion(bf16[4,264,2048]{2,1,0:T(8,128)(2,1)} %collective-permute-done.4, f32[4,264]{1,0:T(4,128)S(1)} %add_rsqrt_fusion.1, f32[2048]{0:T(1024)S(1)} %bitcast.246, f32[4,264]{1,0:T(4,128)S(1)} %rsqrt.42, bf16[4,264,2048]{2,1,0:T(8,128)(2,1)} %bitcast.205), kind=kLoop, calls=%fused_computation.4 | loop fusion | flops 17301504 | bytes 17318144 | tf_op jit(solution)/shard_map/convert_element_type | solution.py:1195
  129.1 33.7 %mixer_forward.1 = (bf16[8,264,384]{2,1,0:T(8,128)(2,1)}, bf16[8,264,384]{2,1,0:T(8,128)(2,1)}, bf16[8,264,384]{2,1,0:T(8,128)(2,1)}, f32[8,264,384]{2,1,0:T(8,1...) custom-call(s32[5]{0:T(128)} %pad_add_fusion.info_ref, ...), custom_call_target="tpu_custom_call" | custom-call | tf_op jit(solution)/shard_map/mixer_forward/pallas_call | solution.py:757
  162.8 9.4 %collective-permute-done.7 = bf16[264,2048]{1,0:T(8,128)(2,1)} collective-permute-done((bf16[264,2048]{1,0:T(8,128)(2,1)}, bf16[264,2048]{1,0:T(8,128)(2,1)}, u32[]{:S(2)}, u32[]{:S(2)}) %collective-permute-start.7) | collective-permute-done | bytes 1081376 | tf_op jit(solution)/shard_map/ppermute | solution.py:307
  173.8 4.5 convolution_convert_fusion.3
  178.6 3.9 pad_maximum_fusion.1
  193.0 11.0 %collective-permute-done.10 = bf16[128,2048]{1,0:T(8,128)(2,1)S(1)} collective-permute-done((bf16[128,2048]{1,0:T(8,128)(2,1)S(1)}, bf16[128,2048]{1,0:T(8,128)(2,1)S(1)}, u32[]{:S(2)}, u32[]{:S(2)}) %collective-permute-start.10) | collective-permute-done | bytes 524320 | tf_op jit(solution)/shard_map/ppermute | solution.py:307
  208.7 23.1 %collective-permute-done.12 = bf16[264,2048]{1,0:T(8,128)(2,1)S(1)} collective-permute-done((bf16[264,2048]{1,0:T(8,128)(2,1)S(1)}, bf16[264,2048]{1,0:T(8,128)(2,1)S(1)}, u32[]{:S(2)}, u32[]{:S(2)}) %collective-permute-start.12) | collective-permute-done | bytes 1081376 | tf_op jit(solution)/shard_map/ppermute | solution.py:307
  237.9 21.8 %collective-permute-done.15 = bf16[264,2048]{1,0:T(8,128)(2,1)S(1)} collective-permute-done((bf16[264,2048]{1,0:T(8,128)(2,1)S(1)}, bf16[264,2048]{1,0:T(8,128)(2,1)S(1)}, u32[]{:S(2)}, u32[]{:S(2)}) %collective-permute-start.15) | collective-permute-done | bytes 1081376 | tf_op jit(solution)/shard_map/ppermute | solution.py:307
  264.3 7.7 %collective-permute-done.16 = bf16[128,2048]{1,0:T(8,128)(2,1)S(1)} collective-permute-done((bf16[128,2048]{1,0:T(8,128)(2,1)S(1)}, bf16[128,2048]{1,0:T(8,128)(2,1)S(1)}, u32[]{:S(2)}, u32[]{:S(2)}) %collective-permute-start.16) | collective-permute-done | bytes 524320 | tf_op jit(solution)/shard_map/ppermute | solution.py:307
  273.7 7.7 %pad_maximum_fusion = bf16[8,264,2048]{2,1,0:T(8,128)(2,1)} fusion(bf16[4,264,2048]{2,1,0:T(8,128)(2,1)} %collective-permute-done.19, bf16[4,264,2048]{2,1,0:T(8,128)(2,1)} %pad_maximum_fusion.1), kind=kLoop, calls=%fused_computation.5 | loop fusion | flops 4325376 | bytes 17301504 | tf_op jit(solution)/shard_map/concatenate | solution.py:1224
  281.4 12.5 %feed_backward.1 = (f32[2112,768]{1,0:T(8,128)}, bf16[768,2048]{1,0:T(8,128)(2,1)}) custom-call(bf16[2112,2048]{1,0:T(8,128)(2,1)} %bitcast.211, bf16[4,192,2048]{2,1,0:T(8,128)(2,1)} %bitcast.258), custom_call_target="tpu_custom_call" | custom-call | flops 6643777536 | tf_op jit(solution)/shard_map/feed_backward/pallas_call | solution.py:1040
  294.0 27.2 %feed_forward.1 = (bf16[2112,768]{1,0:T(8,128)(2,1)}, bf16[2112,1536]{1,0:T(8,128)(2,1)}, bf16[2112,2048]{1,0:T(8,128)(2,1)}) custom-call(bf16[1056,2048]{1,0:T(8,128)(2,1)} %constant_dynamic-update-slice_fusion.5.near_ref, bf16[1056,2048]{1,0:T(8,128)(2,1)} %bitcast.36.far_ref, bf16[2048,1536]{1,0:T(8,128)(2,1)} %all-gather.10.cloned.1.call-done.wide_ref, ...), custom_call_target="tpu_custom_call" | custom-call | flops 13287555072 | tf_op jit(solution)/shard_map/feed_forward/pallas_call | solution.py:981
  321.2 11.6 %convolution_convert_fusion.5 = bf16[1056,2048]{1,0:T(8,128)(2,1)} fusion(bf16[2048,1536]{1,0:T(8,128)(2,1)} %all-gather.10.cloned.1.call-done.wide_ref, bf16[2112,1536]{1,0:T(8,128)(2,1)} %get-tuple-element.117), kind=kOutput, calls=%fused_computation.13 | convolution fusion | flops 6645940224 | bytes 13860864 | tf_op jit(solution)/shard_map/dot_general | solution.py:68
  333.3 7.8 %convolution_convert_fusion.7 = bf16[768,2048]{1,0:T(8,128)(2,1)S(1)} fusion(bf16[2112,768]{1,0:T(8,128)(2,1)S(1)} %copy-done.26, bf16[2112,2048]{1,0:T(8,128)(2,1)S(1)} %bitcast.214), kind=kOutput, calls=%fused_computation.22 | convolution fusion | flops 6645350400 | bytes 15040512 | tf_op jit(solution)/shard_map/dot_general | solution.py:74
  343.1 10.5 %convolution_convert_fusion.6 = bf16[1056,2048]{1,0:T(8,128)(2,1)S(1)} fusion(bf16[2048,1536]{1,0:T(8,128)(2,1)} %all-gather.10.cloned.1.call-done.wide_ref, bf16[2112,1536]{1,0:T(8,128)(2,1)} %get-tuple-element.117), kind=kOutput, calls=%fused_computation.14 | convolution fusion | flops 6645940224 | bytes 13860864 | tf_op jit(solution)/shard_map/dot_general | solution.py:68
  360.7 9.8 %collective-permute-done.21 = bf16[128,2048]{1,0:T(8,128)(2,1)S(1)} collective-permute-done((bf16[128,2048]{1,0:T(8,128)(2,1)S(1)}, bf16[128,2048]{1,0:T(8,128)(2,1)S(1)}, u32[]{:S(2)}, u32[]{:S(2)}) %collective-permute-start.21) | collective-permute-done | bytes 524320 | tf_op jit(solution)/shard_map/ppermute | solution.py:307
  377.4 18.7 %convolution_convert_fusion = bf16[2048,1536]{1,0:T(8,128)(2,1)} fusion(bf16[2112,2048]{1,0:T(8,128)(2,1)} %get-tuple-element.123, bf16[2112,1536]{1,0:T(8,128)(2,1)S(1)} %bitcast.264), kind=kOutput, calls=%fused_computation.8 | convolution fusion | flops 13290700800 | bytes 21430272 | tf_op jit(solution)/shard_map/dot_general | solution.py:74
  396.1 4.2 collective-permute-done.23
  404.1 4.3 fusion.22
  408.5 3.5 constant_dynamic-update-slice_fusion.14
  414.0 7.7 %convolution_convert_fusion.1 = bf16[1056,2048]{1,0:T(8,128)(2,1)} fusion(bf16[768,2048]{1,0:T(8,128)(2,1)} %get-tuple-element.126, bf16[2112,768]{1,0:T(8,128)(2,1)S(1)} %copy-done.27), kind=kOutput, calls=%fused_computation.9 | convolution fusion | flops 3324051456 | bytes 9093120 | tf_op jit(solution)/shard_map/dot_general | solution.py:1255
  421.7 5.1 convolution_convert_fusion.2
  429.3 6.4 %collective-permute-done.25 = bf16[264,2048]{1,0:T(8,128)(2,1)S(1)} collective-permute-done((bf16[264,2048]{1,0:T(8,128)(2,1)}, bf16[264,2048]{1,0:T(8,128)(2,1)S(1)}, u32[]{:S(2)}, u32[]{:S(2)}) %collective-permute-start.25) | collective-permute-done | bytes 1081376 | tf_op jit(solution)/shard_map/ppermute | solution.py:307
  443.1 4.8 collective-permute-done.27
  448.7 5.1 collective-permute-done.28
  465.9 32.1 %mixer_backward.1 = (bf16[4,264,640]{2,1,0:T(8,128)(2,1)}, bf16[4,264,640]{2,1,0:T(8,128)(2,1)}, f32[384,768]{1,0:T(8,128)}, f32[8,384]{1,0:T(8,128)}) custom-call(s32[5]{0:T(128)} %pad_add_fusion.info_ref, bf16[4,264,2048]{2,1,0:T(8,128)(2,1)} %bitcast.197, bf16[4,264,2048]{2,1,0:T(8,128)(2,1)} %collective-permute-done.29.far_ref, ...), custom_call_target="tpu_custom_call" | custom-call | tf_op jit(solution)/shard_map/mixer_backward/pallas_call | solution.py:813
  498.0 6.5 %fusion.72 = f32[2048,640,1]{1,0,2:T(8,128)S(1)} fusion(bf16[4,264,2048]{2,1,0:T(8,128)(2,1)} %get-tuple-element.100.near_ref, bf16[4,264,640]{2,1,0:T(8,128)(2,1)} %get-tuple-element.145), kind=kOutput, calls=%fused_computation.181 | convolution fusion | flops 2768240640 | bytes 10919936 | tf_op jit(solution)/shard_map/dot_general | solution.py:74
  504.5 5.8 fusion.3
  510.3 8.1 %reduce-scatter.7.cloned.1.call-done = bf16[512,1536]{1,0:T(8,128)(2,1)} async-done(((bf16[2048,1536]{1,0:T(8,128)(2,1)}), bf16[512,1536]{1,0:T(8,128)(2,1)}) %reduce-scatter.7.cloned.1.call-update) | async-done | bytes 1572880 | tf_op jit(solution)/shard_map/reduce_scatter | solution.py:917
  520.9 7.1 %proj_backward.3 = bf16[1056,2048]{1,0:T(8,128)(2,1)} custom-call(bf16[1056,640]{1,0:T(8,128)(2,1)} %bitcast.240, bf16[2048,640]{1,0:T(8,128)(2,1)} %all-gather.8.cloned.1.call-done.proj_ref, bf16[16,128]{1,0:T(8,128)(2,1)} %copy-done.21), custom_call_target="tpu_custom_call" | custom-call | tf_op jit(solution)/shard_map/proj_backward/pallas_call | solution.py:868
  529.4 4.3 all-to-all-start.3
  533.8 7.0 %proj_backward.2 = bf16[1056,2048]{1,0:T(8,128)(2,1)} custom-call(bf16[1056,640]{1,0:T(8,128)(2,1)} %bitcast.239, bf16[2048,640]{1,0:T(8,128)(2,1)} %all-gather.8.cloned.1.call-done.proj_ref, bf16[16,128]{1,0:T(8,128)(2,1)} %copy-done.21), custom_call_target="tpu_custom_call" | custom-call | tf_op jit(solution)/shard_map/proj_backward/pallas_call | solution.py:868
  540.9 4.9 fusion.28
  552.0 4.5 convolution_bitcast_fusion
  564.7 9.5 %collective-permute-done.36 = bf16[128,2048]{1,0:T(8,128)(2,1)S(1)} collective-permute-done((bf16[128,2048]{1,0:T(8,128)(2,1)S(1)}, bf16[128,2048]{1,0:T(8,128)(2,1)S(1)}, u32[]{:S(2)}, u32[]{:S(2)}) %collective-permute-start.36) | collective-permute-done | bytes 524320 | tf_op jit(solution)/shard_map/ppermute | solution.py:307
  582.9 4.9 collect_columns.3
  589.1 4.4 all-to-all-start.2
  593.6 14.3 %collective-permute-done.38 = bf16[264,2048]{1,0:T(8,128)(2,1)S(1)} collective-permute-done((bf16[264,2048]{1,0:T(8,128)(2,1)}, bf16[264,2048]{1,0:T(8,128)(2,1)S(1)}, u32[]{:S(2)}, u32[]{:S(2)}) %collective-permute-start.38) | collective-permute-done | bytes 1081376 | tf_op jit(solution)/shard_map/ppermute | solution.py:307
  611.6 4.3 fusion.10
  (297 shorter events, 166.6 us)
Async XLA Ops:
  7.2 45.6 %all-gather.12.cloned.1.call-start = ((), (), s32[]{:S(2)}) async-start(), calls=%async_computation.14 | async-start | bytes 1945600 | tf_op jit(solution)/shard_map/all_gather | solution.py:1119
  13.1 27.7 %collective-permute-start = (bf16[264,2048]{1,0:T(8,128)(2,1)S(1)}, bf16[264,2048]{1,0:T(8,128)(2,1)S(1)}, u32[]{:S(2)}, u32[]{:S(2)}) collective-permute-start(bf16[264,2048]{1,0:T(8,128)(2,1)S(1)} %bitcast.208), channel_id=1, source_target_pairs={{0,2},{1,3},{2,0},{3,1},{4,6},{5,7},{6,4},{7,5},{8,10},{9,11},{10,... | collective-permute-start | bytes 3244040 | tf_op jit(solution)/shard_map/ppermute | solution.py:307
  16.1 27.8 %collective-permute-start.1 = (bf16[264,2048]{1,0:T(8,128)(2,1)S(1)}, bf16[264,2048]{1,0:T(8,128)(2,1)}, u32[]{:S(2)}, u32[]{:S(2)}) collective-permute-start(bf16[264,2048]{1,0:T(8,128)(2,1)S(1)} %bitcast.209), channel_id=1, source_target_pairs={{0,4},{1,5},{2,6},{3,7},{4,0},{5,1},{6,2},{7,3},{8,12},{9,13},{10,... | collective-permute-start | bytes 3244040 | tf_op jit(solution)/shard_map/ppermute | solution.py:307
  19.8 37.4 %all-to-all-start = ((bf16[8,64,640]{2,1,0:T(8,128)(2,1)}), bf16[8,64,640]{2,1,0:T(8,128)(2,1)S(1)}, u32[]{:S(2)}, u32[]{:S(2)}) async-start(bf16[8,64,640]{2,1,0:T(8,128)(2,1)} %deal_columns.2), calls=%async_computation | async-start | bytes 1310720 | tf_op jit(solution)/shard_map/all_to_all | solution.py:912
  23.4 105.7 %all-gather.8.cloned.1.call-start = ((), (), s32[]{:S(2)}) async-start(), calls=%async_computation.8 | async-start | bytes 3276800 | tf_op jit(solution)/shard_map/all_gather | solution.py:1154
  54.7 13.2 %collective-permute-start.2 = (bf16[128,2048]{1,0:T(8,128)(2,1)}, bf16[128,2048]{1,0:T(8,128)(2,1)}, u32[]{:S(2)}, u32[]{:S(2)}) collective-permute-start(bf16[128,2048]{1,0:T(8,128)(2,1)} %slice.292), channel_id=1, source_target_pairs={{0,2},{1,3},{2,0},{3,1},{4,6},{5,7},{6,4},{7,5},{8,10},{9,11},{10,... | collective-permute-start | bytes 1572872 | tf_op jit(solution)/shard_map/ppermute | solution.py:307
  58.1 13.3 %collective-permute-start.3 = (bf16[136,2048]{1,0:T(8,128)(2,1)S(1)}, bf16[136,2048]{1,0:T(8,128)(2,1)S(1)}, u32[]{:S(2)}, u32[]{:S(2)}) collective-permute-start(bf16[136,2048]{1,0:T(8,128)(2,1)S(1)} %slice.293), channel_id=1, source_target_pairs={{0,4},{1,5},{2,6},{3,7},{4,0},{5,1},{6,2},{7,3},{8,12},{9,13},{10,... | collective-permute-start | bytes 1671176 | tf_op jit(solution)/shard_map/ppermute | solution.py:307
  72.3 40.1 %collective-permute-start.4 = (bf16[4,264,2048]{2,1,0:T(8,128)(2,1)}, bf16[4,264,2048]{2,1,0:T(8,128)(2,1)}, u32[]{:S(2)}, u32[]{:S(2)}) collective-permute-start(bf16[4,264,2048]{2,1,0:T(8,128)(2,1)} %bitcast.204), channel_id=1, source_target_pairs={{0,1},{1,0},{2,3},{3,2},{4,5},{5,4},{6,7},{7,6},{8,9},{9,8},{10,11... | collective-permute-start | bytes 12976136 | tf_op jit(solution)/shard_map/ppermute | solution.py:307
  76.0 30.1 %all-to-all-start.1 = ((bf16[8,64,1536]{2,1,0:T(8,128)(2,1)}), bf16[8,64,1536]{2,1,0:T(8,128)(2,1)S(1)}, u32[]{:S(2)}, u32[]{:S(2)}) async-start(bf16[8,64,1536]{2,1,0:T(8,128)(2,1)} %deal_columns.3), calls=%async_computation.1 | async-start | bytes 3145728 | tf_op jit(solution)/shard_map/all_to_all | solution.py:912
  79.5 127.3 %all-gather.14.cloned.1.call-start = ((), (), s32[]{:S(2)}) async-start(), calls=%async_computation.15 | async-start | bytes 3932160 | tf_op jit(solution)/shard_map/all_gather | solution.py:1203
  85.3 24.6 %collective-permute-start.5 = (bf16[2,80,2432]{2,1,0:T(8,128)(2,1)}, bf16[2,80,2432]{2,1,0:T(8,128)(2,1)}, u32[]{:S(2)}, u32[]{:S(2)}) collective-permute-start(bf16[2,80,2432]{2,1,0:T(8,128)(2,1)} %get-tuple-element.223), channel_id=1, source_target_pairs={{0,1},{1,0},{2,3},{3,2},{4,5},{5,4},{6,7},{7,6},{8,9},{9,8},{10,11... | collective-permute-start | bytes 2334728 | tf_op jit(solution)/shard_map/ppermute | solution.py:307
  106.1 187.9 %all-gather.10.cloned.1.call-start = ((), (), s32[]{:S(2)}) async-start(), calls=%async_computation.9 | async-start | bytes 7864320 | tf_op jit(solution)/shard_map/all_gather | solution.py:1204
  122.6 40.2 %collective-permute-start.6 = (bf16[264,2048]{1,0:T(8,128)(2,1)}, bf16[264,2048]{1,0:T(8,128)(2,1)}, u32[]{:S(2)}, u32[]{:S(2)}) collective-permute-start(bf16[264,2048]{1,0:T(8,128)(2,1)} %fusion.23), channel_id=1, source_target_pairs={{0,2},{1,3},{2,0},{3,1},{4,6},{5,7},{6,4},{7,5},{8,10},{9,11},{10,... | collective-permute-start | bytes 3244040 | tf_op jit(solution)/shard_map/ppermute | solution.py:307
  122.8 49.4 %collective-permute-start.7 = (bf16[264,2048]{1,0:T(8,128)(2,1)}, bf16[264,2048]{1,0:T(8,128)(2,1)}, u32[]{:S(2)}, u32[]{:S(2)}) collective-permute-start(bf16[264,2048]{1,0:T(8,128)(2,1)} %fusion.23), channel_id=1, source_target_pairs={{0,4},{1,5},{2,6},{3,7},{4,0},{5,1},{6,2},{7,3},{8,12},{9,13},{10,... | collective-permute-start | bytes 3244040 | tf_op jit(solution)/shard_map/ppermute | solution.py:307
  124.4 47.9 %collective-permute-start.8 = (bf16[264,2048]{1,0:T(8,128)(2,1)}, bf16[264,2048]{1,0:T(8,128)(2,1)}, u32[]{:S(2)}, u32[]{:S(2)}) collective-permute-start(bf16[264,2048]{1,0:T(8,128)(2,1)} %fusion.23), channel_id=1, source_target_pairs={{0,6},{1,7},{2,4},{3,5},{4,2},{5,3},{6,0},{7,1},{8,14},{9,15},{10,... | collective-permute-start | bytes 3244040 | tf_op jit(solution)/shard_map/ppermute | solution.py:307
  178.3 248.5 %reduce-scatter.5.cloned.1.call-start = ((), (), s32[]{:S(2)}) async-start(), calls=%async_computation.10 | async-start | bytes 3932160 | tf_op jit(solution)/shard_map/reduce_scatter | solution.py:917
  188.5 16.9 %collective-permute-start.11 = (bf16[136,2048]{1,0:T(8,128)(2,1)S(1)}, bf16[136,2048]{1,0:T(8,128)(2,1)S(1)}, u32[]{:S(2)}, u32[]{:S(2)}) collective-permute-start(bf16[136,2048]{1,0:T(8,128)(2,1)S(1)} %slice.401), channel_id=1, source_target_pairs={{0,2},{1,3},{2,0},{3,1},{4,6},{5,7},{6,4},{7,5},{8,10},{9,11},{10,... | collective-permute-start | bytes 1671176 | tf_op jit(solution)/shard_map/ppermute | solution.py:307
  190.3 13.7 %collective-permute-start.10 = (bf16[128,2048]{1,0:T(8,128)(2,1)S(1)}, bf16[128,2048]{1,0:T(8,128)(2,1)S(1)}, u32[]{:S(2)}, u32[]{:S(2)}) collective-permute-start(bf16[128,2048]{1,0:T(8,128)(2,1)S(1)} %slice.394), channel_id=1, source_target_pairs={{0,4},{1,5},{2,6},{3,7},{4,0},{5,1},{6,2},{7,3},{8,12},{9,13},{10,... | collective-permute-start | bytes 1572872 | tf_op jit(solution)/shard_map/ppermute | solution.py:307
  206.8 25.0 %collective-permute-start.12 = (bf16[264,2048]{1,0:T(8,128)(2,1)S(1)}, bf16[264,2048]{1,0:T(8,128)(2,1)S(1)}, u32[]{:S(2)}, u32[]{:S(2)}) collective-permute-start(bf16[264,2048]{1,0:T(8,128)(2,1)S(1)} %pad_maximum_fusion.2), channel_id=1, source_target_pairs={{0,2},{1,3},{2,0},{3,1},{4,6},{5,7},{6,4},{7,5},{8,10},{9,11},{10,... | collective-permute-start | bytes 3244040 | tf_op jit(solution)/shard_map/ppermute | solution.py:307
  207.3 24.7 %collective-permute-start.13 = (bf16[264,2048]{1,0:T(8,128)(2,1)S(1)}, bf16[264,2048]{1,0:T(8,128)(2,1)S(1)}, u32[]{:S(2)}, u32[]{:S(2)}) collective-permute-start(bf16[264,2048]{1,0:T(8,128)(2,1)S(1)} %pad_maximum_fusion.3), channel_id=1, source_target_pairs={{0,4},{1,5},{2,6},{3,7},{4,0},{5,1},{6,2},{7,3},{8,12},{9,13},{10,... | collective-permute-start | bytes 3244040 | tf_op jit(solution)/shard_map/ppermute | solution.py:307
  235.7 24.0 %collective-permute-start.15 = (bf16[264,2048]{1,0:T(8,128)(2,1)S(1)}, bf16[264,2048]{1,0:T(8,128)(2,1)S(1)}, u32[]{:S(2)}, u32[]{:S(2)}) collective-permute-start(bf16[264,2048]{1,0:T(8,128)(2,1)S(1)} %get-tuple-element.208), channel_id=1, source_target_pairs={{0,4},{1,5},{2,6},{3,7},{4,0},{5,1},{6,2},{7,3},{8,12},{9,13},{10,... | collective-permute-start | bytes 3244040 | tf_op jit(solution)/shard_map/ppermute | solution.py:307
  237.1 24.4 %collective-permute-start.14 = (bf16[264,2048]{1,0:T(8,128)(2,1)S(1)}, bf16[264,2048]{1,0:T(8,128)(2,1)S(1)}, u32[]{:S(2)}, u32[]{:S(2)}) collective-permute-start(bf16[264,2048]{1,0:T(8,128)(2,1)S(1)} %get-tuple-element.208), channel_id=1, source_target_pairs={{0,2},{1,3},{2,0},{3,1},{4,6},{5,7},{6,4},{7,5},{8,10},{9,11},{10,... | collective-permute-start | bytes 3244040 | tf_op jit(solution)/shard_map/ppermute | solution.py:307
  237.9 35.9 %collective-permute-start.19 = (bf16[4,264,2048]{2,1,0:T(8,128)(2,1)}, bf16[4,264,2048]{2,1,0:T(8,128)(2,1)}, u32[]{:S(2)}, u32[]{:S(2)}) collective-permute-start(bf16[4,264,2048]{2,1,0:T(8,128)(2,1)} %pad_maximum_fusion.1), channel_id=1, source_target_pairs={{0,1},{1,0},{2,3},{3,2},{4,5},{5,4},{6,7},{7,6},{8,9},{9,8},{10,11... | collective-permute-start | bytes 12976136 | tf_op jit(solution)/shard_map/ppermute | solution.py:307
  259.7 12.2 %collective-permute-start.16 = (bf16[128,2048]{1,0:T(8,128)(2,1)S(1)}, bf16[128,2048]{1,0:T(8,128)(2,1)S(1)}, u32[]{:S(2)}, u32[]{:S(2)}) collective-permute-start(bf16[128,2048]{1,0:T(8,128)(2,1)S(1)} %slice.403), channel_id=1, source_target_pairs={{0,2},{1,3},{2,0},{3,1},{4,6},{5,7},{6,4},{7,5},{8,10},{9,11},{10,... | collective-permute-start | bytes 1572872 | tf_op jit(solution)/shard_map/ppermute | solution.py:307
  273.7 20.2 %collective-permute-start.18 = (bf16[4,264,2048]{2,1,0:T(8,128)(2,1)}, bf16[4,264,2048]{2,1,0:T(8,128)(2,1)}, u32[]{:S(2)}, u32[]{:S(2)}) collective-permute-start(bf16[4,264,2048]{2,1,0:T(8,128)(2,1)} %bitcast.35), channel_id=1, source_target_pairs={{0,1},{1,0},{2,3},{3,2},{4,5},{5,4},{6,7},{7,6},{8,9},{9,8},{10,11... | collective-permute-start | bytes 12976136 | tf_op jit(solution)/shard_map/ppermute | solution.py:307
  332.7 20.8 %collective-permute-start.20 = (bf16[4,264,2048]{2,1,0:T(8,128)(2,1)}, bf16[4,264,2048]{2,1,0:T(8,128)(2,1)}, u32[]{:S(2)}, u32[]{:S(2)}) collective-permute-start(bf16[4,264,2048]{2,1,0:T(8,128)(2,1)} %bitcast.38), channel_id=1, source_target_pairs={{0,1},{1,0},{2,3},{3,2},{4,5},{5,4},{6,7},{7,6},{8,9},{9,8},{10,11... | collective-permute-start | bytes 12976136 | tf_op jit(solution)/shard_map/ppermute | solution.py:307
  343.0 175.4 %reduce-scatter.7.cloned.1.call-start = ((), (), s32[]{:S(2)}) async-start(), calls=%async_computation.11 | async-start | bytes 7864320 | tf_op jit(solution)/shard_map/reduce_scatter | solution.py:917
  356.1 16.8 %collective-permute-start.22 = (bf16[136,2048]{1,0:T(8,128)(2,1)S(1)}, bf16[136,2048]{1,0:T(8,128)(2,1)S(1)}, u32[]{:S(2)}, u32[]{:S(2)}) collective-permute-start(bf16[136,2048]{1,0:T(8,128)(2,1)S(1)} %slice.336), channel_id=1, source_target_pairs={{0,2},{1,3},{2,0},{3,1},{4,6},{5,7},{6,4},{7,5},{8,10},{9,11},{10,... | collective-permute-start | bytes 1671176 | tf_op jit(solution)/shard_map/ppermute | solution.py:307
  356.9 13.6 %collective-permute-start.21 = (bf16[128,2048]{1,0:T(8,128)(2,1)S(1)}, bf16[128,2048]{1,0:T(8,128)(2,1)S(1)}, u32[]{:S(2)}, u32[]{:S(2)}) collective-permute-start(bf16[128,2048]{1,0:T(8,128)(2,1)S(1)} %slice.329), channel_id=1, source_target_pairs={{0,4},{1,5},{2,6},{3,7},{4,0},{5,1},{6,2},{7,3},{8,12},{9,13},{10,... | collective-permute-start | bytes 1572872 | tf_op jit(solution)/shard_map/ppermute | solution.py:307
  375.3 24.9 %collective-permute-start.23 = (bf16[264,2048]{1,0:T(8,128)(2,1)}, bf16[264,2048]{1,0:T(8,128)(2,1)S(1)}, u32[]{:S(2)}, u32[]{:S(2)}) collective-permute-start(bf16[264,2048]{1,0:T(8,128)(2,1)} %pad_maximum_fusion.4), channel_id=1, source_target_pairs={{0,2},{1,3},{2,0},{3,1},{4,6},{5,7},{6,4},{7,5},{8,10},{9,11},{10,... | collective-permute-start | bytes 3244040 | tf_op jit(solution)/shard_map/ppermute | solution.py:307
  376.6 24.8 %collective-permute-start.24 = (bf16[264,2048]{1,0:T(8,128)(2,1)}, bf16[264,2048]{1,0:T(8,128)(2,1)}, u32[]{:S(2)}, u32[]{:S(2)}) collective-permute-start(bf16[264,2048]{1,0:T(8,128)(2,1)} %pad_maximum_fusion.5), channel_id=1, source_target_pairs={{0,4},{1,5},{2,6},{3,7},{4,0},{5,1},{6,2},{7,3},{8,12},{9,13},{10,... | collective-permute-start | bytes 3244040 | tf_op jit(solution)/shard_map/ppermute | solution.py:307
  408.5 180.7 %reduce-scatter.9.cloned.1.call-start = ((), (), s32[]{:S(2)}) async-start(), calls=%async_computation.12 | async-start | bytes 3276800 | tf_op jit(solution)/shard_map/reduce_scatter | solution.py:917
  412.0 23.7 %collective-permute-start.25 = (bf16[264,2048]{1,0:T(8,128)(2,1)}, bf16[264,2048]{1,0:T(8,128)(2,1)S(1)}, u32[]{:S(2)}, u32[]{:S(2)}) collective-permute-start(bf16[264,2048]{1,0:T(8,128)(2,1)} %get-tuple-element.206), channel_id=1, source_target_pairs={{0,2},{1,3},{2,0},{3,1},{4,6},{5,7},{6,4},{7,5},{8,10},{9,11},{10,... | collective-permute-start | bytes 3244040 | tf_op jit(solution)/shard_map/ppermute | solution.py:307
  412.7 23.6 %collective-permute-start.26 = (bf16[264,2048]{1,0:T(8,128)(2,1)}, bf16[264,2048]{1,0:T(8,128)(2,1)}, u32[]{:S(2)}, u32[]{:S(2)}) collective-permute-start(bf16[264,2048]{1,0:T(8,128)(2,1)} %get-tuple-element.206), channel_id=1, source_target_pairs={{0,4},{1,5},{2,6},{3,7},{4,0},{5,1},{6,2},{7,3},{8,12},{9,13},{10,... | collective-permute-start | bytes 3244040 | tf_op jit(solution)/shard_map/ppermute | solution.py:307
  438.7 17.3 %collective-permute-start.30 = (bf16[4,264,2048]{2,1,0:T(8,128)(2,1)}, bf16[4,264,2048]{2,1,0:T(8,128)(2,1)S(1)}, u32[]{:S(2)}, u32[]{:S(2)}) collective-permute-start(bf16[4,264,2048]{2,1,0:T(8,128)(2,1)} %bitcast.257), channel_id=1, source_target_pairs={{0,1},{1,0},{2,3},{3,2},{4,5},{5,4},{6,7},{7,6},{8,9},{9,8},{10,11... | collective-permute-start | bytes 12976136 | tf_op jit(solution)/shard_map/ppermute | solution.py:307
  438.7 15.1 %collective-permute-start.28 = (bf16[136,2048]{1,0:T(8,128)(2,1)S(1)}, bf16[136,2048]{1,0:T(8,128)(2,1)S(1)}, u32[]{:S(2)}, u32[]{:S(2)}) collective-permute-start(bf16[136,2048]{1,0:T(8,128)(2,1)S(1)} %slice.340), channel_id=1, source_target_pairs={{0,4},{1,5},{2,6},{3,7},{4,0},{5,1},{6,2},{7,3},{8,12},{9,13},{10,... | collective-permute-start | bytes 1671176 | tf_op jit(solution)/shard_map/ppermute | solution.py:307
  462.4 65.6 %collective-permute-start.32 = (bf16[264,2048]{1,0:T(8,128)(2,1)}, bf16[264,2048]{1,0:T(8,128)(2,1)}, u32[]{:S(2)}, u32[]{:S(2)}) collective-permute-start(bf16[264,2048]{1,0:T(8,128)(2,1)} %get-tuple-element.148), channel_id=1, source_target_pairs={{0,2},{1,3},{2,0},{3,1},{4,6},{5,7},{6,4},{7,5},{8,10},{9,11},{10,... | collective-permute-start | bytes 3244040 | tf_op jit(solution)/shard_map/ppermute | solution.py:307
  463.2 64.8 %collective-permute-start.33 = (bf16[264,2048]{1,0:T(8,128)(2,1)}, bf16[264,2048]{1,0:T(8,128)(2,1)}, u32[]{:S(2)}, u32[]{:S(2)}) collective-permute-start(bf16[264,2048]{1,0:T(8,128)(2,1)} %get-tuple-element.149), channel_id=1, source_target_pairs={{0,4},{1,5},{2,6},{3,7},{4,0},{5,1},{6,2},{7,3},{8,12},{9,13},{10,... | collective-permute-start | bytes 3244040 | tf_op jit(solution)/shard_map/ppermute | solution.py:307
  464.5 63.5 %collective-permute-start.34 = (bf16[264,2048]{1,0:T(8,128)(2,1)}, bf16[264,2048]{1,0:T(8,128)(2,1)}, u32[]{:S(2)}, u32[]{:S(2)}) collective-permute-start(bf16[264,2048]{1,0:T(8,128)(2,1)} %get-tuple-element.150), channel_id=1, source_target_pairs={{0,6},{1,7},{2,4},{3,5},{4,2},{5,3},{6,0},{7,1},{8,14},{9,15},{10,... | collective-permute-start | bytes 3244040 | tf_op jit(solution)/shard_map/ppermute | solution.py:307
  528.0 17.8 %collective-permute-start.35 = (bf16[4,264,2048]{2,1,0:T(8,128)(2,1)}, bf16[4,264,2048]{2,1,0:T(8,128)(2,1)}, u32[]{:S(2)}, u32[]{:S(2)}) collective-permute-start(bf16[4,264,2048]{2,1,0:T(8,128)(2,1)} %bitcast.228), channel_id=1, source_target_pairs={{0,1},{1,0},{2,3},{3,2},{4,5},{5,4},{6,7},{7,6},{8,9},{9,8},{10,11... | collective-permute-start | bytes 12976136 | tf_op jit(solution)/shard_map/ppermute | solution.py:307
  529.4 53.5 %all-to-all-start.3 = ((bf16[8,64,1536]{2,1,0:T(8,128)(2,1)}), bf16[8,64,1536]{2,1,0:T(8,128)(2,1)}, u32[]{:S(2)}, u32[]{:S(2)}) async-start(bf16[8,64,1536]{2,1,0:T(8,128)(2,1)} %bitcast.238), calls=%async_computation.7 | async-start | bytes 3145728 | tf_op jit(solution)/shard_map/all_to_all | solution.py:925
  533.8 86.2 %reduce-scatter.11.cloned.1.call-start = ((), (), s32[]{:S(2)}) async-start(), calls=%async_computation.13 | async-start | bytes 1945600 | tf_op jit(solution)/shard_map/reduce_scatter | solution.py:917
  557.8 19.1 %collective-permute-start.40 = (bf16[2,80,2432]{2,1,0:T(8,128)(2,1)S(1)}, bf16[2,80,2432]{2,1,0:T(8,128)(2,1)S(1)}, u32[]{:S(2)}, u32[]{:S(2)}) collective-permute-start(bf16[2,80,2432]{2,1,0:T(8,128)(2,1)S(1)} %get-tuple-element.217), channel_id=1, source_target_pairs={{0,1},{1,0},{2,3},{3,2},{4,5},{5,4},{6,7},{7,6},{8,9},{9,8},{10,11... | collective-permute-start | bytes 2334728 | tf_op jit(solution)/shard_map/ppermute | solution.py:307
  558.7 19.6 %collective-permute-start.37 = (bf16[136,2048]{1,0:T(8,128)(2,1)S(1)}, bf16[136,2048]{1,0:T(8,128)(2,1)S(1)}, u32[]{:S(2)}, u32[]{:S(2)}) collective-permute-start(bf16[136,2048]{1,0:T(8,128)(2,1)S(1)} %copy-done.16), channel_id=1, source_target_pairs={{0,2},{1,3},{2,0},{3,1},{4,6},{5,7},{6,4},{7,5},{8,10},{9,11},{10,... | collective-permute-start | bytes 1671176 | tf_op jit(solution)/shard_map/ppermute | solution.py:307
  560.6 13.7 %collective-permute-start.36 = (bf16[128,2048]{1,0:T(8,128)(2,1)S(1)}, bf16[128,2048]{1,0:T(8,128)(2,1)S(1)}, u32[]{:S(2)}, u32[]{:S(2)}) collective-permute-start(bf16[128,2048]{1,0:T(8,128)(2,1)S(1)} %copy-done.17), channel_id=1, source_target_pairs={{0,4},{1,5},{2,6},{3,7},{4,0},{5,1},{6,2},{7,3},{8,12},{9,13},{10,... | collective-permute-start | bytes 1572872 | tf_op jit(solution)/shard_map/ppermute | solution.py:307
  580.9 27.0 %collective-permute-start.38 = (bf16[264,2048]{1,0:T(8,128)(2,1)}, bf16[264,2048]{1,0:T(8,128)(2,1)S(1)}, u32[]{:S(2)}, u32[]{:S(2)}) collective-permute-start(bf16[264,2048]{1,0:T(8,128)(2,1)} %pad_maximum_fusion.6), channel_id=1, source_target_pairs={{0,2},{1,3},{2,0},{3,1},{4,6},{5,7},{6,4},{7,5},{8,10},{9,11},{10,... | collective-permute-start | bytes 3244040 | tf_op jit(solution)/shard_map/ppermute | solution.py:307
  581.3 27.7 %collective-permute-start.39 = (bf16[264,2048]{1,0:T(8,128)(2,1)}, bf16[264,2048]{1,0:T(8,128)(2,1)S(1)}, u32[]{:S(2)}, u32[]{:S(2)}) collective-permute-start(bf16[264,2048]{1,0:T(8,128)(2,1)} %pad_maximum_fusion.7), channel_id=1, source_target_pairs={{0,4},{1,5},{2,6},{3,7},{4,0},{5,1},{6,2},{7,3},{8,12},{9,13},{10,... | collective-permute-start | bytes 3244040 | tf_op jit(solution)/shard_map/ppermute | solution.py:307
  589.1 26.7 %all-to-all-start.2 = ((bf16[8,64,640]{2,1,0:T(8,128)(2,1)}), bf16[8,64,640]{2,1,0:T(8,128)(2,1)}, u32[]{:S(2)}, u32[]{:S(2)}) async-start(bf16[8,64,640]{2,1,0:T(8,128)(2,1)} %bitcast.244), calls=%async_computation.5 | async-start | bytes 1310720 | tf_op jit(solution)/shard_map/all_to_all | solution.py:925
  (43 other events, 547.7 us)
Sparse Core Ops, SparseCore 0:
  13.2 39.5 all-gather.11
  58.2 52.7 all-gather.7
  112.6 62.2 all-gather.13
  178.5 114.3 all-gather.9
  343.1 59.3 reduce-scatter.4
  408.6 109.8 reduce-scatter.6
  529.6 52.6 reduce-scatter.8
  584.5 34.8 reduce-scatter.10

commit v6 on v5

--- a/solution.py
+++ b/solution.py
@@ -376,12 +376,17 @@
     return (finish, *others)
 
 
-def split_mixer_rows(joined_ref, out_ref, gate_ref, small_ref):
+def split_mixer_rows(joined_ref, out_ref, gate_ref, *small_refs):
     depth, gates = out_ref.shape[1], gate_ref.shape[1]
     joined = joined_ref[...].astype(jnp.float32)
     out_ref[...] = joined[:, :depth]
     gate_ref[...] = joined[:, depth : depth + gates]
-    small_ref[...] = joined[:, depth + gates : depth + gates + small_ref.shape[1]]
+    first = (depth + gates) // 128 * 128
+    turned = joined[:, first : first + 128].T
+    row = depth + gates - first
+    for small_ref in small_refs:
+        small_ref[...] = turned[row : row + small_ref.shape[0]]
+        row += small_ref.shape[0]
 
 
 def place_of(chunk, me, count):
@@ -538,7 +543,7 @@
         gate_i = jax.nn.sigmoid(gates[at, lanes:] + channel_ref[BIAS_I : BIAS_I + 1, :])
         less = series_expm1(-gate_scale * gate_r * channel_ref[RATE : RATE + 1, :])
         plain = 1.0 + less
-        root = jnp.sqrt(-less * (2.0 + less))
+        root = jnp.sqrt(jnp.maximum(-less * (2.0 + less), 1e-37))
         decay = jnp.where(starts, 0.0, plain)
         scaling = jnp.where(starts, 1.0, root)
         conv = convolved[at, :]
@@ -1329,24 +1334,26 @@
     token_grad, proj_blocks = lax.optimization_barrier((token_grad, spread_rows(proj_summed)))
     in_proj_grad, norm_gain_grad = hand_back(proj_blocks, in_proj, norm_gain, proj_moves)
     by_row_grad = by_row_grad.astype(jnp.float32)
-    out_proj_grad, gate_weight_grad, small_grad = pl.pallas_call(
+    out_proj_grad, gate_weight_grad, *small_grads = pl.pallas_call(
         split_mixer_rows,
         out_shape=[
             jax.ShapeDtypeStruct((chunk_rows, columns), jnp.float32)
-            for columns in (depth, gate_columns, taps + 4)
-        ],
+            for columns in (depth, gate_columns)
+        ]
+        + [jax.ShapeDtypeStruct((count_of, chunk_rows), jnp.float32) for count_of in (taps, 1, 2, 1)],
         name="split_mixer_rows",
     )(by_row_grad)
+    conv_weight_grad, conv_bias_grad, gate_bias_grad, decay_grad = small_grads
     return (
         mixed[None],
         token_grad[None],
         norm_gain_grad,
         in_proj_grad,
-        small_grad[:, :taps],
-        small_grad[:, taps],
+        conv_weight_grad.T,
+        conv_bias_grad[0],
         gate_weight_grad,
-        small_grad[:, taps + 1 : taps + 3],
-        small_grad[:, taps + 3],
+        gate_bias_grad.T,
+        decay_grad[0],
         out_proj_grad,
         mlp_gain_grad,
         gate_up_grad,

time: 643 us -> 639 us (level)
    unnamed x94 -> x92, local copies, waits for them, and re-layouts: 20.8 us -> 18.8 us
  transfers between devices with their start and end apart: 53 -> 53, of which waited for: 27 -> 27; matrix products, arithmetic and copies ran while one was open for 32% -> 33% of each run, Pallas kernels for 17% -> 17%
where the time goes in v6:
time: 639 us; the launch traced here: 631 us
  waiting for transfers between devices  179 us (28%)
  Pallas kernels  135 us (21%)
  other arithmetic  99 us (15%)
  matrix products  87 us (14%)
  starting transfers between devices  55 us (9%)
  local copies, waits for them, and re-layouts  41.7 us (7%)
  blocking collectives  19.2 us (3%)
  between operations  15.2 us (2%)
    ppermute x41, waiting for transfers between devices, swap_with(): return lax.ppermute(block, 'seq', route)  162 us
    dot_general x6, matrix products, contract_first(): lax.dot_general(left, right, (((0,), (0,)), ((), ())), preferred_element_...  45.6 us
    ppermute x41, starting transfers between devices, swap_with(): return lax.ppermute(block, 'seq', route)  38 us
    pallas_call x1, Pallas kernels, run_forward(): pl.pallas_call(partial(mixer_forward, taps, slots), grid_spec=pltpu.Prefe...  33.8 us
    pallas_call x1, Pallas kernels, run_backward(): pl.pallas_call(partial(mixer_backward, taps, slots), grid_spec=pltpu.Pref...  32.1 us
    pallas_call x1, Pallas kernels, run_feed_forward(): pl.pallas_call(feed_forward, grid=(2, tiles), in_specs=[pl.BlockSpec((row...  27.7 us
    dot_general x2, matrix products, contract_last(): lax.dot_general(left, right, (((1,), (1,)), ((), ())), preferred_element_...  21.8 us
    all_gather x1, blocking collectives, by_channels(): lax.all_gather(gains.transpose(2, 0, 1), 'seq', axis=2).astype(jnp.float32)  19.2 us
  transfers between devices with their start and end apart: 53, of which 27 were waited for; matrix products, arithmetic and copies ran while one was open for 33% of the time, Pallas kernels for 17%

profile of v6, /device:TPU:0, one launch (start us, length us, event | category | flops | bytes accessed | tf_op | source)
XLA Modules:
  0.0 631.1 jit_solution(11839440378387999085)
XLA Ops:
  19.8 3.5 all-to-all-start
  23.5 17.4 %collective-permute-done = bf16[264,2048]{1,0:T(8,128)(2,1)S(1)} collective-permute-done((bf16[264,2048]{1,0:T(8,128)(2,1)S(1)}, bf16[264,2048]{1,0:T(8,128)(2,1)S(1)}, u32[]{:S(2)}, u32[]{:S(2)}) %collective-permute-start) | collective-permute-done | bytes 1081376 | tf_op jit(solution)/shard_map/ppermute | solution.py:307
  43.9 8.9 %all-gather.12.cloned.1.call-done = bf16[320,2432]{1,0:T(8,128)(2,1)} async-done(((bf16[80,2432]{1,0:T(8,128)(2,1)}), bf16[320,2432]{1,0:T(8,128)(2,1)}) %all-gather.12.cloned.1.call-update) | async-done | bytes 1556496 | tf_op jit(solution)/shard_map/all_gather | solution.py:1124
  63.2 4.6 collective-permute-done.2
  72.5 3.4 deal_columns.3
  76.0 3.6 all-to-all-start.1
  85.8 19.2 %all-gather.1 = bf16[2,4,512]{0,2,1:T(8,128)(2,1)S(1)} all-gather(bf16[2,4,64]{0,2,1:T(8,128)(2,1)S(1)} %slice_bitcast_fusion.6), channel_id=3, replica_groups=mesh['bucket'=4,'seq'=8] {'seq'}, dimensions={2}, use_global_device_ids=true | all-gather | bytes 9216 | tf_op jit(solution)/shard_map/all_gather | solution.py:1155
  106.4 3.4 multiply_reduce_fusion
  112.4 3.2 fusion
  115.6 7.0 %fusion.2 = (bf16[4,264,2048]{2,1,0:T(8,128)(2,1)}, bf16[4,264,2048]{2,1,0:T(8,128)(2,1)}) fusion(bf16[4,264,2048]{2,1,0:T(8,128)(2,1)} %collective-permute-done.4, f32[4,264]{1,0:T(4,128)S(1)} %add_rsqrt_fusion.1, f32[2048]{0:T(1024)S(1)} %bitcast.248, f32[4,264]{1,0:T(4,128)S(1)} %rsqrt.42, bf16[4,264,2048]{2,1,0:T(8,128)(2,1)} %bitcast.208), kind=kLoop, calls=%fused_computation.4 | loop fusion | flops 17301504 | bytes 17318144 | tf_op jit(solution)/shard_map/convert_element_type | solution.py:1200
  129.2 33.8 %mixer_forward.1 = (bf16[8,264,384]{2,1,0:T(8,128)(2,1)}, bf16[8,264,384]{2,1,0:T(8,128)(2,1)}, bf16[8,264,384]{2,1,0:T(8,128)(2,1)}, f32[8,264,384]{2,1,0:T(8,1...) custom-call(s32[5]{0:T(128)} %pad_add_fusion.info_ref, ...), custom_call_target="tpu_custom_call" | custom-call | tf_op jit(solution)/shard_map/mixer_forward/pallas_call | solution.py:762
  163.0 9.4 %collective-permute-done.7 = bf16[264,2048]{1,0:T(8,128)(2,1)} collective-permute-done((bf16[264,2048]{1,0:T(8,128)(2,1)}, bf16[264,2048]{1,0:T(8,128)(2,1)}, u32[]{:S(2)}, u32[]{:S(2)}) %collective-permute-start.7) | collective-permute-done | bytes 1081376 | tf_op jit(solution)/shard_map/ppermute | solution.py:307
  173.9 4.4 convolution_convert_fusion.3
  178.7 3.9 pad_maximum_fusion.1
  193.1 11.0 %collective-permute-done.10 = bf16[128,2048]{1,0:T(8,128)(2,1)S(1)} collective-permute-done((bf16[128,2048]{1,0:T(8,128)(2,1)S(1)}, bf16[128,2048]{1,0:T(8,128)(2,1)S(1)}, u32[]{:S(2)}, u32[]{:S(2)}) %collective-permute-start.10) | collective-permute-done | bytes 524320 | tf_op jit(solution)/shard_map/ppermute | solution.py:307
  208.8 23.1 %collective-permute-done.12 = bf16[264,2048]{1,0:T(8,128)(2,1)S(1)} collective-permute-done((bf16[264,2048]{1,0:T(8,128)(2,1)S(1)}, bf16[264,2048]{1,0:T(8,128)(2,1)S(1)}, u32[]{:S(2)}, u32[]{:S(2)}) %collective-permute-start.12) | collective-permute-done | bytes 1081376 | tf_op jit(solution)/shard_map/ppermute | solution.py:307
  237.8 21.9 %collective-permute-done.15 = bf16[264,2048]{1,0:T(8,128)(2,1)S(1)} collective-permute-done((bf16[264,2048]{1,0:T(8,128)(2,1)S(1)}, bf16[264,2048]{1,0:T(8,128)(2,1)S(1)}, u32[]{:S(2)}, u32[]{:S(2)}) %collective-permute-start.15) | collective-permute-done | bytes 1081376 | tf_op jit(solution)/shard_map/ppermute | solution.py:307
  264.3 7.6 %collective-permute-done.16 = bf16[128,2048]{1,0:T(8,128)(2,1)S(1)} collective-permute-done((bf16[128,2048]{1,0:T(8,128)(2,1)S(1)}, bf16[128,2048]{1,0:T(8,128)(2,1)S(1)}, u32[]{:S(2)}, u32[]{:S(2)}) %collective-permute-start.16) | collective-permute-done | bytes 524320 | tf_op jit(solution)/shard_map/ppermute | solution.py:307
  273.7 7.7 %pad_maximum_fusion = bf16[8,264,2048]{2,1,0:T(8,128)(2,1)} fusion(bf16[4,264,2048]{2,1,0:T(8,128)(2,1)} %collective-permute-done.19, bf16[4,264,2048]{2,1,0:T(8,128)(2,1)} %pad_maximum_fusion.1), kind=kLoop, calls=%fused_computation.5 | loop fusion | flops 4325376 | bytes 17301504 | tf_op jit(solution)/shard_map/concatenate | solution.py:1229
  281.4 12.6 %feed_backward.1 = (f32[2112,768]{1,0:T(8,128)}, bf16[768,2048]{1,0:T(8,128)(2,1)}) custom-call(bf16[2112,2048]{1,0:T(8,128)(2,1)} %bitcast.214, bf16[4,192,2048]{2,1,0:T(8,128)(2,1)} %bitcast.260), custom_call_target="tpu_custom_call" | custom-call | flops 6643777536 | tf_op jit(solution)/shard_map/feed_backward/pallas_call | solution.py:1045
  294.0 27.7 %feed_forward.1 = (bf16[2112,768]{1,0:T(8,128)(2,1)}, bf16[2112,1536]{1,0:T(8,128)(2,1)}, bf16[2112,2048]{1,0:T(8,128)(2,1)}) custom-call(bf16[1056,2048]{1,0:T(8,128)(2,1)} %constant_dynamic-update-slice_fusion.5.near_ref, bf16[1056,2048]{1,0:T(8,128)(2,1)} %bitcast.36.far_ref, bf16[2048,1536]{1,0:T(8,128)(2,1)} %all-gather.10.cloned.1.call-done.wide_ref, ...), custom_call_target="tpu_custom_call" | custom-call | flops 13287555072 | tf_op jit(solution)/shard_map/feed_forward/pallas_call | solution.py:986
  321.7 11.6 %convolution_convert_fusion.5 = bf16[1056,2048]{1,0:T(8,128)(2,1)} fusion(bf16[2048,1536]{1,0:T(8,128)(2,1)} %all-gather.10.cloned.1.call-done.wide_ref, bf16[2112,1536]{1,0:T(8,128)(2,1)} %get-tuple-element.120), kind=kOutput, calls=%fused_computation.13 | convolution fusion | flops 6645940224 | bytes 13860864 | tf_op jit(solution)/shard_map/dot_general | solution.py:68
  333.8 7.8 %convolution_convert_fusion.7 = bf16[768,2048]{1,0:T(8,128)(2,1)S(1)} fusion(bf16[2112,768]{1,0:T(8,128)(2,1)S(1)} %copy-done.26, bf16[2112,2048]{1,0:T(8,128)(2,1)S(1)} %bitcast.217), kind=kOutput, calls=%fused_computation.22 | convolution fusion | flops 6645350400 | bytes 15040512 | tf_op jit(solution)/shard_map/dot_general | solution.py:74
  343.6 10.2 %convolution_convert_fusion.6 = bf16[1056,2048]{1,0:T(8,128)(2,1)S(1)} fusion(bf16[2048,1536]{1,0:T(8,128)(2,1)} %all-gather.10.cloned.1.call-done.wide_ref, bf16[2112,1536]{1,0:T(8,128)(2,1)} %get-tuple-element.120), kind=kOutput, calls=%fused_computation.14 | convolution fusion | flops 6645940224 | bytes 13860864 | tf_op jit(solution)/shard_map/dot_general | solution.py:68
  361.1 9.7 %collective-permute-done.21 = bf16[128,2048]{1,0:T(8,128)(2,1)S(1)} collective-permute-done((bf16[128,2048]{1,0:T(8,128)(2,1)S(1)}, bf16[128,2048]{1,0:T(8,128)(2,1)S(1)}, u32[]{:S(2)}, u32[]{:S(2)}) %collective-permute-start.21) | collective-permute-done | bytes 524320 | tf_op jit(solution)/shard_map/ppermute | solution.py:307
  377.6 18.7 %convolution_convert_fusion = bf16[2048,1536]{1,0:T(8,128)(2,1)} fusion(bf16[2112,2048]{1,0:T(8,128)(2,1)} %get-tuple-element.126, bf16[2112,1536]{1,0:T(8,128)(2,1)S(1)} %bitcast.270), kind=kOutput, calls=%fused_computation.8 | convolution fusion | flops 13290700800 | bytes 21430272 | tf_op jit(solution)/shard_map/dot_general | solution.py:74
  396.4 4.2 collective-permute-done.23
  404.5 4.3 fusion.22
  408.9 3.5 constant_dynamic-update-slice_fusion.14
  414.4 7.6 %convolution_convert_fusion.1 = bf16[1056,2048]{1,0:T(8,128)(2,1)} fusion(bf16[768,2048]{1,0:T(8,128)(2,1)} %get-tuple-element.129, bf16[2112,768]{1,0:T(8,128)(2,1)S(1)} %copy-done.27), kind=kOutput, calls=%fused_computation.9 | convolution fusion | flops 3324051456 | bytes 9093120 | tf_op jit(solution)/shard_map/dot_general | solution.py:1260
  422.0 5.1 convolution_convert_fusion.2
  429.6 6.4 %collective-permute-done.25 = bf16[264,2048]{1,0:T(8,128)(2,1)S(1)} collective-permute-done((bf16[264,2048]{1,0:T(8,128)(2,1)}, bf16[264,2048]{1,0:T(8,128)(2,1)S(1)}, u32[]{:S(2)}, u32[]{:S(2)}) %collective-permute-start.25) | collective-permute-done | bytes 1081376 | tf_op jit(solution)/shard_map/ppermute | solution.py:307
  443.4 4.9 collective-permute-done.27
  449.1 5.0 collective-permute-done.28
  466.2 32.1 %mixer_backward.1 = (bf16[4,264,640]{2,1,0:T(8,128)(2,1)}, bf16[4,264,640]{2,1,0:T(8,128)(2,1)}, f32[384,768]{1,0:T(8,128)}, f32[8,384]{1,0:T(8,128)}) custom-call(s32[5]{0:T(128)} %pad_add_fusion.info_ref, bf16[4,264,2048]{2,1,0:T(8,128)(2,1)} %bitcast.200, bf16[4,264,2048]{2,1,0:T(8,128)(2,1)} %collective-permute-done.29.far_ref, ...), custom_call_target="tpu_custom_call" | custom-call | tf_op jit(solution)/shard_map/mixer_backward/pallas_call | solution.py:818
  498.3 6.5 %fusion.72 = f32[2048,640,1]{1,0,2:T(8,128)S(1)} fusion(bf16[4,264,2048]{2,1,0:T(8,128)(2,1)} %get-tuple-element.103.near_ref, bf16[4,264,640]{2,1,0:T(8,128)(2,1)} %get-tuple-element.148), kind=kOutput, calls=%fused_computation.179 | convolution fusion | flops 2768240640 | bytes 10919936 | tf_op jit(solution)/shard_map/dot_general | solution.py:74
  504.9 5.8 fusion.3
  510.7 7.9 %reduce-scatter.7.cloned.1.call-done = bf16[512,1536]{1,0:T(8,128)(2,1)} async-done(((bf16[2048,1536]{1,0:T(8,128)(2,1)}), bf16[512,1536]{1,0:T(8,128)(2,1)}) %reduce-scatter.7.cloned.1.call-update) | async-done | bytes 1572880 | tf_op jit(solution)/shard_map/reduce_scatter | solution.py:922
  521.1 7.1 %proj_backward.3 = bf16[1056,2048]{1,0:T(8,128)(2,1)} custom-call(bf16[1056,640]{1,0:T(8,128)(2,1)} %bitcast.243, bf16[2048,640]{1,0:T(8,128)(2,1)} %all-gather.8.cloned.1.call-done.proj_ref, bf16[16,128]{1,0:T(8,128)(2,1)} %copy-done.21), custom_call_target="tpu_custom_call" | custom-call | tf_op jit(solution)/shard_map/proj_backward/pallas_call | solution.py:873
  529.6 4.3 all-to-all-start.3
  534.0 7.1 %proj_backward.2 = bf16[1056,2048]{1,0:T(8,128)(2,1)} custom-call(bf16[1056,640]{1,0:T(8,128)(2,1)} %bitcast.242, bf16[2048,640]{1,0:T(8,128)(2,1)} %all-gather.8.cloned.1.call-done.proj_ref, bf16[16,128]{1,0:T(8,128)(2,1)} %copy-done.21), custom_call_target="tpu_custom_call" | custom-call | tf_op jit(solution)/shard_map/proj_backward/pallas_call | solution.py:873
  541.1 4.9 fusion.28
  552.2 4.5 convolution_bitcast_fusion
  565.0 9.5 %collective-permute-done.36 = bf16[128,2048]{1,0:T(8,128)(2,1)S(1)} collective-permute-done((bf16[128,2048]{1,0:T(8,128)(2,1)S(1)}, bf16[128,2048]{1,0:T(8,128)(2,1)S(1)}, u32[]{:S(2)}, u32[]{:S(2)}) %collective-permute-start.36) | collective-permute-done | bytes 524320 | tf_op jit(solution)/shard_map/ppermute | solution.py:307
  583.1 4.9 collect_columns.3
  589.4 4.7 all-to-all-start.2
  594.1 14.1 %collective-permute-done.38 = bf16[264,2048]{1,0:T(8,128)(2,1)S(1)} collective-permute-done((bf16[264,2048]{1,0:T(8,128)(2,1)}, bf16[264,2048]{1,0:T(8,128)(2,1)S(1)}, u32[]{:S(2)}, u32[]{:S(2)}) %collective-permute-start.38) | collective-permute-done | bytes 1081376 | tf_op jit(solution)/shard_map/ppermute | solution.py:307
  611.8 4.3 fusion.10
  (293 shorter events, 162.0 us)
Async XLA Ops:
  7.2 45.6 %all-gather.12.cloned.1.call-start = ((), (), s32[]{:S(2)}) async-start(), calls=%async_computation.14 | async-start | bytes 1945600 | tf_op jit(solution)/shard_map/all_gather | solution.py:1124
  13.1 27.7 %collective-permute-start = (bf16[264,2048]{1,0:T(8,128)(2,1)S(1)}, bf16[264,2048]{1,0:T(8,128)(2,1)S(1)}, u32[]{:S(2)}, u32[]{:S(2)}) collective-permute-start(bf16[264,2048]{1,0:T(8,128)(2,1)S(1)} %bitcast.211), channel_id=1, source_target_pairs={{0,2},{1,3},{2,0},{3,1},{4,6},{5,7},{6,4},{7,5},{8,10},{9,11},{10,... | collective-permute-start | bytes 3244040 | tf_op jit(solution)/shard_map/ppermute | solution.py:307
  16.1 27.8 %collective-permute-start.1 = (bf16[264,2048]{1,0:T(8,128)(2,1)S(1)}, bf16[264,2048]{1,0:T(8,128)(2,1)}, u32[]{:S(2)}, u32[]{:S(2)}) collective-permute-start(bf16[264,2048]{1,0:T(8,128)(2,1)S(1)} %bitcast.212), channel_id=1, source_target_pairs={{0,4},{1,5},{2,6},{3,7},{4,0},{5,1},{6,2},{7,3},{8,12},{9,13},{10,... | collective-permute-start | bytes 3244040 | tf_op jit(solution)/shard_map/ppermute | solution.py:307
  19.8 37.4 %all-to-all-start = ((bf16[8,64,640]{2,1,0:T(8,128)(2,1)}), bf16[8,64,640]{2,1,0:T(8,128)(2,1)S(1)}, u32[]{:S(2)}, u32[]{:S(2)}) async-start(bf16[8,64,640]{2,1,0:T(8,128)(2,1)} %deal_columns.2), calls=%async_computation | async-start | bytes 1310720 | tf_op jit(solution)/shard_map/all_to_all | solution.py:917
  23.4 105.8 %all-gather.8.cloned.1.call-start = ((), (), s32[]{:S(2)}) async-start(), calls=%async_computation.8 | async-start | bytes 3276800 | tf_op jit(solution)/shard_map/all_gather | solution.py:1159
  54.7 13.2 %collective-permute-start.2 = (bf16[128,2048]{1,0:T(8,128)(2,1)}, bf16[128,2048]{1,0:T(8,128)(2,1)}, u32[]{:S(2)}, u32[]{:S(2)}) collective-permute-start(bf16[128,2048]{1,0:T(8,128)(2,1)} %slice.280), channel_id=1, source_target_pairs={{0,2},{1,3},{2,0},{3,1},{4,6},{5,7},{6,4},{7,5},{8,10},{9,11},{10,... | collective-permute-start | bytes 1572872 | tf_op jit(solution)/shard_map/ppermute | solution.py:307
  58.1 13.3 %collective-permute-start.3 = (bf16[136,2048]{1,0:T(8,128)(2,1)S(1)}, bf16[136,2048]{1,0:T(8,128)(2,1)S(1)}, u32[]{:S(2)}, u32[]{:S(2)}) collective-permute-start(bf16[136,2048]{1,0:T(8,128)(2,1)S(1)} %slice.281), channel_id=1, source_target_pairs={{0,4},{1,5},{2,6},{3,7},{4,0},{5,1},{6,2},{7,3},{8,12},{9,13},{10,... | collective-permute-start | bytes 1671176 | tf_op jit(solution)/shard_map/ppermute | solution.py:307
  72.3 40.1 %collective-permute-start.4 = (bf16[4,264,2048]{2,1,0:T(8,128)(2,1)}, bf16[4,264,2048]{2,1,0:T(8,128)(2,1)}, u32[]{:S(2)}, u32[]{:S(2)}) collective-permute-start(bf16[4,264,2048]{2,1,0:T(8,128)(2,1)} %bitcast.207), channel_id=1, source_target_pairs={{0,1},{1,0},{2,3},{3,2},{4,5},{5,4},{6,7},{7,6},{8,9},{9,8},{10,11... | collective-permute-start | bytes 12976136 | tf_op jit(solution)/shard_map/ppermute | solution.py:307
  76.0 30.1 %all-to-all-start.1 = ((bf16[8,64,1536]{2,1,0:T(8,128)(2,1)}), bf16[8,64,1536]{2,1,0:T(8,128)(2,1)S(1)}, u32[]{:S(2)}, u32[]{:S(2)}) async-start(bf16[8,64,1536]{2,1,0:T(8,128)(2,1)} %deal_columns.3), calls=%async_computation.1 | async-start | bytes 3145728 | tf_op jit(solution)/shard_map/all_to_all | solution.py:917
  79.6 127.3 %all-gather.14.cloned.1.call-start = ((), (), s32[]{:S(2)}) async-start(), calls=%async_computation.15 | async-start | bytes 3932160 | tf_op jit(solution)/shard_map/all_gather | solution.py:1208
  85.3 24.5 %collective-permute-start.5 = (bf16[2,80,2432]{2,1,0:T(8,128)(2,1)}, bf16[2,80,2432]{2,1,0:T(8,128)(2,1)}, u32[]{:S(2)}, u32[]{:S(2)}) collective-permute-start(bf16[2,80,2432]{2,1,0:T(8,128)(2,1)} %get-tuple-element.201), channel_id=1, source_target_pairs={{0,1},{1,0},{2,3},{3,2},{4,5},{5,4},{6,7},{7,6},{8,9},{9,8},{10,11... | collective-permute-start | bytes 2334728 | tf_op jit(solution)/shard_map/ppermute | solution.py:307
  106.1 187.9 %all-gather.10.cloned.1.call-start = ((), (), s32[]{:S(2)}) async-start(), calls=%async_computation.9 | async-start | bytes 7864320 | tf_op jit(solution)/shard_map/all_gather | solution.py:1209
  122.6 40.3 %collective-permute-start.6 = (bf16[264,2048]{1,0:T(8,128)(2,1)}, bf16[264,2048]{1,0:T(8,128)(2,1)}, u32[]{:S(2)}, u32[]{:S(2)}) collective-permute-start(bf16[264,2048]{1,0:T(8,128)(2,1)} %fusion.23), channel_id=1, source_target_pairs={{0,2},{1,3},{2,0},{3,1},{4,6},{5,7},{6,4},{7,5},{8,10},{9,11},{10,... | collective-permute-start | bytes 3244040 | tf_op jit(solution)/shard_map/ppermute | solution.py:307
  122.9 49.5 %collective-permute-start.7 = (bf16[264,2048]{1,0:T(8,128)(2,1)}, bf16[264,2048]{1,0:T(8,128)(2,1)}, u32[]{:S(2)}, u32[]{:S(2)}) collective-permute-start(bf16[264,2048]{1,0:T(8,128)(2,1)} %fusion.23), channel_id=1, source_target_pairs={{0,4},{1,5},{2,6},{3,7},{4,0},{5,1},{6,2},{7,3},{8,12},{9,13},{10,... | collective-permute-start | bytes 3244040 | tf_op jit(solution)/shard_map/ppermute | solution.py:307
  124.4 47.9 %collective-permute-start.8 = (bf16[264,2048]{1,0:T(8,128)(2,1)}, bf16[264,2048]{1,0:T(8,128)(2,1)}, u32[]{:S(2)}, u32[]{:S(2)}) collective-permute-start(bf16[264,2048]{1,0:T(8,128)(2,1)} %fusion.23), channel_id=1, source_target_pairs={{0,6},{1,7},{2,4},{3,5},{4,2},{5,3},{6,0},{7,1},{8,14},{9,15},{10,... | collective-permute-start | bytes 3244040 | tf_op jit(solution)/shard_map/ppermute | solution.py:307
  178.4 248.8 %reduce-scatter.5.cloned.1.call-start = ((), (), s32[]{:S(2)}) async-start(), calls=%async_computation.10 | async-start | bytes 3932160 | tf_op jit(solution)/shard_map/reduce_scatter | solution.py:922
  188.6 16.8 %collective-permute-start.11 = (bf16[136,2048]{1,0:T(8,128)(2,1)S(1)}, bf16[136,2048]{1,0:T(8,128)(2,1)S(1)}, u32[]{:S(2)}, u32[]{:S(2)}) collective-permute-start(bf16[136,2048]{1,0:T(8,128)(2,1)S(1)} %slice.385), channel_id=1, source_target_pairs={{0,2},{1,3},{2,0},{3,1},{4,6},{5,7},{6,4},{7,5},{8,10},{9,11},{10,... | collective-permute-start | bytes 1671176 | tf_op jit(solution)/shard_map/ppermute | solution.py:307
  190.4 13.7 %collective-permute-start.10 = (bf16[128,2048]{1,0:T(8,128)(2,1)S(1)}, bf16[128,2048]{1,0:T(8,128)(2,1)S(1)}, u32[]{:S(2)}, u32[]{:S(2)}) collective-permute-start(bf16[128,2048]{1,0:T(8,128)(2,1)S(1)} %slice.378), channel_id=1, source_target_pairs={{0,4},{1,5},{2,6},{3,7},{4,0},{5,1},{6,2},{7,3},{8,12},{9,13},{10,... | collective-permute-start | bytes 1572872 | tf_op jit(solution)/shard_map/ppermute | solution.py:307
  206.9 24.9 %collective-permute-start.12 = (bf16[264,2048]{1,0:T(8,128)(2,1)S(1)}, bf16[264,2048]{1,0:T(8,128)(2,1)S(1)}, u32[]{:S(2)}, u32[]{:S(2)}) collective-permute-start(bf16[264,2048]{1,0:T(8,128)(2,1)S(1)} %pad_maximum_fusion.2), channel_id=1, source_target_pairs={{0,2},{1,3},{2,0},{3,1},{4,6},{5,7},{6,4},{7,5},{8,10},{9,11},{10,... | collective-permute-start | bytes 3244040 | tf_op jit(solution)/shard_map/ppermute | solution.py:307
  207.3 24.6 %collective-permute-start.13 = (bf16[264,2048]{1,0:T(8,128)(2,1)S(1)}, bf16[264,2048]{1,0:T(8,128)(2,1)S(1)}, u32[]{:S(2)}, u32[]{:S(2)}) collective-permute-start(bf16[264,2048]{1,0:T(8,128)(2,1)S(1)} %pad_maximum_fusion.3), channel_id=1, source_target_pairs={{0,4},{1,5},{2,6},{3,7},{4,0},{5,1},{6,2},{7,3},{8,12},{9,13},{10,... | collective-permute-start | bytes 3244040 | tf_op jit(solution)/shard_map/ppermute | solution.py:307
  235.7 24.0 %collective-permute-start.15 = (bf16[264,2048]{1,0:T(8,128)(2,1)S(1)}, bf16[264,2048]{1,0:T(8,128)(2,1)S(1)}, u32[]{:S(2)}, u32[]{:S(2)}) collective-permute-start(bf16[264,2048]{1,0:T(8,128)(2,1)S(1)} %get-tuple-element.186), channel_id=1, source_target_pairs={{0,4},{1,5},{2,6},{3,7},{4,0},{5,1},{6,2},{7,3},{8,12},{9,13},{10,... | collective-permute-start | bytes 3244040 | tf_op jit(solution)/shard_map/ppermute | solution.py:307
  237.1 24.3 %collective-permute-start.14 = (bf16[264,2048]{1,0:T(8,128)(2,1)S(1)}, bf16[264,2048]{1,0:T(8,128)(2,1)S(1)}, u32[]{:S(2)}, u32[]{:S(2)}) collective-permute-start(bf16[264,2048]{1,0:T(8,128)(2,1)S(1)} %get-tuple-element.186), channel_id=1, source_target_pairs={{0,2},{1,3},{2,0},{3,1},{4,6},{5,7},{6,4},{7,5},{8,10},{9,11},{10,... | collective-permute-start | bytes 3244040 | tf_op jit(solution)/shard_map/ppermute | solution.py:307
  237.8 35.9 %collective-permute-start.19 = (bf16[4,264,2048]{2,1,0:T(8,128)(2,1)}, bf16[4,264,2048]{2,1,0:T(8,128)(2,1)}, u32[]{:S(2)}, u32[]{:S(2)}) collective-permute-start(bf16[4,264,2048]{2,1,0:T(8,128)(2,1)} %pad_maximum_fusion.1), channel_id=1, source_target_pairs={{0,1},{1,0},{2,3},{3,2},{4,5},{5,4},{6,7},{7,6},{8,9},{9,8},{10,11... | collective-permute-start | bytes 12976136 | tf_op jit(solution)/shard_map/ppermute | solution.py:307
  259.7 12.1 %collective-permute-start.16 = (bf16[128,2048]{1,0:T(8,128)(2,1)S(1)}, bf16[128,2048]{1,0:T(8,128)(2,1)S(1)}, u32[]{:S(2)}, u32[]{:S(2)}) collective-permute-start(bf16[128,2048]{1,0:T(8,128)(2,1)S(1)} %slice.387), channel_id=1, source_target_pairs={{0,2},{1,3},{2,0},{3,1},{4,6},{5,7},{6,4},{7,5},{8,10},{9,11},{10,... | collective-permute-start | bytes 1572872 | tf_op jit(solution)/shard_map/ppermute | solution.py:307
  273.7 20.3 %collective-permute-start.18 = (bf16[4,264,2048]{2,1,0:T(8,128)(2,1)}, bf16[4,264,2048]{2,1,0:T(8,128)(2,1)}, u32[]{:S(2)}, u32[]{:S(2)}) collective-permute-start(bf16[4,264,2048]{2,1,0:T(8,128)(2,1)} %bitcast.35), channel_id=1, source_target_pairs={{0,1},{1,0},{2,3},{3,2},{4,5},{5,4},{6,7},{7,6},{8,9},{9,8},{10,11... | collective-permute-start | bytes 12976136 | tf_op jit(solution)/shard_map/ppermute | solution.py:307
  333.3 20.6 %collective-permute-start.20 = (bf16[4,264,2048]{2,1,0:T(8,128)(2,1)}, bf16[4,264,2048]{2,1,0:T(8,128)(2,1)}, u32[]{:S(2)}, u32[]{:S(2)}) collective-permute-start(bf16[4,264,2048]{2,1,0:T(8,128)(2,1)} %bitcast.38), channel_id=1, source_target_pairs={{0,1},{1,0},{2,3},{3,2},{4,5},{5,4},{6,7},{7,6},{8,9},{9,8},{10,11... | collective-permute-start | bytes 12976136 | tf_op jit(solution)/shard_map/ppermute | solution.py:307
  343.6 175.0 %reduce-scatter.7.cloned.1.call-start = ((), (), s32[]{:S(2)}) async-start(), calls=%async_computation.11 | async-start | bytes 7864320 | tf_op jit(solution)/shard_map/reduce_scatter | solution.py:922
  356.5 16.8 %collective-permute-start.22 = (bf16[136,2048]{1,0:T(8,128)(2,1)S(1)}, bf16[136,2048]{1,0:T(8,128)(2,1)S(1)}, u32[]{:S(2)}, u32[]{:S(2)}) collective-permute-start(bf16[136,2048]{1,0:T(8,128)(2,1)S(1)} %slice.324), channel_id=1, source_target_pairs={{0,2},{1,3},{2,0},{3,1},{4,6},{5,7},{6,4},{7,5},{8,10},{9,11},{10,... | collective-permute-start | bytes 1671176 | tf_op jit(solution)/shard_map/ppermute | solution.py:307
  357.3 13.6 %collective-permute-start.21 = (bf16[128,2048]{1,0:T(8,128)(2,1)S(1)}, bf16[128,2048]{1,0:T(8,128)(2,1)S(1)}, u32[]{:S(2)}, u32[]{:S(2)}) collective-permute-start(bf16[128,2048]{1,0:T(8,128)(2,1)S(1)} %slice.317), channel_id=1, source_target_pairs={{0,4},{1,5},{2,6},{3,7},{4,0},{5,1},{6,2},{7,3},{8,12},{9,13},{10,... | collective-permute-start | bytes 1572872 | tf_op jit(solution)/shard_map/ppermute | solution.py:307
  375.7 24.9 %collective-permute-start.23 = (bf16[264,2048]{1,0:T(8,128)(2,1)}, bf16[264,2048]{1,0:T(8,128)(2,1)S(1)}, u32[]{:S(2)}, u32[]{:S(2)}) collective-permute-start(bf16[264,2048]{1,0:T(8,128)(2,1)} %pad_maximum_fusion.4), channel_id=1, source_target_pairs={{0,2},{1,3},{2,0},{3,1},{4,6},{5,7},{6,4},{7,5},{8,10},{9,11},{10,... | collective-permute-start | bytes 3244040 | tf_op jit(solution)/shard_map/ppermute | solution.py:307
  377.0 24.7 %collective-permute-start.24 = (bf16[264,2048]{1,0:T(8,128)(2,1)}, bf16[264,2048]{1,0:T(8,128)(2,1)}, u32[]{:S(2)}, u32[]{:S(2)}) collective-permute-start(bf16[264,2048]{1,0:T(8,128)(2,1)} %pad_maximum_fusion.5), channel_id=1, source_target_pairs={{0,4},{1,5},{2,6},{3,7},{4,0},{5,1},{6,2},{7,3},{8,12},{9,13},{10,... | collective-permute-start | bytes 3244040 | tf_op jit(solution)/shard_map/ppermute | solution.py:307
  408.8 180.6 %reduce-scatter.9.cloned.1.call-start = ((), (), s32[]{:S(2)}) async-start(), calls=%async_computation.12 | async-start | bytes 3276800 | tf_op jit(solution)/shard_map/reduce_scatter | solution.py:922
  412.3 23.7 %collective-permute-start.25 = (bf16[264,2048]{1,0:T(8,128)(2,1)}, bf16[264,2048]{1,0:T(8,128)(2,1)S(1)}, u32[]{:S(2)}, u32[]{:S(2)}) collective-permute-start(bf16[264,2048]{1,0:T(8,128)(2,1)} %get-tuple-element.184), channel_id=1, source_target_pairs={{0,2},{1,3},{2,0},{3,1},{4,6},{5,7},{6,4},{7,5},{8,10},{9,11},{10,... | collective-permute-start | bytes 3244040 | tf_op jit(solution)/shard_map/ppermute | solution.py:307
  413.0 23.6 %collective-permute-start.26 = (bf16[264,2048]{1,0:T(8,128)(2,1)}, bf16[264,2048]{1,0:T(8,128)(2,1)}, u32[]{:S(2)}, u32[]{:S(2)}) collective-permute-start(bf16[264,2048]{1,0:T(8,128)(2,1)} %get-tuple-element.184), channel_id=1, source_target_pairs={{0,4},{1,5},{2,6},{3,7},{4,0},{5,1},{6,2},{7,3},{8,12},{9,13},{10,... | collective-permute-start | bytes 3244040 | tf_op jit(solution)/shard_map/ppermute | solution.py:307
  439.0 17.3 %collective-permute-start.30 = (bf16[4,264,2048]{2,1,0:T(8,128)(2,1)}, bf16[4,264,2048]{2,1,0:T(8,128)(2,1)S(1)}, u32[]{:S(2)}, u32[]{:S(2)}) collective-permute-start(bf16[4,264,2048]{2,1,0:T(8,128)(2,1)} %bitcast.259), channel_id=1, source_target_pairs={{0,1},{1,0},{2,3},{3,2},{4,5},{5,4},{6,7},{7,6},{8,9},{9,8},{10,11... | collective-permute-start | bytes 12976136 | tf_op jit(solution)/shard_map/ppermute | solution.py:307
  439.1 15.1 %collective-permute-start.28 = (bf16[136,2048]{1,0:T(8,128)(2,1)S(1)}, bf16[136,2048]{1,0:T(8,128)(2,1)S(1)}, u32[]{:S(2)}, u32[]{:S(2)}) collective-permute-start(bf16[136,2048]{1,0:T(8,128)(2,1)S(1)} %slice.328), channel_id=1, source_target_pairs={{0,4},{1,5},{2,6},{3,7},{4,0},{5,1},{6,2},{7,3},{8,12},{9,13},{10,... | collective-permute-start | bytes 1671176 | tf_op jit(solution)/shard_map/ppermute | solution.py:307
  462.7 65.4 %collective-permute-start.32 = (bf16[264,2048]{1,0:T(8,128)(2,1)}, bf16[264,2048]{1,0:T(8,128)(2,1)}, u32[]{:S(2)}, u32[]{:S(2)}) collective-permute-start(bf16[264,2048]{1,0:T(8,128)(2,1)} %get-tuple-element.151), channel_id=1, source_target_pairs={{0,2},{1,3},{2,0},{3,1},{4,6},{5,7},{6,4},{7,5},{8,10},{9,11},{10,... | collective-permute-start | bytes 3244040 | tf_op jit(solution)/shard_map/ppermute | solution.py:307
  463.5 64.6 %collective-permute-start.33 = (bf16[264,2048]{1,0:T(8,128)(2,1)}, bf16[264,2048]{1,0:T(8,128)(2,1)}, u32[]{:S(2)}, u32[]{:S(2)}) collective-permute-start(bf16[264,2048]{1,0:T(8,128)(2,1)} %get-tuple-element.152), channel_id=1, source_target_pairs={{0,4},{1,5},{2,6},{3,7},{4,0},{5,1},{6,2},{7,3},{8,12},{9,13},{10,... | collective-permute-start | bytes 3244040 | tf_op jit(solution)/shard_map/ppermute | solution.py:307
  464.9 63.2 %collective-permute-start.34 = (bf16[264,2048]{1,0:T(8,128)(2,1)}, bf16[264,2048]{1,0:T(8,128)(2,1)}, u32[]{:S(2)}, u32[]{:S(2)}) collective-permute-start(bf16[264,2048]{1,0:T(8,128)(2,1)} %get-tuple-element.153), channel_id=1, source_target_pairs={{0,6},{1,7},{2,4},{3,5},{4,2},{5,3},{6,0},{7,1},{8,14},{9,15},{10,... | collective-permute-start | bytes 3244040 | tf_op jit(solution)/shard_map/ppermute | solution.py:307
  528.2 17.8 %collective-permute-start.35 = (bf16[4,264,2048]{2,1,0:T(8,128)(2,1)}, bf16[4,264,2048]{2,1,0:T(8,128)(2,1)}, u32[]{:S(2)}, u32[]{:S(2)}) collective-permute-start(bf16[4,264,2048]{2,1,0:T(8,128)(2,1)} %bitcast.231), channel_id=1, source_target_pairs={{0,1},{1,0},{2,3},{3,2},{4,5},{5,4},{6,7},{7,6},{8,9},{9,8},{10,11... | collective-permute-start | bytes 12976136 | tf_op jit(solution)/shard_map/ppermute | solution.py:307
  529.6 53.5 %all-to-all-start.3 = ((bf16[8,64,1536]{2,1,0:T(8,128)(2,1)}), bf16[8,64,1536]{2,1,0:T(8,128)(2,1)}, u32[]{:S(2)}, u32[]{:S(2)}) async-start(bf16[8,64,1536]{2,1,0:T(8,128)(2,1)} %bitcast.241), calls=%async_computation.7 | async-start | bytes 3145728 | tf_op jit(solution)/shard_map/all_to_all | solution.py:930
  533.9 86.2 %reduce-scatter.11.cloned.1.call-start = ((), (), s32[]{:S(2)}) async-start(), calls=%async_computation.13 | async-start | bytes 1945600 | tf_op jit(solution)/shard_map/reduce_scatter | solution.py:922
  558.0 19.1 %collective-permute-start.40 = (bf16[2,80,2432]{2,1,0:T(8,128)(2,1)S(1)}, bf16[2,80,2432]{2,1,0:T(8,128)(2,1)S(1)}, u32[]{:S(2)}, u32[]{:S(2)}) collective-permute-start(bf16[2,80,2432]{2,1,0:T(8,128)(2,1)S(1)} %get-tuple-element.195), channel_id=1, source_target_pairs={{0,1},{1,0},{2,3},{3,2},{4,5},{5,4},{6,7},{7,6},{8,9},{9,8},{10,11... | collective-permute-start | bytes 2334728 | tf_op jit(solution)/shard_map/ppermute | solution.py:307
  558.9 19.6 %collective-permute-start.37 = (bf16[136,2048]{1,0:T(8,128)(2,1)S(1)}, bf16[136,2048]{1,0:T(8,128)(2,1)S(1)}, u32[]{:S(2)}, u32[]{:S(2)}) collective-permute-start(bf16[136,2048]{1,0:T(8,128)(2,1)S(1)} %copy-done.16), channel_id=1, source_target_pairs={{0,2},{1,3},{2,0},{3,1},{4,6},{5,7},{6,4},{7,5},{8,10},{9,11},{10,... | collective-permute-start | bytes 1671176 | tf_op jit(solution)/shard_map/ppermute | solution.py:307
  560.8 13.7 %collective-permute-start.36 = (bf16[128,2048]{1,0:T(8,128)(2,1)S(1)}, bf16[128,2048]{1,0:T(8,128)(2,1)S(1)}, u32[]{:S(2)}, u32[]{:S(2)}) collective-permute-start(bf16[128,2048]{1,0:T(8,128)(2,1)S(1)} %copy-done.17), channel_id=1, source_target_pairs={{0,4},{1,5},{2,6},{3,7},{4,0},{5,1},{6,2},{7,3},{8,12},{9,13},{10,... | collective-permute-start | bytes 1572872 | tf_op jit(solution)/shard_map/ppermute | solution.py:307
  581.1 27.0 %collective-permute-start.38 = (bf16[264,2048]{1,0:T(8,128)(2,1)}, bf16[264,2048]{1,0:T(8,128)(2,1)S(1)}, u32[]{:S(2)}, u32[]{:S(2)}) collective-permute-start(bf16[264,2048]{1,0:T(8,128)(2,1)} %pad_maximum_fusion.6), channel_id=1, source_target_pairs={{0,2},{1,3},{2,0},{3,1},{4,6},{5,7},{6,4},{7,5},{8,10},{9,11},{10,... | collective-permute-start | bytes 3244040 | tf_op jit(solution)/shard_map/ppermute | solution.py:307
  581.5 27.7 %collective-permute-start.39 = (bf16[264,2048]{1,0:T(8,128)(2,1)}, bf16[264,2048]{1,0:T(8,128)(2,1)S(1)}, u32[]{:S(2)}, u32[]{:S(2)}) collective-permute-start(bf16[264,2048]{1,0:T(8,128)(2,1)} %pad_maximum_fusion.7), channel_id=1, source_target_pairs={{0,4},{1,5},{2,6},{3,7},{4,0},{5,1},{6,2},{7,3},{8,12},{9,13},{10,... | collective-permute-start | bytes 3244040 | tf_op jit(solution)/shard_map/ppermute | solution.py:307
  589.4 26.7 %all-to-all-start.2 = ((bf16[8,64,640]{2,1,0:T(8,128)(2,1)}), bf16[8,64,640]{2,1,0:T(8,128)(2,1)}, u32[]{:S(2)}, u32[]{:S(2)}) async-start(bf16[8,64,640]{2,1,0:T(8,128)(2,1)} %bitcast.247), calls=%async_computation.5 | async-start | bytes 1310720 | tf_op jit(solution)/shard_map/all_to_all | solution.py:930
  (43 other events, 548.3 us)
Sparse Core Ops, SparseCore 0:
  13.2 39.5 all-gather.11
  58.2 52.7 all-gather.7
  112.6 62.2 all-gather.13
  178.5 114.3 all-gather.9
  343.7 59.2 reduce-scatter.4
  408.9 109.6 reduce-scatter.6
  529.7 52.6 reduce-scatter.8
  584.7 34.8 reduce-scatter.10
